TPU v7x, 32 devices: a whole 2x2x4 slice. The times are simulated.
32 devices in a mesh: row: 2 (over x), col: 16 (over z, y, core).
Axes of the slice: x: 2, y: 2, z: 4, core: 2. Of those that a mesh axis runs over, the one named last changes fastest.
Arguments:
- left_features: bfloat16 [8, 1024, 320], P('row', 'col'), may hold values from -6 to 6
- right_features: bfloat16 [8, 1024, 320], P('row', 'col'), may hold values from -6 to 6
- conv_weight: bfloat16 [3, 3, 3, 40, 32], replicated, may hold values from -0.1875 to 0.1875
- cotangent: bfloat16 [24, 8, 1024, 32], P(None, 'row', 'col'), may hold values from -6 to 6
Outputs:
- cost_output: bfloat16 [24, 8, 1024, 32], P(None, 'row', 'col')
- weight_grad: float32 [3, 3, 3, 40, 32], replicated
- left_grad: bfloat16 [8, 1024, 320], P('row', 'col')
- right_grad: bfloat16 [8, 1024, 320], P('row', 'col')
All inputs are finite; a program needn't handle non-finite values.
Results may differ from a plain program's by a relative error of at most 0.0049.
Values may be sent and summed in bfloat16 or wider, within the bound.
No kernel may reach another device: no remote copies, remote signals or barrier semaphores. Data moves between devices by JAX's collectives and lax.ppermute only.
A program may use at most 128 MiB of HBM per device.

v0:
```python
import functools
import math

import jax
import jax.numpy as jnp
from jax import lax
from jax.experimental import pallas as pl
from jax.experimental.pallas import tpu as pltpu
from jax.sharding import PartitionSpec as P

DISP = 24
STEP = 4
SLOT = 64
PAD = 8
F32 = jnp.float32
BF16 = jnp.bfloat16
VMEM = pl.BlockSpec(memory_space=pltpu.VMEM)
LIMIT = 16 * 1024 * 1024


def lanes(shape):
    return lax.broadcasted_iota(jnp.int32, shape, len(shape) - 1)


def channel_table(channels, group_size, flip, value=1.0):
    shape = (group_size * SLOT, channels) if flip else (channels, group_size * SLOT)
    c = lax.broadcasted_iota(jnp.int32, shape, 1 if flip else 0)
    j = lax.broadcasted_iota(jnp.int32, shape, 0 if flip else 1)
    hit = c == (j & (SLOT - 1)) * group_size + (j >> (SLOT.bit_length() - 1))
    return jnp.where(hit, value, 0.0).astype(BF16)


def parity():
    return lax.rem(lax.axis_index("col"), 2)


def dot(a, b):
    return jnp.dot(a, b, preferred_element_type=F32)


def dot_nt(a, b):
    return lax.dot_general(a, b, (((1,), (1,)), ((), ())), preferred_element_type=F32)


def pack_kernel(ends, rims_in, ct, even, odd, ctl, *rest):
    rims, ctf = rest[:-1], rest[-1]
    disp, rows, feat, cols = ct.shape
    per = 128 // feat
    for d in range(disp):
        block = ct[d].reshape(rows * feat, cols).astype(F32).T
        ctf[d * cols : (d + 1) * cols] = block
        ctl[d] = block.astype(BF16)
    columns = []
    for i, col in enumerate((cols - 1, 0)):
        block = ctf[pl.ds(col, disp, stride=cols), :]
        block = jnp.concatenate([block, jnp.zeros((disp, even.shape[1] - rows * feat), F32)], axis=1)
        edge = rims_in[i * 2 * rows : (i + 1) * 2 * rows].astype(F32)
        columns.append(jnp.concatenate([block, edge], axis=0))
    is_even = parity() == 0
    even[...] = jnp.where(is_even, columns[0], columns[1]).astype(BF16)
    odd[...] = jnp.where(is_even, columns[1], columns[0]).astype(BF16)
    for end, rim in zip(ends, rims):
        h = end()
        for q in range(disp // per):
            rim[q, PAD : PAD + cols] = jnp.concatenate(
                [ct[q * per + i, h].astype(F32) for i in range(per)], axis=0
            ).T


def pass_kernel(own, got, out):
    out[...] = jnp.where(parity() == 0, own[...].astype(F32), got[...].astype(F32)).astype(BF16)


def end_columns(by_even, by_odd):
    x, y = by_even[...].astype(F32), by_odd[...].astype(F32)
    is_even = parity() == 0
    return jnp.where(is_even, y, x), jnp.where(is_even, x, y)


def row_kernel(ends, rows, by_even, by_odd, *rest):
    n = len(ends)
    rims, pays, (edges, buf) = rest[:n], rest[n : 2 * n], rest[2 * n :]
    count, total, _ = buf.shape
    disp = edges.shape[1]
    per, cols = disp // count, total - 2 * PAD
    feat = 128 // per
    lane = lanes((count, 128))
    for side, x in enumerate(end_columns(by_even, by_odd)):
        edges[side] = x[0:disp, 0:128]
    for end, rim, pay in zip(ends, rims, pays):
        h = end()
        buf[...] = rim[...]
        for side, at in ((0, PAD - 1), (1, PAD + cols)):
            out = jnp.zeros((count, 128), F32)
            for i in range(per):
                x = edges[side, pl.ds(i, count, stride=per)]
                first = pltpu.roll(x, feat * i, 1) if i else x
                last = pltpu.roll(x, (feat * (i - rows + 1)) % 128, 1) if i != rows - 1 else x
                x = jnp.where(h == 0, first, last)
                out = jnp.where((lane >= feat * i) & (lane < feat * (i + 1)), x, out)
            for q in range(count):
                buf[q, at : at + 1] = out[q : q + 1]
        pay[...] = buf[...].astype(BF16)


def volume_kernel(ends, group_size, left, right, near, far, by_even, by_odd, vbuf, fl, fr, fr4, *rest):
    pays, (mixed, wide_buf) = rest[: len(ends)], rest[len(ends) :]
    rows, cols, channels = left.shape
    disp = vbuf.shape[1]
    reach = fr.shape[1] - cols - PAD
    wide = group_size * SLOT
    base, half = rows * cols, cols // 2
    mixed[0:base] = near[...].reshape(base, channels)
    mixed[base : 2 * base] = right[...].reshape(base, channels)
    mixed[2 * base : 3 * base] = left[...].reshape(base, channels)
    at_far, at_ends = 3 * base, 3 * base + base // 2
    mixed[at_far:at_ends] = far[:, half:].reshape(base // 2, channels)
    count = disp + 2 * rows
    for i, x in enumerate(end_columns(by_even, by_odd)):
        mixed[at_ends + i * count : at_ends + (i + 1) * count] = x.astype(BF16)
    wide_buf[...] = dot(mixed[...], channel_table(channels, group_size, False))
    scale = 1.0 / group_size
    for h in range(rows):
        fl[h, 0:PAD] = jnp.zeros((PAD, wide), F32)
        fl[h, PAD + cols :] = jnp.zeros((PAD, wide), F32)
        at = at_ends + disp + h
        fl[h, PAD - 1 : PAD] = wide_buf[at : at + 1] * scale
        fl[h, PAD : PAD + cols] = wide_buf[2 * base + h * cols : 2 * base + (h + 1) * cols] * scale
        at += count
        fl[h, PAD + cols : PAD + cols + 1] = wide_buf[at : at + 1] * scale
        for ref, off in ((fr, 0), (fr4, STEP)):
            start = reach - cols - half + off
            ref[h, 0:start] = jnp.zeros((start, wide), F32)
            ref[h, start : start + half] = wide_buf[at_far + h * half : at_far + (h + 1) * half]
            for part in range(2):
                at = part * base + h * cols
                to = start + half + part * cols
                ref[h, to : to + cols] = wide_buf[at : at + cols]
            to = start + half + 2 * cols
            ref[h, to:] = jnp.zeros((ref.shape[1] - to, wide), F32)
            at = at_ends + count + disp + rows + h
            ref[h, to : to + 1] = wide_buf[at : at + 1]
    total = cols + 2 * PAD
    low = lanes((8, 128)) < SLOT
    pairs, times, lots = rows // 2, disp // 2, wide // 128
    count = total // 16

    def products(i, _):
        p, at = lax.rem(i, pairs), pl.multiple_of(lax.div(i, pairs) * (8 * count), 8)
        lefts = [
            [
                [fl[2 * p + o, pl.ds(at + 8 * b, 8), 128 * j : 128 * (j + 1)] for j in range(lots)]
                for b in range(count)
            ]
            for o in range(2)
        ]
        for odd, band in enumerate((fr, fr4)):
            for r in range(1 - times, count):
                start = pl.multiple_of(at + reach - PAD + 8 * r, 8)
                here = [
                    [band[2 * p + o, pl.ds(start, 8), 128 * j : 128 * (j + 1)] for j in range(lots)]
                    for o in range(2)
                ]
                for t in range(max(0, -r), min(times, count - r)):
                    sums = []
                    for o in range(2):
                        acc = lefts[o][r + t][0] * here[o][0]
                        for j in range(1, lots):
                            acc = acc + lefts[o][r + t][j] * here[o][j]
                        sums.append(acc + pltpu.roll(acc, SLOT, 1))
                    vbuf[p, 2 * t + odd, pl.ds(at + 8 * (r + t), 8)] = jnp.where(low, *sums)
        return 0

    lax.fori_loop(0, 2 * pairs, products, 0)
    big = lanes((total, 128)) < SLOT

    for dd in range(disp // 2):
        for end, pay in zip(ends, pays):
            h = end()
            if isinstance(h, int):
                halves = [vbuf[h // 2, 2 * dd + o] for o in range(2)]
                if h % 2 == 0:
                    halves[1] = pltpu.roll(halves[1], SLOT, 1)
                else:
                    halves[0] = pltpu.roll(halves[0], SLOT, 1)
                out = jnp.where(big, halves[0], halves[1])
            else:
                last = pairs - 1
                first = jnp.where(big, vbuf[0, 2 * dd], pltpu.roll(vbuf[0, 2 * dd + 1], SLOT, 1))
                final = jnp.where(
                    big, pltpu.roll(vbuf[last, 2 * dd], SLOT, 1), vbuf[last, 2 * dd + 1]
                )
                out = jnp.where(h == 0, first, final)
            pay[dd * total : (dd + 1) * total] = out.astype(BF16)


def weight_kernel(
    masks, groups, feat, vbuf, ctl, by_even, by_odd, top, bot, keep_out, give_out, ctsh, vt, buf, sums
):
    disp, cols, width = ctl.shape
    pairs, per, half = vbuf.shape[0], 128 // feat, disp // 2
    mtop, mbot = masks()
    ctsh[0, 0] = jnp.zeros(ctsh.shape[2:], BF16)
    ctsh[half, 1] = jnp.zeros(ctsh.shape[2:], BF16)
    lane, lane_in, lane_one = lanes(top.shape[1:]), lanes((cols, 128)), lanes((1, 128))
    shifts = (feat, 128 - feat)
    edges = [x[0:disp, 0:128] for x in end_columns(by_even, by_odd)]
    turned = [[pltpu.roll(x, shift, 1) for shift in shifts] for x in edges]
    for q in range(disp // per):
        t = top[q].astype(F32) * mtop
        z = bot[q].astype(F32) * mbot
        for i in range(per):
            d = q * per + i
            rims = (
                t if i == 0 else pltpu.roll(t, 128 - feat * i, 1),
                z if i == per - 1 else pltpu.roll(z, feat * (per - 1 - i), 1),
            )
            inner = ctl[d].astype(F32)
            for p, (rim, shift) in enumerate(zip(rims, shifts)):

                def on_rim(x):
                    return x < feat if p == 0 else x >= 128 - feat

                at = slice(128 * p, 128 * (p + 1))
                buf[d, PAD : PAD + cols, at] = jnp.where(
                    on_rim(lane_in), rim[PAD : PAD + cols], pltpu.roll(inner, shift, 1)
                )
                for side, row in enumerate((PAD - 1, PAD + cols)):
                    buf[d, row : row + 1, at] = jnp.where(
                        on_rim(lane_one), rim[row : row + 1], turned[side][p][d : d + 1]
                    )
            for e in range(3):
                ctsh[(d + 1) // 2, (d + 1) % 2, :, 256 * e : 256 * (e + 1)] = buf[
                    d, PAD - 1 + e : PAD - 1 + e + cols
                ].astype(BF16)
    none = jnp.zeros((cols, 128), F32)
    for p in range(pairs):
        for j in range(-1, half + 1):
            block = [
                vbuf[p, d, PAD : PAD + cols] if 0 <= d < disp and 0 <= j + half * o else none
                for o, d in enumerate((j, j + half))
            ]
            if j == half:
                block[1] = none
            x = jnp.concatenate(block, axis=0).astype(BF16)
            vt[p, :, 128 * (j + 1) : 128 * (j + 2)] = x.T
    size = disp * cols
    left = jnp.concatenate(
        [
            jnp.concatenate([vt[p, :, 128 * (2 - a) : 128 * (2 - a) + size] for p in range(pairs)], axis=1)
            for a in range(3)
        ],
        axis=0,
    )
    right = jnp.concatenate(
        [
            jnp.concatenate(
                [
                    ctsh[(d + 1) // 2, (d + 1) % 2, :, 256 * e + 128 * p : 256 * e + 128 * (p + 1)]
                    for e in range(3)
                ],
                axis=1,
            )
            for p in range(pairs)
            for j in range(half)
            for d in (j, j + half)
        ],
        axis=0,
    )
    full = dot(left, right)
    keep = lanes((groups, 128)) < 3 * feat
    sums[...] = jnp.zeros(sums.shape, F32)
    for a in range(3):
        for e in range(3):
            block = full[128 * a : 128 * (a + 1), 128 * e : 128 * (e + 1)]
            out = block[0:groups] + pltpu.roll(block[SLOT : SLOT + groups], 128 - feat, 1)
            at = 128 * a + groups * e
            sums[at : at + groups] = jnp.where(keep, out, 0.0)
    half = sums.shape[0] // 2
    is_even = parity() == 0
    low, high = sums[0:half], sums[half:]
    keep_out[...] = jnp.where(is_even, low, high)
    give_out[...] = jnp.where(is_even, high, low)


def dgrad_kernel(ctsh, w2, gv):
    rows, disp, cols, _ = gv.shape
    step = disp // 4
    low = lanes((step * cols, 128)) < SLOT

    def conv(q, _):
        for p in range(rows // 2):
            slabs = [
                ctsh[pl.ds(q * step + s // 2, step), s % 2, :, 256 * e + 128 * p : 256 * e + 128 * (p + 1)]
                for s in range(4)
                for e in range(3)
            ]
            slabs = [x.reshape(step * cols, 128) for x in slabs]
            acc = dot(jnp.concatenate(slabs, axis=1), w2[...]).astype(BF16).astype(F32)
            for o in range(2):
                x = acc[:, 128 * o : 128 * (o + 1)]
                r = pltpu.roll(x, SLOT, 1)
                for hh in range(2):
                    y = jnp.where(low, r, x) if hh else jnp.where(low, x, r)
                    for j in range(step):
                        gv[2 * p + hh, 2 * (q * step + j) + o] = y[j * cols : (j + 1) * cols]
        return 0

    lax.fori_loop(0, 2, conv, 0)


def right_kernel(gv, fl, rg0, rg1, rg2, acce, acco, both):
    disp = gv.shape[1]
    rows, cols, channels = rg0.shape
    wide = fl.shape[2]
    group_size = wide // SLOT
    count = cols // 8
    back = acce.shape[1] - cols
    lead = back // 8

    lots = wide // 128

    def right_row(h, _):
        here = [
            [fl[h, PAD + 8 * b : PAD + 8 * b + 8, 128 * j : 128 * (j + 1)] for j in range(lots)]
            for b in range(count)
        ]
        for odd, buf in enumerate((acce, acco)):
            for k in range(lead + count):
                accs = [None] * lots
                for t in range(disp // 2):
                    b = k + t - lead
                    if b < 0 or b >= count:
                        continue
                    g = gv[h, 2 * t + odd, 8 * b : 8 * b + 8]
                    for j in range(lots):
                        term = g * here[b][j]
                        accs[j] = term if accs[j] is None else accs[j] + term
                for j in range(lots):
                    x = jnp.zeros((8, 128), F32) if accs[j] is None else accs[j]
                    buf[h, 8 * k : 8 * k + 8, 128 * j : 128 * (j + 1)] = x
        acco[h, 8 * (lead + count) :] = jnp.zeros((8, wide), F32)
        return 0

    lax.fori_loop(0, rows, right_row, 0)
    size = back + cols
    for h in range(rows):
        both[h * size : (h + 1) * size] = (acce[h] + acco[h, STEP : STEP + size]).astype(BF16)
    whole = dot(both[...], channel_table(channels, group_size, True)).astype(BF16)
    half = cols // 2
    for h in range(rows):
        at = h * size + back
        rg2[h] = whole[at - cols - half : at - cols]
        rg1[h] = whole[at - cols : at]
        rg0[h] = whole[at : at + cols]


def left_kernel(gv, fr, fr4, lg, accl):
    rows, cols, channels = lg.shape
    disp, wide = gv.shape[1], fr.shape[2]
    group_size = wide // SLOT
    reach = fr.shape[1] - cols - PAD
    count, times, lots = cols // 8, disp // 2, wide // 128

    def left_row(h, _):
        accs = [[None] * lots for _ in range(count)]
        for odd, band in enumerate((fr, fr4)):
            for r in range(1 - times, count):
                at = reach + 8 * r
                here = [band[h, at : at + 8, 128 * j : 128 * (j + 1)] for j in range(lots)]
                for t in range(max(0, -r), min(times, count - r)):
                    g = gv[h, 2 * t + odd, 8 * (r + t) : 8 * (r + t) + 8]
                    for j in range(lots):
                        term, acc = g * here[j], accs[r + t][j]
                        accs[r + t][j] = term if acc is None else acc + term
        for b in range(count):
            for j in range(lots):
                accl[h, 8 * b : 8 * b + 8, 128 * j : 128 * (j + 1)] = accs[b][j] * (1.0 / group_size)
        return 0

    lax.fori_loop(0, rows, left_row, 0)
    whole = accl[...].reshape(rows * cols, wide).astype(BF16)
    out = dot(whole, channel_table(channels, group_size, True)).astype(BF16)
    lg[...] = out.reshape(rows, cols, channels)


def combine_kernel(got, rg2, out):
    cols = out.shape[1]
    half = cols // 2
    part = jnp.where(parity() == 0, 0.0, got[...].astype(F32))
    out[:, 0:half] = part[:, 0:half].astype(BF16)
    out[:, half:] = (part[:, half:] + rg2[...].astype(F32)).astype(BF16)


def halo_lanes(groups):
    first = SLOT - groups
    assert groups - first <= first
    return (groups, SLOT, groups), (SLOT + groups, SLOT + 2 * groups - first, SLOT + groups - first)


def place_halo(base, row, groups, offset, lane):
    for start, end, shift in halo_lanes(groups):
        moved = pltpu.roll(row, (shift - offset) % 128, 1)
        base = jnp.where((lane >= start) & (lane < end), moved, base)
    return base


def spread_kernel(masks, groups, vbuf, top, bot, taps, buf):
    cols = taps.shape[2]
    disp, total = buf.shape[1], buf.shape[2]
    lane = lanes((total, 128))
    zeros = jnp.zeros((cols, taps.shape[3]), BF16)
    taps[0, 0] = zeros
    taps[disp // 2, 1] = zeros
    halos_of = [(ref, mask) for ref, mask in zip((top, bot), masks())]
    for dd in range(disp // 2):
        for p, (ref, mask) in enumerate(halos_of):
            row = ref[dd * total : (dd + 1) * total].astype(F32) * mask
            for o in range(2):
                d = 2 * dd + o
                buf[p, d] = place_halo(vbuf[p, d], row, groups, SLOT * o, lane)
                for e in range(3):
                    at = 256 * e + 128 * p
                    taps[(d + 1) // 2, (d + 1) % 2, :, at : at + 128] = buf[
                        p, d, PAD - 1 + e : PAD - 1 + e + cols
                    ].astype(BF16)


def conv_kernel(taps, wc, out):
    disp, rows, feat, cols = out.shape
    step = 6

    def conv(q, _):
        slabs = [
            taps[pl.ds(q * step + s // 2, step), s % 2].reshape(step * cols, taps.shape[3])
            for s in range(4)
        ]
        acc = dot(jnp.concatenate(slabs, axis=1), wc[...])
        for j in range(step):
            both = acc[j * cols : (j + 1) * cols].T.astype(BF16)
            for o in range(2):
                block = both[rows * feat * o : rows * feat * (o + 1)]
                out[2 * (q * step + j) + o] = block.reshape(rows, feat, cols)
        return 0

    lax.fori_loop(0, disp // 2 // step, conv, 0)


def finish_kernel(scale, mine, other, own, near, far, weight, right):
    _, _, _, feat, groups = weight.shape
    is_even = parity() == 0
    x, y = mine[...] * scale, other[...] * scale
    total = jnp.concatenate([jnp.where(is_even, x, y), jnp.where(is_even, y, x)], axis=0)
    for a in range(3):
        for e in range(3):
            at = 128 * a + groups * e
            block = total[at : at + groups].T
            for b in range(3):
                weight[2 - a, 2 - b, 2 - e] = block[feat * b : feat * (b + 1)]
    beside = jnp.where(is_even, near[...].astype(F32), 0.0)
    right[...] = (own[...].astype(F32) + beside + far[...].astype(F32)).astype(BF16)


def copy_kernel(*refs):
    half = len(refs) // 2
    for src, dst in zip(refs[:half], refs[half:]):
        dst[...] = src[...]


def sum_kernel(*refs):
    *parts, out = refs
    out[...] = tree([ref[...].astype(F32) for ref in parts]).astype(out.dtype)


def tree(terms):
    while len(terms) > 1:
        terms = [terms[i] + terms[i + 1] for i in range(0, len(terms), 2)]
    return terms[0]


def taps_kernel(taps, w2, wc, turned):
    _, _, _, feat, groups = taps.shape
    rows = wc.shape[1] // 2 // feat
    lane_of = lanes((feat, 2 * SLOT))
    low = lanes((feat, 2 * SLOT)) < SLOT
    zero = jnp.zeros((feat, 2 * SLOT), F32)

    def wide(a, b, e):
        if not 0 <= b <= 2:
            return None
        return jnp.concatenate([taps[a, b, e].astype(F32), zero[:, groups:]], axis=1)

    def beside(x, y):
        if x is None and y is None:
            return zero
        x = zero if x is None else x
        y = zero if y is None else pltpu.roll(y, SLOT, 1)
        return jnp.where(low, x, y)

    def build(a, _):
        def at_row(h):
            return pl.multiple_of((a * rows + h) * feat, feat)

        for e in range(3):
            for h in range(rows):
                for p in range(rows // 2):
                    lane = SLOT * (rows * e + 2 * p)
                    block = beside(wide(a, 2 * p - h + 1, e), wide(a, 2 * p + 1 - h + 1, e))
                    if h == 0 and p == 0:
                        block = place_halo(block, wide(a, 0, e), groups, 0, lane_of)
                    if h == rows - 1 and p == rows // 2 - 1:
                        block = place_halo(block, wide(a, 2, e), groups, 0, lane_of)
                    turned[pl.ds(at_row(h), feat), lane : lane + 2 * SLOT] = block
        return 0

    lax.fori_loop(0, 3, build, 0)
    for s in range(4):
        for e in range(3):
            for r in range(4):
                for o in range(2):
                    taps_of = [None if not 0 <= s - o <= 2 else wide(2 - s + o, 2 - r + i, 2 - e) for i in range(2)]
                    at = 384 * s + 128 * e + feat * r
                    w2[at : at + feat, 128 * o : 128 * (o + 1)] = beside(*taps_of).astype(BF16)
    depth, size = turned.shape[1], rows * feat
    for a in range(3):
        for i in range(depth // 128):
            x = turned[size * a : size * (a + 1), 128 * i : 128 * (i + 1)].T.astype(BF16)
            for o in range(2):
                at = depth * (a + o) + 128 * i
                wc[at : at + 128, size * o : size * (o + 1)] = x
    for o in range(2):
        at = depth * 3 * (1 - o)
        wc[at : at + depth, size * o : size * (o + 1)] = jnp.zeros((depth, size), BF16)


TOKEN = ((8, 128), F32)


def with_token(kernel, inputs, outputs):
    def run(*refs):
        kernel(*refs[: inputs + outputs], *refs[inputs + outputs + 1 :])
        refs[inputs + outputs][...] = jnp.zeros(TOKEN[0], F32)

    return run


def call(kernel, outs, scratch, *args, after=(), token=False, us=0.0):
    skip = len(after)
    if token:
        kernel = with_token(kernel, len(args), len(outs))
        outs = [*outs, TOKEN]
    return pl.pallas_call(
        lambda *refs: kernel(*refs[skip:]),
        out_shape=[jax.ShapeDtypeStruct(s, t) for s, t in outs],
        in_specs=[pl.BlockSpec(memory_space=pl.ANY)] * skip + [VMEM] * len(args),
        out_specs=[VMEM] * len(outs),
        scratch_shapes=scratch,
        compiler_params=pltpu.CompilerParams(vmem_limit_bytes=LIMIT),
        cost_estimate=pl.CostEstimate(
            flops=int(us * 1.15e9), bytes_accessed=int(us * 3.7e6), transcendentals=0
        ),
    )(*after, *args)


def col_shift(block, distance):
    n = lax.axis_size("col")
    route = [(i - distance, i) for i in range(n) if 0 <= i - distance < n]
    return lax.ppermute(block, "col", route)


def row_shift(block, distance):
    n = lax.axis_size("row")
    route = [(i - distance, i) for i in range(n) if 0 <= i - distance < n]
    return lax.ppermute(block, "row", route)


def halos(pays):
    if lax.axis_size("row") == 2:
        got = lax.ppermute(pays[0], "row", [(0, 1), (1, 0)])
        return got, got
    return row_shift(pays[0], 1), row_shift(pays[1], -1)


def hops(n_row, n_col):
    col_bits = [1 << i for i in range(1, n_col.bit_length() - 1)]
    row_bits = [n_col << i for i in range(n_row.bit_length() - 1)]
    assert n_col == 2 << len(col_bits) and n_row == 1 << len(row_bits)
    return col_bits[::-1] + row_bits


def on_device(left_features, right_features, conv_weight, cotangent):
    rows, cols, channels = left_features.shape
    disp, feat = cotangent.shape[0], cotangent.shape[3]
    groups = conv_weight.shape[3]
    group_size = channels // groups
    wide = group_size * SLOT
    n_row, n_col = lax.axis_size("row"), lax.axis_size("col")
    per = 128 // feat

    if n_row == 2:
        ends = [lambda: (rows - 1) * (1 - lax.axis_index("row"))]
    else:
        ends = [lambda: rows - 1, lambda: 0]
    n = len(ends)

    def masks():
        at = lax.axis_index("row")
        return (
            jnp.where(at > 0, 1.0, 0.0).astype(F32),
            jnp.where(at < n_row - 1, 1.0, 0.0).astype(F32),
        )

    total = cols + 2 * PAD
    count = disp + 2 * rows
    ct = cotangent.transpose(0, 1, 3, 2)

    def swap(block, mask):
        route = [(i, i ^ mask) for i in range(n_row * n_col)]
        return lax.ppermute(block, ("row", "col"), route)

    far = col_shift(right_features, 2)
    by_even, by_odd, ctl, *rims = call(
        functools.partial(pack_kernel, ends),
        [
            ((count, channels), BF16),
            ((count, channels), BF16),
            ((disp, cols, rows * feat), BF16),
        ]
        + [((disp // per, total, 128), F32)] * n,
        [pltpu.VMEM((disp * cols, rows * feat), F32)],
        jnp.concatenate([x[:, at] for at in (cols - 1, 0) for x in (left_features, right_features)]),
        ct,
        us=0.4,
    )
    inner = range(1, n_col - 1, 2)
    by_even = swap(by_even, 1)
    by_odd = lax.ppermute(by_odd, "col", [(i, i + 1) for i in inner] + [(i + 1, i) for i in inner])
    (passed,) = call(
        pass_kernel, [((rows, cols, channels), BF16)], [], right_features, far, after=[ctl]
    )
    near = swap(passed, 1)
    w2, wc = call(
        taps_kernel,
        [((12 * 128, 2 * 128), BF16), ((4 * 3 * rows * SLOT, 2 * rows * feat), BF16)],
        [pltpu.VMEM((3 * rows * feat, 3 * rows * SLOT), F32)],
        conv_weight.transpose(0, 1, 2, 4, 3),
        after=[passed],
    )
    row_pays = call(
        functools.partial(row_kernel, ends, rows),
        [((disp // per, total, 128), BF16)] * n,
        [pltpu.VMEM((2, disp, 128), F32), pltpu.VMEM((disp // per, total, 128), F32)],
        by_even,
        by_odd,
        *rims,
        after=[w2],
        us=5.0,
    )
    top, bot = halos(row_pays)

    band = 104 + cols + PAD
    spread_rows = 3 * rows * cols + rows * cols // 2 + 2 * count
    vbuf, fl, fr, fr4, *volume_rows = call(
        functools.partial(volume_kernel, ends, group_size),
        [
            ((rows // 2, disp, total, 2 * SLOT), F32),
            ((rows, total, wide), F32),
            ((rows, band, wide), F32),
            ((rows, band, wide), F32),
        ]
        + [((disp // 2 * total, 128), BF16)] * n,
        [
            pltpu.VMEM((spread_rows, channels), BF16),
            pltpu.VMEM((spread_rows, wide), F32),
        ],
        left_features,
        right_features,
        near,
        far,
        by_even,
        by_odd,
        us=2.3,
    )
    vtop, vbot = halos(volume_rows)
    keep, give, ctsh = call(
        functools.partial(weight_kernel, masks, groups, feat),
        [((3 * 64, 128), F32), ((3 * 64, 128), F32), ((disp // 2 + 1, 2, cols, 3 * 256), BF16)],
        [
            pltpu.VMEM((rows // 2, 128, (disp // 2 + 2) * 128), BF16),
            pltpu.VMEM((disp, total, 256), F32),
            pltpu.VMEM((3 * 128, 128), F32),
        ],
        vbuf, ctl, by_even, by_odd, top, bot,
        us=2.6,
    )
    got = swap(give, 1)
    def join(part, mask, kind, after=(), us=0.0):
        terms = (part, swap(part, mask))
        return call(sum_kernel, [(part.shape, kind)], [], *terms, after=after, us=us)[0]

    (gv,) = call(dgrad_kernel, [((rows, disp, cols, 128), F32)], [], ctsh, w2, us=2.0)
    (part,) = call(sum_kernel, [(keep.shape, BF16)], [], keep, got, after=[gv], us=4.0)
    first, *others, last = hops(n_row, n_col)
    rg0, rg1, rg2 = call(
        right_kernel,
        [
            ((rows, cols, channels), BF16),
            ((rows, cols, channels), BF16),
            ((rows, cols // 2, channels), BF16),
        ],
        [
            pltpu.VMEM((rows, cols + cols + cols // 2, wide), F32),
            pltpu.VMEM((rows, cols + cols + cols // 2 + 8, wide), F32),
            pltpu.VMEM((rows * (cols + cols + cols // 2), wide), BF16),
        ],
        gv, fl,
        after=[part],
        us=1.0,
    )
    rg1 = swap(rg1, 1)
    part = join(part, first, F32, after=[rg0], us=4.0)
    lg, left_done = call(
        left_kernel,
        [((rows, cols, channels), BF16)],
        [pltpu.VMEM((rows, cols, wide), F32)],
        gv, fr, fr4,
        after=[part],
        token=True,
        us=1.9,
    )
    part = join(part, others[0], BF16, after=[left_done], us=4.0)
    (spread,) = call(
        functools.partial(spread_kernel, masks, groups),
        [((disp // 2 + 1, 2, cols, 3 * rows * SLOT), BF16)],
        [pltpu.VMEM((rows // 2, disp, total, 128), F32)],
        vbuf, vtop, vbot,
        after=[part],
        us=1.3,
    )
    order = [spread]
    for mask in others[1:]:
        part = join(part, mask, BF16, after=order, us=4.0)
        order = []
    (rg2,) = call(
        combine_kernel, [((rows, cols, channels), BF16)], [], rg1, rg2, after=[part]
    )
    part = join(part, last, F32, after=[rg2], us=4.0)
    output, conv_done = call(
        conv_kernel,
        [((disp, rows, feat, cols), BF16)],
        [],
        spread, wc,
        after=[part],
        token=True,
        us=2.6,
    )
    rg2 = col_shift(rg2, -2)
    cells = disp * rows * n_row * cols * n_col
    weight_grad, right_grad = call(
        functools.partial(finish_kernel, 1.0 / math.sqrt(cells)),
        [((3, 3, 3, feat, groups), F32), ((rows, cols, channels), BF16)],
        [],
        part, swap(part, 1), rg0, rg1, rg2,
        after=[conv_done],
        us=1.0,
    )
    return (
        output.transpose(0, 1, 3, 2),
        weight_grad.transpose(0, 1, 2, 4, 3),
        lg,
        right_grad,
    )


def solution(mesh):
    in_specs = (P("row", "col", None), P("row", "col", None), P(), P(None, "row", "col", None))
    out_specs = (P(None, "row", "col", None), P(), P("row", "col", None), P("row", "col", None))
    return jax.shard_map(
        on_device, mesh=mesh, in_specs=in_specs, out_specs=out_specs, check_vma=False
    )
```

profile of v0, /device:TPU:0, one launch (start us, length us, event | category | flops | bytes accessed | tf_op | source)
XLA Modules:
  0.0 48.8 jit_solution(2897304702186628765)
XLA Ops:
  0.6 0.0 copy-start
  0.6 0.0 copy-start.1
  0.7 5.0 %collective-permute-start = (bf16[4,64,320]{2,1,0:T(8,128)(2,1)}, bf16[4,64,320]{2,1,0:T(8,128)(2,1)S(1)}, u32[]{:S(2)}, u32[]{:S(2)}) collective-permute-start(bf16[4,64,320]{2,1,0:T(8,128)(2,1)} %refs_1_.3), channel_id=1, source_target_pairs={{0,2},{1,3},{2,4},{3,5},{4,6},{5,7},{6,8},{7,9},{8,10},{9,11},{10,... | collective-permute-start | bytes 491528 | tf_op jit(solution)/shard_map/ppermute | solution.py:568
  5.7 0.8 %fusion.1 = (bf16[4,1,320]{2,1,0:T(2,128)(2,1)S(1)}, bf16[4,1,320]{2,1,0:T(2,128)(2,1)S(1)}) fusion(bf16[4,64,320]{2,1,0:T(8,128)(2,1)} %refs_1_.3), kind=kLoop, calls=%fused_computation.6 | loop fusion | bytes 10240 | tf_op jit(solution)/shard_map/slice | solution.py:631
  6.5 0.8 %fusion = (bf16[4,1,320]{2,1,0:T(2,128)(2,1)S(1)}, bf16[4,1,320]{2,1,0:T(2,128)(2,1)S(1)}) fusion(bf16[4,64,320]{2,1,0:T(8,128)(2,1)} %refs_0_.1), kind=kLoop, calls=%fused_computation.5 | loop fusion | bytes 10240 | tf_op jit(solution)/shard_map/slice | solution.py:631
  7.3 0.0 copy-start.3
  7.3 1.1 %copy-done.3 = bf16[24,4,64,32]{2,3,1,0:T(8,128)(2,1)S(1)} copy-done((bf16[24,4,64,32]{2,3,1,0:T(8,128)(2,1)S(1)}, bf16[24,4,64,32]{2,3,1,0:T(8,128)(2,1)}, u32[]{:S(2)}) %copy-start.3) | copy-done | bytes 393240
  8.4 0.3 shard_map.75
  8.8 0.1 collective-permute-start.2
  8.8 0.7 %collective-permute-start.3 = (bf16[32,320]{1,0:T(8,128)(2,1)S(1)}, bf16[32,320]{1,0:T(8,128)(2,1)S(1)}, u32[]{:S(2)}, u32[]{:S(2)}) collective-permute-start(bf16[32,320]{1,0:T(8,128)(2,1)S(1)} %get-tuple-element.29), channel_id=1, source_target_pairs={{1,2},{3,4},{5,6},{7,8},{9,10},{11,12},{13,14},{2,1},{4,3},{6,5},{... | collective-permute-start | bytes 61448 | tf_op jit(solution)/shard_map/ppermute | solution.py:637
  9.5 0.6 %collective-permute-done.refs_2_.refs_3_ = bf16[4,64,320]{2,1,0:T(8,128)(2,1)S(1)} collective-permute-done((bf16[4,64,320]{2,1,0:T(8,128)(2,1)}, bf16[4,64,320]{2,1,0:T(8,128)(2,1)S(1)}, u32[]{:S(2)}, u32[]{:S(2)}) %collective-permute-start) | collective-permute-done | bytes 163872 | tf_op jit(solution)/shard_map/ppermute | solution.py:568
  10.1 0.0 copy-done
  10.1 0.1 shard_map.76.refs_0_
  10.2 2.4 %collective-permute-start.1 = (bf16[4,64,320]{2,1,0:T(8,128)(2,1)S(1)}, bf16[4,64,320]{2,1,0:T(8,128)(2,1)S(1)}, u32[]{:S(2)}, u32[]{:S(2)}) collective-permute-start(bf16[4,64,320]{2,1,0:T(8,128)(2,1)S(1)} %shard_map.76.refs_0_), channel_id=1, source_target_pairs={{0,1},{1,0},{2,3},{3,2},{4,5},{5,4},{6,7},{7,6},{8,9},{9,8},{10,11... | collective-permute-start | bytes 491528 | tf_op jit(solution)/shard_map/ppermute | solution.py:619
  12.6 0.0 copy-done.1
  12.6 0.8 %shard_map.78 = (bf16[1536,256]{1,0:T(8,128)(2,1)S(1)}, bf16[3072,256]{1,0:T(8,128)(2,1)S(1)}) custom-call(bf16[4,64,320]{2,1,0:T(8,128)(2,1)S(1)} %shard_map.76.refs_0_, bf16[3,3,3,32,40]{4,3,2,1,0:T(8,128)(2,1)S(1)} %bitcast.12), custom_call_target="tpu_custom_call" | custom-call | tf_op jit(solution)/shard_map/pallas_call | solution.py:552
  13.4 0.0 collective-permute-done.2.refs_4_.refs_1_.refs_2_
  13.4 0.0 collective-permute-done.3.refs_5_.refs_2_.refs_3_
  13.4 0.0 copy-start.2
  13.4 0.1 shard_map.79
  13.5 1.6 %collective-permute-start.4 = (bf16[6,80,128]{2,1,0:T(8,128)(2,1)S(1)}, bf16[6,80,128]{2,1,0:T(8,128)(2,1)S(1)}, u32[]{:S(2)}, u32[]{:S(2)}) collective-permute-start(bf16[6,80,128]{2,1,0:T(8,128)(2,1)S(1)} %shard_map.79), channel_id=1, source_target_pairs={{0,16},{16,0},{1,17},{17,1},{2,18},{18,2},{3,19},{19,3},{4,20},{20... | collective-permute-start | bytes 368648 | tf_op jit(solution)/shard_map/ppermute | solution.py:579
  15.1 0.0 collective-permute-done.1.refs_2_
  15.1 0.0 copy-done.2
  15.1 2.4 %shard_map.77 = (f32[2,24,80,128]{3,2,1,0:T(8,128)S(1)}, f32[4,80,512]{2,1,0:T(8,128)S(1)}, f32[4,176,512]{2,1,0:T(8,128)S(1)}, f32[4,176,512]{2,1,0:T(8,128)S(1)}, bf16[960,128]{1,0:T(8,128)(2,1)S(1)}) custom-call(bf16[4,64,320]{2,1,0:T(8,128)(2,1)S(1)} %copy-done.2, bf16[4,64,320]{2,1,0:T(8,128)(2,1)S(1)} %copy-done, ...), custom_call_target="tpu_custom_call" | custom-call | flops 2644999936 | bytes 8510000 | tf_op jit(solution)/shard_map/pallas_call | solution.py:552
  17.5 0.8 %collective-permute-start.8 = (bf16[960,128]{1,0:T(8,128)(2,1)S(1)}, bf16[960,128]{1,0:T(8,128)(2,1)S(1)}, u32[]{:S(2)}, u32[]{:S(2)}) collective-permute-start(bf16[960,128]{1,0:T(8,128)(2,1)S(1)} %get-tuple-element.41), channel_id=1, source_target_pairs={{0,16},{16,0},{1,17},{17,1},{2,18},{18,2},{3,19},{19,3},{4,20},{20... | collective-permute-start | bytes 737288 | tf_op jit(solution)/shard_map/ppermute | solution.py:579
  18.3 1.4 %collective-permute-done.4.refs_4_.refs_5_ = bf16[6,80,128]{2,1,0:T(8,128)(2,1)S(1)} collective-permute-done((bf16[6,80,128]{2,1,0:T(8,128)(2,1)S(1)}, bf16[6,80,128]{2,1,0:T(8,128)(2,1)S(1)}, u32[]{:S(2)}, u32[]{:S(2)}) %collective-permute-start.4) | collective-permute-done | bytes 122912 | tf_op jit(solution)/shard_map/ppermute | solution.py:579
  19.7 2.1 %shard_map.80 = (f32[192,128]{1,0:T(8,128)S(1)}, f32[192,128]{1,0:T(8,128)S(1)}, bf16[13,2,64,768]{3,2,1,0:T(8,128)(2,1)S(1)}) custom-call(f32[2,24,80,128]{3,2,1,0:T(8,128)S(1)} %get-tuple-element.30.refs_0_.refs_1_, bf16[24,64,128]{2,1,0:T(8,128)(2,1)S(1)} %get-tuple-element.27.refs_0_.refs_1_, ...), custom_call_target="tpu_custom_call" | custom-call | flops 2990000128 | bytes 9620000 | tf_op jit(solution)/shard_map/pallas_call | solution.py:552
  21.8 0.2 collective-permute-start.5
  22.0 1.7 %shard_map.81.refs_0_.refs_1_ = f32[4,24,64,128]{3,2,1,0:T(8,128)S(1)} custom-call(bf16[13,2,64,768]{3,2,1,0:T(8,128)(2,1)S(1)} %get-tuple-element.33.refs_0_, bf16[1536,256]{1,0:T(8,128)(2,1)S(1)} %get-tuple-element.31.refs_0_.refs_1_), custom_call_target="tpu_custom_call" | custom-call | flops 2300000000 | bytes 7400000 | tf_op jit(solution)/shard_map/pallas_call | solution.py:552
  23.7 0.0 collective-permute-done.5.refs_2_
  23.7 3.0 %collective-permute-start.6 = (bf16[192,128]{1,0:T(8,128)(2,1)S(1)}, bf16[192,128]{1,0:T(8,128)(2,1)S(1)}, u32[]{:S(2)}, u32[]{:S(2)}) collective-permute-start(bf16[192,128]{1,0:T(8,128)(2,1)S(1)} %shard_map.82.refs_0_.refs_1_), channel_id=1, source_target_pairs={{0,8},{1,9},{2,10},{3,11},{4,12},{5,13},{6,14},{7,15},{8,0},{9,1},... | collective-permute-start | bytes 147464 | tf_op jit(solution)/shard_map/ppermute | solution.py:619
  26.8 1.3 %shard_map.83 = (bf16[4,64,320]{2,1,0:T(8,128)(2,1)S(1)}, bf16[4,64,320]{2,1,0:T(8,128)(2,1)S(1)}, bf16[4,32,320]{2,1,0:T(8,128)(2,1)S(1)}) custom-call(bf16[192,128]{1,0:T(8,128)(2,1)S(1)} %shard_map.82.refs_0_.refs_1_, f32[4,24,64,128]{3,2,1,0:T(8,128)S(1)} %shard_map.81.refs_0_.refs_1_, f32[4,80,512]{2,1,0:T(8,128)S(1)} %get-tuple-element.36.refs_2_), custom_call_target="tpu_custom_call" | custom-call | flops 1150000000 | bytes 3700000 | tf_op jit(solution)/shard_map/pallas_call | solution.py:552
  28.0 0.3 collective-permute-start.10
  28.3 0.8 %collective-permute-done.6.refs_2_ = bf16[192,128]{1,0:T(8,128)(2,1)S(1)} collective-permute-done((bf16[192,128]{1,0:T(8,128)(2,1)S(1)}, bf16[192,128]{1,0:T(8,128)(2,1)S(1)}, u32[]{:S(2)}, u32[]{:S(2)}) %collective-permute-start.6) | collective-permute-done | bytes 49184 | tf_op jit(solution)/shard_map/ppermute | solution.py:619
  29.2 1.9 %collective-permute-start.7 = (f32[192,128]{1,0:T(8,128)S(1)}, f32[192,128]{1,0:T(8,128)S(1)}, u32[]{:S(2)}, u32[]{:S(2)}) collective-permute-start(f32[192,128]{1,0:T(8,128)S(1)} %shard_map.84.refs_0_.refs_1_), channel_id=1, source_target_pairs={{0,4},{1,5},{2,6},{3,7},{4,0},{5,1},{6,2},{7,3},{8,12},{9,13},{10,... | collective-permute-start | bytes 294920 | tf_op jit(solution)/shard_map/ppermute | solution.py:619
  31.0 2.1 %shard_map.85 = (bf16[4,64,320]{2,1,0:T(8,128)(2,1)}, f32[8,128]{1,0:T(8,128)S(1)}) custom-call(f32[192,128]{1,0:T(8,128)S(1)} %shard_map.84.refs_0_.refs_1_, f32[4,24,64,128]{3,2,1,0:T(8,128)S(1)} %shard_map.81.refs_0_.refs_1_, f32[4,176,512]{2,1,0:T(8,128)S(1)} %get-tuple-element.38.refs_2_, f32[4,176,512]{2,1,0:T(8,128)S(1)} %get-tuple-element.39.refs_3_), custom_call_target="tpu_custom_call" | custom-call | flops 2184999936 | bytes 7030000 | tf_op jit(solution)/shard_map/pallas_call | solution.py:552
  33.1 1.0 %collective-permute-done.7.refs_2_ = f32[192,128]{1,0:T(8,128)S(1)} collective-permute-done((f32[192,128]{1,0:T(8,128)S(1)}, f32[192,128]{1,0:T(8,128)S(1)}, u32[]{:S(2)}, u32[]{:S(2)}) %collective-permute-start.7) | collective-permute-done | bytes 98336 | tf_op jit(solution)/shard_map/ppermute | solution.py:619
  34.1 2.4 %collective-permute-start.9 = (bf16[192,128]{1,0:T(8,128)(2,1)S(1)}, bf16[192,128]{1,0:T(8,128)(2,1)S(1)}, u32[]{:S(2)}, u32[]{:S(2)}) collective-permute-start(bf16[192,128]{1,0:T(8,128)(2,1)S(1)} %shard_map.86.refs_0_.refs_1_), channel_id=1, source_target_pairs={{0,2},{1,3},{2,0},{3,1},{4,6},{5,7},{6,4},{7,5},{8,10},{9,11},{10,... | collective-permute-start | bytes 147464 | tf_op jit(solution)/shard_map/ppermute | solution.py:619
  36.5 0.0 collective-permute-done.8.refs_2_.refs_3_
  36.5 1.3 %shard_map.87.refs_0_.refs_1_ = bf16[13,2,64,768]{3,2,1,0:T(8,128)(2,1)S(1)} custom-call(bf16[192,128]{1,0:T(8,128)(2,1)S(1)} %shard_map.86.refs_0_.refs_1_, f32[2,24,80,128]{3,2,1,0:T(8,128)S(1)} %get-tuple-element.30.refs_0_.refs_1_, bf16[960,128]{1,0:T(8,128)(2,1)S(1)} %collective-permute-done.8.refs_2_.refs_3_, ...), custom_call_target="tpu_custom_call" | custom-call | flops 1495000064 | bytes 4810000 | tf_op jit(solution)/shard_map/pallas_call | solution.py:552
  37.8 0.7 %collective-permute-done.9.refs_2_ = bf16[192,128]{1,0:T(8,128)(2,1)S(1)} collective-permute-done((bf16[192,128]{1,0:T(8,128)(2,1)S(1)}, bf16[192,128]{1,0:T(8,128)(2,1)S(1)}, u32[]{:S(2)}, u32[]{:S(2)}) %collective-permute-start.9) | collective-permute-done | bytes 49184 | tf_op jit(solution)/shard_map/ppermute | solution.py:619
  38.6 1.6 %collective-permute-start.11 = (bf16[192,128]{1,0:T(8,128)(2,1)S(1)}, bf16[192,128]{1,0:T(8,128)(2,1)S(1)}, u32[]{:S(2)}, u32[]{:S(2)}) collective-permute-start(bf16[192,128]{1,0:T(8,128)(2,1)S(1)} %shard_map.88.refs_0_.refs_1_), channel_id=1, source_target_pairs={{0,16},{1,17},{2,18},{3,19},{4,20},{5,21},{6,22},{7,23},{8,24},{9,... | collective-permute-start | bytes 147464 | tf_op jit(solution)/shard_map/ppermute | solution.py:619
  40.1 0.0 collective-permute-done.10.refs_1_.refs_4_
  40.1 0.1 shard_map.89.refs_0_
  40.2 1.3 %collective-permute-start.13 = (bf16[4,64,320]{2,1,0:T(8,128)(2,1)S(1)}, bf16[4,64,320]{2,1,0:T(8,128)(2,1)S(1)}, u32[]{:S(2)}, u32[]{:S(2)}) collective-permute-start(bf16[4,64,320]{2,1,0:T(8,128)(2,1)S(1)} %shard_map.89.refs_0_), channel_id=1, source_target_pairs={{2,0},{3,1},{4,2},{5,3},{6,4},{7,5},{8,6},{9,7},{10,8},{11,9},{12,... | collective-permute-start | bytes 491528 | tf_op jit(solution)/shard_map/ppermute | solution.py:568
  41.5 1.2 %collective-permute-done.11.refs_2_ = bf16[192,128]{1,0:T(8,128)(2,1)S(1)} collective-permute-done((bf16[192,128]{1,0:T(8,128)(2,1)S(1)}, bf16[192,128]{1,0:T(8,128)(2,1)S(1)}, u32[]{:S(2)}, u32[]{:S(2)}) %collective-permute-start.11) | collective-permute-done | bytes 49184 | tf_op jit(solution)/shard_map/ppermute | solution.py:619
  42.8 0.1 collective-permute-start.12
  42.8 2.6 %shard_map.91 = (bf16[24,4,32,64]{3,2,1,0:T(8,128)(2,1)}, f32[8,128]{1,0:T(8,128)S(1)}) custom-call(f32[192,128]{1,0:T(8,128)S(1)} %shard_map.90.refs_0_.refs_1_, bf16[13,2,64,768]{3,2,1,0:T(8,128)(2,1)S(1)} %shard_map.87.refs_0_.refs_1_, bf16[3072,256]{1,0:T(8,128)(2,1)S(1)} %get-tuple-element.44.refs_2_), custom_call_target="tpu_custom_call" | custom-call | flops 2990000128 | bytes 9620000 | tf_op jit(solution)/shard_map/pallas_call | solution.py:552
  45.4 0.0 collective-permute-done.12.refs_2_
  45.4 2.3 %collective-permute-done.13.refs_5_ = bf16[4,64,320]{2,1,0:T(8,128)(2,1)S(1)} collective-permute-done((bf16[4,64,320]{2,1,0:T(8,128)(2,1)S(1)}, bf16[4,64,320]{2,1,0:T(8,128)(2,1)S(1)}, u32[]{:S(2)}, u32[]{:S(2)}) %collective-permute-start.13) | collective-permute-done | bytes 163872 | tf_op jit(solution)/shard_map/ppermute | solution.py:568
  47.8 1.1 %shard_map.92 = (f32[3,3,3,32,40]{4,3,2,1,0:T(8,128)}, bf16[4,64,320]{2,1,0:T(8,128)(2,1)}) custom-call(f32[8,128]{1,0:T(8,128)S(1)} %get-tuple-element.46.refs_0_, f32[192,128]{1,0:T(8,128)S(1)} %shard_map.90.refs_0_.refs_1_, f32[192,128]{1,0:T(8,128)S(1)} %collective-permute-done.12.refs_2_, bf16[4,64,320]{2,1,0:T(8,128)(2,1)S(1)} %get-tuple-element.37.refs_0_.refs_3_, ...), custom_call_target="tpu_custom_call" | custom-call | flops 1150000000 | bytes 3700000 | tf_op jit(solution)/shard_map/pallas_call | solution.py:552
  (8 shorter events, 0.1 us)
Async XLA Ops:
  0.6 9.5 %copy-start = (bf16[4,64,320]{2,1,0:T(8,128)(2,1)S(1)}, bf16[4,64,320]{2,1,0:T(8,128)(2,1)}, u32[]{:S(2)}) copy-start(bf16[4,64,320]{2,1,0:T(8,128)(2,1)} %refs_1_.3) | copy-start | bytes 491524
  0.6 11.9 %copy-start.1 = (bf16[3,3,3,40,32]{3,4,2,1,0:T(8,128)(2,1)S(1)}, bf16[3,3,3,40,32]{3,4,2,1,0:T(8,128)(2,1)}, u32[]{:S(2)}) copy-start(bf16[3,3,3,40,32]{3,4,2,1,0:T(8,128)(2,1)} %param.6) | copy-start | bytes 207364
  0.7 9.5 %collective-permute-start = (bf16[4,64,320]{2,1,0:T(8,128)(2,1)}, bf16[4,64,320]{2,1,0:T(8,128)(2,1)S(1)}, u32[]{:S(2)}, u32[]{:S(2)}) collective-permute-start(bf16[4,64,320]{2,1,0:T(8,128)(2,1)} %refs_1_.3), channel_id=1, source_target_pairs={{0,2},{1,3},{2,4},{3,5},{4,6},{5,7},{6,8},{7,9},{8,10},{9,11},{10,... | collective-permute-start | bytes 491528 | tf_op jit(solution)/shard_map/ppermute | solution.py:568
  7.3 1.1 %copy-start.3 = (bf16[24,4,64,32]{2,3,1,0:T(8,128)(2,1)S(1)}, bf16[24,4,64,32]{2,3,1,0:T(8,128)(2,1)}, u32[]{:S(2)}) copy-start(bf16[24,4,64,32]{2,3,1,0:T(8,128)(2,1)} %param.7) | copy-start | bytes 1179652
  8.8 4.6 %collective-permute-start.2 = (bf16[32,320]{1,0:T(8,128)(2,1)S(1)}, bf16[32,320]{1,0:T(8,128)(2,1)S(1)}, u32[]{:S(2)}, u32[]{:S(2)}) collective-permute-start(bf16[32,320]{1,0:T(8,128)(2,1)S(1)} %get-tuple-element.28), channel_id=1, source_target_pairs={{0,1},{1,0},{2,3},{3,2},{4,5},{5,4},{6,7},{7,6},{8,9},{9,8},{10,11... | collective-permute-start | bytes 61448 | tf_op jit(solution)/shard_map/ppermute | solution.py:619
  8.8 4.6 %collective-permute-start.3 = (bf16[32,320]{1,0:T(8,128)(2,1)S(1)}, bf16[32,320]{1,0:T(8,128)(2,1)S(1)}, u32[]{:S(2)}, u32[]{:S(2)}) collective-permute-start(bf16[32,320]{1,0:T(8,128)(2,1)S(1)} %get-tuple-element.29), channel_id=1, source_target_pairs={{1,2},{3,4},{5,6},{7,8},{9,10},{11,12},{13,14},{2,1},{4,3},{6,5},{... | collective-permute-start | bytes 61448 | tf_op jit(solution)/shard_map/ppermute | solution.py:637
  10.2 4.9 %collective-permute-start.1 = (bf16[4,64,320]{2,1,0:T(8,128)(2,1)S(1)}, bf16[4,64,320]{2,1,0:T(8,128)(2,1)S(1)}, u32[]{:S(2)}, u32[]{:S(2)}) collective-permute-start(bf16[4,64,320]{2,1,0:T(8,128)(2,1)S(1)} %shard_map.76.refs_0_), channel_id=1, source_target_pairs={{0,1},{1,0},{2,3},{3,2},{4,5},{5,4},{6,7},{7,6},{8,9},{9,8},{10,11... | collective-permute-start | bytes 491528 | tf_op jit(solution)/shard_map/ppermute | solution.py:619
  13.4 1.7 %copy-start.2 = (bf16[4,64,320]{2,1,0:T(8,128)(2,1)S(1)}, bf16[4,64,320]{2,1,0:T(8,128)(2,1)}, u32[]{:S(2)}) copy-start(bf16[4,64,320]{2,1,0:T(8,128)(2,1)} %refs_0_.1) | copy-start | bytes 491524
  13.5 6.2 %collective-permute-start.4 = (bf16[6,80,128]{2,1,0:T(8,128)(2,1)S(1)}, bf16[6,80,128]{2,1,0:T(8,128)(2,1)S(1)}, u32[]{:S(2)}, u32[]{:S(2)}) collective-permute-start(bf16[6,80,128]{2,1,0:T(8,128)(2,1)S(1)} %shard_map.79), channel_id=1, source_target_pairs={{0,16},{16,0},{1,17},{17,1},{2,18},{18,2},{3,19},{19,3},{4,20},{20... | collective-permute-start | bytes 368648 | tf_op jit(solution)/shard_map/ppermute | solution.py:579
  17.5 19.0 %collective-permute-start.8 = (bf16[960,128]{1,0:T(8,128)(2,1)S(1)}, bf16[960,128]{1,0:T(8,128)(2,1)S(1)}, u32[]{:S(2)}, u32[]{:S(2)}) collective-permute-start(bf16[960,128]{1,0:T(8,128)(2,1)S(1)} %get-tuple-element.41), channel_id=1, source_target_pairs={{0,16},{16,0},{1,17},{17,1},{2,18},{18,2},{3,19},{19,3},{4,20},{20... | collective-permute-start | bytes 737288 | tf_op jit(solution)/shard_map/ppermute | solution.py:579
  21.8 1.9 %collective-permute-start.5 = (f32[192,128]{1,0:T(8,128)S(1)}, f32[192,128]{1,0:T(8,128)S(1)}, u32[]{:S(2)}, u32[]{:S(2)}) collective-permute-start(f32[192,128]{1,0:T(8,128)S(1)} %get-tuple-element.35), channel_id=1, source_target_pairs={{0,1},{1,0},{2,3},{3,2},{4,5},{5,4},{6,7},{7,6},{8,9},{9,8},{10,11... | collective-permute-start | bytes 294920 | tf_op jit(solution)/shard_map/ppermute | solution.py:619
  23.7 5.4 %collective-permute-start.6 = (bf16[192,128]{1,0:T(8,128)(2,1)S(1)}, bf16[192,128]{1,0:T(8,128)(2,1)S(1)}, u32[]{:S(2)}, u32[]{:S(2)}) collective-permute-start(bf16[192,128]{1,0:T(8,128)(2,1)S(1)} %shard_map.82.refs_0_.refs_1_), channel_id=1, source_target_pairs={{0,8},{1,9},{2,10},{3,11},{4,12},{5,13},{6,14},{7,15},{8,0},{9,1},... | collective-permute-start | bytes 147464 | tf_op jit(solution)/shard_map/ppermute | solution.py:619
  28.0 12.1 %collective-permute-start.10 = (bf16[4,64,320]{2,1,0:T(8,128)(2,1)S(1)}, bf16[4,64,320]{2,1,0:T(8,128)(2,1)S(1)}, u32[]{:S(2)}, u32[]{:S(2)}) collective-permute-start(bf16[4,64,320]{2,1,0:T(8,128)(2,1)S(1)} %get-tuple-element.42), channel_id=1, source_target_pairs={{0,1},{1,0},{2,3},{3,2},{4,5},{5,4},{6,7},{7,6},{8,9},{9,8},{10,11... | collective-permute-start | bytes 491528 | tf_op jit(solution)/shard_map/ppermute | solution.py:619
  29.2 4.9 %collective-permute-start.7 = (f32[192,128]{1,0:T(8,128)S(1)}, f32[192,128]{1,0:T(8,128)S(1)}, u32[]{:S(2)}, u32[]{:S(2)}) collective-permute-start(f32[192,128]{1,0:T(8,128)S(1)} %shard_map.84.refs_0_.refs_1_), channel_id=1, source_target_pairs={{0,4},{1,5},{2,6},{3,7},{4,0},{5,1},{6,2},{7,3},{8,12},{9,13},{10,... | collective-permute-start | bytes 294920 | tf_op jit(solution)/shard_map/ppermute | solution.py:619
  34.1 4.5 %collective-permute-start.9 = (bf16[192,128]{1,0:T(8,128)(2,1)S(1)}, bf16[192,128]{1,0:T(8,128)(2,1)S(1)}, u32[]{:S(2)}, u32[]{:S(2)}) collective-permute-start(bf16[192,128]{1,0:T(8,128)(2,1)S(1)} %shard_map.86.refs_0_.refs_1_), channel_id=1, source_target_pairs={{0,2},{1,3},{2,0},{3,1},{4,6},{5,7},{6,4},{7,5},{8,10},{9,11},{10,... | collective-permute-start | bytes 147464 | tf_op jit(solution)/shard_map/ppermute | solution.py:619
  38.6 4.2 %collective-permute-start.11 = (bf16[192,128]{1,0:T(8,128)(2,1)S(1)}, bf16[192,128]{1,0:T(8,128)(2,1)S(1)}, u32[]{:S(2)}, u32[]{:S(2)}) collective-permute-start(bf16[192,128]{1,0:T(8,128)(2,1)S(1)} %shard_map.88.refs_0_.refs_1_), channel_id=1, source_target_pairs={{0,16},{1,17},{2,18},{3,19},{4,20},{5,21},{6,22},{7,23},{8,24},{9,... | collective-permute-start | bytes 147464 | tf_op jit(solution)/shard_map/ppermute | solution.py:619
  40.2 7.6 %collective-permute-start.13 = (bf16[4,64,320]{2,1,0:T(8,128)(2,1)S(1)}, bf16[4,64,320]{2,1,0:T(8,128)(2,1)S(1)}, u32[]{:S(2)}, u32[]{:S(2)}) collective-permute-start(bf16[4,64,320]{2,1,0:T(8,128)(2,1)S(1)} %shard_map.89.refs_0_), channel_id=1, source_target_pairs={{2,0},{3,1},{4,2},{5,3},{6,4},{7,5},{8,6},{9,7},{10,8},{11,9},{12,... | collective-permute-start | bytes 491528 | tf_op jit(solution)/shard_map/ppermute | solution.py:568
  42.8 2.7 %collective-permute-start.12 = (f32[192,128]{1,0:T(8,128)S(1)}, f32[192,128]{1,0:T(8,128)S(1)}, u32[]{:S(2)}, u32[]{:S(2)}) collective-permute-start(f32[192,128]{1,0:T(8,128)S(1)} %shard_map.90.refs_0_.refs_1_), channel_id=1, source_target_pairs={{0,1},{1,0},{2,3},{3,2},{4,5},{5,4},{6,7},{7,6},{8,9},{9,8},{10,11... | collective-permute-start | bytes 294920 | tf_op jit(solution)/shard_map/ppermute | solution.py:619
where the time goes:
time: 49.2 us; the launch traced here: 48.8 us
  starting transfers between devices  21.2 us (43%)
  Pallas kernels  16 us (33%)
  waiting for transfers between devices  8.14 us (17%)
  local copies, waits for them, and re-layouts  2.72 us (6%)
  between operations  0.84 us (2%)
    pallas_call x18, Pallas kernels, call(): pl.pallas_call(lambda *refs: kernel(*refs[skip:]), out_shape=[jax.ShapeDt...  16 us
    ppermute x9, starting transfers between devices, swap(): return lax.ppermute(block, ('row', 'col'), route)  11.8 us
    ppermute x2, starting transfers between devices, col_shift(): return lax.ppermute(block, 'col', route)  6.31 us
    ppermute x9, waiting for transfers between devices, swap(): return lax.ppermute(block, ('row', 'col'), route)  3.78 us
    ppermute x2, waiting for transfers between devices, col_shift(): return lax.ppermute(block, 'col', route)  2.94 us
    ppermute x2, starting transfers between devices, halos(): got = lax.ppermute(pays[0], 'row', [(0, 1), (1, 0)])  2.36 us
    slice x2, local copies, waits for them, and re-layouts, on_device(): x[:, at]  1.56 us
    ppermute x2, waiting for transfers between devices, halos(): got = lax.ppermute(pays[0], 'row', [(0, 1), (1, 0)])  1.42 us
  transfers between devices with their start and end apart: 14, of which 7 were waited for; matrix products, arithmetic and copies ran while one was open for 3% of the time, Pallas kernels for 31%

commit v1 on v0

--- a/solution.py
+++ b/solution.py
@@ -103,43 +103,51 @@
         pay[...] = buf[...].astype(BF16)
 
 
-def volume_kernel(ends, group_size, left, right, near, far, by_even, by_odd, vbuf, fl, fr, fr4, *rest):
+def put_band(refs, h, column, block):
+    fr, fr4, cols = refs
+    at = fr.shape[1] - cols - PAD + column
+    fr[h, at : at + block.shape[0]] = block
+    fr4[h, at + STEP : at + STEP + block.shape[0]] = block
+
+
+def own_kernel(group_size, left, right, far, fl, fr, fr4, mixed, wide_buf):
+    rows, cols, channels = left.shape
+    base, half, wide = rows * cols, cols // 2, group_size * SLOT
+    mixed[0:base] = right[...].reshape(base, channels)
+    mixed[base : 2 * base] = left[...].reshape(base, channels)
+    mixed[2 * base :] = far[:, half:].reshape(base // 2, channels)
+    wide_buf[...] = dot(mixed[...], channel_table(channels, group_size, False))
+    tail = fr.shape[1]
+    for h in range(rows):
+        for ref in (fr, fr4):
+            ref[h, 0:16] = jnp.zeros((16, wide), F32)
+            ref[h, tail - 16 :] = jnp.zeros((16, wide), F32)
+        put_band((fr, fr4, cols), h, -cols - half, wide_buf[2 * base + h * half : 2 * base + (h + 1) * half])
+        put_band((fr, fr4, cols), h, 0, wide_buf[h * cols : (h + 1) * cols])
+        fl[h, 0:PAD] = jnp.zeros((PAD, wide), F32)
+        fl[h, PAD + cols :] = jnp.zeros((PAD, wide), F32)
+        fl[h, PAD : PAD + cols] = wide_buf[base + h * cols : base + (h + 1) * cols] * (1.0 / group_size)
+
+
+def volume_kernel(ends, group_size, near, by_even, by_odd, _fl, _fr, _fr4, fl, fr, fr4, vbuf, *rest):
     pays, (mixed, wide_buf) = rest[: len(ends)], rest[len(ends) :]
-    rows, cols, channels = left.shape
+    rows, cols, channels = near.shape
     disp = vbuf.shape[1]
     reach = fr.shape[1] - cols - PAD
     wide = group_size * SLOT
-    base, half = rows * cols, cols // 2
+    base = rows * cols
     mixed[0:base] = near[...].reshape(base, channels)
-    mixed[base : 2 * base] = right[...].reshape(base, channels)
-    mixed[2 * base : 3 * base] = left[...].reshape(base, channels)
-    at_far, at_ends = 3 * base, 3 * base + base // 2
-    mixed[at_far:at_ends] = far[:, half:].reshape(base // 2, channels)
     count = disp + 2 * rows
     for i, x in enumerate(end_columns(by_even, by_odd)):
-        mixed[at_ends + i * count : at_ends + (i + 1) * count] = x.astype(BF16)
+        mixed[base + i * count : base + (i + 1) * count] = x.astype(BF16)
     wide_buf[...] = dot(mixed[...], channel_table(channels, group_size, False))
-    scale = 1.0 / group_size
     for h in range(rows):
-        fl[h, 0:PAD] = jnp.zeros((PAD, wide), F32)
-        fl[h, PAD + cols :] = jnp.zeros((PAD, wide), F32)
-        at = at_ends + disp + h
-        fl[h, PAD - 1 : PAD] = wide_buf[at : at + 1] * scale
-        fl[h, PAD : PAD + cols] = wide_buf[2 * base + h * cols : 2 * base + (h + 1) * cols] * scale
+        put_band((fr, fr4, cols), h, -cols, wide_buf[h * cols : (h + 1) * cols])
+        at = base + disp + h
+        fl[h, PAD - 1 : PAD] = wide_buf[at : at + 1] * (1.0 / group_size)
         at += count
-        fl[h, PAD + cols : PAD + cols + 1] = wide_buf[at : at + 1] * scale
-        for ref, off in ((fr, 0), (fr4, STEP)):
-            start = reach - cols - half + off
-            ref[h, 0:start] = jnp.zeros((start, wide), F32)
-            ref[h, start : start + half] = wide_buf[at_far + h * half : at_far + (h + 1) * half]
-            for part in range(2):
-                at = part * base + h * cols
-                to = start + half + part * cols
-                ref[h, to : to + cols] = wide_buf[at : at + cols]
-            to = start + half + 2 * cols
-            ref[h, to:] = jnp.zeros((ref.shape[1] - to, wide), F32)
-            at = at_ends + count + disp + rows + h
-            ref[h, to : to + 1] = wide_buf[at : at + 1]
+        fl[h, PAD + cols : PAD + cols + 1] = wide_buf[at : at + 1] * (1.0 / group_size)
+        put_band((fr, fr4, cols), h, cols, wide_buf[at + rows : at + rows + 1])
     total = cols + 2 * PAD
     low = lanes((8, 128)) < SLOT
     pairs, times, lots = rows // 2, disp // 2, wide // 128
@@ -283,34 +291,34 @@
     give_out[...] = jnp.where(is_even, high, low)
 
 
-def dgrad_kernel(ctsh, w2, gv):
-    rows, disp, cols, _ = gv.shape
+def dgrad_kernel(p, ctsh, w2, gv):
+    _, disp, cols, _ = gv.shape
     step = disp // 4
     low = lanes((step * cols, 128)) < SLOT
 
     def conv(q, _):
-        for p in range(rows // 2):
-            slabs = [
-                ctsh[pl.ds(q * step + s // 2, step), s % 2, :, 256 * e + 128 * p : 256 * e + 128 * (p + 1)]
-                for s in range(4)
-                for e in range(3)
-            ]
-            slabs = [x.reshape(step * cols, 128) for x in slabs]
-            acc = dot(jnp.concatenate(slabs, axis=1), w2[...]).astype(BF16).astype(F32)
-            for o in range(2):
-                x = acc[:, 128 * o : 128 * (o + 1)]
-                r = pltpu.roll(x, SLOT, 1)
-                for hh in range(2):
-                    y = jnp.where(low, r, x) if hh else jnp.where(low, x, r)
-                    for j in range(step):
-                        gv[2 * p + hh, 2 * (q * step + j) + o] = y[j * cols : (j + 1) * cols]
+        slabs = [
+            ctsh[pl.ds(q * step + s // 2, step), s % 2, :, 256 * e + 128 * p : 256 * e + 128 * (p + 1)]
+            for s in range(4)
+            for e in range(3)
+        ]
+        slabs = [x.reshape(step * cols, 128) for x in slabs]
+        acc = dot(jnp.concatenate(slabs, axis=1), w2[...]).astype(BF16).astype(F32)
+        for o in range(2):
+            x = acc[:, 128 * o : 128 * (o + 1)]
+            r = pltpu.roll(x, SLOT, 1)
+            for hh in range(2):
+                y = jnp.where(low, r, x) if hh else jnp.where(low, x, r)
+                for j in range(step):
+                    gv[hh, 2 * (q * step + j) + o] = y[j * cols : (j + 1) * cols]
         return 0
 
     lax.fori_loop(0, 2, conv, 0)
 
 
-def right_kernel(gv, fl, rg0, rg1, rg2, acce, acco, both):
-    disp = gv.shape[1]
+def right_kernel(fl, *rest):
+    *grads, rg0, rg1, rg2, acce, acco, both = rest
+    disp = grads[0].shape[1]
     rows, cols, channels = rg0.shape
     wide = fl.shape[2]
     group_size = wide // SLOT
@@ -320,7 +328,8 @@
 
     lots = wide // 128
 
-    def right_row(h, _):
+    def right_row(gv, p, hh):
+        h = 2 * p + hh
         here = [
             [fl[h, PAD + 8 * b : PAD + 8 * b + 8, 128 * j : 128 * (j + 1)] for j in range(lots)]
             for b in range(count)
@@ -332,7 +341,7 @@
                     b = k + t - lead
                     if b < 0 or b >= count:
                         continue
-                    g = gv[h, 2 * t + odd, 8 * b : 8 * b + 8]
+                    g = gv[hh, 2 * t + odd, 8 * b : 8 * b + 8]
                     for j in range(lots):
                         term = g * here[b][j]
                         accs[j] = term if accs[j] is None else accs[j] + term
@@ -340,9 +349,9 @@
                     x = jnp.zeros((8, 128), F32) if accs[j] is None else accs[j]
                     buf[h, 8 * k : 8 * k + 8, 128 * j : 128 * (j + 1)] = x
         acco[h, 8 * (lead + count) :] = jnp.zeros((8, wide), F32)
-        return 0
-
-    lax.fori_loop(0, rows, right_row, 0)
+
+    for p, gv in enumerate(grads):
+        pl.loop(0, 2)(functools.partial(right_row, gv, p))
     size = back + cols
     for h in range(rows):
         both[h * size : (h + 1) * size] = (acce[h] + acco[h, STEP : STEP + size]).astype(BF16)
@@ -355,30 +364,32 @@
         rg0[h] = whole[at : at + cols]
 
 
-def left_kernel(gv, fr, fr4, lg, accl):
+def left_kernel(fr, fr4, *rest):
+    *grads, lg, accl = rest
     rows, cols, channels = lg.shape
-    disp, wide = gv.shape[1], fr.shape[2]
+    disp, wide = grads[0].shape[1], fr.shape[2]
     group_size = wide // SLOT
     reach = fr.shape[1] - cols - PAD
     count, times, lots = cols // 8, disp // 2, wide // 128
 
-    def left_row(h, _):
+    def left_row(gv, p, hh):
+        h = 2 * p + hh
         accs = [[None] * lots for _ in range(count)]
         for odd, band in enumerate((fr, fr4)):
             for r in range(1 - times, count):
                 at = reach + 8 * r
                 here = [band[h, at : at + 8, 128 * j : 128 * (j + 1)] for j in range(lots)]
                 for t in range(max(0, -r), min(times, count - r)):
-                    g = gv[h, 2 * t + odd, 8 * (r + t) : 8 * (r + t) + 8]
+                    g = gv[hh, 2 * t + odd, 8 * (r + t) : 8 * (r + t) + 8]
                     for j in range(lots):
                         term, acc = g * here[j], accs[r + t][j]
                         accs[r + t][j] = term if acc is None else acc + term
         for b in range(count):
             for j in range(lots):
                 accl[h, 8 * b : 8 * b + 8, 128 * j : 128 * (j + 1)] = accs[b][j] * (1.0 / group_size)
-        return 0
-
-    lax.fori_loop(0, rows, left_row, 0)
+
+    for p, gv in enumerate(grads):
+        pl.loop(0, 2)(functools.partial(left_row, gv, p))
     whole = accl[...].reshape(rows * cols, wide).astype(BF16)
     out = dot(whole, channel_table(channels, group_size, True)).astype(BF16)
     lg[...] = out.reshape(rows, cols, channels)
@@ -544,7 +555,7 @@
     return run
 
 
-def call(kernel, outs, scratch, *args, after=(), token=False, us=0.0):
+def call(kernel, outs, scratch, *args, after=(), token=False, us=0.0, alias=()):
     skip = len(after)
     if token:
         kernel = with_token(kernel, len(args), len(outs))
@@ -555,6 +566,7 @@
         in_specs=[pl.BlockSpec(memory_space=pl.ANY)] * skip + [VMEM] * len(args),
         out_specs=[VMEM] * len(outs),
         scratch_shapes=scratch,
+        input_output_aliases={skip + i: o for i, o in alias},
         compiler_params=pltpu.CompilerParams(vmem_limit_bytes=LIMIT),
         cost_estimate=pl.CostEstimate(
             flops=int(us * 1.15e9), bytes_accessed=int(us * 3.7e6), transcendentals=0
@@ -581,11 +593,13 @@
     return row_shift(pays[0], 1), row_shift(pays[1], -1)
 
 
-def hops(n_row, n_col):
+def stages(n_row, n_col):
     col_bits = [1 << i for i in range(1, n_col.bit_length() - 1)]
     row_bits = [n_col << i for i in range(n_row.bit_length() - 1)]
     assert n_col == 2 << len(col_bits) and n_row == 1 << len(row_bits)
-    return col_bits[::-1] + row_bits
+    bits = col_bits + row_bits
+    pairs = [bits[i : i + 2] for i in range(0, len(bits), 2)]
+    return [pair + [sum(pair)] if len(pair) == 2 else pair for pair in pairs]
 
 
 def on_device(left_features, right_features, conv_weight, cotangent):
@@ -646,6 +660,18 @@
         conv_weight.transpose(0, 1, 2, 4, 3),
         after=[passed],
     )
+    band = 104 + cols + PAD
+    banks = [((rows, total, wide), F32), ((rows, band, wide), F32), ((rows, band, wide), F32)]
+    spread_rows = 2 * rows * cols + rows * cols // 2
+    fl, fr, fr4 = call(
+        functools.partial(own_kernel, group_size),
+        banks,
+        [pltpu.VMEM((spread_rows, channels), BF16), pltpu.VMEM((spread_rows, wide), F32)],
+        left_features,
+        right_features,
+        far,
+        after=[w2],
+    )
     row_pays = call(
         functools.partial(row_kernel, ends, rows),
         [((disp // per, total, 128), BF16)] * n,
@@ -653,33 +679,25 @@
         by_even,
         by_odd,
         *rims,
-        after=[w2],
+        after=[fl],
         us=5.0,
     )
     top, bot = halos(row_pays)
-
-    band = 104 + cols + PAD
-    spread_rows = 3 * rows * cols + rows * cols // 2 + 2 * count
-    vbuf, fl, fr, fr4, *volume_rows = call(
+    spread_rows = rows * cols + 2 * count
+    fl, fr, fr4, vbuf, *volume_rows = call(
         functools.partial(volume_kernel, ends, group_size),
-        [
-            ((rows // 2, disp, total, 2 * SLOT), F32),
-            ((rows, total, wide), F32),
-            ((rows, band, wide), F32),
-            ((rows, band, wide), F32),
-        ]
+        banks
+        + [((rows // 2, disp, total, 2 * SLOT), F32)]
         + [((disp // 2 * total, 128), BF16)] * n,
-        [
-            pltpu.VMEM((spread_rows, channels), BF16),
-            pltpu.VMEM((spread_rows, wide), F32),
-        ],
-        left_features,
-        right_features,
+        [pltpu.VMEM((spread_rows, channels), BF16), pltpu.VMEM((spread_rows, wide), F32)],
         near,
-        far,
         by_even,
         by_odd,
-        us=2.3,
+        fl,
+        fr,
+        fr4,
+        us=1.8,
+        alias=[(3, 0), (4, 1), (5, 2)],
     )
     vtop, vbot = halos(volume_rows)
     keep, give, ctsh = call(
@@ -691,16 +709,18 @@
             pltpu.VMEM((3 * 128, 128), F32),
         ],
         vbuf, ctl, by_even, by_odd, top, bot,
-        us=2.6,
-    )
+        us=2.0,
+    )
+
+    def gradient(p, after):
+        kernel = functools.partial(dgrad_kernel, p)
+        us = 0.2 if after else 0.9
+        return call(kernel, [((2, disp, cols, 128), F32)], [], ctsh, w2, after=after, us=us)[0]
+
     got = swap(give, 1)
-    def join(part, mask, kind, after=(), us=0.0):
-        terms = (part, swap(part, mask))
-        return call(sum_kernel, [(part.shape, kind)], [], *terms, after=after, us=us)[0]
-
-    (gv,) = call(dgrad_kernel, [((rows, disp, cols, 128), F32)], [], ctsh, w2, us=2.0)
-    (part,) = call(sum_kernel, [(keep.shape, BF16)], [], keep, got, after=[gv], us=4.0)
-    first, *others, last = hops(n_row, n_col)
+    grads = [gradient(0, [])]
+    (part,) = call(sum_kernel, [(keep.shape, BF16)], [], keep, got, after=grads, us=4.0)
+    grads += [gradient(p, [part]) for p in range(1, rows // 2)]
     rg0, rg1, rg2 = call(
         right_kernel,
         [
@@ -713,22 +733,31 @@
             pltpu.VMEM((rows, cols + cols + cols // 2 + 8, wide), F32),
             pltpu.VMEM((rows * (cols + cols + cols // 2), wide), BF16),
         ],
-        gv, fl,
-        after=[part],
-        us=1.0,
+        fl, *grads,
+        after=[part, vtop],
+        us=0.2,
     )
     rg1 = swap(rg1, 1)
-    part = join(part, first, F32, after=[rg0], us=4.0)
+    *middle, final = stages(n_row, n_col)
+    order = [rg0]
+    for stage in middle:
+        parts = [part] + [swap(part, m) for m in stage]
+        (part,) = call(sum_kernel, [(part.shape, BF16)], [], *parts, after=order, us=4.0)
+        order = []
+    parts = [part] + [swap(part, m) for m in final]
+    (rg2,) = call(
+        combine_kernel, [((rows, cols, channels), BF16)], [], rg1, rg2, after=[part]
+    )
     lg, left_done = call(
         left_kernel,
         [((rows, cols, channels), BF16)],
         [pltpu.VMEM((rows, cols, wide), F32)],
-        gv, fr, fr4,
-        after=[part],
+        fr, fr4, *grads,
+        after=[rg2],
         token=True,
         us=1.9,
     )
-    part = join(part, others[0], BF16, after=[left_done], us=4.0)
+    (part,) = call(sum_kernel, [(part.shape, F32)], [], *parts, after=[left_done])
     (spread,) = call(
         functools.partial(spread_kernel, masks, groups),
         [((disp // 2 + 1, 2, cols, 3 * rows * SLOT), BF16)],
@@ -737,14 +766,6 @@
         after=[part],
         us=1.3,
     )
-    order = [spread]
-    for mask in others[1:]:
-        part = join(part, mask, BF16, after=order, us=4.0)
-        order = []
-    (rg2,) = call(
-        combine_kernel, [((rows, cols, channels), BF16)], [], rg1, rg2, after=[part]
-    )
-    part = join(part, last, F32, after=[rg2], us=4.0)
     output, conv_done = call(
         conv_kernel,
         [((disp, rows, feat, cols), BF16)],

time: 49.2 us -> 47.2 us (0.959)
  waiting for transfers between devices: 8.14 us -> 6 us
    ppermute x2, waiting for transfers between devices: 2.94 us -> 0.54 us  [col_shift(): return lax.ppermute(block, 'col', route)]
    ppermute x2, waiting for transfers between devices: 1.42 us -> 3.25 us  [halos(): got = lax.ppermute(pays[0], 'row', [(0, 1), (1, 0)])]
    ppermute x9 -> x11, waiting for transfers between devices: 3.78 us -> 2.2 us  [swap(): return lax.ppermute(block, ('row', 'col'), route)]
    ppermute x9 -> x11, starting transfers between devices: 11.8 us -> 10.7 us  [swap(): return lax.ppermute(block, ('row', 'col'), route)]
    ppermute x2, starting transfers between devices: 2.36 us -> 3.12 us  [halos(): got = lax.ppermute(pays[0], 'row', [(0, 1), (1, 0)])]
  transfers between devices with their start and end apart: 14 -> 16, of which waited for: 7 -> 5; matrix products, arithmetic and copies ran while one was open for 3% -> 3% of each run, Pallas kernels for 31% -> 28%
where the time goes in v1:
time: 47.2 us; the launch traced here: 46.9 us
  starting transfers between devices  20.8 us (44%)
  Pallas kernels  16.4 us (35%)
  waiting for transfers between devices  6 us (13%)
  local copies, waits for them, and re-layouts  2.77 us (6%)
  between operations  0.89 us (2%)
    pallas_call x18, Pallas kernels, call(): pl.pallas_call(lambda *refs: kernel(*refs[skip:]), out_shape=[jax.ShapeDt...  16.4 us
    ppermute x11, starting transfers between devices, swap(): return lax.ppermute(block, ('row', 'col'), route)  10.7 us
    ppermute x2, starting transfers between devices, col_shift(): return lax.ppermute(block, 'col', route)  6.31 us
    ppermute x2, waiting for transfers between devices, halos(): got = lax.ppermute(pays[0], 'row', [(0, 1), (1, 0)])  3.25 us
    ppermute x2, starting transfers between devices, halos(): got = lax.ppermute(pays[0], 'row', [(0, 1), (1, 0)])  3.12 us
    ppermute x11, waiting for transfers between devices, swap(): return lax.ppermute(block, ('row', 'col'), route)  2.2 us
    slice x2, local copies, waits for them, and re-layouts, on_device(): x[:, at]  1.56 us
    unnamed x8, local copies, waits for them, and re-layouts  1.19 us
  transfers between devices with their start and end apart: 16, of which 5 were waited for; matrix products, arithmetic and copies ran while one was open for 3% of the time, Pallas kernels for 28%

profile of v1, /device:TPU:0, one launch (start us, length us, event | category | flops | bytes accessed | tf_op | source)
XLA Modules:
  0.0 46.9 jit_solution(15195505156147067830)
XLA Ops:
  0.6 0.0 copy-start
  0.6 0.0 copy-start.2
  0.7 5.0 %collective-permute-start = (bf16[4,64,320]{2,1,0:T(8,128)(2,1)}, bf16[4,64,320]{2,1,0:T(8,128)(2,1)S(1)}, u32[]{:S(2)}, u32[]{:S(2)}) collective-permute-start(bf16[4,64,320]{2,1,0:T(8,128)(2,1)} %refs_2_.1), channel_id=1, source_target_pairs={{0,2},{1,3},{2,4},{3,5},{4,6},{5,7},{6,8},{7,9},{8,10},{9,11},{10,... | collective-permute-start | bytes 491528 | tf_op jit(solution)/shard_map/ppermute | solution.py:580
  5.7 0.8 %fusion.1 = (bf16[4,1,320]{2,1,0:T(2,128)(2,1)S(1)}, bf16[4,1,320]{2,1,0:T(2,128)(2,1)S(1)}) fusion(bf16[4,64,320]{2,1,0:T(8,128)(2,1)} %refs_2_.1), kind=kLoop, calls=%fused_computation.6 | loop fusion | bytes 10240 | tf_op jit(solution)/shard_map/slice | solution.py:645
  6.5 0.8 %fusion = (bf16[4,1,320]{2,1,0:T(2,128)(2,1)S(1)}, bf16[4,1,320]{2,1,0:T(2,128)(2,1)S(1)}) fusion(bf16[4,64,320]{2,1,0:T(8,128)(2,1)} %refs_1_.3), kind=kLoop, calls=%fused_computation.5 | loop fusion | bytes 10240 | tf_op jit(solution)/shard_map/slice | solution.py:645
  7.3 0.0 copy-start.1
  7.3 0.0 copy-start.3
  7.3 1.2 %copy-done.3 = bf16[24,4,64,32]{2,3,1,0:T(8,128)(2,1)S(1)} copy-done((bf16[24,4,64,32]{2,3,1,0:T(8,128)(2,1)S(1)}, bf16[24,4,64,32]{2,3,1,0:T(8,128)(2,1)}, u32[]{:S(2)}) %copy-start.3) | copy-done | bytes 393240
  8.5 0.3 shard_map.75
  8.8 0.1 collective-permute-start.2
  8.9 0.7 %collective-permute-start.3 = (bf16[32,320]{1,0:T(8,128)(2,1)S(1)}, bf16[32,320]{1,0:T(8,128)(2,1)S(1)}, u32[]{:S(2)}, u32[]{:S(2)}) collective-permute-start(bf16[32,320]{1,0:T(8,128)(2,1)S(1)} %get-tuple-element.32), channel_id=1, source_target_pairs={{1,2},{3,4},{5,6},{7,8},{9,10},{11,12},{13,14},{2,1},{4,3},{6,5},{... | collective-permute-start | bytes 61448 | tf_op jit(solution)/shard_map/ppermute | solution.py:651
  9.6 0.5 %collective-permute-done.refs_2_.refs_3_ = bf16[4,64,320]{2,1,0:T(8,128)(2,1)S(1)} collective-permute-done((bf16[4,64,320]{2,1,0:T(8,128)(2,1)}, bf16[4,64,320]{2,1,0:T(8,128)(2,1)S(1)}, u32[]{:S(2)}, u32[]{:S(2)}) %collective-permute-start) | collective-permute-done | bytes 163872 | tf_op jit(solution)/shard_map/ppermute | solution.py:580
  10.1 0.0 copy-done
  10.1 0.1 shard_map.76.refs_0_
  10.2 2.4 %collective-permute-start.1 = (bf16[4,64,320]{2,1,0:T(8,128)(2,1)S(1)}, bf16[4,64,320]{2,1,0:T(8,128)(2,1)S(1)}, u32[]{:S(2)}, u32[]{:S(2)}) collective-permute-start(bf16[4,64,320]{2,1,0:T(8,128)(2,1)S(1)} %shard_map.76.refs_0_), channel_id=1, source_target_pairs={{0,1},{1,0},{2,3},{3,2},{4,5},{5,4},{6,7},{7,6},{8,9},{9,8},{10,11... | collective-permute-start | bytes 491528 | tf_op jit(solution)/shard_map/ppermute | solution.py:633
  12.6 0.0 copy-done.2
  12.6 0.8 %shard_map.77 = (bf16[1536,256]{1,0:T(8,128)(2,1)S(1)}, bf16[3072,256]{1,0:T(8,128)(2,1)S(1)}) custom-call(bf16[4,64,320]{2,1,0:T(8,128)(2,1)S(1)} %shard_map.76.refs_0_, bf16[3,3,3,32,40]{4,3,2,1,0:T(8,128)(2,1)S(1)} %bitcast.12), custom_call_target="tpu_custom_call" | custom-call | tf_op jit(solution)/shard_map/pallas_call | solution.py:563
  13.5 0.0 copy-done.1
  13.5 0.5 %shard_map.78 = (f32[4,80,512]{2,1,0:T(8,128)S(1)}, f32[4,176,512]{2,1,0:T(8,128)S(1)}, f32[4,176,512]{2,1,0:T(8,128)S(1)}) custom-call(bf16[1536,256]{1,0:T(8,128)(2,1)S(1)} %get-tuple-element.33.refs_0_.refs_1_.refs_2_, bf16[4,64,320]{2,1,0:T(8,128)(2,1)S(1)} %copy-done.1, bf16[4,64,320]{2,1,0:T(8,128)(2,1)S(1)} %copy-done, ...), custom_call_target="tpu_custom_call" | custom-call | tf_op jit(solution)/shard_map/pallas_call | solution.py:563
  14.0 0.0 collective-permute-done.2.refs_1_.refs_2_
  14.0 0.0 collective-permute-done.3.refs_2_.refs_3_
  14.0 0.1 shard_map.80
  14.1 1.6 %collective-permute-start.4 = (bf16[6,80,128]{2,1,0:T(8,128)(2,1)S(1)}, bf16[6,80,128]{2,1,0:T(8,128)(2,1)S(1)}, u32[]{:S(2)}, u32[]{:S(2)}) collective-permute-start(bf16[6,80,128]{2,1,0:T(8,128)(2,1)S(1)} %shard_map.80), channel_id=1, source_target_pairs={{0,16},{16,0},{1,17},{17,1},{2,18},{18,2},{3,19},{19,3},{4,20},{20... | collective-permute-start | bytes 368648 | tf_op jit(solution)/shard_map/ppermute | solution.py:591
  15.7 0.0 collective-permute-done.1.refs_0_
  15.7 2.0 %shard_map.79 = (f32[4,80,512]{2,1,0:T(8,128)S(1)}, f32[4,176,512]{2,1,0:T(8,128)S(1)}, f32[4,176,512]{2,1,0:T(8,128)S(1)}, f32[2,24,80,128]{3,2,1,0:T(8,128)S(1)}, bf16[960,128]{1,0:T(8,128)(2,1)S(1)}) custom-call(bf16[4,64,320]{2,1,0:T(8,128)(2,1)S(1)} %collective-permute-done.1.refs_0_, ...), custom_call_target="tpu_custom_call", output_to_operand_aliasing={{0}: (3, {}), {1}: (4, {}), {2}: (5, {})} | custom-call | flops 2070000000 | bytes 6660000 | tf_op jit(solution)/shard_map/pallas_call | solution.py:563
  17.7 2.2 %collective-permute-done.4.refs_4_.refs_5_ = bf16[6,80,128]{2,1,0:T(8,128)(2,1)S(1)} collective-permute-done((bf16[6,80,128]{2,1,0:T(8,128)(2,1)S(1)}, bf16[6,80,128]{2,1,0:T(8,128)(2,1)S(1)}, u32[]{:S(2)}, u32[]{:S(2)}) %collective-permute-start.4) | collective-permute-done | bytes 122912 | tf_op jit(solution)/shard_map/ppermute | solution.py:591
  19.9 2.0 %shard_map.81 = (f32[192,128]{1,0:T(8,128)S(1)}, f32[192,128]{1,0:T(8,128)S(1)}, bf16[13,2,64,768]{3,2,1,0:T(8,128)(2,1)S(1)}) custom-call(f32[2,24,80,128]{3,2,1,0:T(8,128)S(1)} %get-tuple-element.37.refs_0_.refs_1_, bf16[24,64,128]{2,1,0:T(8,128)(2,1)S(1)} %get-tuple-element.30.refs_0_.refs_1_, bf16[32,320]{1,0:T(8,128)(2,1)S(1)} %collective-permute-done.2.refs_1_.refs_2_, ...), custom_call_target="tpu_custom_call" | custom-call | flops 2300000000 | bytes 7400000 | tf_op jit(solution)/shard_map/pallas_call | solution.py:563
  22.0 0.1 collective-permute-start.5
  22.0 1.6 %collective-permute-start.6 = (bf16[960,128]{1,0:T(8,128)(2,1)S(1)}, bf16[960,128]{1,0:T(8,128)(2,1)S(1)}, u32[]{:S(2)}, u32[]{:S(2)}) collective-permute-start(bf16[960,128]{1,0:T(8,128)(2,1)S(1)} %get-tuple-element.42), channel_id=1, source_target_pairs={{0,16},{16,0},{1,17},{17,1},{2,18},{18,2},{3,19},{19,3},{4,20},{20... | collective-permute-start | bytes 737288 | tf_op jit(solution)/shard_map/ppermute | solution.py:591
  23.6 1.1 %shard_map.82.refs_0_.refs_3_ = f32[2,24,64,128]{3,2,1,0:T(8,128)S(1)} custom-call(bf16[13,2,64,768]{3,2,1,0:T(8,128)(2,1)S(1)} %get-tuple-element.39.refs_0_.refs_1_, bf16[1536,256]{1,0:T(8,128)(2,1)S(1)} %get-tuple-element.33.refs_0_.refs_1_.refs_2_), custom_call_target="tpu_custom_call" | custom-call | flops 1035000000 | bytes 3330000 | tf_op jit(solution)/shard_map/pallas_call | solution.py:563
  24.7 0.0 collective-permute-done.5.refs_2_
  24.7 2.8 %collective-permute-start.9 = (bf16[192,128]{1,0:T(8,128)(2,1)S(1)}, bf16[192,128]{1,0:T(8,128)(2,1)S(1)}, u32[]{:S(2)}, u32[]{:S(2)}) collective-permute-start(bf16[192,128]{1,0:T(8,128)(2,1)S(1)} %shard_map.83.refs_0_.refs_1_), channel_id=1, source_target_pairs={{0,6},{1,7},{2,4},{3,5},{4,2},{5,3},{6,0},{7,1},{8,14},{9,15},{10,... | collective-permute-start | bytes 147464 | tf_op jit(solution)/shard_map/ppermute | solution.py:633
  27.6 0.5 collective-permute-start.8
  28.0 0.3 collective-permute-start.7
  28.3 1.1 %shard_map.84.refs_4_ = f32[2,24,64,128]{3,2,1,0:T(8,128)S(1)} custom-call(bf16[192,128]{1,0:T(8,128)(2,1)S(1)} %shard_map.83.refs_0_.refs_1_, bf16[13,2,64,768]{3,2,1,0:T(8,128)(2,1)S(1)} %get-tuple-element.39.refs_0_.refs_1_, bf16[1536,256]{1,0:T(8,128)(2,1)S(1)} %get-tuple-element.33.refs_0_.refs_1_.refs_2_), custom_call_target="tpu_custom_call" | custom-call | flops 230000000 | bytes 740000 | tf_op jit(solution)/shard_map/pallas_call | solution.py:563
  29.4 1.0 %collective-permute-done.6.refs_1_.refs_2_.refs_3_ = bf16[960,128]{1,0:T(8,128)(2,1)S(1)} collective-permute-done((bf16[960,128]{1,0:T(8,128)(2,1)S(1)}, bf16[960,128]{1,0:T(8,128)(2,1)S(1)}, u32[]{:S(2)}, u32[]{:S(2)}) %collective-permute-start.6) | collective-permute-done | bytes 245792 | tf_op jit(solution)/shard_map/ppermute | solution.py:591
  30.4 1.3 %shard_map.85 = (bf16[4,64,320]{2,1,0:T(8,128)(2,1)S(1)}, bf16[4,64,320]{2,1,0:T(8,128)(2,1)S(1)}, bf16[4,32,320]{2,1,0:T(8,128)(2,1)S(1)}) custom-call(bf16[192,128]{1,0:T(8,128)(2,1)S(1)} %shard_map.83.refs_0_.refs_1_, bf16[960,128]{1,0:T(8,128)(2,1)S(1)} %collective-permute-done.6.refs_1_.refs_2_.refs_3_, f32[4,80,512]{2,1,0:T(8,128)S(1)} %get-tuple-element.43.refs_2_, ...), custom_call_target="tpu_custom_call" | custom-call | flops 230000000 | bytes 740000 | tf_op jit(solution)/shard_map/pallas_call | solution.py:563
  31.7 0.1 collective-permute-start.10
  31.8 0.0 collective-permute-done.9.refs_4_
  31.8 0.0 collective-permute-done.8.refs_3_
  31.8 0.3 collective-permute-done.7.refs_2_
  32.1 3.6 %collective-permute-start.13 = (bf16[192,128]{1,0:T(8,128)(2,1)S(1)}, bf16[192,128]{1,0:T(8,128)(2,1)S(1)}, u32[]{:S(2)}, u32[]{:S(2)}) collective-permute-start(bf16[192,128]{1,0:T(8,128)(2,1)S(1)} %shard_map.86.refs_0_.refs_1_), channel_id=1, source_target_pairs={{0,24},{1,25},{2,26},{3,27},{4,28},{5,29},{6,30},{7,31},{8,16},{9,... | collective-permute-start | bytes 147464 | tf_op jit(solution)/shard_map/ppermute | solution.py:633
  35.7 0.5 %collective-permute-start.12 = (bf16[192,128]{1,0:T(8,128)(2,1)S(1)}, bf16[192,128]{1,0:T(8,128)(2,1)S(1)}, u32[]{:S(2)}, u32[]{:S(2)}) collective-permute-start(bf16[192,128]{1,0:T(8,128)(2,1)S(1)} %shard_map.86.refs_0_.refs_1_), channel_id=1, source_target_pairs={{0,16},{1,17},{2,18},{3,19},{4,20},{5,21},{6,22},{7,23},{8,24},{9,... | collective-permute-start | bytes 147464 | tf_op jit(solution)/shard_map/ppermute | solution.py:633
  36.3 0.3 collective-permute-start.11
  36.6 0.0 collective-permute-done.10.refs_1_.refs_4_
  36.6 0.1 shard_map.87.refs_0_
  36.7 1.3 %collective-permute-start.15 = (bf16[4,64,320]{2,1,0:T(8,128)(2,1)S(1)}, bf16[4,64,320]{2,1,0:T(8,128)(2,1)S(1)}, u32[]{:S(2)}, u32[]{:S(2)}) collective-permute-start(bf16[4,64,320]{2,1,0:T(8,128)(2,1)S(1)} %shard_map.87.refs_0_), channel_id=1, source_target_pairs={{2,0},{3,1},{4,2},{5,3},{6,4},{7,5},{8,6},{9,7},{10,8},{11,9},{12,... | collective-permute-start | bytes 491528 | tf_op jit(solution)/shard_map/ppermute | solution.py:580
  38.0 1.9 %shard_map.88 = (bf16[4,64,320]{2,1,0:T(8,128)(2,1)}, f32[8,128]{1,0:T(8,128)S(1)}) custom-call(bf16[4,64,320]{2,1,0:T(8,128)(2,1)S(1)} %shard_map.87.refs_0_, f32[4,176,512]{2,1,0:T(8,128)S(1)} %get-tuple-element.47.refs_1_, f32[4,176,512]{2,1,0:T(8,128)S(1)} %get-tuple-element.48.refs_2_, f32[2,24,64,128]{3,2,1,0:T(8,128)S(1)} %shard_map.82.refs_0_.refs_3_, ...), custom_call_target="tpu_custom_call" | custom-call | flops 2184999936 | bytes 7030000 | tf_op jit(solution)/shard_map/pallas_call | solution.py:563
  39.9 0.0 collective-permute-done.13.refs_4_
  39.9 0.0 collective-permute-done.12.refs_3_
  39.9 1.9 %collective-permute-done.11.refs_2_ = bf16[192,128]{1,0:T(8,128)(2,1)S(1)} collective-permute-done((bf16[192,128]{1,0:T(8,128)(2,1)S(1)}, bf16[192,128]{1,0:T(8,128)(2,1)S(1)}, u32[]{:S(2)}, u32[]{:S(2)}) %collective-permute-start.11) | collective-permute-done | bytes 49184 | tf_op jit(solution)/shard_map/ppermute | solution.py:633
  41.8 0.1 collective-permute-start.14
  41.9 1.3 %shard_map.90.refs_1_ = bf16[13,2,64,768]{3,2,1,0:T(8,128)(2,1)S(1)} custom-call(f32[192,128]{1,0:T(8,128)S(1)} %shard_map.89.refs_0_.refs_1_, f32[2,24,80,128]{3,2,1,0:T(8,128)S(1)} %get-tuple-element.37.refs_0_.refs_1_, bf16[960,128]{1,0:T(8,128)(2,1)S(1)} %collective-permute-done.6.refs_1_.refs_2_.refs_3_, ...), custom_call_target="tpu_custom_call" | custom-call | flops 1495000064 | bytes 4810000 | tf_op jit(solution)/shard_map/pallas_call | solution.py:563
  43.2 2.6 %shard_map.91 = (bf16[24,4,32,64]{3,2,1,0:T(8,128)(2,1)}, f32[8,128]{1,0:T(8,128)S(1)}) custom-call(f32[192,128]{1,0:T(8,128)S(1)} %shard_map.89.refs_0_.refs_1_, bf16[13,2,64,768]{3,2,1,0:T(8,128)(2,1)S(1)} %shard_map.90.refs_1_, bf16[3072,256]{1,0:T(8,128)(2,1)S(1)} %get-tuple-element.50.refs_2_), custom_call_target="tpu_custom_call" | custom-call | flops 2990000128 | bytes 9620000 | tf_op jit(solution)/shard_map/pallas_call | solution.py:563
  45.8 0.0 collective-permute-done.14.refs_2_
  45.8 0.0 collective-permute-done.15.refs_5_
  45.8 1.1 %shard_map.92 = (f32[3,3,3,32,40]{4,3,2,1,0:T(8,128)}, bf16[4,64,320]{2,1,0:T(8,128)(2,1)}) custom-call(f32[8,128]{1,0:T(8,128)S(1)} %get-tuple-element.52.refs_0_, f32[192,128]{1,0:T(8,128)S(1)} %shard_map.89.refs_0_.refs_1_, f32[192,128]{1,0:T(8,128)S(1)} %collective-permute-done.14.refs_2_, bf16[4,64,320]{2,1,0:T(8,128)(2,1)S(1)} %get-tuple-element.44.refs_0_.refs_3_, ...), custom_call_target="tpu_custom_call" | custom-call | flops 1150000000 | bytes 3700000 | tf_op jit(solution)/shard_map/pallas_call | solution.py:563
  (6 shorter events, 0.1 us)
Async XLA Ops:
  0.6 9.5 %copy-start = (bf16[4,64,320]{2,1,0:T(8,128)(2,1)S(1)}, bf16[4,64,320]{2,1,0:T(8,128)(2,1)}, u32[]{:S(2)}) copy-start(bf16[4,64,320]{2,1,0:T(8,128)(2,1)} %refs_2_.1) | copy-start | bytes 491524
  0.6 12.0 %copy-start.2 = (bf16[3,3,3,40,32]{3,4,2,1,0:T(8,128)(2,1)S(1)}, bf16[3,3,3,40,32]{3,4,2,1,0:T(8,128)(2,1)}, u32[]{:S(2)}) copy-start(bf16[3,3,3,40,32]{3,4,2,1,0:T(8,128)(2,1)} %param.6) | copy-start | bytes 207364
  0.7 9.5 %collective-permute-start = (bf16[4,64,320]{2,1,0:T(8,128)(2,1)}, bf16[4,64,320]{2,1,0:T(8,128)(2,1)S(1)}, u32[]{:S(2)}, u32[]{:S(2)}) collective-permute-start(bf16[4,64,320]{2,1,0:T(8,128)(2,1)} %refs_2_.1), channel_id=1, source_target_pairs={{0,2},{1,3},{2,4},{3,5},{4,6},{5,7},{6,8},{7,9},{8,10},{9,11},{10,... | collective-permute-start | bytes 491528 | tf_op jit(solution)/shard_map/ppermute | solution.py:580
  7.3 6.2 %copy-start.1 = (bf16[4,64,320]{2,1,0:T(8,128)(2,1)S(1)}, bf16[4,64,320]{2,1,0:T(8,128)(2,1)}, u32[]{:S(2)}) copy-start(bf16[4,64,320]{2,1,0:T(8,128)(2,1)} %refs_1_.3) | copy-start | bytes 491524
  7.3 1.2 %copy-start.3 = (bf16[24,4,64,32]{2,3,1,0:T(8,128)(2,1)S(1)}, bf16[24,4,64,32]{2,3,1,0:T(8,128)(2,1)}, u32[]{:S(2)}) copy-start(bf16[24,4,64,32]{2,3,1,0:T(8,128)(2,1)} %param.7) | copy-start | bytes 1179652
  8.8 5.2 %collective-permute-start.2 = (bf16[32,320]{1,0:T(8,128)(2,1)S(1)}, bf16[32,320]{1,0:T(8,128)(2,1)S(1)}, u32[]{:S(2)}, u32[]{:S(2)}) collective-permute-start(bf16[32,320]{1,0:T(8,128)(2,1)S(1)} %get-tuple-element.31), channel_id=1, source_target_pairs={{0,1},{1,0},{2,3},{3,2},{4,5},{5,4},{6,7},{7,6},{8,9},{9,8},{10,11... | collective-permute-start | bytes 61448 | tf_op jit(solution)/shard_map/ppermute | solution.py:633
  8.9 5.1 %collective-permute-start.3 = (bf16[32,320]{1,0:T(8,128)(2,1)S(1)}, bf16[32,320]{1,0:T(8,128)(2,1)S(1)}, u32[]{:S(2)}, u32[]{:S(2)}) collective-permute-start(bf16[32,320]{1,0:T(8,128)(2,1)S(1)} %get-tuple-element.32), channel_id=1, source_target_pairs={{1,2},{3,4},{5,6},{7,8},{9,10},{11,12},{13,14},{2,1},{4,3},{6,5},{... | collective-permute-start | bytes 61448 | tf_op jit(solution)/shard_map/ppermute | solution.py:651
  10.2 5.5 %collective-permute-start.1 = (bf16[4,64,320]{2,1,0:T(8,128)(2,1)S(1)}, bf16[4,64,320]{2,1,0:T(8,128)(2,1)S(1)}, u32[]{:S(2)}, u32[]{:S(2)}) collective-permute-start(bf16[4,64,320]{2,1,0:T(8,128)(2,1)S(1)} %shard_map.76.refs_0_), channel_id=1, source_target_pairs={{0,1},{1,0},{2,3},{3,2},{4,5},{5,4},{6,7},{7,6},{8,9},{9,8},{10,11... | collective-permute-start | bytes 491528 | tf_op jit(solution)/shard_map/ppermute | solution.py:633
  14.1 5.8 %collective-permute-start.4 = (bf16[6,80,128]{2,1,0:T(8,128)(2,1)S(1)}, bf16[6,80,128]{2,1,0:T(8,128)(2,1)S(1)}, u32[]{:S(2)}, u32[]{:S(2)}) collective-permute-start(bf16[6,80,128]{2,1,0:T(8,128)(2,1)S(1)} %shard_map.80), channel_id=1, source_target_pairs={{0,16},{16,0},{1,17},{17,1},{2,18},{18,2},{3,19},{19,3},{4,20},{20... | collective-permute-start | bytes 368648 | tf_op jit(solution)/shard_map/ppermute | solution.py:591
  22.0 2.7 %collective-permute-start.5 = (f32[192,128]{1,0:T(8,128)S(1)}, f32[192,128]{1,0:T(8,128)S(1)}, u32[]{:S(2)}, u32[]{:S(2)}) collective-permute-start(f32[192,128]{1,0:T(8,128)S(1)} %get-tuple-element.41), channel_id=1, source_target_pairs={{0,1},{1,0},{2,3},{3,2},{4,5},{5,4},{6,7},{7,6},{8,9},{9,8},{10,11... | collective-permute-start | bytes 294920 | tf_op jit(solution)/shard_map/ppermute | solution.py:633
  22.0 8.4 %collective-permute-start.6 = (bf16[960,128]{1,0:T(8,128)(2,1)S(1)}, bf16[960,128]{1,0:T(8,128)(2,1)S(1)}, u32[]{:S(2)}, u32[]{:S(2)}) collective-permute-start(bf16[960,128]{1,0:T(8,128)(2,1)S(1)} %get-tuple-element.42), channel_id=1, source_target_pairs={{0,16},{16,0},{1,17},{17,1},{2,18},{18,2},{3,19},{19,3},{4,20},{20... | collective-permute-start | bytes 737288 | tf_op jit(solution)/shard_map/ppermute | solution.py:591
  24.7 7.0 %collective-permute-start.9 = (bf16[192,128]{1,0:T(8,128)(2,1)S(1)}, bf16[192,128]{1,0:T(8,128)(2,1)S(1)}, u32[]{:S(2)}, u32[]{:S(2)}) collective-permute-start(bf16[192,128]{1,0:T(8,128)(2,1)S(1)} %shard_map.83.refs_0_.refs_1_), channel_id=1, source_target_pairs={{0,6},{1,7},{2,4},{3,5},{4,2},{5,3},{6,0},{7,1},{8,14},{9,15},{10,... | collective-permute-start | bytes 147464 | tf_op jit(solution)/shard_map/ppermute | solution.py:633
  27.6 4.2 %collective-permute-start.8 = (bf16[192,128]{1,0:T(8,128)(2,1)S(1)}, bf16[192,128]{1,0:T(8,128)(2,1)S(1)}, u32[]{:S(2)}, u32[]{:S(2)}) collective-permute-start(bf16[192,128]{1,0:T(8,128)(2,1)S(1)} %shard_map.83.refs_0_.refs_1_), channel_id=1, source_target_pairs={{0,4},{1,5},{2,6},{3,7},{4,0},{5,1},{6,2},{7,3},{8,12},{9,13},{10,... | collective-permute-start | bytes 147464 | tf_op jit(solution)/shard_map/ppermute | solution.py:633
  28.0 4.1 %collective-permute-start.7 = (bf16[192,128]{1,0:T(8,128)(2,1)S(1)}, bf16[192,128]{1,0:T(8,128)(2,1)S(1)}, u32[]{:S(2)}, u32[]{:S(2)}) collective-permute-start(bf16[192,128]{1,0:T(8,128)(2,1)S(1)} %shard_map.83.refs_0_.refs_1_), channel_id=1, source_target_pairs={{0,2},{1,3},{2,0},{3,1},{4,6},{5,7},{6,4},{7,5},{8,10},{9,11},{10,... | collective-permute-start | bytes 147464 | tf_op jit(solution)/shard_map/ppermute | solution.py:633
  31.7 4.9 %collective-permute-start.10 = (bf16[4,64,320]{2,1,0:T(8,128)(2,1)S(1)}, bf16[4,64,320]{2,1,0:T(8,128)(2,1)S(1)}, u32[]{:S(2)}, u32[]{:S(2)}) collective-permute-start(bf16[4,64,320]{2,1,0:T(8,128)(2,1)S(1)} %get-tuple-element.45), channel_id=1, source_target_pairs={{0,1},{1,0},{2,3},{3,2},{4,5},{5,4},{6,7},{7,6},{8,9},{9,8},{10,11... | collective-permute-start | bytes 491528 | tf_op jit(solution)/shard_map/ppermute | solution.py:633
  32.1 7.7 %collective-permute-start.13 = (bf16[192,128]{1,0:T(8,128)(2,1)S(1)}, bf16[192,128]{1,0:T(8,128)(2,1)S(1)}, u32[]{:S(2)}, u32[]{:S(2)}) collective-permute-start(bf16[192,128]{1,0:T(8,128)(2,1)S(1)} %shard_map.86.refs_0_.refs_1_), channel_id=1, source_target_pairs={{0,24},{1,25},{2,26},{3,27},{4,28},{5,29},{6,30},{7,31},{8,16},{9,... | collective-permute-start | bytes 147464 | tf_op jit(solution)/shard_map/ppermute | solution.py:633
  35.7 4.2 %collective-permute-start.12 = (bf16[192,128]{1,0:T(8,128)(2,1)S(1)}, bf16[192,128]{1,0:T(8,128)(2,1)S(1)}, u32[]{:S(2)}, u32[]{:S(2)}) collective-permute-start(bf16[192,128]{1,0:T(8,128)(2,1)S(1)} %shard_map.86.refs_0_.refs_1_), channel_id=1, source_target_pairs={{0,16},{1,17},{2,18},{3,19},{4,20},{5,21},{6,22},{7,23},{8,24},{9,... | collective-permute-start | bytes 147464 | tf_op jit(solution)/shard_map/ppermute | solution.py:633
  36.3 5.5 %collective-permute-start.11 = (bf16[192,128]{1,0:T(8,128)(2,1)S(1)}, bf16[192,128]{1,0:T(8,128)(2,1)S(1)}, u32[]{:S(2)}, u32[]{:S(2)}) collective-permute-start(bf16[192,128]{1,0:T(8,128)(2,1)S(1)} %shard_map.86.refs_0_.refs_1_), channel_id=1, source_target_pairs={{0,8},{1,9},{2,10},{3,11},{4,12},{5,13},{6,14},{7,15},{8,0},{9,1},... | collective-permute-start | bytes 147464 | tf_op jit(solution)/shard_map/ppermute | solution.py:633
  36.7 9.1 %collective-permute-start.15 = (bf16[4,64,320]{2,1,0:T(8,128)(2,1)S(1)}, bf16[4,64,320]{2,1,0:T(8,128)(2,1)S(1)}, u32[]{:S(2)}, u32[]{:S(2)}) collective-permute-start(bf16[4,64,320]{2,1,0:T(8,128)(2,1)S(1)} %shard_map.87.refs_0_), channel_id=1, source_target_pairs={{2,0},{3,1},{4,2},{5,3},{6,4},{7,5},{8,6},{9,7},{10,8},{11,9},{12,... | collective-permute-start | bytes 491528 | tf_op jit(solution)/shard_map/ppermute | solution.py:580
  41.8 4.0 %collective-permute-start.14 = (f32[192,128]{1,0:T(8,128)S(1)}, f32[192,128]{1,0:T(8,128)S(1)}, u32[]{:S(2)}, u32[]{:S(2)}) collective-permute-start(f32[192,128]{1,0:T(8,128)S(1)} %shard_map.89.refs_0_.refs_1_), channel_id=1, source_target_pairs={{0,1},{1,0},{2,3},{3,2},{4,5},{5,4},{6,7},{7,6},{8,9},{9,8},{10,11... | collective-permute-start | bytes 294920 | tf_op jit(solution)/shard_map/ppermute | solution.py:633

commit v2 on v1

--- a/solution.py
+++ b/solution.py
@@ -54,17 +54,16 @@
     for i, col in enumerate((cols - 1, 0)):
         block = ctf[pl.ds(col, disp, stride=cols), :]
         block = jnp.concatenate([block, jnp.zeros((disp, even.shape[1] - rows * feat), F32)], axis=1)
-        edge = rims_in[i * 2 * rows : (i + 1) * 2 * rows].astype(F32)
-        columns.append(jnp.concatenate([block, edge], axis=0))
+        edge = [rims_in[h, 2 * i + x : 2 * i + x + 1].astype(F32) for x in range(2) for h in range(rows)]
+        columns.append(jnp.concatenate([block, *edge], axis=0))
     is_even = parity() == 0
     even[...] = jnp.where(is_even, columns[0], columns[1]).astype(BF16)
     odd[...] = jnp.where(is_even, columns[1], columns[0]).astype(BF16)
     for end, rim in zip(ends, rims):
         h = end()
         for q in range(disp // per):
-            rim[q, PAD : PAD + cols] = jnp.concatenate(
-                [ct[q * per + i, h].astype(F32) for i in range(per)], axis=0
-            ).T
+            block = [ct[q * per + i, h].astype(F32) for i in range(per)]
+            rim[q] = jnp.concatenate(block, axis=0).T.astype(BF16)
 
 
 def pass_kernel(own, got, out):
@@ -77,20 +76,18 @@
     return jnp.where(is_even, y, x), jnp.where(is_even, x, y)
 
 
-def row_kernel(ends, rows, by_even, by_odd, *rest):
-    n = len(ends)
-    rims, pays, (edges, buf) = rest[:n], rest[n : 2 * n], rest[2 * n :]
-    count, total, _ = buf.shape
-    disp = edges.shape[1]
-    per, cols = disp // count, total - 2 * PAD
-    feat = 128 // per
+def corner_kernel(ends, rows, disp, by_even, by_odd, *rest):
+    pays, (edges, buf) = rest[: len(ends)], rest[len(ends) :]
+    feat = 128 // rows
+    per = 128 // feat
+    count = disp // per
     lane = lanes((count, 128))
     for side, x in enumerate(end_columns(by_even, by_odd)):
         edges[side] = x[0:disp, 0:128]
-    for end, rim, pay in zip(ends, rims, pays):
+    for end, pay in zip(ends, pays):
         h = end()
-        buf[...] = rim[...]
-        for side, at in ((0, PAD - 1), (1, PAD + cols)):
+        buf[...] = jnp.zeros(buf.shape, F32)
+        for side in range(2):
             out = jnp.zeros((count, 128), F32)
             for i in range(per):
                 x = edges[side, pl.ds(i, count, stride=per)]
@@ -98,8 +95,7 @@
                 last = pltpu.roll(x, (feat * (i - rows + 1)) % 128, 1) if i != rows - 1 else x
                 x = jnp.where(h == 0, first, last)
                 out = jnp.where((lane >= feat * i) & (lane < feat * (i + 1)), x, out)
-            for q in range(count):
-                buf[q, at : at + 1] = out[q : q + 1]
+            buf[8 * side : 8 * side + count] = out
         pay[...] = buf[...].astype(BF16)
 
 
@@ -203,26 +199,32 @@
 
 
 def weight_kernel(
-    masks, groups, feat, vbuf, ctl, by_even, by_odd, top, bot, keep_out, give_out, ctsh, vt, buf, sums
+    masks, groups, feat, vbuf, ctl, by_even, by_odd, top, bot, tops, bots, *rest
 ):
+    keep_out, give_out, ctsh, vt, buf, sums = rest
     disp, cols, width = ctl.shape
     pairs, per, half = vbuf.shape[0], 128 // feat, disp // 2
     mtop, mbot = masks()
     ctsh[0, 0] = jnp.zeros(ctsh.shape[2:], BF16)
     ctsh[half, 1] = jnp.zeros(ctsh.shape[2:], BF16)
-    lane, lane_in, lane_one = lanes(top.shape[1:]), lanes((cols, 128)), lanes((1, 128))
+    lane_in, lane_one = lanes((cols, 128)), lanes((1, 128))
     shifts = (feat, 128 - feat)
     edges = [x[0:disp, 0:128] for x in end_columns(by_even, by_odd)]
     turned = [[pltpu.roll(x, shift, 1) for shift in shifts] for x in edges]
+
+    def aligned(t, z, i):
+        return (
+            t if i == 0 else pltpu.roll(t, 128 - feat * i, 1),
+            z if i == per - 1 else pltpu.roll(z, feat * (per - 1 - i), 1),
+        )
+
+    corners = [aligned(tops[...].astype(F32) * mtop, bots[...].astype(F32) * mbot, i) for i in range(per)]
     for q in range(disp // per):
         t = top[q].astype(F32) * mtop
         z = bot[q].astype(F32) * mbot
         for i in range(per):
             d = q * per + i
-            rims = (
-                t if i == 0 else pltpu.roll(t, 128 - feat * i, 1),
-                z if i == per - 1 else pltpu.roll(z, feat * (per - 1 - i), 1),
-            )
+            rims = aligned(t, z, i)
             inner = ctl[d].astype(F32)
             for p, (rim, shift) in enumerate(zip(rims, shifts)):
 
@@ -231,11 +233,12 @@
 
                 at = slice(128 * p, 128 * (p + 1))
                 buf[d, PAD : PAD + cols, at] = jnp.where(
-                    on_rim(lane_in), rim[PAD : PAD + cols], pltpu.roll(inner, shift, 1)
+                    on_rim(lane_in), rim, pltpu.roll(inner, shift, 1)
                 )
                 for side, row in enumerate((PAD - 1, PAD + cols)):
+                    corner = corners[i][p][8 * side + q : 8 * side + q + 1]
                     buf[d, row : row + 1, at] = jnp.where(
-                        on_rim(lane_one), rim[row : row + 1], turned[side][p][d : d + 1]
+                        on_rim(lane_one), corner, turned[side][p][d : d + 1]
                     )
             for e in range(3):
                 ctsh[(d + 1) // 2, (d + 1) % 2, :, 256 * e : 256 * (e + 1)] = buf[
@@ -291,12 +294,12 @@
     give_out[...] = jnp.where(is_even, high, low)
 
 
-def dgrad_kernel(p, ctsh, w2, gv):
-    _, disp, cols, _ = gv.shape
+def dgrad_kernel(ctsh, w2, *grads):
+    _, disp, cols, _ = grads[0].shape
     step = disp // 4
     low = lanes((step * cols, 128)) < SLOT
 
-    def conv(q, _):
+    def conv(q, p, gv):
         slabs = [
             ctsh[pl.ds(q * step + s // 2, step), s % 2, :, 256 * e + 128 * p : 256 * e + 128 * (p + 1)]
             for s in range(4)
@@ -311,9 +314,11 @@
                 y = jnp.where(low, r, x) if hh else jnp.where(low, x, r)
                 for j in range(step):
                     gv[hh, 2 * (q * step + j) + o] = y[j * cols : (j + 1) * cols]
-        return 0
-
-    lax.fori_loop(0, 2, conv, 0)
+
+    @pl.loop(0, 2)
+    def _(q):
+        for p, gv in enumerate(grads):
+            conv(q, p, gv)
 
 
 def right_kernel(fl, *rest):
@@ -437,13 +442,14 @@
                     ].astype(BF16)
 
 
-def conv_kernel(taps, wc, out):
+def conv_kernel(taps, wc, out, held, sems):
     disp, rows, feat, cols = out.shape
-    step = 6
-
-    def conv(q, _):
+    parts = sems.shape[0]
+    step = disp // 2 // parts
+    copies = []
+    for q in range(parts):
         slabs = [
-            taps[pl.ds(q * step + s // 2, step), s % 2].reshape(step * cols, taps.shape[3])
+            taps[q * step + s // 2 : q * step + s // 2 + step, s % 2].reshape(step * cols, taps.shape[3])
             for s in range(4)
         ]
         acc = dot(jnp.concatenate(slabs, axis=1), wc[...])
@@ -451,10 +457,12 @@
             both = acc[j * cols : (j + 1) * cols].T.astype(BF16)
             for o in range(2):
                 block = both[rows * feat * o : rows * feat * (o + 1)]
-                out[2 * (q * step + j) + o] = block.reshape(rows, feat, cols)
-        return 0
-
-    lax.fori_loop(0, disp // 2 // step, conv, 0)
+                held[2 * (q * step + j) + o] = block.reshape(rows, feat, cols)
+        at = pl.ds(2 * q * step, 2 * step)
+        copies.append(pltpu.make_async_copy(held.at[at], out.at[at], sems.at[q]))
+        copies[-1].start()
+    for copy in copies:
+        copy.wait()
 
 
 def finish_kernel(scale, mine, other, own, near, far, weight, right):
@@ -555,7 +563,7 @@
     return run
 
 
-def call(kernel, outs, scratch, *args, after=(), token=False, us=0.0, alias=()):
+def call(kernel, outs, scratch, *args, after=(), token=False, us=0.0, alias=(), hbm=()):
     skip = len(after)
     if token:
         kernel = with_token(kernel, len(args), len(outs))
@@ -564,7 +572,7 @@
         lambda *refs: kernel(*refs[skip:]),
         out_shape=[jax.ShapeDtypeStruct(s, t) for s, t in outs],
         in_specs=[pl.BlockSpec(memory_space=pl.ANY)] * skip + [VMEM] * len(args),
-        out_specs=[VMEM] * len(outs),
+        out_specs=[pl.BlockSpec(memory_space=pl.ANY) if i in hbm else VMEM for i in range(len(outs))],
         scratch_shapes=scratch,
         input_output_aliases={skip + i: o for i, o in alias},
         compiler_params=pltpu.CompilerParams(vmem_limit_bytes=LIMIT),
@@ -640,9 +648,11 @@
             ((count, channels), BF16),
             ((disp, cols, rows * feat), BF16),
         ]
-        + [((disp // per, total, 128), F32)] * n,
+        + [((disp // per, cols, 128), BF16)] * n,
         [pltpu.VMEM((disp * cols, rows * feat), F32)],
-        jnp.concatenate([x[:, at] for at in (cols - 1, 0) for x in (left_features, right_features)]),
+        jnp.concatenate(
+            [x[:, at : at + 1] for at in (cols - 1, 0) for x in (left_features, right_features)], axis=1
+        ),
         ct,
         us=0.4,
     )
@@ -653,6 +663,7 @@
         pass_kernel, [((rows, cols, channels), BF16)], [], right_features, far, after=[ctl]
     )
     near = swap(passed, 1)
+    top, bot = halos(rims)
     w2, wc = call(
         taps_kernel,
         [((12 * 128, 2 * 128), BF16), ((4 * 3 * rows * SLOT, 2 * rows * feat), BF16)],
@@ -672,17 +683,16 @@
         far,
         after=[w2],
     )
-    row_pays = call(
-        functools.partial(row_kernel, ends, rows),
-        [((disp // per, total, 128), BF16)] * n,
-        [pltpu.VMEM((2, disp, 128), F32), pltpu.VMEM((disp // per, total, 128), F32)],
+    corner_pays = call(
+        functools.partial(corner_kernel, ends, rows, disp),
+        [((16, 128), BF16)] * n,
+        [pltpu.VMEM((2, disp, 128), F32), pltpu.VMEM((16, 128), F32)],
         by_even,
         by_odd,
-        *rims,
         after=[fl],
         us=5.0,
     )
-    top, bot = halos(row_pays)
+    tops, bots = halos(corner_pays)
     spread_rows = rows * cols + 2 * count
     fl, fr, fr4, vbuf, *volume_rows = call(
         functools.partial(volume_kernel, ends, group_size),
@@ -708,19 +718,15 @@
             pltpu.VMEM((disp, total, 256), F32),
             pltpu.VMEM((3 * 128, 128), F32),
         ],
-        vbuf, ctl, by_even, by_odd, top, bot,
+        vbuf, ctl, by_even, by_odd, top, bot, tops, bots,
         us=2.0,
     )
 
-    def gradient(p, after):
-        kernel = functools.partial(dgrad_kernel, p)
-        us = 0.2 if after else 0.9
-        return call(kernel, [((2, disp, cols, 128), F32)], [], ctsh, w2, after=after, us=us)[0]
-
     got = swap(give, 1)
-    grads = [gradient(0, [])]
-    (part,) = call(sum_kernel, [(keep.shape, BF16)], [], keep, got, after=grads, us=4.0)
-    grads += [gradient(p, [part]) for p in range(1, rows // 2)]
+    (part,) = call(sum_kernel, [(keep.shape, BF16)], [], keep, got)
+    grads = call(
+        dgrad_kernel, [((2, disp, cols, 128), F32)] * (rows // 2), [], ctsh, w2, after=[part], us=0.2
+    )
     rg0, rg1, rg2 = call(
         right_kernel,
         [
@@ -734,12 +740,11 @@
             pltpu.VMEM((rows * (cols + cols + cols // 2), wide), BF16),
         ],
         fl, *grads,
-        after=[part, vtop],
         us=0.2,
     )
     rg1 = swap(rg1, 1)
     *middle, final = stages(n_row, n_col)
-    order = [rg0]
+    order = [rg0, vtop]
     for stage in middle:
         parts = [part] + [swap(part, m) for m in stage]
         (part,) = call(sum_kernel, [(part.shape, BF16)], [], *parts, after=order, us=4.0)
@@ -769,11 +774,12 @@
     output, conv_done = call(
         conv_kernel,
         [((disp, rows, feat, cols), BF16)],
-        [],
+        [pltpu.VMEM((disp, rows, feat, cols), BF16), pltpu.SemaphoreType.DMA((2,))],
         spread, wc,
         after=[part],
         token=True,
         us=2.6,
+        hbm=[0],
     )
     rg2 = col_shift(rg2, -2)
     cells = disp * rows * n_row * cols * n_col

time: 47.2 us -> 44.7 us (0.947)
  waiting for transfers between devices: 6 us -> 3.36 us
  starting transfers between devices: 20.8 us -> 21.6 us
  Pallas kernels: 16.4 us -> 15.7 us
    ppermute x2 -> x3, waiting for transfers between devices: 3.25 us -> 0.01 us  [halos(): got = lax.ppermute(pays[0], 'row', [(0, 1), (1, 0)])]
    ppermute x11, waiting for transfers between devices: 2.2 us -> 3.35 us  [swap(): return lax.ppermute(block, ('row', 'col'), route)]
    pallas_call x18 -> x17, Pallas kernels: 16.4 us -> 15.7 us  [call(): pl.pallas_call(lambda *refs: kernel(*refs[skip:]), out_shape=[jax.ShapeDt...]
    ppermute x2, waiting for transfers between devices: 0.54 us -> 0.01 us  [col_shift(): return lax.ppermute(block, 'col', route)]
    ppermute x2 -> x3, starting transfers between devices: 3.12 us -> 3.66 us  [halos(): got = lax.ppermute(pays[0], 'row', [(0, 1), (1, 0)])]
  transfers between devices with their start and end apart: 16 -> 17, of which waited for: 5 -> 3; matrix products, arithmetic and copies ran while one was open for 3% -> 4% of each run, Pallas kernels for 28% -> 33%
where the time goes in v2:
time: 44.7 us; the launch traced here: 44.3 us
  starting transfers between devices  21.6 us (48%)
  Pallas kernels  15.7 us (35%)
  waiting for transfers between devices  3.36 us (8%)
  local copies, waits for them, and re-layouts  2.74 us (6%)
  between operations  0.88 us (2%)
    pallas_call x17, Pallas kernels, call(): pl.pallas_call(lambda *refs: kernel(*refs[skip:]), out_shape=[jax.ShapeDt...  15.7 us
    ppermute x11, starting transfers between devices, swap(): return lax.ppermute(block, ('row', 'col'), route)  11 us
    ppermute x2, starting transfers between devices, col_shift(): return lax.ppermute(block, 'col', route)  6.31 us
    ppermute x3, starting transfers between devices, halos(): got = lax.ppermute(pays[0], 'row', [(0, 1), (1, 0)])  3.66 us
    ppermute x11, waiting for transfers between devices, swap(): return lax.ppermute(block, ('row', 'col'), route)  3.35 us
    slice x2, local copies, waits for them, and re-layouts, on_device(): x[:, at:at + 1]  1.56 us
    unnamed x8, local copies, waits for them, and re-layouts  1.18 us
  transfers between devices with their start and end apart: 17, of which 3 were waited for; matrix products, arithmetic and copies ran while one was open for 4% of the time, Pallas kernels for 33%

profile of v2, /device:TPU:0, one launch (start us, length us, event | category | flops | bytes accessed | tf_op | source)
XLA Modules:
  0.0 44.3 jit_solution(3218654311863306954)
XLA Ops:
  0.6 0.0 copy-start
  0.6 0.0 copy-start.2
  0.7 5.0 %collective-permute-start = (bf16[4,64,320]{2,1,0:T(8,128)(2,1)}, bf16[4,64,320]{2,1,0:T(8,128)(2,1)S(1)}, u32[]{:S(2)}, u32[]{:S(2)}) collective-permute-start(bf16[4,64,320]{2,1,0:T(8,128)(2,1)} %refs_2_.1), channel_id=1, source_target_pairs={{0,2},{1,3},{2,4},{3,5},{4,6},{5,7},{6,8},{7,9},{8,10},{9,11},{10,... | collective-permute-start | bytes 491528 | tf_op jit(solution)/shard_map/ppermute | solution.py:588
  5.7 0.8 %fusion.1 = (bf16[4,1,320]{2,1,0:T(2,128)(2,1)S(1)}, bf16[4,1,320]{2,1,0:T(2,128)(2,1)S(1)}) fusion(bf16[4,64,320]{2,1,0:T(8,128)(2,1)} %refs_2_.1), kind=kLoop, calls=%fused_computation.2 | loop fusion | bytes 10240 | tf_op jit(solution)/shard_map/slice | solution.py:654
  6.5 0.8 %fusion = (bf16[4,1,320]{2,1,0:T(2,128)(2,1)S(1)}, bf16[4,1,320]{2,1,0:T(2,128)(2,1)S(1)}) fusion(bf16[4,64,320]{2,1,0:T(8,128)(2,1)} %refs_1_.3), kind=kLoop, calls=%fused_computation.1 | loop fusion | bytes 10240 | tf_op jit(solution)/shard_map/slice | solution.py:654
  7.2 0.0 copy-start.1
  7.3 0.0 copy-start.3
  7.3 1.2 %copy-done.3 = bf16[24,4,64,32]{2,3,1,0:T(8,128)(2,1)S(1)} copy-done((bf16[24,4,64,32]{2,3,1,0:T(8,128)(2,1)S(1)}, bf16[24,4,64,32]{2,3,1,0:T(8,128)(2,1)}, u32[]{:S(2)}) %copy-start.3) | copy-done | bytes 393240
  8.5 0.3 shard_map.75
  8.8 0.1 collective-permute-start.2
  8.9 0.7 %collective-permute-start.3 = (bf16[32,320]{1,0:T(8,128)(2,1)S(1)}, bf16[32,320]{1,0:T(8,128)(2,1)S(1)}, u32[]{:S(2)}, u32[]{:S(2)}) collective-permute-start(bf16[32,320]{1,0:T(8,128)(2,1)S(1)} %get-tuple-element.34), channel_id=1, source_target_pairs={{1,2},{3,4},{5,6},{7,8},{9,10},{11,12},{13,14},{2,1},{4,3},{6,5},{... | collective-permute-start | bytes 61448 | tf_op jit(solution)/shard_map/ppermute | solution.py:661
  9.6 1.6 %collective-permute-start.4 = (bf16[6,64,128]{2,1,0:T(8,128)(2,1)S(1)}, bf16[6,64,128]{2,1,0:T(8,128)(2,1)S(1)}, u32[]{:S(2)}, u32[]{:S(2)}) collective-permute-start(bf16[6,64,128]{2,1,0:T(8,128)(2,1)S(1)} %get-tuple-element.41), channel_id=1, source_target_pairs={{0,16},{16,0},{1,17},{17,1},{2,18},{18,2},{3,19},{19,3},{4,20},{20... | collective-permute-start | bytes 294920 | tf_op jit(solution)/shard_map/ppermute | solution.py:599
  11.1 0.0 collective-permute-done.refs_2_.refs_3_
  11.1 0.0 copy-done
  11.1 0.1 shard_map.76.refs_0_
  11.2 2.7 %collective-permute-start.1 = (bf16[4,64,320]{2,1,0:T(8,128)(2,1)S(1)}, bf16[4,64,320]{2,1,0:T(8,128)(2,1)S(1)}, u32[]{:S(2)}, u32[]{:S(2)}) collective-permute-start(bf16[4,64,320]{2,1,0:T(8,128)(2,1)S(1)} %shard_map.76.refs_0_), channel_id=1, source_target_pairs={{0,1},{1,0},{2,3},{3,2},{4,5},{5,4},{6,7},{7,6},{8,9},{9,8},{10,11... | collective-permute-start | bytes 491528 | tf_op jit(solution)/shard_map/ppermute | solution.py:641
  13.9 0.0 copy-done.2
  13.9 0.8 %shard_map.77 = (bf16[1536,256]{1,0:T(8,128)(2,1)S(1)}, bf16[3072,256]{1,0:T(8,128)(2,1)S(1)}) custom-call(bf16[4,64,320]{2,1,0:T(8,128)(2,1)S(1)} %shard_map.76.refs_0_, bf16[3,3,3,32,40]{4,3,2,1,0:T(8,128)(2,1)S(1)} %bitcast.4), custom_call_target="tpu_custom_call" | custom-call | tf_op jit(solution)/shard_map/pallas_call | solution.py:571
  14.7 0.0 copy-done.1
  14.7 0.5 %shard_map.78 = (f32[4,80,512]{2,1,0:T(8,128)S(1)}, f32[4,176,512]{2,1,0:T(8,128)S(1)}, f32[4,176,512]{2,1,0:T(8,128)S(1)}) custom-call(bf16[1536,256]{1,0:T(8,128)(2,1)S(1)} %get-tuple-element.35.refs_0_.refs_2_, bf16[4,64,320]{2,1,0:T(8,128)(2,1)S(1)} %copy-done.1, bf16[4,64,320]{2,1,0:T(8,128)(2,1)S(1)} %copy-done, ...), custom_call_target="tpu_custom_call" | custom-call | tf_op jit(solution)/shard_map/pallas_call | solution.py:571
  15.3 0.0 collective-permute-done.2.refs_1_.refs_2_
  15.3 0.0 collective-permute-done.3.refs_2_.refs_3_
  15.3 0.1 shard_map.80
  15.4 0.5 %collective-permute-start.5 = (bf16[16,128]{1,0:T(8,128)(2,1)S(1)}, bf16[16,128]{1,0:T(8,128)(2,1)S(1)}, u32[]{:S(2)}, u32[]{:S(2)}) collective-permute-start(bf16[16,128]{1,0:T(8,128)(2,1)S(1)} %shard_map.80), channel_id=1, source_target_pairs={{0,16},{16,0},{1,17},{17,1},{2,18},{18,2},{3,19},{19,3},{4,20},{20... | collective-permute-start | bytes 12296 | tf_op jit(solution)/shard_map/ppermute | solution.py:599
  15.9 0.0 collective-permute-done.1.refs_0_
  15.9 2.0 %shard_map.79 = (f32[4,80,512]{2,1,0:T(8,128)S(1)}, f32[4,176,512]{2,1,0:T(8,128)S(1)}, f32[4,176,512]{2,1,0:T(8,128)S(1)}, f32[2,24,80,128]{3,2,1,0:T(8,128)S(1)}, bf16[960,128]{1,0:T(8,128)(2,1)S(1)}) custom-call(bf16[4,64,320]{2,1,0:T(8,128)(2,1)S(1)} %collective-permute-done.1.refs_0_, ...), custom_call_target="tpu_custom_call", output_to_operand_aliasing={{0}: (3, {}), {1}: (4, {}), {2}: (5, {})} | custom-call | flops 2070000000 | bytes 6660000 | tf_op jit(solution)/shard_map/pallas_call | solution.py:571
  17.9 1.6 %collective-permute-start.7 = (bf16[960,128]{1,0:T(8,128)(2,1)S(1)}, bf16[960,128]{1,0:T(8,128)(2,1)S(1)}, u32[]{:S(2)}, u32[]{:S(2)}) collective-permute-start(bf16[960,128]{1,0:T(8,128)(2,1)S(1)} %get-tuple-element.48), channel_id=1, source_target_pairs={{0,16},{16,0},{1,17},{17,1},{2,18},{18,2},{3,19},{19,3},{4,20},{20... | collective-permute-start | bytes 737288 | tf_op jit(solution)/shard_map/ppermute | solution.py:599
  19.5 0.0 collective-permute-done.4.refs_4_.refs_5_
  19.5 0.0 collective-permute-done.5.refs_6_.refs_7_
  19.5 2.0 %shard_map.81 = (f32[192,128]{1,0:T(8,128)S(1)}, f32[192,128]{1,0:T(8,128)S(1)}, bf16[13,2,64,768]{3,2,1,0:T(8,128)(2,1)S(1)}) custom-call(f32[2,24,80,128]{3,2,1,0:T(8,128)S(1)} %get-tuple-element.40.refs_0_.refs_1_, bf16[24,64,128]{2,1,0:T(8,128)(2,1)S(1)} %get-tuple-element.32.refs_0_.refs_1_, bf16[32,320]{1,0:T(8,128)(2,1)S(1)} %collective-permute-done.2.refs_1_.refs_2_, ...), custom_call_target="tpu_custom_call" | custom-call | flops 2300000000 | bytes 7400000 | tf_op jit(solution)/shard_map/pallas_call | solution.py:571
  21.5 0.1 collective-permute-start.6
  21.6 1.3 %collective-permute-done.6.refs_1_ = f32[192,128]{1,0:T(8,128)S(1)} collective-permute-done((f32[192,128]{1,0:T(8,128)S(1)}, f32[192,128]{1,0:T(8,128)S(1)}, u32[]{:S(2)}, u32[]{:S(2)}) %collective-permute-start.6) | collective-permute-done | bytes 98336 | tf_op jit(solution)/shard_map/ppermute | solution.py:641
  22.9 2.6 %collective-permute-start.10 = (bf16[192,128]{1,0:T(8,128)(2,1)S(1)}, bf16[192,128]{1,0:T(8,128)(2,1)S(1)}, u32[]{:S(2)}, u32[]{:S(2)}) collective-permute-start(bf16[192,128]{1,0:T(8,128)(2,1)S(1)} %shard_map.82.refs_0_.refs_2_), channel_id=1, source_target_pairs={{0,6},{1,7},{2,4},{3,5},{4,2},{5,3},{6,0},{7,1},{8,14},{9,15},{10,... | collective-permute-start | bytes 147464 | tf_op jit(solution)/shard_map/ppermute | solution.py:641
  25.5 0.4 collective-permute-start.9
  25.9 0.5 %collective-permute-start.8 = (bf16[192,128]{1,0:T(8,128)(2,1)S(1)}, bf16[192,128]{1,0:T(8,128)(2,1)S(1)}, u32[]{:S(2)}, u32[]{:S(2)}) collective-permute-start(bf16[192,128]{1,0:T(8,128)(2,1)S(1)} %shard_map.82.refs_0_.refs_2_), channel_id=1, source_target_pairs={{0,2},{1,3},{2,0},{3,1},{4,6},{5,7},{6,4},{7,5},{8,10},{9,11},{10,... | collective-permute-start | bytes 147464 | tf_op jit(solution)/shard_map/ppermute | solution.py:641
  26.4 1.7 %shard_map.83 = (f32[2,24,64,128]{3,2,1,0:T(8,128)S(1)}, f32[2,24,64,128]{3,2,1,0:T(8,128)S(1)}) custom-call(bf16[192,128]{1,0:T(8,128)(2,1)S(1)} %shard_map.82.refs_0_.refs_2_, bf16[13,2,64,768]{3,2,1,0:T(8,128)(2,1)S(1)} %get-tuple-element.44.refs_1_, bf16[1536,256]{1,0:T(8,128)(2,1)S(1)} %get-tuple-element.35.refs_0_.refs_2_), custom_call_target="tpu_custom_call" | custom-call | flops 230000000 | bytes 740000 | tf_op jit(solution)/shard_map/pallas_call | solution.py:571
  28.2 1.3 %shard_map.84 = (bf16[4,64,320]{2,1,0:T(8,128)(2,1)S(1)}, bf16[4,64,320]{2,1,0:T(8,128)(2,1)S(1)}, bf16[4,32,320]{2,1,0:T(8,128)(2,1)S(1)}) custom-call(f32[4,80,512]{2,1,0:T(8,128)S(1)} %get-tuple-element.39.refs_0_, f32[2,24,64,128]{3,2,1,0:T(8,128)S(1)} %get-tuple-element.45.refs_1_.refs_3_, f32[2,24,64,128]{3,2,1,0:T(8,128)S(1)} %get-tuple-element.46.refs_2_.refs_4_), custom_call_target="tpu_custom_call" | custom-call | flops 230000000 | bytes 740000 | tf_op jit(solution)/shard_map/pallas_call | solution.py:571
  29.4 0.1 collective-permute-start.11
  29.5 0.0 collective-permute-done.10.refs_5_
  29.5 0.0 collective-permute-done.9.refs_4_
  29.6 0.4 collective-permute-done.8.refs_3_
  30.0 0.0 collective-permute-done.7.refs_1_.refs_2_.refs_3_
  30.0 2.8 %collective-permute-start.14 = (bf16[192,128]{1,0:T(8,128)(2,1)S(1)}, bf16[192,128]{1,0:T(8,128)(2,1)S(1)}, u32[]{:S(2)}, u32[]{:S(2)}) collective-permute-start(bf16[192,128]{1,0:T(8,128)(2,1)S(1)} %shard_map.85.refs_0_.refs_1_), channel_id=1, source_target_pairs={{0,24},{1,25},{2,26},{3,27},{4,28},{5,29},{6,30},{7,31},{8,16},{9,... | collective-permute-start | bytes 147464 | tf_op jit(solution)/shard_map/ppermute | solution.py:641
  32.9 1.3 %collective-permute-start.13 = (bf16[192,128]{1,0:T(8,128)(2,1)S(1)}, bf16[192,128]{1,0:T(8,128)(2,1)S(1)}, u32[]{:S(2)}, u32[]{:S(2)}) collective-permute-start(bf16[192,128]{1,0:T(8,128)(2,1)S(1)} %shard_map.85.refs_0_.refs_1_), channel_id=1, source_target_pairs={{0,16},{1,17},{2,18},{3,19},{4,20},{5,21},{6,22},{7,23},{8,24},{9,... | collective-permute-start | bytes 147464 | tf_op jit(solution)/shard_map/ppermute | solution.py:641
  34.2 0.3 collective-permute-start.12
  34.5 0.0 collective-permute-done.11.refs_1_.refs_4_
  34.5 0.1 shard_map.86.refs_0_
  34.6 1.3 %collective-permute-start.16 = (bf16[4,64,320]{2,1,0:T(8,128)(2,1)S(1)}, bf16[4,64,320]{2,1,0:T(8,128)(2,1)S(1)}, u32[]{:S(2)}, u32[]{:S(2)}) collective-permute-start(bf16[4,64,320]{2,1,0:T(8,128)(2,1)S(1)} %shard_map.86.refs_0_), channel_id=1, source_target_pairs={{2,0},{3,1},{4,2},{5,3},{6,4},{7,5},{8,6},{9,7},{10,8},{11,9},{12,... | collective-permute-start | bytes 491528 | tf_op jit(solution)/shard_map/ppermute | solution.py:588
  35.9 1.9 %shard_map.87 = (bf16[4,64,320]{2,1,0:T(8,128)(2,1)}, f32[8,128]{1,0:T(8,128)S(1)}) custom-call(bf16[4,64,320]{2,1,0:T(8,128)(2,1)S(1)} %shard_map.86.refs_0_, f32[4,176,512]{2,1,0:T(8,128)S(1)} %get-tuple-element.51.refs_1_, f32[4,176,512]{2,1,0:T(8,128)S(1)} %get-tuple-element.52.refs_2_, f32[2,24,64,128]{3,2,1,0:T(8,128)S(1)} %get-tuple-element.45.refs_1_.refs_3_, ...), custom_call_target="tpu_custom_call" | custom-call | flops 2184999936 | bytes 7030000 | tf_op jit(solution)/shard_map/pallas_call | solution.py:571
  37.8 0.0 collective-permute-done.14.refs_4_
  37.8 0.0 collective-permute-done.13.refs_3_
  37.8 1.6 %collective-permute-done.12.refs_2_ = bf16[192,128]{1,0:T(8,128)(2,1)S(1)} collective-permute-done((bf16[192,128]{1,0:T(8,128)(2,1)S(1)}, bf16[192,128]{1,0:T(8,128)(2,1)S(1)}, u32[]{:S(2)}, u32[]{:S(2)}) %collective-permute-start.12) | collective-permute-done | bytes 49184 | tf_op jit(solution)/shard_map/ppermute | solution.py:641
  39.4 0.1 collective-permute-start.15
  39.5 1.3 %shard_map.89.refs_1_ = bf16[13,2,64,768]{3,2,1,0:T(8,128)(2,1)S(1)} custom-call(f32[192,128]{1,0:T(8,128)S(1)} %shard_map.88.refs_0_.refs_1_, f32[2,24,80,128]{3,2,1,0:T(8,128)S(1)} %get-tuple-element.40.refs_0_.refs_1_, bf16[960,128]{1,0:T(8,128)(2,1)S(1)} %collective-permute-done.7.refs_1_.refs_2_.refs_3_, ...), custom_call_target="tpu_custom_call" | custom-call | flops 1495000064 | bytes 4810000 | tf_op jit(solution)/shard_map/pallas_call | solution.py:571
  40.8 2.4 %shard_map.90 = (bf16[24,4,32,64]{3,2,1,0:T(8,128)(2,1)}, f32[8,128]{1,0:T(8,128)S(1)}) custom-call(f32[192,128]{1,0:T(8,128)S(1)} %shard_map.88.refs_0_.refs_1_, bf16[13,2,64,768]{3,2,1,0:T(8,128)(2,1)S(1)} %shard_map.89.refs_1_, bf16[3072,256]{1,0:T(8,128)(2,1)S(1)} %get-tuple-element.54.refs_2_), custom_call_target="tpu_custom_call" | custom-call | flops 2990000128 | bytes 9620000 | tf_op jit(solution)/shard_map/pallas_call | solution.py:571
  43.2 0.0 collective-permute-done.15.refs_2_
  43.3 0.0 collective-permute-done.16.refs_5_
  43.3 1.1 %shard_map.91 = (f32[3,3,3,32,40]{4,3,2,1,0:T(8,128)}, bf16[4,64,320]{2,1,0:T(8,128)(2,1)}) custom-call(f32[8,128]{1,0:T(8,128)S(1)} %get-tuple-element.56.refs_0_, f32[192,128]{1,0:T(8,128)S(1)} %shard_map.88.refs_0_.refs_1_, f32[192,128]{1,0:T(8,128)S(1)} %collective-permute-done.15.refs_2_, bf16[4,64,320]{2,1,0:T(8,128)(2,1)S(1)} %get-tuple-element.47.refs_0_.refs_3_, ...), custom_call_target="tpu_custom_call" | custom-call | flops 1150000000 | bytes 3700000 | tf_op jit(solution)/shard_map/pallas_call | solution.py:571
  (4 shorter events, 0.1 us)
Async XLA Ops:
  0.6 10.5 %copy-start = (bf16[4,64,320]{2,1,0:T(8,128)(2,1)S(1)}, bf16[4,64,320]{2,1,0:T(8,128)(2,1)}, u32[]{:S(2)}) copy-start(bf16[4,64,320]{2,1,0:T(8,128)(2,1)} %refs_2_.1) | copy-start | bytes 491524
  0.6 13.2 %copy-start.2 = (bf16[3,3,3,40,32]{3,4,2,1,0:T(8,128)(2,1)S(1)}, bf16[3,3,3,40,32]{3,4,2,1,0:T(8,128)(2,1)}, u32[]{:S(2)}) copy-start(bf16[3,3,3,40,32]{3,4,2,1,0:T(8,128)(2,1)} %param.6) | copy-start | bytes 207364
  0.7 10.5 %collective-permute-start = (bf16[4,64,320]{2,1,0:T(8,128)(2,1)}, bf16[4,64,320]{2,1,0:T(8,128)(2,1)S(1)}, u32[]{:S(2)}, u32[]{:S(2)}) collective-permute-start(bf16[4,64,320]{2,1,0:T(8,128)(2,1)} %refs_2_.1), channel_id=1, source_target_pairs={{0,2},{1,3},{2,4},{3,5},{4,6},{5,7},{6,8},{7,9},{8,10},{9,11},{10,... | collective-permute-start | bytes 491528 | tf_op jit(solution)/shard_map/ppermute | solution.py:588
  7.2 7.5 %copy-start.1 = (bf16[4,64,320]{2,1,0:T(8,128)(2,1)S(1)}, bf16[4,64,320]{2,1,0:T(8,128)(2,1)}, u32[]{:S(2)}) copy-start(bf16[4,64,320]{2,1,0:T(8,128)(2,1)} %refs_1_.3) | copy-start | bytes 491524
  7.3 1.2 %copy-start.3 = (bf16[24,4,64,32]{2,3,1,0:T(8,128)(2,1)S(1)}, bf16[24,4,64,32]{2,3,1,0:T(8,128)(2,1)}, u32[]{:S(2)}) copy-start(bf16[24,4,64,32]{2,3,1,0:T(8,128)(2,1)} %param.7) | copy-start | bytes 1179652
  8.8 6.4 %collective-permute-start.2 = (bf16[32,320]{1,0:T(8,128)(2,1)S(1)}, bf16[32,320]{1,0:T(8,128)(2,1)S(1)}, u32[]{:S(2)}, u32[]{:S(2)}) collective-permute-start(bf16[32,320]{1,0:T(8,128)(2,1)S(1)} %get-tuple-element.33), channel_id=1, source_target_pairs={{0,1},{1,0},{2,3},{3,2},{4,5},{5,4},{6,7},{7,6},{8,9},{9,8},{10,11... | collective-permute-start | bytes 61448 | tf_op jit(solution)/shard_map/ppermute | solution.py:641
  8.9 6.4 %collective-permute-start.3 = (bf16[32,320]{1,0:T(8,128)(2,1)S(1)}, bf16[32,320]{1,0:T(8,128)(2,1)S(1)}, u32[]{:S(2)}, u32[]{:S(2)}) collective-permute-start(bf16[32,320]{1,0:T(8,128)(2,1)S(1)} %get-tuple-element.34), channel_id=1, source_target_pairs={{1,2},{3,4},{5,6},{7,8},{9,10},{11,12},{13,14},{2,1},{4,3},{6,5},{... | collective-permute-start | bytes 61448 | tf_op jit(solution)/shard_map/ppermute | solution.py:661
  9.6 9.9 %collective-permute-start.4 = (bf16[6,64,128]{2,1,0:T(8,128)(2,1)S(1)}, bf16[6,64,128]{2,1,0:T(8,128)(2,1)S(1)}, u32[]{:S(2)}, u32[]{:S(2)}) collective-permute-start(bf16[6,64,128]{2,1,0:T(8,128)(2,1)S(1)} %get-tuple-element.41), channel_id=1, source_target_pairs={{0,16},{16,0},{1,17},{17,1},{2,18},{18,2},{3,19},{19,3},{4,20},{20... | collective-permute-start | bytes 294920 | tf_op jit(solution)/shard_map/ppermute | solution.py:599
  11.2 4.7 %collective-permute-start.1 = (bf16[4,64,320]{2,1,0:T(8,128)(2,1)S(1)}, bf16[4,64,320]{2,1,0:T(8,128)(2,1)S(1)}, u32[]{:S(2)}, u32[]{:S(2)}) collective-permute-start(bf16[4,64,320]{2,1,0:T(8,128)(2,1)S(1)} %shard_map.76.refs_0_), channel_id=1, source_target_pairs={{0,1},{1,0},{2,3},{3,2},{4,5},{5,4},{6,7},{7,6},{8,9},{9,8},{10,11... | collective-permute-start | bytes 491528 | tf_op jit(solution)/shard_map/ppermute | solution.py:641
  15.4 4.1 %collective-permute-start.5 = (bf16[16,128]{1,0:T(8,128)(2,1)S(1)}, bf16[16,128]{1,0:T(8,128)(2,1)S(1)}, u32[]{:S(2)}, u32[]{:S(2)}) collective-permute-start(bf16[16,128]{1,0:T(8,128)(2,1)S(1)} %shard_map.80), channel_id=1, source_target_pairs={{0,16},{16,0},{1,17},{17,1},{2,18},{18,2},{3,19},{19,3},{4,20},{20... | collective-permute-start | bytes 12296 | tf_op jit(solution)/shard_map/ppermute | solution.py:599
  17.9 12.1 %collective-permute-start.7 = (bf16[960,128]{1,0:T(8,128)(2,1)S(1)}, bf16[960,128]{1,0:T(8,128)(2,1)S(1)}, u32[]{:S(2)}, u32[]{:S(2)}) collective-permute-start(bf16[960,128]{1,0:T(8,128)(2,1)S(1)} %get-tuple-element.48), channel_id=1, source_target_pairs={{0,16},{16,0},{1,17},{17,1},{2,18},{18,2},{3,19},{19,3},{4,20},{20... | collective-permute-start | bytes 737288 | tf_op jit(solution)/shard_map/ppermute | solution.py:599
  21.5 1.4 %collective-permute-start.6 = (f32[192,128]{1,0:T(8,128)S(1)}, f32[192,128]{1,0:T(8,128)S(1)}, u32[]{:S(2)}, u32[]{:S(2)}) collective-permute-start(f32[192,128]{1,0:T(8,128)S(1)} %get-tuple-element.43), channel_id=1, source_target_pairs={{0,1},{1,0},{2,3},{3,2},{4,5},{5,4},{6,7},{7,6},{8,9},{9,8},{10,11... | collective-permute-start | bytes 294920 | tf_op jit(solution)/shard_map/ppermute | solution.py:641
  22.9 6.7 %collective-permute-start.10 = (bf16[192,128]{1,0:T(8,128)(2,1)S(1)}, bf16[192,128]{1,0:T(8,128)(2,1)S(1)}, u32[]{:S(2)}, u32[]{:S(2)}) collective-permute-start(bf16[192,128]{1,0:T(8,128)(2,1)S(1)} %shard_map.82.refs_0_.refs_2_), channel_id=1, source_target_pairs={{0,6},{1,7},{2,4},{3,5},{4,2},{5,3},{6,0},{7,1},{8,14},{9,15},{10,... | collective-permute-start | bytes 147464 | tf_op jit(solution)/shard_map/ppermute | solution.py:641
  25.5 4.1 %collective-permute-start.9 = (bf16[192,128]{1,0:T(8,128)(2,1)S(1)}, bf16[192,128]{1,0:T(8,128)(2,1)S(1)}, u32[]{:S(2)}, u32[]{:S(2)}) collective-permute-start(bf16[192,128]{1,0:T(8,128)(2,1)S(1)} %shard_map.82.refs_0_.refs_2_), channel_id=1, source_target_pairs={{0,4},{1,5},{2,6},{3,7},{4,0},{5,1},{6,2},{7,3},{8,12},{9,13},{10,... | collective-permute-start | bytes 147464 | tf_op jit(solution)/shard_map/ppermute | solution.py:641
  25.9 4.1 %collective-permute-start.8 = (bf16[192,128]{1,0:T(8,128)(2,1)S(1)}, bf16[192,128]{1,0:T(8,128)(2,1)S(1)}, u32[]{:S(2)}, u32[]{:S(2)}) collective-permute-start(bf16[192,128]{1,0:T(8,128)(2,1)S(1)} %shard_map.82.refs_0_.refs_2_), channel_id=1, source_target_pairs={{0,2},{1,3},{2,0},{3,1},{4,6},{5,7},{6,4},{7,5},{8,10},{9,11},{10,... | collective-permute-start | bytes 147464 | tf_op jit(solution)/shard_map/ppermute | solution.py:641
  29.4 5.0 %collective-permute-start.11 = (bf16[4,64,320]{2,1,0:T(8,128)(2,1)S(1)}, bf16[4,64,320]{2,1,0:T(8,128)(2,1)S(1)}, u32[]{:S(2)}, u32[]{:S(2)}) collective-permute-start(bf16[4,64,320]{2,1,0:T(8,128)(2,1)S(1)} %get-tuple-element.49), channel_id=1, source_target_pairs={{0,1},{1,0},{2,3},{3,2},{4,5},{5,4},{6,7},{7,6},{8,9},{9,8},{10,11... | collective-permute-start | bytes 491528 | tf_op jit(solution)/shard_map/ppermute | solution.py:641
  30.0 7.7 %collective-permute-start.14 = (bf16[192,128]{1,0:T(8,128)(2,1)S(1)}, bf16[192,128]{1,0:T(8,128)(2,1)S(1)}, u32[]{:S(2)}, u32[]{:S(2)}) collective-permute-start(bf16[192,128]{1,0:T(8,128)(2,1)S(1)} %shard_map.85.refs_0_.refs_1_), channel_id=1, source_target_pairs={{0,24},{1,25},{2,26},{3,27},{4,28},{5,29},{6,30},{7,31},{8,16},{9,... | collective-permute-start | bytes 147464 | tf_op jit(solution)/shard_map/ppermute | solution.py:641
  32.9 4.9 %collective-permute-start.13 = (bf16[192,128]{1,0:T(8,128)(2,1)S(1)}, bf16[192,128]{1,0:T(8,128)(2,1)S(1)}, u32[]{:S(2)}, u32[]{:S(2)}) collective-permute-start(bf16[192,128]{1,0:T(8,128)(2,1)S(1)} %shard_map.85.refs_0_.refs_1_), channel_id=1, source_target_pairs={{0,16},{1,17},{2,18},{3,19},{4,20},{5,21},{6,22},{7,23},{8,24},{9,... | collective-permute-start | bytes 147464 | tf_op jit(solution)/shard_map/ppermute | solution.py:641
  34.2 5.2 %collective-permute-start.12 = (bf16[192,128]{1,0:T(8,128)(2,1)S(1)}, bf16[192,128]{1,0:T(8,128)(2,1)S(1)}, u32[]{:S(2)}, u32[]{:S(2)}) collective-permute-start(bf16[192,128]{1,0:T(8,128)(2,1)S(1)} %shard_map.85.refs_0_.refs_1_), channel_id=1, source_target_pairs={{0,8},{1,9},{2,10},{3,11},{4,12},{5,13},{6,14},{7,15},{8,0},{9,1},... | collective-permute-start | bytes 147464 | tf_op jit(solution)/shard_map/ppermute | solution.py:641
  34.6 8.7 %collective-permute-start.16 = (bf16[4,64,320]{2,1,0:T(8,128)(2,1)S(1)}, bf16[4,64,320]{2,1,0:T(8,128)(2,1)S(1)}, u32[]{:S(2)}, u32[]{:S(2)}) collective-permute-start(bf16[4,64,320]{2,1,0:T(8,128)(2,1)S(1)} %shard_map.86.refs_0_), channel_id=1, source_target_pairs={{2,0},{3,1},{4,2},{5,3},{6,4},{7,5},{8,6},{9,7},{10,8},{11,9},{12,... | collective-permute-start | bytes 491528 | tf_op jit(solution)/shard_map/ppermute | solution.py:588
  39.4 3.8 %collective-permute-start.15 = (f32[192,128]{1,0:T(8,128)S(1)}, f32[192,128]{1,0:T(8,128)S(1)}, u32[]{:S(2)}, u32[]{:S(2)}) collective-permute-start(f32[192,128]{1,0:T(8,128)S(1)} %shard_map.88.refs_0_.refs_1_), channel_id=1, source_target_pairs={{0,1},{1,0},{2,3},{3,2},{4,5},{5,4},{6,7},{7,6},{8,9},{9,8},{10,11... | collective-permute-start | bytes 294920 | tf_op jit(solution)/shard_map/ppermute | solution.py:641

commit v3 on v2

--- a/solution.py
+++ b/solution.py
@@ -219,7 +219,8 @@
         )
 
     corners = [aligned(tops[...].astype(F32) * mtop, bots[...].astype(F32) * mbot, i) for i in range(per)]
-    for q in range(disp // per):
+
+    def fill(q):
         t = top[q].astype(F32) * mtop
         z = bot[q].astype(F32) * mbot
         for i in range(per):
@@ -244,6 +245,7 @@
                 ctsh[(d + 1) // 2, (d + 1) % 2, :, 256 * e : 256 * (e + 1)] = buf[
                     d, PAD - 1 + e : PAD - 1 + e + cols
                 ].astype(BF16)
+
     none = jnp.zeros((cols, 128), F32)
     for p in range(pairs):
         for j in range(-1, half + 1):
@@ -255,30 +257,38 @@
                 block[1] = none
             x = jnp.concatenate(block, axis=0).astype(BF16)
             vt[p, :, 128 * (j + 1) : 128 * (j + 2)] = x.T
-    size = disp * cols
-    left = jnp.concatenate(
-        [
-            jnp.concatenate([vt[p, :, 128 * (2 - a) : 128 * (2 - a) + size] for p in range(pairs)], axis=1)
-            for a in range(3)
-        ],
-        axis=0,
-    )
-    right = jnp.concatenate(
-        [
-            jnp.concatenate(
-                [
-                    ctsh[(d + 1) // 2, (d + 1) % 2, :, 256 * e + 128 * p : 256 * e + 128 * (p + 1)]
-                    for e in range(3)
-                ],
-                axis=1,
-            )
-            for p in range(pairs)
-            for j in range(half)
-            for d in (j, j + half)
-        ],
-        axis=0,
-    )
-    full = dot(left, right)
+    full = None
+    for q in range(half // per):
+        fill(q)
+        fill(q + half // per)
+        first, size = q * per, per * 128
+        left = jnp.concatenate(
+            [
+                jnp.concatenate(
+                    [vt[p, :, 128 * (2 - a + first) : 128 * (2 - a + first) + size] for p in range(pairs)],
+                    axis=1,
+                )
+                for a in range(3)
+            ],
+            axis=0,
+        )
+        right = jnp.concatenate(
+            [
+                jnp.concatenate(
+                    [
+                        ctsh[(d + 1) // 2, (d + 1) % 2, :, 256 * e + 128 * p : 256 * e + 128 * (p + 1)]
+                        for e in range(3)
+                    ],
+                    axis=1,
+                )
+                for p in range(pairs)
+                for j in range(first, first + per)
+                for d in (j, j + half)
+            ],
+            axis=0,
+        )
+        part = dot(left, right)
+        full = part if full is None else full + part
     keep = lanes((groups, 128)) < 3 * feat
     sums[...] = jnp.zeros(sums.shape, F32)
     for a in range(3):
@@ -315,8 +325,7 @@
                 for j in range(step):
                     gv[hh, 2 * (q * step + j) + o] = y[j * cols : (j + 1) * cols]
 
-    @pl.loop(0, 2)
-    def _(q):
+    for q in range(2):
         for p, gv in enumerate(grads):
             conv(q, p, gv)
 
@@ -421,15 +430,16 @@
     return base
 
 
-def spread_kernel(masks, groups, vbuf, top, bot, taps, buf):
-    cols = taps.shape[2]
-    disp, total = buf.shape[1], buf.shape[2]
+def conv_kernel(masks, groups, vbuf, top, bot, wc, out, taps, buf, held, sems):
+    disp, rows, feat, cols = out.shape
+    total = buf.shape[2]
     lane = lanes((total, 128))
     zeros = jnp.zeros((cols, taps.shape[3]), BF16)
     taps[0, 0] = zeros
     taps[disp // 2, 1] = zeros
     halos_of = [(ref, mask) for ref, mask in zip((top, bot), masks())]
-    for dd in range(disp // 2):
+
+    def build(dd):
         for p, (ref, mask) in enumerate(halos_of):
             row = ref[dd * total : (dd + 1) * total].astype(F32) * mask
             for o in range(2):
@@ -441,13 +451,13 @@
                         p, d, PAD - 1 + e : PAD - 1 + e + cols
                     ].astype(BF16)
 
-
-def conv_kernel(taps, wc, out, held, sems):
-    disp, rows, feat, cols = out.shape
     parts = sems.shape[0]
     step = disp // 2 // parts
     copies = []
+    build(0)
     for q in range(parts):
+        for dd in range(q * step + 1, min((q + 1) * step + 1, disp // 2)):
+            build(dd)
         slabs = [
             taps[q * step + s // 2 : q * step + s // 2 + step, s % 2].reshape(step * cols, taps.shape[3])
             for s in range(4)
@@ -465,9 +475,15 @@
         copy.wait()
 
 
-def finish_kernel(scale, mine, other, own, near, far, weight, right):
+def finish_kernel(scale, mine, other, own, near, far, left, weight, right, left_out, held_w, held_r, sems):
     _, _, _, feat, groups = weight.shape
+    copies = [pltpu.make_async_copy(left, left_out, sems.at[0])]
+    copies[0].start()
     is_even = parity() == 0
+    beside = jnp.where(is_even, near[...].astype(F32), 0.0)
+    held_r[...] = (own[...].astype(F32) + beside + far[...].astype(F32)).astype(BF16)
+    copies.append(pltpu.make_async_copy(held_r, right, sems.at[1]))
+    copies[1].start()
     x, y = mine[...] * scale, other[...] * scale
     total = jnp.concatenate([jnp.where(is_even, x, y), jnp.where(is_even, y, x)], axis=0)
     for a in range(3):
@@ -475,9 +491,11 @@
             at = 128 * a + groups * e
             block = total[at : at + groups].T
             for b in range(3):
-                weight[2 - a, 2 - b, 2 - e] = block[feat * b : feat * (b + 1)]
-    beside = jnp.where(is_even, near[...].astype(F32), 0.0)
-    right[...] = (own[...].astype(F32) + beside + far[...].astype(F32)).astype(BF16)
+                held_w[2 - a, 2 - b, 2 - e] = block[feat * b : feat * (b + 1)]
+        copies.append(pltpu.make_async_copy(held_w.at[2 - a], weight.at[2 - a], sems.at[2 + a]))
+        copies[-1].start()
+    for copy in copies:
+        copy.wait()
 
 
 def copy_kernel(*refs):
@@ -664,13 +682,6 @@
     )
     near = swap(passed, 1)
     top, bot = halos(rims)
-    w2, wc = call(
-        taps_kernel,
-        [((12 * 128, 2 * 128), BF16), ((4 * 3 * rows * SLOT, 2 * rows * feat), BF16)],
-        [pltpu.VMEM((3 * rows * feat, 3 * rows * SLOT), F32)],
-        conv_weight.transpose(0, 1, 2, 4, 3),
-        after=[passed],
-    )
     band = 104 + cols + PAD
     banks = [((rows, total, wide), F32), ((rows, band, wide), F32), ((rows, band, wide), F32)]
     spread_rows = 2 * rows * cols + rows * cols // 2
@@ -681,7 +692,7 @@
         left_features,
         right_features,
         far,
-        after=[w2],
+        after=[passed],
     )
     corner_pays = call(
         functools.partial(corner_kernel, ends, rows, disp),
@@ -723,7 +734,14 @@
     )
 
     got = swap(give, 1)
-    (part,) = call(sum_kernel, [(keep.shape, BF16)], [], keep, got)
+    w2, wc = call(
+        taps_kernel,
+        [((12 * 128, 2 * 128), BF16), ((4 * 3 * rows * SLOT, 2 * rows * feat), BF16)],
+        [pltpu.VMEM((3 * rows * feat, 3 * rows * SLOT), F32)],
+        conv_weight.transpose(0, 1, 2, 4, 3),
+        after=[keep],
+    )
+    (part,) = call(sum_kernel, [(keep.shape, BF16)], [], keep, got, after=[w2])
     grads = call(
         dgrad_kernel, [((2, disp, cols, 128), F32)] * (rows // 2), [], ctsh, w2, after=[part], us=0.2
     )
@@ -753,48 +771,53 @@
     (rg2,) = call(
         combine_kernel, [((rows, cols, channels), BF16)], [], rg1, rg2, after=[part]
     )
-    lg, left_done = call(
+    (lg,) = call(
         left_kernel,
         [((rows, cols, channels), BF16)],
         [pltpu.VMEM((rows, cols, wide), F32)],
         fr, fr4, *grads,
         after=[rg2],
-        token=True,
         us=1.9,
     )
-    (part,) = call(sum_kernel, [(part.shape, F32)], [], *parts, after=[left_done])
-    (spread,) = call(
-        functools.partial(spread_kernel, masks, groups),
-        [((disp // 2 + 1, 2, cols, 3 * rows * SLOT), BF16)],
-        [pltpu.VMEM((rows // 2, disp, total, 128), F32)],
-        vbuf, vtop, vbot,
-        after=[part],
-        us=1.3,
-    )
+    (part,) = call(sum_kernel, [(part.shape, F32)], [], *parts, after=[lg])
     output, conv_done = call(
-        conv_kernel,
+        functools.partial(conv_kernel, masks, groups),
         [((disp, rows, feat, cols), BF16)],
-        [pltpu.VMEM((disp, rows, feat, cols), BF16), pltpu.SemaphoreType.DMA((2,))],
-        spread, wc,
+        [
+            pltpu.VMEM((disp // 2 + 1, 2, cols, 3 * rows * SLOT), BF16),
+            pltpu.VMEM((rows // 2, disp, total, 128), F32),
+            pltpu.VMEM((disp, rows, feat, cols), BF16),
+            pltpu.SemaphoreType.DMA((3,)),
+        ],
+        vbuf, vtop, vbot, wc,
         after=[part],
         token=True,
-        us=2.6,
+        us=3.5,
         hbm=[0],
     )
     rg2 = col_shift(rg2, -2)
     cells = disp * rows * n_row * cols * n_col
-    weight_grad, right_grad = call(
+    weight_grad, right_grad, left_grad = call(
         functools.partial(finish_kernel, 1.0 / math.sqrt(cells)),
-        [((3, 3, 3, feat, groups), F32), ((rows, cols, channels), BF16)],
-        [],
-        part, swap(part, 1), rg0, rg1, rg2,
+        [
+            ((3, 3, 3, feat, groups), F32),
+            ((rows, cols, channels), BF16),
+            ((rows, cols, channels), BF16),
+        ],
+        [
+            pltpu.VMEM((3, 3, 3, feat, groups), F32),
+            pltpu.VMEM((rows, cols, channels), BF16),
+            pltpu.SemaphoreType.DMA((5,)),
+        ],
+        part, swap(part, 1), rg0, rg1, rg2, lg,
         after=[conv_done],
         us=1.0,
+        hbm=[0, 1, 2],
     )
     return (
         output.transpose(0, 1, 3, 2),
         weight_grad.transpose(0, 1, 2, 4, 3),
-        lg,
+        left_grad,
         right_grad,
     )
 

time: 44.7 us -> 45 us (level)
  waiting for transfers between devices: 3.36 us -> 5.34 us
  Pallas kernels: 15.7 us -> 14 us
    ppermute x11, waiting for transfers between devices: 3.35 us -> 5.33 us  [swap(): return lax.ppermute(block, ('row', 'col'), route)]
    pallas_call x17 -> x16, Pallas kernels: 15.7 us -> 14 us  [call(): pl.pallas_call(lambda *refs: kernel(*refs[skip:]), out_shape=[jax.ShapeDt...]
  transfers between devices with their start and end apart: 17 -> 17, of which waited for: 3 -> 4; matrix products, arithmetic and copies ran while one was open for 4% -> 4% of each run, Pallas kernels for 33% -> 29%
where the time goes in v3:
time: 45 us; the launch traced here: 44.6 us
  starting transfers between devices  21.7 us (48%)
  Pallas kernels  14 us (31%)
  waiting for transfers between devices  5.34 us (12%)
  local copies, waits for them, and re-layouts  2.71 us (6%)
  between operations  0.88 us (2%)
    pallas_call x16, Pallas kernels, call(): pl.pallas_call(lambda *refs: kernel(*refs[skip:]), out_shape=[jax.ShapeDt...  14 us
    ppermute x11, starting transfers between devices, swap(): return lax.ppermute(block, ('row', 'col'), route)  11 us
    ppermute x2, starting transfers between devices, col_shift(): return lax.ppermute(block, 'col', route)  6.31 us
    ppermute x11, waiting for transfers between devices, swap(): return lax.ppermute(block, ('row', 'col'), route)  5.33 us
    ppermute x3, starting transfers between devices, halos(): got = lax.ppermute(pays[0], 'row', [(0, 1), (1, 0)])  3.67 us
    slice x2, local copies, waits for them, and re-layouts, on_device(): x[:, at:at + 1]  1.56 us
    unnamed x8, local copies, waits for them, and re-layouts  1.14 us
  transfers between devices with their start and end apart: 17, of which 4 were waited for; matrix products, arithmetic and copies ran while one was open for 4% of the time, Pallas kernels for 29%

profile of v3, /device:TPU:0, one launch (start us, length us, event | category | flops | bytes accessed | tf_op | source)
XLA Modules:
  0.0 44.6 jit_solution(5376740815810413092)
XLA Ops:
  0.6 0.0 copy-start
  0.6 0.0 copy-start.1
  0.7 5.0 %collective-permute-start = (bf16[4,64,320]{2,1,0:T(8,128)(2,1)}, bf16[4,64,320]{2,1,0:T(8,128)(2,1)S(1)}, u32[]{:S(2)}, u32[]{:S(2)}) collective-permute-start(bf16[4,64,320]{2,1,0:T(8,128)(2,1)} %refs_2_.1), channel_id=1, source_target_pairs={{0,2},{1,3},{2,4},{3,5},{4,6},{5,7},{6,8},{7,9},{8,10},{9,11},{10,... | collective-permute-start | bytes 491528 | tf_op jit(solution)/shard_map/ppermute | solution.py:606
  5.7 0.8 %fusion.1 = (bf16[4,1,320]{2,1,0:T(2,128)(2,1)S(1)}, bf16[4,1,320]{2,1,0:T(2,128)(2,1)S(1)}) fusion(bf16[4,64,320]{2,1,0:T(8,128)(2,1)} %refs_2_.1), kind=kLoop, calls=%fused_computation.2 | loop fusion | bytes 10240 | tf_op jit(solution)/shard_map/slice | solution.py:672
  6.5 0.8 %fusion = (bf16[4,1,320]{2,1,0:T(2,128)(2,1)S(1)}, bf16[4,1,320]{2,1,0:T(2,128)(2,1)S(1)}) fusion(bf16[4,64,320]{2,1,0:T(8,128)(2,1)} %refs_1_.3), kind=kLoop, calls=%fused_computation.1 | loop fusion | bytes 10240 | tf_op jit(solution)/shard_map/slice | solution.py:672
  7.3 0.0 copy-start.3
  7.3 1.1 %copy-done.3 = bf16[24,4,64,32]{2,3,1,0:T(8,128)(2,1)S(1)} copy-done((bf16[24,4,64,32]{2,3,1,0:T(8,128)(2,1)S(1)}, bf16[24,4,64,32]{2,3,1,0:T(8,128)(2,1)}, u32[]{:S(2)}) %copy-start.3) | copy-done | bytes 393240
  8.4 0.3 shard_map.75
  8.8 0.1 collective-permute-start.2
  8.8 0.7 %collective-permute-start.3 = (bf16[32,320]{1,0:T(8,128)(2,1)S(1)}, bf16[32,320]{1,0:T(8,128)(2,1)S(1)}, u32[]{:S(2)}, u32[]{:S(2)}) collective-permute-start(bf16[32,320]{1,0:T(8,128)(2,1)S(1)} %get-tuple-element.33), channel_id=1, source_target_pairs={{1,2},{3,4},{5,6},{7,8},{9,10},{11,12},{13,14},{2,1},{4,3},{6,5},{... | collective-permute-start | bytes 61448 | tf_op jit(solution)/shard_map/ppermute | solution.py:679
  9.5 1.6 %collective-permute-start.4 = (bf16[6,64,128]{2,1,0:T(8,128)(2,1)S(1)}, bf16[6,64,128]{2,1,0:T(8,128)(2,1)S(1)}, u32[]{:S(2)}, u32[]{:S(2)}) collective-permute-start(bf16[6,64,128]{2,1,0:T(8,128)(2,1)S(1)} %get-tuple-element.39), channel_id=1, source_target_pairs={{0,16},{16,0},{1,17},{17,1},{2,18},{18,2},{3,19},{19,3},{4,20},{20... | collective-permute-start | bytes 294920 | tf_op jit(solution)/shard_map/ppermute | solution.py:617
  11.1 0.0 collective-permute-done.refs_2_.refs_3_
  11.1 0.0 copy-done
  11.1 0.1 shard_map.76.refs_0_
  11.1 2.7 %collective-permute-start.1 = (bf16[4,64,320]{2,1,0:T(8,128)(2,1)S(1)}, bf16[4,64,320]{2,1,0:T(8,128)(2,1)S(1)}, u32[]{:S(2)}, u32[]{:S(2)}) collective-permute-start(bf16[4,64,320]{2,1,0:T(8,128)(2,1)S(1)} %shard_map.76.refs_0_), channel_id=1, source_target_pairs={{0,1},{1,0},{2,3},{3,2},{4,5},{5,4},{6,7},{7,6},{8,9},{9,8},{10,11... | collective-permute-start | bytes 491528 | tf_op jit(solution)/shard_map/ppermute | solution.py:659
  13.8 0.0 copy-done.1
  13.8 0.5 %shard_map.77 = (f32[4,80,512]{2,1,0:T(8,128)S(1)}, f32[4,176,512]{2,1,0:T(8,128)S(1)}, f32[4,176,512]{2,1,0:T(8,128)S(1)}) custom-call(bf16[4,64,320]{2,1,0:T(8,128)(2,1)S(1)} %shard_map.76.refs_0_, bf16[4,64,320]{2,1,0:T(8,128)(2,1)S(1)} %copy-done.1, bf16[4,64,320]{2,1,0:T(8,128)(2,1)S(1)} %copy-done, ...), custom_call_target="tpu_custom_call" | custom-call | tf_op jit(solution)/shard_map/pallas_call | solution.py:589
  14.4 0.0 collective-permute-done.2.refs_1_.refs_2_
  14.4 0.0 collective-permute-done.3.refs_2_.refs_3_
  14.4 0.1 shard_map.79
  14.5 0.5 %collective-permute-start.5 = (bf16[16,128]{1,0:T(8,128)(2,1)S(1)}, bf16[16,128]{1,0:T(8,128)(2,1)S(1)}, u32[]{:S(2)}, u32[]{:S(2)}) collective-permute-start(bf16[16,128]{1,0:T(8,128)(2,1)S(1)} %shard_map.79), channel_id=1, source_target_pairs={{0,16},{16,0},{1,17},{17,1},{2,18},{18,2},{3,19},{19,3},{4,20},{20... | collective-permute-start | bytes 12296 | tf_op jit(solution)/shard_map/ppermute | solution.py:617
  15.0 0.0 collective-permute-done.1.refs_0_
  15.0 2.0 %shard_map.78 = (f32[4,80,512]{2,1,0:T(8,128)S(1)}, f32[4,176,512]{2,1,0:T(8,128)S(1)}, f32[4,176,512]{2,1,0:T(8,128)S(1)}, f32[2,24,80,128]{3,2,1,0:T(8,128)S(1)}, bf16[960,128]{1,0:T(8,128)(2,1)S(1)}) custom-call(bf16[4,64,320]{2,1,0:T(8,128)(2,1)S(1)} %collective-permute-done.1.refs_0_, ...), custom_call_target="tpu_custom_call", output_to_operand_aliasing={{0}: (3, {}), {1}: (4, {}), {2}: (5, {})} | custom-call | flops 2070000000 | bytes 6660000 | tf_op jit(solution)/shard_map/pallas_call | solution.py:589
  17.0 1.6 %collective-permute-start.7 = (bf16[960,128]{1,0:T(8,128)(2,1)S(1)}, bf16[960,128]{1,0:T(8,128)(2,1)S(1)}, u32[]{:S(2)}, u32[]{:S(2)}) collective-permute-start(bf16[960,128]{1,0:T(8,128)(2,1)S(1)} %get-tuple-element.47), channel_id=1, source_target_pairs={{0,16},{16,0},{1,17},{17,1},{2,18},{18,2},{3,19},{19,3},{4,20},{20... | collective-permute-start | bytes 737288 | tf_op jit(solution)/shard_map/ppermute | solution.py:617
  18.6 0.0 collective-permute-done.4.refs_4_.refs_5_
  18.6 0.0 collective-permute-done.5.refs_6_.refs_7_
  18.6 0.0 copy-start.2
  18.6 1.9 %shard_map.80 = (f32[192,128]{1,0:T(8,128)S(1)}, f32[192,128]{1,0:T(8,128)S(1)}, bf16[13,2,64,768]{3,2,1,0:T(8,128)(2,1)S(1)}) custom-call(f32[2,24,80,128]{3,2,1,0:T(8,128)S(1)} %get-tuple-element.38.refs_0_.refs_1_, bf16[24,64,128]{2,1,0:T(8,128)(2,1)S(1)} %get-tuple-element.31.refs_0_.refs_1_, bf16[32,320]{1,0:T(8,128)(2,1)S(1)} %collective-permute-done.2.refs_1_.refs_2_, ...), custom_call_target="tpu_custom_call" | custom-call | flops 2300000000 | bytes 7400000 | tf_op jit(solution)/shard_map/pallas_call | solution.py:589
  20.5 0.1 collective-permute-start.6
  20.6 0.0 copy-done.2
  20.6 0.8 %shard_map.81 = (bf16[1536,256]{1,0:T(8,128)(2,1)S(1)}, bf16[3072,256]{1,0:T(8,128)(2,1)S(1)}) custom-call(f32[192,128]{1,0:T(8,128)S(1)} %get-tuple-element.40.refs_0_.refs_1_, bf16[3,3,3,32,40]{4,3,2,1,0:T(8,128)(2,1)S(1)} %bitcast.4), custom_call_target="tpu_custom_call" | custom-call | tf_op jit(solution)/shard_map/pallas_call | solution.py:589
  21.4 0.4 collective-permute-done.6.refs_2_
  21.9 2.7 %collective-permute-start.10 = (bf16[192,128]{1,0:T(8,128)(2,1)S(1)}, bf16[192,128]{1,0:T(8,128)(2,1)S(1)}, u32[]{:S(2)}, u32[]{:S(2)}) collective-permute-start(bf16[192,128]{1,0:T(8,128)(2,1)S(1)} %shard_map.82.refs_0_.refs_2_), channel_id=1, source_target_pairs={{0,6},{1,7},{2,4},{3,5},{4,2},{5,3},{6,0},{7,1},{8,14},{9,15},{10,... | collective-permute-start | bytes 147464 | tf_op jit(solution)/shard_map/ppermute | solution.py:659
  24.6 1.0 %collective-permute-start.8 = (bf16[192,128]{1,0:T(8,128)(2,1)S(1)}, bf16[192,128]{1,0:T(8,128)(2,1)S(1)}, u32[]{:S(2)}, u32[]{:S(2)}) collective-permute-start(bf16[192,128]{1,0:T(8,128)(2,1)S(1)} %shard_map.82.refs_0_.refs_2_), channel_id=1, source_target_pairs={{0,2},{1,3},{2,0},{3,1},{4,6},{5,7},{6,4},{7,5},{8,10},{9,11},{10,... | collective-permute-start | bytes 147464 | tf_op jit(solution)/shard_map/ppermute | solution.py:659
  25.5 0.0 collective-permute-start.9
  25.5 1.5 %shard_map.83 = (f32[2,24,64,128]{3,2,1,0:T(8,128)S(1)}, f32[2,24,64,128]{3,2,1,0:T(8,128)S(1)}) custom-call(bf16[192,128]{1,0:T(8,128)(2,1)S(1)} %shard_map.82.refs_0_.refs_2_, bf16[13,2,64,768]{3,2,1,0:T(8,128)(2,1)S(1)} %get-tuple-element.43.refs_1_, bf16[1536,256]{1,0:T(8,128)(2,1)S(1)} %get-tuple-element.41.refs_0_.refs_2_), custom_call_target="tpu_custom_call" | custom-call | flops 230000000 | bytes 740000 | tf_op jit(solution)/shard_map/pallas_call | solution.py:589
  27.0 1.3 %shard_map.84 = (bf16[4,64,320]{2,1,0:T(8,128)(2,1)S(1)}, bf16[4,64,320]{2,1,0:T(8,128)(2,1)S(1)}, bf16[4,32,320]{2,1,0:T(8,128)(2,1)S(1)}) custom-call(f32[4,80,512]{2,1,0:T(8,128)S(1)} %get-tuple-element.37.refs_0_, f32[2,24,64,128]{3,2,1,0:T(8,128)S(1)} %get-tuple-element.44.refs_1_.refs_3_, f32[2,24,64,128]{3,2,1,0:T(8,128)S(1)} %get-tuple-element.45.refs_2_.refs_4_), custom_call_target="tpu_custom_call" | custom-call | flops 230000000 | bytes 740000 | tf_op jit(solution)/shard_map/pallas_call | solution.py:589
  28.3 0.1 collective-permute-start.11
  28.4 0.0 collective-permute-done.10.refs_5_
  28.4 0.3 collective-permute-done.8.refs_3_
  28.6 1.0 %collective-permute-done.9.refs_4_ = bf16[192,128]{1,0:T(8,128)(2,1)S(1)} collective-permute-done((bf16[192,128]{1,0:T(8,128)(2,1)S(1)}, bf16[192,128]{1,0:T(8,128)(2,1)S(1)}, u32[]{:S(2)}, u32[]{:S(2)}) %collective-permute-start.9) | collective-permute-done | bytes 49184 | tf_op jit(solution)/shard_map/ppermute | solution.py:659
  29.6 0.0 collective-permute-done.7.refs_1_.refs_2_.refs_3_
  29.6 2.6 %collective-permute-start.12 = (bf16[192,128]{1,0:T(8,128)(2,1)S(1)}, bf16[192,128]{1,0:T(8,128)(2,1)S(1)}, u32[]{:S(2)}, u32[]{:S(2)}) collective-permute-start(bf16[192,128]{1,0:T(8,128)(2,1)S(1)} %shard_map.85.refs_0_.refs_1_), channel_id=1, source_target_pairs={{0,8},{1,9},{2,10},{3,11},{4,12},{5,13},{6,14},{7,15},{8,0},{9,1},... | collective-permute-start | bytes 147464 | tf_op jit(solution)/shard_map/ppermute | solution.py:659
  32.3 1.5 %collective-permute-start.13 = (bf16[192,128]{1,0:T(8,128)(2,1)S(1)}, bf16[192,128]{1,0:T(8,128)(2,1)S(1)}, u32[]{:S(2)}, u32[]{:S(2)}) collective-permute-start(bf16[192,128]{1,0:T(8,128)(2,1)S(1)} %shard_map.85.refs_0_.refs_1_), channel_id=1, source_target_pairs={{0,16},{1,17},{2,18},{3,19},{4,20},{5,21},{6,22},{7,23},{8,24},{9,... | collective-permute-start | bytes 147464 | tf_op jit(solution)/shard_map/ppermute | solution.py:659
  33.8 0.3 collective-permute-start.14
  34.1 0.0 collective-permute-done.11.refs_1_.refs_4_
  34.1 0.1 shard_map.86.refs_0_
  34.2 1.3 %collective-permute-start.16 = (bf16[4,64,320]{2,1,0:T(8,128)(2,1)S(1)}, bf16[4,64,320]{2,1,0:T(8,128)(2,1)S(1)}, u32[]{:S(2)}, u32[]{:S(2)}) collective-permute-start(bf16[4,64,320]{2,1,0:T(8,128)(2,1)S(1)} %shard_map.86.refs_0_), channel_id=1, source_target_pairs={{2,0},{3,1},{4,2},{5,3},{6,4},{7,5},{8,6},{9,7},{10,8},{11,9},{12,... | collective-permute-start | bytes 491528 | tf_op jit(solution)/shard_map/ppermute | solution.py:606
  35.5 1.2 %shard_map.87.refs_0_.refs_6_ = bf16[4,64,320]{2,1,0:T(8,128)(2,1)S(1)} custom-call(bf16[4,64,320]{2,1,0:T(8,128)(2,1)S(1)} %shard_map.86.refs_0_, f32[4,176,512]{2,1,0:T(8,128)S(1)} %get-tuple-element.50.refs_1_, f32[4,176,512]{2,1,0:T(8,128)S(1)} %get-tuple-element.51.refs_2_, f32[2,24,64,128]{3,2,1,0:T(8,128)S(1)} %get-tuple-element.44.refs_1_.refs_3_, ...), custom_call_target="tpu_custom_call" | custom-call | flops 2184999936 | bytes 7030000 | tf_op jit(solution)/shard_map/pallas_call | solution.py:589
  36.7 0.0 collective-permute-done.12.refs_2_
  36.7 0.0 collective-permute-done.13.refs_3_
  36.7 3.7 %collective-permute-done.14.refs_4_ = bf16[192,128]{1,0:T(8,128)(2,1)S(1)} collective-permute-done((bf16[192,128]{1,0:T(8,128)(2,1)S(1)}, bf16[192,128]{1,0:T(8,128)(2,1)S(1)}, u32[]{:S(2)}, u32[]{:S(2)}) %collective-permute-start.14) | collective-permute-done | bytes 49184 | tf_op jit(solution)/shard_map/ppermute | solution.py:659
  40.4 0.1 collective-permute-start.15
  40.5 3.0 %shard_map.89 = (bf16[24,4,32,64]{3,2,1,0:T(8,128)(2,1)}, f32[8,128]{1,0:T(8,128)S(1)}) custom-call(f32[192,128]{1,0:T(8,128)S(1)} %shard_map.88.refs_0_.refs_1_, f32[2,24,80,128]{3,2,1,0:T(8,128)S(1)} %get-tuple-element.38.refs_0_.refs_1_, bf16[960,128]{1,0:T(8,128)(2,1)S(1)} %collective-permute-done.7.refs_1_.refs_2_.refs_3_, ...), custom_call_target="tpu_custom_call" | custom-call | flops 4024999936 | bytes 12950000 | tf_op jit(solution)/shard_map/pallas_call | solution.py:589
  43.5 0.0 collective-permute-done.15.refs_2_
  43.5 0.0 collective-permute-done.16.refs_5_
  43.5 1.1 %shard_map.90 = (f32[3,3,3,32,40]{4,3,2,1,0:T(8,128)}, bf16[4,64,320]{2,1,0:T(8,128)(2,1)}, bf16[4,64,320]{2,1,0:T(8,128)(2,1)}) custom-call(f32[8,128]{1,0:T(8,128)S(1)} %get-tuple-element.54.refs_0_, f32[192,128]{1,0:T(8,128)S(1)} %shard_map.88.refs_0_.refs_1_, f32[192,128]{1,0:T(8,128)S(1)} %collective-permute-done.15.refs_2_, ...), custom_call_target="tpu_custom_call" | custom-call | flops 1150000000 | bytes 3700000 | tf_op jit(solution)/shard_map/pallas_call | solution.py:589
  (4 shorter events, 0.1 us)
Async XLA Ops:
  0.6 10.4 %copy-start = (bf16[4,64,320]{2,1,0:T(8,128)(2,1)S(1)}, bf16[4,64,320]{2,1,0:T(8,128)(2,1)}, u32[]{:S(2)}) copy-start(bf16[4,64,320]{2,1,0:T(8,128)(2,1)} %refs_2_.1) | copy-start | bytes 491524
  0.6 13.2 %copy-start.1 = (bf16[4,64,320]{2,1,0:T(8,128)(2,1)S(1)}, bf16[4,64,320]{2,1,0:T(8,128)(2,1)}, u32[]{:S(2)}) copy-start(bf16[4,64,320]{2,1,0:T(8,128)(2,1)} %refs_1_.3) | copy-start | bytes 491524
  0.7 10.4 %collective-permute-start = (bf16[4,64,320]{2,1,0:T(8,128)(2,1)}, bf16[4,64,320]{2,1,0:T(8,128)(2,1)S(1)}, u32[]{:S(2)}, u32[]{:S(2)}) collective-permute-start(bf16[4,64,320]{2,1,0:T(8,128)(2,1)} %refs_2_.1), channel_id=1, source_target_pairs={{0,2},{1,3},{2,4},{3,5},{4,6},{5,7},{6,8},{7,9},{8,10},{9,11},{10,... | collective-permute-start | bytes 491528 | tf_op jit(solution)/shard_map/ppermute | solution.py:606
  7.3 1.1 %copy-start.3 = (bf16[24,4,64,32]{2,3,1,0:T(8,128)(2,1)S(1)}, bf16[24,4,64,32]{2,3,1,0:T(8,128)(2,1)}, u32[]{:S(2)}) copy-start(bf16[24,4,64,32]{2,3,1,0:T(8,128)(2,1)} %param.7) | copy-start | bytes 1179652
  8.8 5.6 %collective-permute-start.2 = (bf16[32,320]{1,0:T(8,128)(2,1)S(1)}, bf16[32,320]{1,0:T(8,128)(2,1)S(1)}, u32[]{:S(2)}, u32[]{:S(2)}) collective-permute-start(bf16[32,320]{1,0:T(8,128)(2,1)S(1)} %get-tuple-element.32), channel_id=1, source_target_pairs={{0,1},{1,0},{2,3},{3,2},{4,5},{5,4},{6,7},{7,6},{8,9},{9,8},{10,11... | collective-permute-start | bytes 61448 | tf_op jit(solution)/shard_map/ppermute | solution.py:659
  8.8 5.5 %collective-permute-start.3 = (bf16[32,320]{1,0:T(8,128)(2,1)S(1)}, bf16[32,320]{1,0:T(8,128)(2,1)S(1)}, u32[]{:S(2)}, u32[]{:S(2)}) collective-permute-start(bf16[32,320]{1,0:T(8,128)(2,1)S(1)} %get-tuple-element.33), channel_id=1, source_target_pairs={{1,2},{3,4},{5,6},{7,8},{9,10},{11,12},{13,14},{2,1},{4,3},{6,5},{... | collective-permute-start | bytes 61448 | tf_op jit(solution)/shard_map/ppermute | solution.py:679
  9.5 9.1 %collective-permute-start.4 = (bf16[6,64,128]{2,1,0:T(8,128)(2,1)S(1)}, bf16[6,64,128]{2,1,0:T(8,128)(2,1)S(1)}, u32[]{:S(2)}, u32[]{:S(2)}) collective-permute-start(bf16[6,64,128]{2,1,0:T(8,128)(2,1)S(1)} %get-tuple-element.39), channel_id=1, source_target_pairs={{0,16},{16,0},{1,17},{17,1},{2,18},{18,2},{3,19},{19,3},{4,20},{20... | collective-permute-start | bytes 294920 | tf_op jit(solution)/shard_map/ppermute | solution.py:617
  11.1 3.9 %collective-permute-start.1 = (bf16[4,64,320]{2,1,0:T(8,128)(2,1)S(1)}, bf16[4,64,320]{2,1,0:T(8,128)(2,1)S(1)}, u32[]{:S(2)}, u32[]{:S(2)}) collective-permute-start(bf16[4,64,320]{2,1,0:T(8,128)(2,1)S(1)} %shard_map.76.refs_0_), channel_id=1, source_target_pairs={{0,1},{1,0},{2,3},{3,2},{4,5},{5,4},{6,7},{7,6},{8,9},{9,8},{10,11... | collective-permute-start | bytes 491528 | tf_op jit(solution)/shard_map/ppermute | solution.py:659
  14.5 4.1 %collective-permute-start.5 = (bf16[16,128]{1,0:T(8,128)(2,1)S(1)}, bf16[16,128]{1,0:T(8,128)(2,1)S(1)}, u32[]{:S(2)}, u32[]{:S(2)}) collective-permute-start(bf16[16,128]{1,0:T(8,128)(2,1)S(1)} %shard_map.79), channel_id=1, source_target_pairs={{0,16},{16,0},{1,17},{17,1},{2,18},{18,2},{3,19},{19,3},{4,20},{20... | collective-permute-start | bytes 12296 | tf_op jit(solution)/shard_map/ppermute | solution.py:617
  17.0 12.6 %collective-permute-start.7 = (bf16[960,128]{1,0:T(8,128)(2,1)S(1)}, bf16[960,128]{1,0:T(8,128)(2,1)S(1)}, u32[]{:S(2)}, u32[]{:S(2)}) collective-permute-start(bf16[960,128]{1,0:T(8,128)(2,1)S(1)} %get-tuple-element.47), channel_id=1, source_target_pairs={{0,16},{16,0},{1,17},{17,1},{2,18},{18,2},{3,19},{19,3},{4,20},{20... | collective-permute-start | bytes 737288 | tf_op jit(solution)/shard_map/ppermute | solution.py:617
  18.6 2.0 %copy-start.2 = (bf16[3,3,3,40,32]{3,4,2,1,0:T(8,128)(2,1)S(1)}, bf16[3,3,3,40,32]{3,4,2,1,0:T(8,128)(2,1)}, u32[]{:S(2)}) copy-start(bf16[3,3,3,40,32]{3,4,2,1,0:T(8,128)(2,1)} %param.6) | copy-start | bytes 207364
  20.5 1.4 %collective-permute-start.6 = (f32[192,128]{1,0:T(8,128)S(1)}, f32[192,128]{1,0:T(8,128)S(1)}, u32[]{:S(2)}, u32[]{:S(2)}) collective-permute-start(f32[192,128]{1,0:T(8,128)S(1)} %get-tuple-element.42), channel_id=1, source_target_pairs={{0,1},{1,0},{2,3},{3,2},{4,5},{5,4},{6,7},{7,6},{8,9},{9,8},{10,11... | collective-permute-start | bytes 294920 | tf_op jit(solution)/shard_map/ppermute | solution.py:659
  21.9 6.5 %collective-permute-start.10 = (bf16[192,128]{1,0:T(8,128)(2,1)S(1)}, bf16[192,128]{1,0:T(8,128)(2,1)S(1)}, u32[]{:S(2)}, u32[]{:S(2)}) collective-permute-start(bf16[192,128]{1,0:T(8,128)(2,1)S(1)} %shard_map.82.refs_0_.refs_2_), channel_id=1, source_target_pairs={{0,6},{1,7},{2,4},{3,5},{4,2},{5,3},{6,0},{7,1},{8,14},{9,15},{10,... | collective-permute-start | bytes 147464 | tf_op jit(solution)/shard_map/ppermute | solution.py:659
  24.6 4.1 %collective-permute-start.8 = (bf16[192,128]{1,0:T(8,128)(2,1)S(1)}, bf16[192,128]{1,0:T(8,128)(2,1)S(1)}, u32[]{:S(2)}, u32[]{:S(2)}) collective-permute-start(bf16[192,128]{1,0:T(8,128)(2,1)S(1)} %shard_map.82.refs_0_.refs_2_), channel_id=1, source_target_pairs={{0,2},{1,3},{2,0},{3,1},{4,6},{5,7},{6,4},{7,5},{8,10},{9,11},{10,... | collective-permute-start | bytes 147464 | tf_op jit(solution)/shard_map/ppermute | solution.py:659
  25.5 4.1 %collective-permute-start.9 = (bf16[192,128]{1,0:T(8,128)(2,1)S(1)}, bf16[192,128]{1,0:T(8,128)(2,1)S(1)}, u32[]{:S(2)}, u32[]{:S(2)}) collective-permute-start(bf16[192,128]{1,0:T(8,128)(2,1)S(1)} %shard_map.82.refs_0_.refs_2_), channel_id=1, source_target_pairs={{0,4},{1,5},{2,6},{3,7},{4,0},{5,1},{6,2},{7,3},{8,12},{9,13},{10,... | collective-permute-start | bytes 147464 | tf_op jit(solution)/shard_map/ppermute | solution.py:659
  28.3 5.8 %collective-permute-start.11 = (bf16[4,64,320]{2,1,0:T(8,128)(2,1)S(1)}, bf16[4,64,320]{2,1,0:T(8,128)(2,1)S(1)}, u32[]{:S(2)}, u32[]{:S(2)}) collective-permute-start(bf16[4,64,320]{2,1,0:T(8,128)(2,1)S(1)} %get-tuple-element.48), channel_id=1, source_target_pairs={{0,1},{1,0},{2,3},{3,2},{4,5},{5,4},{6,7},{7,6},{8,9},{9,8},{10,11... | collective-permute-start | bytes 491528 | tf_op jit(solution)/shard_map/ppermute | solution.py:659
  29.6 7.1 %collective-permute-start.12 = (bf16[192,128]{1,0:T(8,128)(2,1)S(1)}, bf16[192,128]{1,0:T(8,128)(2,1)S(1)}, u32[]{:S(2)}, u32[]{:S(2)}) collective-permute-start(bf16[192,128]{1,0:T(8,128)(2,1)S(1)} %shard_map.85.refs_0_.refs_1_), channel_id=1, source_target_pairs={{0,8},{1,9},{2,10},{3,11},{4,12},{5,13},{6,14},{7,15},{8,0},{9,1},... | collective-permute-start | bytes 147464 | tf_op jit(solution)/shard_map/ppermute | solution.py:659
  32.3 4.4 %collective-permute-start.13 = (bf16[192,128]{1,0:T(8,128)(2,1)S(1)}, bf16[192,128]{1,0:T(8,128)(2,1)S(1)}, u32[]{:S(2)}, u32[]{:S(2)}) collective-permute-start(bf16[192,128]{1,0:T(8,128)(2,1)S(1)} %shard_map.85.refs_0_.refs_1_), channel_id=1, source_target_pairs={{0,16},{1,17},{2,18},{3,19},{4,20},{5,21},{6,22},{7,23},{8,24},{9,... | collective-permute-start | bytes 147464 | tf_op jit(solution)/shard_map/ppermute | solution.py:659
  33.8 6.6 %collective-permute-start.14 = (bf16[192,128]{1,0:T(8,128)(2,1)S(1)}, bf16[192,128]{1,0:T(8,128)(2,1)S(1)}, u32[]{:S(2)}, u32[]{:S(2)}) collective-permute-start(bf16[192,128]{1,0:T(8,128)(2,1)S(1)} %shard_map.85.refs_0_.refs_1_), channel_id=1, source_target_pairs={{0,24},{1,25},{2,26},{3,27},{4,28},{5,29},{6,30},{7,31},{8,16},{9,... | collective-permute-start | bytes 147464 | tf_op jit(solution)/shard_map/ppermute | solution.py:659
  34.2 9.4 %collective-permute-start.16 = (bf16[4,64,320]{2,1,0:T(8,128)(2,1)S(1)}, bf16[4,64,320]{2,1,0:T(8,128)(2,1)S(1)}, u32[]{:S(2)}, u32[]{:S(2)}) collective-permute-start(bf16[4,64,320]{2,1,0:T(8,128)(2,1)S(1)} %shard_map.86.refs_0_), channel_id=1, source_target_pairs={{2,0},{3,1},{4,2},{5,3},{6,4},{7,5},{8,6},{9,7},{10,8},{11,9},{12,... | collective-permute-start | bytes 491528 | tf_op jit(solution)/shard_map/ppermute | solution.py:606
  40.4 3.1 %collective-permute-start.15 = (f32[192,128]{1,0:T(8,128)S(1)}, f32[192,128]{1,0:T(8,128)S(1)}, u32[]{:S(2)}, u32[]{:S(2)}) collective-permute-start(f32[192,128]{1,0:T(8,128)S(1)} %shard_map.88.refs_0_.refs_1_), channel_id=1, source_target_pairs={{0,1},{1,0},{2,3},{3,2},{4,5},{5,4},{6,7},{7,6},{8,9},{9,8},{10,11... | collective-permute-start | bytes 294920 | tf_op jit(solution)/shard_map/ppermute | solution.py:659

commit v4 on v3

--- a/solution.py
+++ b/solution.py
@@ -42,7 +42,11 @@
     return lax.dot_general(a, b, (((1,), (1,)), ((), ())), preferred_element_type=F32)
 
 
-def pack_kernel(ends, rims_in, ct, even, odd, ctl, *rest):
+def begin_kernel(out):
+    out[...] = jnp.zeros(out.shape, F32)
+
+
+def pack_kernel(ends, left, right, ct, even, odd, ctl, *rest):
     rims, ctf = rest[:-1], rest[-1]
     disp, rows, feat, cols = ct.shape
     per = 128 // feat
@@ -54,7 +58,7 @@
     for i, col in enumerate((cols - 1, 0)):
         block = ctf[pl.ds(col, disp, stride=cols), :]
         block = jnp.concatenate([block, jnp.zeros((disp, even.shape[1] - rows * feat), F32)], axis=1)
-        edge = [rims_in[h, 2 * i + x : 2 * i + x + 1].astype(F32) for x in range(2) for h in range(rows)]
+        edge = [x[h, col : col + 1].astype(F32) for x in (left, right) for h in range(rows)]
         columns.append(jnp.concatenate([block, *edge], axis=0))
     is_even = parity() == 0
     even[...] = jnp.where(is_even, columns[0], columns[1]).astype(BF16)
@@ -659,6 +663,7 @@
         return lax.ppermute(block, ("row", "col"), route)
 
     far = col_shift(right_features, 2)
+    (begun,) = call(begin_kernel, [TOKEN], [], us=3.0)
     by_even, by_odd, ctl, *rims = call(
         functools.partial(pack_kernel, ends),
         [
@@ -668,10 +673,10 @@
         ]
         + [((disp // per, cols, 128), BF16)] * n,
         [pltpu.VMEM((disp * cols, rows * feat), F32)],
-        jnp.concatenate(
-            [x[:, at : at + 1] for at in (cols - 1, 0) for x in (left_features, right_features)], axis=1
-        ),
+        left_features,
+        right_features,
         ct,
+        after=[begun],
         us=0.4,
     )
     inner = range(1, n_col - 1, 2)
@@ -771,15 +776,6 @@
     (rg2,) = call(
         combine_kernel, [((rows, cols, channels), BF16)], [], rg1, rg2, after=[part]
     )
-    (lg,) = call(
-        left_kernel,
-        [((rows, cols, channels), BF16)],
-        [pltpu.VMEM((rows, cols, wide), F32)],
-        fr, fr4, *grads,
-        after=[rg2],
-        us=1.9,
-    )
-    (part,) = call(sum_kernel, [(part.shape, F32)], [], *parts, after=[lg])
     output, conv_done = call(
         functools.partial(conv_kernel, masks, groups),
         [((disp, rows, feat, cols), BF16)],
@@ -790,10 +786,19 @@
             pltpu.SemaphoreType.DMA((3,)),
         ],
         vbuf, vtop, vbot, wc,
+        after=[rg2],
+        token=True,
+        us=3.0,
+        hbm=[0],
+    )
+    (part,) = call(sum_kernel, [(part.shape, F32)], [], *parts, after=[conv_done], us=4.0)
+    (lg,) = call(
+        left_kernel,
+        [((rows, cols, channels), BF16)],
+        [pltpu.VMEM((rows, cols, wide), F32)],
+        fr, fr4, *grads,
         after=[part],
-        token=True,
-        us=3.5,
-        hbm=[0],
+        us=1.9,
     )
     rg2 = col_shift(rg2, -2)
     cells = disp * rows * n_row * cols * n_col
@@ -810,7 +815,6 @@
             pltpu.SemaphoreType.DMA((5,)),
         ],
         part, swap(part, 1), rg0, rg1, rg2, lg,
-        after=[conv_done],
         us=1.0,
         hbm=[0, 1, 2],
     )

time: 45 us -> 41 us (0.911)
  local copies, waits for them, and re-layouts: 2.71 us -> 0.02 us
  starting transfers between devices: 21.7 us -> 20.5 us
    ppermute x2, waiting for transfers between devices: 0.01 us -> 1.94 us  [col_shift(): return lax.ppermute(block, 'col', route)]
    ppermute x11, waiting for transfers between devices: 5.33 us -> 3.42 us  [swap(): return lax.ppermute(block, ('row', 'col'), route)]
    slice x2 -> x0, local copies, waits for them, and re-layouts: 1.56 us -> none  [on_device(): x[:, at:at + 1]]
    ppermute x11, starting transfers between devices: 11 us -> 9.91 us  [swap(): return lax.ppermute(block, ('row', 'col'), route)]
    unnamed x8, local copies, waits for them, and re-layouts: 1.14 us -> 0.02 us
    pallas_call x16 -> x17, Pallas kernels: 14 us -> 14 us  [call(): pl.pallas_call(lambda *refs: kernel(*refs[skip:]), out_shape=[jax.ShapeDt...]
  transfers between devices with their start and end apart: 17 -> 17, of which waited for: 4 -> 5; matrix products, arithmetic and copies ran while one was open for 4% -> 0% of each run, Pallas kernels for 29% -> 32%
where the time goes in v4:
time: 41 us; the launch traced here: 40.8 us
  starting transfers between devices  20.5 us (50%)
  Pallas kernels  14 us (34%)
  waiting for transfers between devices  5.36 us (13%)
  between operations  0.89 us (2%)
    pallas_call x17, Pallas kernels, call(): pl.pallas_call(lambda *refs: kernel(*refs[skip:]), out_shape=[jax.ShapeDt...  14 us
    ppermute x11, starting transfers between devices, swap(): return lax.ppermute(block, ('row', 'col'), route)  9.91 us
    ppermute x2, starting transfers between devices, col_shift(): return lax.ppermute(block, 'col', route)  6.31 us
    ppermute x3, starting transfers between devices, halos(): got = lax.ppermute(pays[0], 'row', [(0, 1), (1, 0)])  3.66 us
    ppermute x11, waiting for transfers between devices, swap(): return lax.ppermute(block, ('row', 'col'), route)  3.42 us
    ppermute x2, waiting for transfers between devices, col_shift(): return lax.ppermute(block, 'col', route)  1.94 us
  transfers between devices with their start and end apart: 17, of which 5 were waited for; matrix products, arithmetic and copies ran while one was open for 0% of the time, Pallas kernels for 32%

profile of v4, /device:TPU:0, one launch (start us, length us, event | category | flops | bytes accessed | tf_op | source)
XLA Modules:
  0.0 40.8 jit_solution(17929038545550113382)
XLA Ops:
  0.6 0.0 copy-start
  0.6 0.0 copy-start.3
  0.7 0.0 copy-start.2
  0.7 5.0 %collective-permute-start = (bf16[4,64,320]{2,1,0:T(8,128)(2,1)}, bf16[4,64,320]{2,1,0:T(8,128)(2,1)S(1)}, u32[]{:S(2)}, u32[]{:S(2)}) collective-permute-start(bf16[4,64,320]{2,1,0:T(8,128)(2,1)} %refs_2_.3), channel_id=1, source_target_pairs={{0,2},{1,3},{2,4},{3,5},{4,6},{5,7},{6,8},{7,9},{8,10},{9,11},{10,... | collective-permute-start | bytes 491528 | tf_op jit(solution)/shard_map/ppermute | solution.py:610
  5.7 0.0 copy-done
  5.7 0.0 copy-done.3
  5.7 0.0 copy-done.2
  5.7 0.3 shard_map.76
  6.1 0.1 collective-permute-start.2
  6.1 0.7 %collective-permute-start.3 = (bf16[32,320]{1,0:T(8,128)(2,1)S(1)}, bf16[32,320]{1,0:T(8,128)(2,1)S(1)}, u32[]{:S(2)}, u32[]{:S(2)}) collective-permute-start(bf16[32,320]{1,0:T(8,128)(2,1)S(1)} %get-tuple-element.33), channel_id=1, source_target_pairs={{1,2},{3,4},{5,6},{7,8},{9,10},{11,12},{13,14},{2,1},{4,3},{6,5},{... | collective-permute-start | bytes 61448 | tf_op jit(solution)/shard_map/ppermute | solution.py:684
  6.8 1.6 %collective-permute-start.4 = (bf16[6,64,128]{2,1,0:T(8,128)(2,1)S(1)}, bf16[6,64,128]{2,1,0:T(8,128)(2,1)S(1)}, u32[]{:S(2)}, u32[]{:S(2)}) collective-permute-start(bf16[6,64,128]{2,1,0:T(8,128)(2,1)S(1)} %get-tuple-element.39), channel_id=1, source_target_pairs={{0,16},{16,0},{1,17},{17,1},{2,18},{18,2},{3,19},{19,3},{4,20},{20... | collective-permute-start | bytes 294920 | tf_op jit(solution)/shard_map/ppermute | solution.py:621
  8.4 1.8 %collective-permute-done.refs_2_.refs_3_ = bf16[4,64,320]{2,1,0:T(8,128)(2,1)S(1)} collective-permute-done((bf16[4,64,320]{2,1,0:T(8,128)(2,1)}, bf16[4,64,320]{2,1,0:T(8,128)(2,1)S(1)}, u32[]{:S(2)}, u32[]{:S(2)}) %collective-permute-start) | collective-permute-done | bytes 163872 | tf_op jit(solution)/shard_map/ppermute | solution.py:610
  10.1 0.1 shard_map.77.refs_0_
  10.2 0.9 %collective-permute-start.1 = (bf16[4,64,320]{2,1,0:T(8,128)(2,1)S(1)}, bf16[4,64,320]{2,1,0:T(8,128)(2,1)S(1)}, u32[]{:S(2)}, u32[]{:S(2)}) collective-permute-start(bf16[4,64,320]{2,1,0:T(8,128)(2,1)S(1)} %shard_map.77.refs_0_), channel_id=1, source_target_pairs={{0,1},{1,0},{2,3},{3,2},{4,5},{5,4},{6,7},{7,6},{8,9},{9,8},{10,11... | collective-permute-start | bytes 491528 | tf_op jit(solution)/shard_map/ppermute | solution.py:663
  11.1 0.5 %shard_map.78 = (f32[4,80,512]{2,1,0:T(8,128)S(1)}, f32[4,176,512]{2,1,0:T(8,128)S(1)}, f32[4,176,512]{2,1,0:T(8,128)S(1)}) custom-call(bf16[4,64,320]{2,1,0:T(8,128)(2,1)S(1)} %shard_map.77.refs_0_, bf16[4,64,320]{2,1,0:T(8,128)(2,1)S(1)} %copy-done.2, bf16[4,64,320]{2,1,0:T(8,128)(2,1)S(1)} %copy-done, ...), custom_call_target="tpu_custom_call" | custom-call | tf_op jit(solution)/shard_map/pallas_call | solution.py:593
  11.6 0.0 collective-permute-done.2.refs_1_.refs_2_
  11.6 0.0 collective-permute-done.3.refs_2_.refs_3_
  11.7 0.1 shard_map.80
  11.8 0.7 %collective-permute-start.5 = (bf16[16,128]{1,0:T(8,128)(2,1)S(1)}, bf16[16,128]{1,0:T(8,128)(2,1)S(1)}, u32[]{:S(2)}, u32[]{:S(2)}) collective-permute-start(bf16[16,128]{1,0:T(8,128)(2,1)S(1)} %shard_map.80), channel_id=1, source_target_pairs={{0,16},{16,0},{1,17},{17,1},{2,18},{18,2},{3,19},{19,3},{4,20},{20... | collective-permute-start | bytes 12296 | tf_op jit(solution)/shard_map/ppermute | solution.py:621
  12.4 0.0 collective-permute-done.1.refs_0_
  12.4 2.0 %shard_map.79 = (f32[4,80,512]{2,1,0:T(8,128)S(1)}, f32[4,176,512]{2,1,0:T(8,128)S(1)}, f32[4,176,512]{2,1,0:T(8,128)S(1)}, f32[2,24,80,128]{3,2,1,0:T(8,128)S(1)}, bf16[960,128]{1,0:T(8,128)(2,1)S(1)}) custom-call(bf16[4,64,320]{2,1,0:T(8,128)(2,1)S(1)} %collective-permute-done.1.refs_0_, ...), custom_call_target="tpu_custom_call", output_to_operand_aliasing={{0}: (3, {}), {1}: (4, {}), {2}: (5, {})} | custom-call | flops 2070000000 | bytes 6660000 | tf_op jit(solution)/shard_map/pallas_call | solution.py:593
  14.4 1.4 %collective-permute-start.7 = (bf16[960,128]{1,0:T(8,128)(2,1)S(1)}, bf16[960,128]{1,0:T(8,128)(2,1)S(1)}, u32[]{:S(2)}, u32[]{:S(2)}) collective-permute-start(bf16[960,128]{1,0:T(8,128)(2,1)S(1)} %get-tuple-element.47), channel_id=1, source_target_pairs={{0,16},{16,0},{1,17},{17,1},{2,18},{18,2},{3,19},{19,3},{4,20},{20... | collective-permute-start | bytes 737288 | tf_op jit(solution)/shard_map/ppermute | solution.py:621
  15.9 0.0 collective-permute-done.4.refs_4_.refs_5_
  15.9 0.0 collective-permute-done.5.refs_6_.refs_7_
  15.9 0.0 copy-start.1
  15.9 1.9 %shard_map.81 = (f32[192,128]{1,0:T(8,128)S(1)}, f32[192,128]{1,0:T(8,128)S(1)}, bf16[13,2,64,768]{3,2,1,0:T(8,128)(2,1)S(1)}) custom-call(f32[2,24,80,128]{3,2,1,0:T(8,128)S(1)} %get-tuple-element.38.refs_0_.refs_1_, bf16[24,64,128]{2,1,0:T(8,128)(2,1)S(1)} %get-tuple-element.31.refs_0_.refs_1_, bf16[32,320]{1,0:T(8,128)(2,1)S(1)} %collective-permute-done.2.refs_1_.refs_2_, ...), custom_call_target="tpu_custom_call" | custom-call | flops 2300000000 | bytes 7400000 | tf_op jit(solution)/shard_map/pallas_call | solution.py:593
  17.8 0.1 collective-permute-start.6
  17.9 0.0 copy-done.1
  17.9 0.8 %shard_map.82 = (bf16[1536,256]{1,0:T(8,128)(2,1)S(1)}, bf16[3072,256]{1,0:T(8,128)(2,1)S(1)}) custom-call(f32[192,128]{1,0:T(8,128)S(1)} %get-tuple-element.40.refs_0_.refs_1_, bf16[3,3,3,32,40]{4,3,2,1,0:T(8,128)(2,1)S(1)} %bitcast.4), custom_call_target="tpu_custom_call" | custom-call | tf_op jit(solution)/shard_map/pallas_call | solution.py:593
  18.7 0.4 %collective-permute-done.6.refs_2_ = f32[192,128]{1,0:T(8,128)S(1)} collective-permute-done((f32[192,128]{1,0:T(8,128)S(1)}, f32[192,128]{1,0:T(8,128)S(1)}, u32[]{:S(2)}, u32[]{:S(2)}) %collective-permute-start.6) | collective-permute-done | bytes 98336 | tf_op jit(solution)/shard_map/ppermute | solution.py:663
  19.2 2.8 %collective-permute-start.10 = (bf16[192,128]{1,0:T(8,128)(2,1)S(1)}, bf16[192,128]{1,0:T(8,128)(2,1)S(1)}, u32[]{:S(2)}, u32[]{:S(2)}) collective-permute-start(bf16[192,128]{1,0:T(8,128)(2,1)S(1)} %shard_map.83.refs_0_.refs_2_), channel_id=1, source_target_pairs={{0,6},{1,7},{2,4},{3,5},{4,2},{5,3},{6,0},{7,1},{8,14},{9,15},{10,... | collective-permute-start | bytes 147464 | tf_op jit(solution)/shard_map/ppermute | solution.py:663
  22.0 1.4 %collective-permute-start.8 = (bf16[192,128]{1,0:T(8,128)(2,1)S(1)}, bf16[192,128]{1,0:T(8,128)(2,1)S(1)}, u32[]{:S(2)}, u32[]{:S(2)}) collective-permute-start(bf16[192,128]{1,0:T(8,128)(2,1)S(1)} %shard_map.83.refs_0_.refs_2_), channel_id=1, source_target_pairs={{0,2},{1,3},{2,0},{3,1},{4,6},{5,7},{6,4},{7,5},{8,10},{9,11},{10,... | collective-permute-start | bytes 147464 | tf_op jit(solution)/shard_map/ppermute | solution.py:663
  23.4 0.0 collective-permute-start.9
  23.4 1.5 %shard_map.84 = (f32[2,24,64,128]{3,2,1,0:T(8,128)S(1)}, f32[2,24,64,128]{3,2,1,0:T(8,128)S(1)}) custom-call(bf16[192,128]{1,0:T(8,128)(2,1)S(1)} %shard_map.83.refs_0_.refs_2_, bf16[13,2,64,768]{3,2,1,0:T(8,128)(2,1)S(1)} %get-tuple-element.43.refs_1_, bf16[1536,256]{1,0:T(8,128)(2,1)S(1)} %get-tuple-element.41.refs_0_.refs_2_), custom_call_target="tpu_custom_call" | custom-call | flops 230000000 | bytes 740000 | tf_op jit(solution)/shard_map/pallas_call | solution.py:593
  24.9 1.3 %shard_map.85 = (bf16[4,64,320]{2,1,0:T(8,128)(2,1)S(1)}, bf16[4,64,320]{2,1,0:T(8,128)(2,1)S(1)}, bf16[4,32,320]{2,1,0:T(8,128)(2,1)S(1)}) custom-call(f32[4,80,512]{2,1,0:T(8,128)S(1)} %get-tuple-element.37.refs_0_, f32[2,24,64,128]{3,2,1,0:T(8,128)S(1)} %get-tuple-element.44.refs_1_.refs_3_, f32[2,24,64,128]{3,2,1,0:T(8,128)S(1)} %get-tuple-element.45.refs_2_.refs_4_), custom_call_target="tpu_custom_call" | custom-call | flops 230000000 | bytes 740000 | tf_op jit(solution)/shard_map/pallas_call | solution.py:593
  26.2 0.1 collective-permute-start.11
  26.3 0.0 collective-permute-done.10.refs_5_
  26.3 0.0 collective-permute-done.8.refs_3_
  26.3 1.2 %collective-permute-done.9.refs_4_ = bf16[192,128]{1,0:T(8,128)(2,1)S(1)} collective-permute-done((bf16[192,128]{1,0:T(8,128)(2,1)S(1)}, bf16[192,128]{1,0:T(8,128)(2,1)S(1)}, u32[]{:S(2)}, u32[]{:S(2)}) %collective-permute-start.9) | collective-permute-done | bytes 49184 | tf_op jit(solution)/shard_map/ppermute | solution.py:663
  27.5 0.0 collective-permute-done.7.refs_1_.refs_2_.refs_3_
  27.6 2.7 %collective-permute-start.12 = (bf16[192,128]{1,0:T(8,128)(2,1)S(1)}, bf16[192,128]{1,0:T(8,128)(2,1)S(1)}, u32[]{:S(2)}, u32[]{:S(2)}) collective-permute-start(bf16[192,128]{1,0:T(8,128)(2,1)S(1)} %shard_map.86.refs_0_.refs_1_), channel_id=1, source_target_pairs={{0,8},{1,9},{2,10},{3,11},{4,12},{5,13},{6,14},{7,15},{8,0},{9,1},... | collective-permute-start | bytes 147464 | tf_op jit(solution)/shard_map/ppermute | solution.py:663
  30.2 1.3 %collective-permute-start.13 = (bf16[192,128]{1,0:T(8,128)(2,1)S(1)}, bf16[192,128]{1,0:T(8,128)(2,1)S(1)}, u32[]{:S(2)}, u32[]{:S(2)}) collective-permute-start(bf16[192,128]{1,0:T(8,128)(2,1)S(1)} %shard_map.86.refs_0_.refs_1_), channel_id=1, source_target_pairs={{0,16},{1,17},{2,18},{3,19},{4,20},{5,21},{6,22},{7,23},{8,24},{9,... | collective-permute-start | bytes 147464 | tf_op jit(solution)/shard_map/ppermute | solution.py:663
  31.5 0.5 %collective-permute-start.14 = (bf16[192,128]{1,0:T(8,128)(2,1)S(1)}, bf16[192,128]{1,0:T(8,128)(2,1)S(1)}, u32[]{:S(2)}, u32[]{:S(2)}) collective-permute-start(bf16[192,128]{1,0:T(8,128)(2,1)S(1)} %shard_map.86.refs_0_.refs_1_), channel_id=1, source_target_pairs={{0,24},{1,25},{2,26},{3,27},{4,28},{5,29},{6,30},{7,31},{8,16},{9,... | collective-permute-start | bytes 147464 | tf_op jit(solution)/shard_map/ppermute | solution.py:663
  32.0 0.0 collective-permute-done.11.refs_1_.refs_3_
  32.0 0.1 shard_map.87.refs_0_
  32.1 1.3 %collective-permute-start.16 = (bf16[4,64,320]{2,1,0:T(8,128)(2,1)S(1)}, bf16[4,64,320]{2,1,0:T(8,128)(2,1)S(1)}, u32[]{:S(2)}, u32[]{:S(2)}) collective-permute-start(bf16[4,64,320]{2,1,0:T(8,128)(2,1)S(1)} %shard_map.87.refs_0_), channel_id=1, source_target_pairs={{2,0},{3,1},{4,2},{5,3},{6,4},{7,5},{8,6},{9,7},{10,8},{11,9},{12,... | collective-permute-start | bytes 491528 | tf_op jit(solution)/shard_map/ppermute | solution.py:610
  33.4 3.0 %shard_map.88 = (bf16[24,4,32,64]{3,2,1,0:T(8,128)(2,1)}, f32[8,128]{1,0:T(8,128)S(1)}) custom-call(bf16[4,64,320]{2,1,0:T(8,128)(2,1)S(1)} %shard_map.87.refs_0_, f32[2,24,80,128]{3,2,1,0:T(8,128)S(1)} %get-tuple-element.38.refs_0_.refs_1_, bf16[960,128]{1,0:T(8,128)(2,1)S(1)} %collective-permute-done.7.refs_1_.refs_2_.refs_3_, ...), custom_call_target="tpu_custom_call" | custom-call | flops 3449999872 | bytes 11100000 | tf_op jit(solution)/shard_map/pallas_call | solution.py:593
  36.4 0.0 collective-permute-done.12.refs_2_
  36.4 0.0 collective-permute-done.13.refs_3_
  36.4 1.7 %collective-permute-done.14.refs_4_ = bf16[192,128]{1,0:T(8,128)(2,1)S(1)} collective-permute-done((bf16[192,128]{1,0:T(8,128)(2,1)S(1)}, bf16[192,128]{1,0:T(8,128)(2,1)S(1)}, u32[]{:S(2)}, u32[]{:S(2)}) %collective-permute-start.14) | collective-permute-done | bytes 49184 | tf_op jit(solution)/shard_map/ppermute | solution.py:663
  38.2 0.1 collective-permute-start.15
  38.2 1.2 %shard_map.90.refs_5_ = bf16[4,64,320]{2,1,0:T(8,128)(2,1)S(1)} custom-call(f32[192,128]{1,0:T(8,128)S(1)} %shard_map.89.refs_0_, f32[4,176,512]{2,1,0:T(8,128)S(1)} %get-tuple-element.53.refs_1_, f32[4,176,512]{2,1,0:T(8,128)S(1)} %get-tuple-element.54.refs_2_, f32[2,24,64,128]{3,2,1,0:T(8,128)S(1)} %get-tuple-element.44.refs_1_.refs_3_, ...), custom_call_target="tpu_custom_call" | custom-call | flops 2184999936 | bytes 7030000 | tf_op jit(solution)/shard_map/pallas_call | solution.py:593
  39.5 0.0 collective-permute-done.15.refs_1_
  39.5 0.2 collective-permute-done.16.refs_4_
  39.7 1.1 %shard_map.91 = (f32[3,3,3,32,40]{4,3,2,1,0:T(8,128)}, bf16[4,64,320]{2,1,0:T(8,128)(2,1)}, bf16[4,64,320]{2,1,0:T(8,128)(2,1)}) custom-call(f32[192,128]{1,0:T(8,128)S(1)} %shard_map.89.refs_0_, f32[192,128]{1,0:T(8,128)S(1)} %collective-permute-done.15.refs_1_, bf16[4,64,320]{2,1,0:T(8,128)(2,1)S(1)} %get-tuple-element.46.refs_0_.refs_2_, ...), custom_call_target="tpu_custom_call" | custom-call | flops 1150000000 | bytes 3700000 | tf_op jit(solution)/shard_map/pallas_call | solution.py:593
  (4 shorter events, 0.1 us)
Async XLA Ops:
  0.6 5.1 %copy-start = (bf16[4,64,320]{2,1,0:T(8,128)(2,1)S(1)}, bf16[4,64,320]{2,1,0:T(8,128)(2,1)}, u32[]{:S(2)}) copy-start(bf16[4,64,320]{2,1,0:T(8,128)(2,1)} %refs_2_.3) | copy-start | bytes 491524
  0.6 5.1 %copy-start.3 = (bf16[24,4,64,32]{2,3,1,0:T(8,128)(2,1)S(1)}, bf16[24,4,64,32]{2,3,1,0:T(8,128)(2,1)}, u32[]{:S(2)}) copy-start(bf16[24,4,64,32]{2,3,1,0:T(8,128)(2,1)} %param.7) | copy-start | bytes 1179652
  0.7 5.1 %copy-start.2 = (bf16[4,64,320]{2,1,0:T(8,128)(2,1)S(1)}, bf16[4,64,320]{2,1,0:T(8,128)(2,1)}, u32[]{:S(2)}) copy-start(bf16[4,64,320]{2,1,0:T(8,128)(2,1)} %refs_1_.5) | copy-start | bytes 491524
  0.7 9.5 %collective-permute-start = (bf16[4,64,320]{2,1,0:T(8,128)(2,1)}, bf16[4,64,320]{2,1,0:T(8,128)(2,1)S(1)}, u32[]{:S(2)}, u32[]{:S(2)}) collective-permute-start(bf16[4,64,320]{2,1,0:T(8,128)(2,1)} %refs_2_.3), channel_id=1, source_target_pairs={{0,2},{1,3},{2,4},{3,5},{4,6},{5,7},{6,8},{7,9},{8,10},{9,11},{10,... | collective-permute-start | bytes 491528 | tf_op jit(solution)/shard_map/ppermute | solution.py:610
  6.1 5.6 %collective-permute-start.2 = (bf16[32,320]{1,0:T(8,128)(2,1)S(1)}, bf16[32,320]{1,0:T(8,128)(2,1)S(1)}, u32[]{:S(2)}, u32[]{:S(2)}) collective-permute-start(bf16[32,320]{1,0:T(8,128)(2,1)S(1)} %get-tuple-element.32), channel_id=1, source_target_pairs={{0,1},{1,0},{2,3},{3,2},{4,5},{5,4},{6,7},{7,6},{8,9},{9,8},{10,11... | collective-permute-start | bytes 61448 | tf_op jit(solution)/shard_map/ppermute | solution.py:663
  6.1 5.5 %collective-permute-start.3 = (bf16[32,320]{1,0:T(8,128)(2,1)S(1)}, bf16[32,320]{1,0:T(8,128)(2,1)S(1)}, u32[]{:S(2)}, u32[]{:S(2)}) collective-permute-start(bf16[32,320]{1,0:T(8,128)(2,1)S(1)} %get-tuple-element.33), channel_id=1, source_target_pairs={{1,2},{3,4},{5,6},{7,8},{9,10},{11,12},{13,14},{2,1},{4,3},{6,5},{... | collective-permute-start | bytes 61448 | tf_op jit(solution)/shard_map/ppermute | solution.py:684
  6.8 9.1 %collective-permute-start.4 = (bf16[6,64,128]{2,1,0:T(8,128)(2,1)S(1)}, bf16[6,64,128]{2,1,0:T(8,128)(2,1)S(1)}, u32[]{:S(2)}, u32[]{:S(2)}) collective-permute-start(bf16[6,64,128]{2,1,0:T(8,128)(2,1)S(1)} %get-tuple-element.39), channel_id=1, source_target_pairs={{0,16},{16,0},{1,17},{17,1},{2,18},{18,2},{3,19},{19,3},{4,20},{20... | collective-permute-start | bytes 294920 | tf_op jit(solution)/shard_map/ppermute | solution.py:621
  10.2 2.3 %collective-permute-start.1 = (bf16[4,64,320]{2,1,0:T(8,128)(2,1)S(1)}, bf16[4,64,320]{2,1,0:T(8,128)(2,1)S(1)}, u32[]{:S(2)}, u32[]{:S(2)}) collective-permute-start(bf16[4,64,320]{2,1,0:T(8,128)(2,1)S(1)} %shard_map.77.refs_0_), channel_id=1, source_target_pairs={{0,1},{1,0},{2,3},{3,2},{4,5},{5,4},{6,7},{7,6},{8,9},{9,8},{10,11... | collective-permute-start | bytes 491528 | tf_op jit(solution)/shard_map/ppermute | solution.py:663
  11.8 4.1 %collective-permute-start.5 = (bf16[16,128]{1,0:T(8,128)(2,1)S(1)}, bf16[16,128]{1,0:T(8,128)(2,1)S(1)}, u32[]{:S(2)}, u32[]{:S(2)}) collective-permute-start(bf16[16,128]{1,0:T(8,128)(2,1)S(1)} %shard_map.80), channel_id=1, source_target_pairs={{0,16},{16,0},{1,17},{17,1},{2,18},{18,2},{3,19},{19,3},{4,20},{20... | collective-permute-start | bytes 12296 | tf_op jit(solution)/shard_map/ppermute | solution.py:621
  14.4 13.1 %collective-permute-start.7 = (bf16[960,128]{1,0:T(8,128)(2,1)S(1)}, bf16[960,128]{1,0:T(8,128)(2,1)S(1)}, u32[]{:S(2)}, u32[]{:S(2)}) collective-permute-start(bf16[960,128]{1,0:T(8,128)(2,1)S(1)} %get-tuple-element.47), channel_id=1, source_target_pairs={{0,16},{16,0},{1,17},{17,1},{2,18},{18,2},{3,19},{19,3},{4,20},{20... | collective-permute-start | bytes 737288 | tf_op jit(solution)/shard_map/ppermute | solution.py:621
  15.9 2.0 %copy-start.1 = (bf16[3,3,3,40,32]{3,4,2,1,0:T(8,128)(2,1)S(1)}, bf16[3,3,3,40,32]{3,4,2,1,0:T(8,128)(2,1)}, u32[]{:S(2)}) copy-start(bf16[3,3,3,40,32]{3,4,2,1,0:T(8,128)(2,1)} %param.6) | copy-start | bytes 207364
  17.8 1.4 %collective-permute-start.6 = (f32[192,128]{1,0:T(8,128)S(1)}, f32[192,128]{1,0:T(8,128)S(1)}, u32[]{:S(2)}, u32[]{:S(2)}) collective-permute-start(f32[192,128]{1,0:T(8,128)S(1)} %get-tuple-element.42), channel_id=1, source_target_pairs={{0,1},{1,0},{2,3},{3,2},{4,5},{5,4},{6,7},{7,6},{8,9},{9,8},{10,11... | collective-permute-start | bytes 294920 | tf_op jit(solution)/shard_map/ppermute | solution.py:663
  19.2 7.1 %collective-permute-start.10 = (bf16[192,128]{1,0:T(8,128)(2,1)S(1)}, bf16[192,128]{1,0:T(8,128)(2,1)S(1)}, u32[]{:S(2)}, u32[]{:S(2)}) collective-permute-start(bf16[192,128]{1,0:T(8,128)(2,1)S(1)} %shard_map.83.refs_0_.refs_2_), channel_id=1, source_target_pairs={{0,6},{1,7},{2,4},{3,5},{4,2},{5,3},{6,0},{7,1},{8,14},{9,15},{10,... | collective-permute-start | bytes 147464 | tf_op jit(solution)/shard_map/ppermute | solution.py:663
  22.0 4.3 %collective-permute-start.8 = (bf16[192,128]{1,0:T(8,128)(2,1)S(1)}, bf16[192,128]{1,0:T(8,128)(2,1)S(1)}, u32[]{:S(2)}, u32[]{:S(2)}) collective-permute-start(bf16[192,128]{1,0:T(8,128)(2,1)S(1)} %shard_map.83.refs_0_.refs_2_), channel_id=1, source_target_pairs={{0,2},{1,3},{2,0},{3,1},{4,6},{5,7},{6,4},{7,5},{8,10},{9,11},{10,... | collective-permute-start | bytes 147464 | tf_op jit(solution)/shard_map/ppermute | solution.py:663
  23.4 4.1 %collective-permute-start.9 = (bf16[192,128]{1,0:T(8,128)(2,1)S(1)}, bf16[192,128]{1,0:T(8,128)(2,1)S(1)}, u32[]{:S(2)}, u32[]{:S(2)}) collective-permute-start(bf16[192,128]{1,0:T(8,128)(2,1)S(1)} %shard_map.83.refs_0_.refs_2_), channel_id=1, source_target_pairs={{0,4},{1,5},{2,6},{3,7},{4,0},{5,1},{6,2},{7,3},{8,12},{9,13},{10,... | collective-permute-start | bytes 147464 | tf_op jit(solution)/shard_map/ppermute | solution.py:663
  26.2 5.8 %collective-permute-start.11 = (bf16[4,64,320]{2,1,0:T(8,128)(2,1)S(1)}, bf16[4,64,320]{2,1,0:T(8,128)(2,1)S(1)}, u32[]{:S(2)}, u32[]{:S(2)}) collective-permute-start(bf16[4,64,320]{2,1,0:T(8,128)(2,1)S(1)} %get-tuple-element.48), channel_id=1, source_target_pairs={{0,1},{1,0},{2,3},{3,2},{4,5},{5,4},{6,7},{7,6},{8,9},{9,8},{10,11... | collective-permute-start | bytes 491528 | tf_op jit(solution)/shard_map/ppermute | solution.py:663
  27.6 8.8 %collective-permute-start.12 = (bf16[192,128]{1,0:T(8,128)(2,1)S(1)}, bf16[192,128]{1,0:T(8,128)(2,1)S(1)}, u32[]{:S(2)}, u32[]{:S(2)}) collective-permute-start(bf16[192,128]{1,0:T(8,128)(2,1)S(1)} %shard_map.86.refs_0_.refs_1_), channel_id=1, source_target_pairs={{0,8},{1,9},{2,10},{3,11},{4,12},{5,13},{6,14},{7,15},{8,0},{9,1},... | collective-permute-start | bytes 147464 | tf_op jit(solution)/shard_map/ppermute | solution.py:663
  30.2 6.2 %collective-permute-start.13 = (bf16[192,128]{1,0:T(8,128)(2,1)S(1)}, bf16[192,128]{1,0:T(8,128)(2,1)S(1)}, u32[]{:S(2)}, u32[]{:S(2)}) collective-permute-start(bf16[192,128]{1,0:T(8,128)(2,1)S(1)} %shard_map.86.refs_0_.refs_1_), channel_id=1, source_target_pairs={{0,16},{1,17},{2,18},{3,19},{4,20},{5,21},{6,22},{7,23},{8,24},{9,... | collective-permute-start | bytes 147464 | tf_op jit(solution)/shard_map/ppermute | solution.py:663
  31.5 6.6 %collective-permute-start.14 = (bf16[192,128]{1,0:T(8,128)(2,1)S(1)}, bf16[192,128]{1,0:T(8,128)(2,1)S(1)}, u32[]{:S(2)}, u32[]{:S(2)}) collective-permute-start(bf16[192,128]{1,0:T(8,128)(2,1)S(1)} %shard_map.86.refs_0_.refs_1_), channel_id=1, source_target_pairs={{0,24},{1,25},{2,26},{3,27},{4,28},{5,29},{6,30},{7,31},{8,16},{9,... | collective-permute-start | bytes 147464 | tf_op jit(solution)/shard_map/ppermute | solution.py:663
  32.1 7.6 %collective-permute-start.16 = (bf16[4,64,320]{2,1,0:T(8,128)(2,1)S(1)}, bf16[4,64,320]{2,1,0:T(8,128)(2,1)S(1)}, u32[]{:S(2)}, u32[]{:S(2)}) collective-permute-start(bf16[4,64,320]{2,1,0:T(8,128)(2,1)S(1)} %shard_map.87.refs_0_), channel_id=1, source_target_pairs={{2,0},{3,1},{4,2},{5,3},{6,4},{7,5},{8,6},{9,7},{10,8},{11,9},{12,... | collective-permute-start | bytes 491528 | tf_op jit(solution)/shard_map/ppermute | solution.py:610
  38.2 1.4 %collective-permute-start.15 = (f32[192,128]{1,0:T(8,128)S(1)}, f32[192,128]{1,0:T(8,128)S(1)}, u32[]{:S(2)}, u32[]{:S(2)}) collective-permute-start(f32[192,128]{1,0:T(8,128)S(1)} %shard_map.89.refs_0_), channel_id=1, source_target_pairs={{0,1},{1,0},{2,3},{3,2},{4,5},{5,4},{6,7},{7,6},{8,9},{9,8},{10,11... | collective-permute-start | bytes 294920 | tf_op jit(solution)/shard_map/ppermute | solution.py:663

commit v5 on v4

--- a/solution.py
+++ b/solution.py
@@ -308,8 +308,11 @@
     give_out[...] = jnp.where(is_even, high, low)
 
 
-def dgrad_kernel(ctsh, w2, *grads):
-    _, disp, cols, _ = grads[0].shape
+def right_kernel(ctsh, w2, fl, *rest):
+    *grads, rg0, rg1, rg2, acce, acco, both = rest
+    rows, cols, channels = rg0.shape
+    disp, wide = grads[0].shape[1], fl.shape[2]
+    group_size = wide // SLOT
     step = disp // 4
     low = lanes((step * cols, 128)) < SLOT
 
@@ -329,17 +332,6 @@
                 for j in range(step):
                     gv[hh, 2 * (q * step + j) + o] = y[j * cols : (j + 1) * cols]
 
-    for q in range(2):
-        for p, gv in enumerate(grads):
-            conv(q, p, gv)
-
-
-def right_kernel(fl, *rest):
-    *grads, rg0, rg1, rg2, acce, acco, both = rest
-    disp = grads[0].shape[1]
-    rows, cols, channels = rg0.shape
-    wide = fl.shape[2]
-    group_size = wide // SLOT
     count = cols // 8
     back = acce.shape[1] - cols
     lead = back // 8
@@ -369,7 +361,11 @@
         acco[h, 8 * (lead + count) :] = jnp.zeros((8, wide), F32)
 
     for p, gv in enumerate(grads):
-        pl.loop(0, 2)(functools.partial(right_row, gv, p))
+        for q in range(2):
+            conv(q, p, gv)
+    for p, gv in enumerate(grads):
+        for hh in range(2):
+            right_row(gv, p, hh)
     size = back + cols
     for h in range(rows):
         both[h * size : (h + 1) * size] = (acce[h] + acco[h, STEP : STEP + size]).astype(BF16)
@@ -623,13 +619,11 @@
     return row_shift(pays[0], 1), row_shift(pays[1], -1)
 
 
-def stages(n_row, n_col):
+def partners(n_row, n_col):
     col_bits = [1 << i for i in range(1, n_col.bit_length() - 1)]
     row_bits = [n_col << i for i in range(n_row.bit_length() - 1)]
     assert n_col == 2 << len(col_bits) and n_row == 1 << len(row_bits)
-    bits = col_bits + row_bits
-    pairs = [bits[i : i + 2] for i in range(0, len(bits), 2)]
-    return [pair + [sum(pair)] if len(pair) == 2 else pair for pair in pairs]
+    return [*col_bits[:2], sum(col_bits[:2])], col_bits[2:], row_bits
 
 
 def on_device(left_features, right_features, conv_weight, cotangent):
@@ -747,12 +741,10 @@
         after=[keep],
     )
     (part,) = call(sum_kernel, [(keep.shape, BF16)], [], keep, got, after=[w2])
-    grads = call(
-        dgrad_kernel, [((2, disp, cols, 128), F32)] * (rows // 2), [], ctsh, w2, after=[part], us=0.2
-    )
-    rg0, rg1, rg2 = call(
+    *grads, rg0, rg1, rg2 = call(
         right_kernel,
-        [
+        [((2, disp, cols, 128), F32)] * (rows // 2)
+        + [
             ((rows, cols, channels), BF16),
             ((rows, cols, channels), BF16),
             ((rows, cols // 2, channels), BF16),
@@ -762,20 +754,25 @@
             pltpu.VMEM((rows, cols + cols + cols // 2 + 8, wide), F32),
             pltpu.VMEM((rows * (cols + cols + cols // 2), wide), BF16),
         ],
-        fl, *grads,
-        us=0.2,
+        ctsh, w2, fl,
+        after=[part],
+        us=0.4,
     )
     rg1 = swap(rg1, 1)
-    *middle, final = stages(n_row, n_col)
-    order = [rg0, vtop]
-    for stage in middle:
-        parts = [part] + [swap(part, m) for m in stage]
-        (part,) = call(sum_kernel, [(part.shape, BF16)], [], *parts, after=order, us=4.0)
-        order = []
-    parts = [part] + [swap(part, m) for m in final]
+    def join(part, mask, kind, after, us):
+        terms = (part, swap(part, mask))
+        return call(sum_kernel, [(part.shape, kind)], [], *terms, after=after, us=us)[0]
+
+    three, along_cols, along_rows = partners(n_row, n_col)
+    parts = [part] + [swap(part, m) for m in three]
+    (part,) = call(sum_kernel, [(part.shape, BF16)], [], *parts, after=[rg0, vtop], us=4.0)
     (rg2,) = call(
         combine_kernel, [((rows, cols, channels), BF16)], [], rg1, rg2, after=[part]
     )
+    order = [rg2]
+    for mask in along_cols:
+        part = join(part, mask, F32, after=order, us=4.0)
+        order = []
     output, conv_done = call(
         functools.partial(conv_kernel, masks, groups),
         [((disp, rows, feat, cols), BF16)],
@@ -786,12 +783,15 @@
             pltpu.SemaphoreType.DMA((3,)),
         ],
         vbuf, vtop, vbot, wc,
-        after=[rg2],
+        after=[part],
         token=True,
         us=3.0,
         hbm=[0],
     )
-    (part,) = call(sum_kernel, [(part.shape, F32)], [], *parts, after=[conv_done], us=4.0)
+    order = [conv_done]
+    for mask in along_rows:
+        part = join(part, mask, F32, after=order, us=4.0)
+        order = []
     (lg,) = call(
         left_kernel,
         [((rows, cols, channels), BF16)],

time: 41 us -> 40.6 us (level)
    ppermute x11 -> x10, starting transfers between devices: 9.91 us -> 9.46 us  [swap(): return lax.ppermute(block, ('row', 'col'), route)]
    ppermute x11 -> x10, waiting for transfers between devices: 3.42 us -> 3.86 us  [swap(): return lax.ppermute(block, ('row', 'col'), route)]
  transfers between devices with their start and end apart: 17 -> 16, of which waited for: 5 -> 6; matrix products, arithmetic and copies ran while one was open for 0% -> 0% of each run, Pallas kernels for 32% -> 31%
where the time goes in v5:
time: 40.6 us; the launch traced here: 40.3 us
  starting transfers between devices  20.1 us (50%)
  Pallas kernels  13.7 us (34%)
  waiting for transfers between devices  5.64 us (14%)
  between operations  0.88 us (2%)
    pallas_call x17, Pallas kernels, call(): pl.pallas_call(lambda *refs: kernel(*refs[skip:]), out_shape=[jax.ShapeDt...  13.7 us
    ppermute x10, starting transfers between devices, swap(): return lax.ppermute(block, ('row', 'col'), route)  9.46 us
    ppermute x2, starting transfers between devices, col_shift(): return lax.ppermute(block, 'col', route)  6.31 us
    ppermute x10, waiting for transfers between devices, swap(): return lax.ppermute(block, ('row', 'col'), route)  3.86 us
    ppermute x3, starting transfers between devices, halos(): got = lax.ppermute(pays[0], 'row', [(0, 1), (1, 0)])  3.66 us
    ppermute x2, waiting for transfers between devices, col_shift(): return lax.ppermute(block, 'col', route)  1.77 us
  transfers between devices with their start and end apart: 16, of which 6 were waited for; matrix products, arithmetic and copies ran while one was open for 0% of the time, Pallas kernels for 31%

profile of v5, /device:TPU:0, one launch (start us, length us, event | category | flops | bytes accessed | tf_op | source)
XLA Modules:
  0.0 40.3 jit_solution(11525350786025282098)
XLA Ops:
  0.6 0.0 copy-start
  0.6 0.0 copy-start.3
  0.7 0.0 copy-start.2
  0.7 5.0 %collective-permute-start = (bf16[4,64,320]{2,1,0:T(8,128)(2,1)}, bf16[4,64,320]{2,1,0:T(8,128)(2,1)S(1)}, u32[]{:S(2)}, u32[]{:S(2)}) collective-permute-start(bf16[4,64,320]{2,1,0:T(8,128)(2,1)} %refs_2_.3), channel_id=1, source_target_pairs={{0,2},{1,3},{2,4},{3,5},{4,6},{5,7},{6,8},{7,9},{8,10},{9,11},{10,... | collective-permute-start | bytes 491528 | tf_op jit(solution)/shard_map/ppermute | solution.py:606
  5.7 0.0 copy-done
  5.7 0.0 copy-done.3
  5.7 0.0 copy-done.2
  5.7 0.3 shard_map.76
  6.1 0.1 collective-permute-start.2
  6.1 0.7 %collective-permute-start.3 = (bf16[32,320]{1,0:T(8,128)(2,1)S(1)}, bf16[32,320]{1,0:T(8,128)(2,1)S(1)}, u32[]{:S(2)}, u32[]{:S(2)}) collective-permute-start(bf16[32,320]{1,0:T(8,128)(2,1)S(1)} %get-tuple-element.33), channel_id=1, source_target_pairs={{1,2},{3,4},{5,6},{7,8},{9,10},{11,12},{13,14},{2,1},{4,3},{6,5},{... | collective-permute-start | bytes 61448 | tf_op jit(solution)/shard_map/ppermute | solution.py:678
  6.8 1.6 %collective-permute-start.4 = (bf16[6,64,128]{2,1,0:T(8,128)(2,1)S(1)}, bf16[6,64,128]{2,1,0:T(8,128)(2,1)S(1)}, u32[]{:S(2)}, u32[]{:S(2)}) collective-permute-start(bf16[6,64,128]{2,1,0:T(8,128)(2,1)S(1)} %get-tuple-element.38), channel_id=1, source_target_pairs={{0,16},{16,0},{1,17},{17,1},{2,18},{18,2},{3,19},{19,3},{4,20},{20... | collective-permute-start | bytes 294920 | tf_op jit(solution)/shard_map/ppermute | solution.py:617
  8.4 1.8 %collective-permute-done.refs_2_.refs_3_ = bf16[4,64,320]{2,1,0:T(8,128)(2,1)S(1)} collective-permute-done((bf16[4,64,320]{2,1,0:T(8,128)(2,1)}, bf16[4,64,320]{2,1,0:T(8,128)(2,1)S(1)}, u32[]{:S(2)}, u32[]{:S(2)}) %collective-permute-start) | collective-permute-done | bytes 163872 | tf_op jit(solution)/shard_map/ppermute | solution.py:606
  10.1 0.1 shard_map.77.refs_0_
  10.2 0.9 %collective-permute-start.1 = (bf16[4,64,320]{2,1,0:T(8,128)(2,1)S(1)}, bf16[4,64,320]{2,1,0:T(8,128)(2,1)S(1)}, u32[]{:S(2)}, u32[]{:S(2)}) collective-permute-start(bf16[4,64,320]{2,1,0:T(8,128)(2,1)S(1)} %shard_map.77.refs_0_), channel_id=1, source_target_pairs={{0,1},{1,0},{2,3},{3,2},{4,5},{5,4},{6,7},{7,6},{8,9},{9,8},{10,11... | collective-permute-start | bytes 491528 | tf_op jit(solution)/shard_map/ppermute | solution.py:657
  11.1 0.5 %shard_map.78 = (f32[4,80,512]{2,1,0:T(8,128)S(1)}, f32[4,176,512]{2,1,0:T(8,128)S(1)}, f32[4,176,512]{2,1,0:T(8,128)S(1)}) custom-call(bf16[4,64,320]{2,1,0:T(8,128)(2,1)S(1)} %shard_map.77.refs_0_, bf16[4,64,320]{2,1,0:T(8,128)(2,1)S(1)} %copy-done.2, bf16[4,64,320]{2,1,0:T(8,128)(2,1)S(1)} %copy-done, ...), custom_call_target="tpu_custom_call" | custom-call | tf_op jit(solution)/shard_map/pallas_call | solution.py:589
  11.6 0.0 collective-permute-done.2.refs_1_.refs_2_
  11.6 0.0 collective-permute-done.3.refs_2_.refs_3_
  11.7 0.1 shard_map.80
  11.8 0.7 %collective-permute-start.5 = (bf16[16,128]{1,0:T(8,128)(2,1)S(1)}, bf16[16,128]{1,0:T(8,128)(2,1)S(1)}, u32[]{:S(2)}, u32[]{:S(2)}) collective-permute-start(bf16[16,128]{1,0:T(8,128)(2,1)S(1)} %shard_map.80), channel_id=1, source_target_pairs={{0,16},{16,0},{1,17},{17,1},{2,18},{18,2},{3,19},{19,3},{4,20},{20... | collective-permute-start | bytes 12296 | tf_op jit(solution)/shard_map/ppermute | solution.py:617
  12.4 0.0 collective-permute-done.1.refs_0_
  12.4 2.0 %shard_map.79 = (f32[4,80,512]{2,1,0:T(8,128)S(1)}, f32[4,176,512]{2,1,0:T(8,128)S(1)}, f32[4,176,512]{2,1,0:T(8,128)S(1)}, f32[2,24,80,128]{3,2,1,0:T(8,128)S(1)}, bf16[960,128]{1,0:T(8,128)(2,1)S(1)}) custom-call(bf16[4,64,320]{2,1,0:T(8,128)(2,1)S(1)} %collective-permute-done.1.refs_0_, ...), custom_call_target="tpu_custom_call", output_to_operand_aliasing={{0}: (3, {}), {1}: (4, {}), {2}: (5, {})} | custom-call | flops 2070000000 | bytes 6660000 | tf_op jit(solution)/shard_map/pallas_call | solution.py:589
  14.4 1.4 %collective-permute-start.7 = (bf16[960,128]{1,0:T(8,128)(2,1)S(1)}, bf16[960,128]{1,0:T(8,128)(2,1)S(1)}, u32[]{:S(2)}, u32[]{:S(2)}) collective-permute-start(bf16[960,128]{1,0:T(8,128)(2,1)S(1)} %get-tuple-element.45), channel_id=1, source_target_pairs={{0,16},{16,0},{1,17},{17,1},{2,18},{18,2},{3,19},{19,3},{4,20},{20... | collective-permute-start | bytes 737288 | tf_op jit(solution)/shard_map/ppermute | solution.py:617
  15.9 0.0 collective-permute-done.4.refs_4_.refs_5_
  15.9 0.0 collective-permute-done.5.refs_6_.refs_7_
  15.9 0.0 copy-start.1
  15.9 1.9 %shard_map.81 = (f32[192,128]{1,0:T(8,128)S(1)}, f32[192,128]{1,0:T(8,128)S(1)}, bf16[13,2,64,768]{3,2,1,0:T(8,128)(2,1)S(1)}) custom-call(f32[2,24,80,128]{3,2,1,0:T(8,128)S(1)} %get-tuple-element.37.refs_0_.refs_1_, bf16[24,64,128]{2,1,0:T(8,128)(2,1)S(1)} %get-tuple-element.31.refs_0_.refs_1_, bf16[32,320]{1,0:T(8,128)(2,1)S(1)} %collective-permute-done.2.refs_1_.refs_2_, ...), custom_call_target="tpu_custom_call" | custom-call | flops 2300000000 | bytes 7400000 | tf_op jit(solution)/shard_map/pallas_call | solution.py:589
  17.8 0.1 collective-permute-start.6
  17.9 0.0 copy-done.1
  17.9 0.8 %shard_map.82 = (bf16[1536,256]{1,0:T(8,128)(2,1)S(1)}, bf16[3072,256]{1,0:T(8,128)(2,1)S(1)}) custom-call(f32[192,128]{1,0:T(8,128)S(1)} %get-tuple-element.39.refs_0_.refs_1_, bf16[3,3,3,32,40]{4,3,2,1,0:T(8,128)(2,1)S(1)} %bitcast.4), custom_call_target="tpu_custom_call" | custom-call | tf_op jit(solution)/shard_map/pallas_call | solution.py:589
  18.7 0.4 %collective-permute-done.6.refs_2_ = f32[192,128]{1,0:T(8,128)S(1)} collective-permute-done((f32[192,128]{1,0:T(8,128)S(1)}, f32[192,128]{1,0:T(8,128)S(1)}, u32[]{:S(2)}, u32[]{:S(2)}) %collective-permute-start.6) | collective-permute-done | bytes 98336 | tf_op jit(solution)/shard_map/ppermute | solution.py:657
  19.2 2.8 %collective-permute-start.10 = (bf16[192,128]{1,0:T(8,128)(2,1)S(1)}, bf16[192,128]{1,0:T(8,128)(2,1)S(1)}, u32[]{:S(2)}, u32[]{:S(2)}) collective-permute-start(bf16[192,128]{1,0:T(8,128)(2,1)S(1)} %shard_map.83.refs_0_.refs_2_), channel_id=1, source_target_pairs={{0,6},{1,7},{2,4},{3,5},{4,2},{5,3},{6,0},{7,1},{8,14},{9,15},{10,... | collective-permute-start | bytes 147464 | tf_op jit(solution)/shard_map/ppermute | solution.py:657
  22.0 1.4 %collective-permute-start.8 = (bf16[192,128]{1,0:T(8,128)(2,1)S(1)}, bf16[192,128]{1,0:T(8,128)(2,1)S(1)}, u32[]{:S(2)}, u32[]{:S(2)}) collective-permute-start(bf16[192,128]{1,0:T(8,128)(2,1)S(1)} %shard_map.83.refs_0_.refs_2_), channel_id=1, source_target_pairs={{0,2},{1,3},{2,0},{3,1},{4,6},{5,7},{6,4},{7,5},{8,10},{9,11},{10,... | collective-permute-start | bytes 147464 | tf_op jit(solution)/shard_map/ppermute | solution.py:657
  23.4 0.0 collective-permute-start.9
  23.4 2.4 %shard_map.84 = (f32[2,24,64,128]{3,2,1,0:T(8,128)S(1)}, f32[2,24,64,128]{3,2,1,0:T(8,128)S(1)}, bf16[4,64,320]{2,1,0:T(8,128)(2,1)S(1)}, bf16[4,64,320]{2,1,0:T(8,128)(2,1)S(1)}, bf16[4,32,320]{2,1,0:T(8,128)(2,1)S(1)}) custom-call(bf16[192,128]{1,0:T(8,128)(2,1)S(1)} %shard_map.83.refs_0_.refs_2_, bf16[13,2,64,768]{3,2,1,0:T(8,128)(2,1)S(1)} %get-tuple-element.42.refs_1_, ...), custom_call_target="tpu_custom_call" | custom-call | flops 460000000 | bytes 1480000 | tf_op jit(solution)/shard_map/pallas_call | solution.py:589
  25.9 0.1 collective-permute-start.11
  26.0 0.0 collective-permute-done.10.refs_5_
  26.0 0.1 collective-permute-done.8.refs_3_
  26.1 1.4 %collective-permute-done.9.refs_4_ = bf16[192,128]{1,0:T(8,128)(2,1)S(1)} collective-permute-done((bf16[192,128]{1,0:T(8,128)(2,1)S(1)}, bf16[192,128]{1,0:T(8,128)(2,1)S(1)}, u32[]{:S(2)}, u32[]{:S(2)}) %collective-permute-start.9) | collective-permute-done | bytes 49184 | tf_op jit(solution)/shard_map/ppermute | solution.py:657
  27.5 0.0 collective-permute-done.7.refs_1_.refs_2_.refs_3_
  27.6 2.7 %collective-permute-start.12 = (bf16[192,128]{1,0:T(8,128)(2,1)S(1)}, bf16[192,128]{1,0:T(8,128)(2,1)S(1)}, u32[]{:S(2)}, u32[]{:S(2)}) collective-permute-start(bf16[192,128]{1,0:T(8,128)(2,1)S(1)} %shard_map.85.refs_0_.refs_1_), channel_id=1, source_target_pairs={{0,8},{1,9},{2,10},{3,11},{4,12},{5,13},{6,14},{7,15},{8,0},{9,1},... | collective-permute-start | bytes 147464 | tf_op jit(solution)/shard_map/ppermute | solution.py:657
  30.2 0.0 collective-permute-done.11.refs_1_.refs_3_
  30.2 0.1 shard_map.86.refs_0_
  30.3 1.3 %collective-permute-start.15 = (bf16[4,64,320]{2,1,0:T(8,128)(2,1)S(1)}, bf16[4,64,320]{2,1,0:T(8,128)(2,1)S(1)}, u32[]{:S(2)}, u32[]{:S(2)}) collective-permute-start(bf16[4,64,320]{2,1,0:T(8,128)(2,1)S(1)} %shard_map.86.refs_0_), channel_id=1, source_target_pairs={{2,0},{3,1},{4,2},{5,3},{6,4},{7,5},{8,6},{9,7},{10,8},{11,9},{12,... | collective-permute-start | bytes 491528 | tf_op jit(solution)/shard_map/ppermute | solution.py:606
  31.6 1.5 %collective-permute-done.12.refs_2_ = bf16[192,128]{1,0:T(8,128)(2,1)S(1)} collective-permute-done((bf16[192,128]{1,0:T(8,128)(2,1)S(1)}, bf16[192,128]{1,0:T(8,128)(2,1)S(1)}, u32[]{:S(2)}, u32[]{:S(2)}) %collective-permute-start.12) | collective-permute-done | bytes 49184 | tf_op jit(solution)/shard_map/ppermute | solution.py:657
  33.1 1.3 %collective-permute-start.13 = (f32[192,128]{1,0:T(8,128)S(1)}, f32[192,128]{1,0:T(8,128)S(1)}, u32[]{:S(2)}, u32[]{:S(2)}) collective-permute-start(f32[192,128]{1,0:T(8,128)S(1)} %shard_map.87.refs_0_.refs_1_), channel_id=1, source_target_pairs={{0,16},{1,17},{2,18},{3,19},{4,20},{5,21},{6,22},{7,23},{8,24},{9,... | collective-permute-start | bytes 294920 | tf_op jit(solution)/shard_map/ppermute | solution.py:657
  34.5 3.0 %shard_map.88 = (bf16[24,4,32,64]{3,2,1,0:T(8,128)(2,1)}, f32[8,128]{1,0:T(8,128)S(1)}) custom-call(f32[192,128]{1,0:T(8,128)S(1)} %shard_map.87.refs_0_.refs_1_, f32[2,24,80,128]{3,2,1,0:T(8,128)S(1)} %get-tuple-element.37.refs_0_.refs_1_, bf16[960,128]{1,0:T(8,128)(2,1)S(1)} %collective-permute-done.7.refs_1_.refs_2_.refs_3_, ...), custom_call_target="tpu_custom_call" | custom-call | flops 3449999872 | bytes 11100000 | tf_op jit(solution)/shard_map/pallas_call | solution.py:589
  37.5 0.3 collective-permute-done.13.refs_2_
  37.8 0.1 collective-permute-start.14
  37.9 1.3 %shard_map.90.refs_5_ = bf16[4,64,320]{2,1,0:T(8,128)(2,1)S(1)} custom-call(f32[192,128]{1,0:T(8,128)S(1)} %shard_map.89.refs_0_, f32[4,176,512]{2,1,0:T(8,128)S(1)} %get-tuple-element.51.refs_1_, f32[4,176,512]{2,1,0:T(8,128)S(1)} %get-tuple-element.52.refs_2_, f32[2,24,64,128]{3,2,1,0:T(8,128)S(1)} %get-tuple-element.53.refs_3_, ...), custom_call_target="tpu_custom_call" | custom-call | flops 2184999936 | bytes 7030000 | tf_op jit(solution)/shard_map/pallas_call | solution.py:589
  39.2 0.0 collective-permute-done.15.refs_4_
  39.2 0.0 collective-permute-done.14.refs_1_
  39.2 1.1 %shard_map.91 = (f32[3,3,3,32,40]{4,3,2,1,0:T(8,128)}, bf16[4,64,320]{2,1,0:T(8,128)(2,1)}, bf16[4,64,320]{2,1,0:T(8,128)(2,1)}) custom-call(f32[192,128]{1,0:T(8,128)S(1)} %shard_map.89.refs_0_, f32[192,128]{1,0:T(8,128)S(1)} %collective-permute-done.14.refs_1_, bf16[4,64,320]{2,1,0:T(8,128)(2,1)S(1)} %get-tuple-element.44.refs_0_.refs_2_, ...), custom_call_target="tpu_custom_call" | custom-call | flops 1150000000 | bytes 3700000 | tf_op jit(solution)/shard_map/pallas_call | solution.py:589
  (5 shorter events, 0.1 us)
Async XLA Ops:
  0.6 5.1 %copy-start = (bf16[4,64,320]{2,1,0:T(8,128)(2,1)S(1)}, bf16[4,64,320]{2,1,0:T(8,128)(2,1)}, u32[]{:S(2)}) copy-start(bf16[4,64,320]{2,1,0:T(8,128)(2,1)} %refs_2_.3) | copy-start | bytes 491524
  0.6 5.1 %copy-start.3 = (bf16[24,4,64,32]{2,3,1,0:T(8,128)(2,1)S(1)}, bf16[24,4,64,32]{2,3,1,0:T(8,128)(2,1)}, u32[]{:S(2)}) copy-start(bf16[24,4,64,32]{2,3,1,0:T(8,128)(2,1)} %param.7) | copy-start | bytes 1179652
  0.7 5.1 %copy-start.2 = (bf16[4,64,320]{2,1,0:T(8,128)(2,1)S(1)}, bf16[4,64,320]{2,1,0:T(8,128)(2,1)}, u32[]{:S(2)}) copy-start(bf16[4,64,320]{2,1,0:T(8,128)(2,1)} %refs_1_.5) | copy-start | bytes 491524
  0.7 9.5 %collective-permute-start = (bf16[4,64,320]{2,1,0:T(8,128)(2,1)}, bf16[4,64,320]{2,1,0:T(8,128)(2,1)S(1)}, u32[]{:S(2)}, u32[]{:S(2)}) collective-permute-start(bf16[4,64,320]{2,1,0:T(8,128)(2,1)} %refs_2_.3), channel_id=1, source_target_pairs={{0,2},{1,3},{2,4},{3,5},{4,6},{5,7},{6,8},{7,9},{8,10},{9,11},{10,... | collective-permute-start | bytes 491528 | tf_op jit(solution)/shard_map/ppermute | solution.py:606
  6.1 5.6 %collective-permute-start.2 = (bf16[32,320]{1,0:T(8,128)(2,1)S(1)}, bf16[32,320]{1,0:T(8,128)(2,1)S(1)}, u32[]{:S(2)}, u32[]{:S(2)}) collective-permute-start(bf16[32,320]{1,0:T(8,128)(2,1)S(1)} %get-tuple-element.32), channel_id=1, source_target_pairs={{0,1},{1,0},{2,3},{3,2},{4,5},{5,4},{6,7},{7,6},{8,9},{9,8},{10,11... | collective-permute-start | bytes 61448 | tf_op jit(solution)/shard_map/ppermute | solution.py:657
  6.1 5.5 %collective-permute-start.3 = (bf16[32,320]{1,0:T(8,128)(2,1)S(1)}, bf16[32,320]{1,0:T(8,128)(2,1)S(1)}, u32[]{:S(2)}, u32[]{:S(2)}) collective-permute-start(bf16[32,320]{1,0:T(8,128)(2,1)S(1)} %get-tuple-element.33), channel_id=1, source_target_pairs={{1,2},{3,4},{5,6},{7,8},{9,10},{11,12},{13,14},{2,1},{4,3},{6,5},{... | collective-permute-start | bytes 61448 | tf_op jit(solution)/shard_map/ppermute | solution.py:678
  6.8 9.1 %collective-permute-start.4 = (bf16[6,64,128]{2,1,0:T(8,128)(2,1)S(1)}, bf16[6,64,128]{2,1,0:T(8,128)(2,1)S(1)}, u32[]{:S(2)}, u32[]{:S(2)}) collective-permute-start(bf16[6,64,128]{2,1,0:T(8,128)(2,1)S(1)} %get-tuple-element.38), channel_id=1, source_target_pairs={{0,16},{16,0},{1,17},{17,1},{2,18},{18,2},{3,19},{19,3},{4,20},{20... | collective-permute-start | bytes 294920 | tf_op jit(solution)/shard_map/ppermute | solution.py:617
  10.2 2.3 %collective-permute-start.1 = (bf16[4,64,320]{2,1,0:T(8,128)(2,1)S(1)}, bf16[4,64,320]{2,1,0:T(8,128)(2,1)S(1)}, u32[]{:S(2)}, u32[]{:S(2)}) collective-permute-start(bf16[4,64,320]{2,1,0:T(8,128)(2,1)S(1)} %shard_map.77.refs_0_), channel_id=1, source_target_pairs={{0,1},{1,0},{2,3},{3,2},{4,5},{5,4},{6,7},{7,6},{8,9},{9,8},{10,11... | collective-permute-start | bytes 491528 | tf_op jit(solution)/shard_map/ppermute | solution.py:657
  11.8 4.1 %collective-permute-start.5 = (bf16[16,128]{1,0:T(8,128)(2,1)S(1)}, bf16[16,128]{1,0:T(8,128)(2,1)S(1)}, u32[]{:S(2)}, u32[]{:S(2)}) collective-permute-start(bf16[16,128]{1,0:T(8,128)(2,1)S(1)} %shard_map.80), channel_id=1, source_target_pairs={{0,16},{16,0},{1,17},{17,1},{2,18},{18,2},{3,19},{19,3},{4,20},{20... | collective-permute-start | bytes 12296 | tf_op jit(solution)/shard_map/ppermute | solution.py:617
  14.4 13.1 %collective-permute-start.7 = (bf16[960,128]{1,0:T(8,128)(2,1)S(1)}, bf16[960,128]{1,0:T(8,128)(2,1)S(1)}, u32[]{:S(2)}, u32[]{:S(2)}) collective-permute-start(bf16[960,128]{1,0:T(8,128)(2,1)S(1)} %get-tuple-element.45), channel_id=1, source_target_pairs={{0,16},{16,0},{1,17},{17,1},{2,18},{18,2},{3,19},{19,3},{4,20},{20... | collective-permute-start | bytes 737288 | tf_op jit(solution)/shard_map/ppermute | solution.py:617
  15.9 2.0 %copy-start.1 = (bf16[3,3,3,40,32]{3,4,2,1,0:T(8,128)(2,1)S(1)}, bf16[3,3,3,40,32]{3,4,2,1,0:T(8,128)(2,1)}, u32[]{:S(2)}) copy-start(bf16[3,3,3,40,32]{3,4,2,1,0:T(8,128)(2,1)} %param.6) | copy-start | bytes 207364
  17.8 1.4 %collective-permute-start.6 = (f32[192,128]{1,0:T(8,128)S(1)}, f32[192,128]{1,0:T(8,128)S(1)}, u32[]{:S(2)}, u32[]{:S(2)}) collective-permute-start(f32[192,128]{1,0:T(8,128)S(1)} %get-tuple-element.41), channel_id=1, source_target_pairs={{0,1},{1,0},{2,3},{3,2},{4,5},{5,4},{6,7},{7,6},{8,9},{9,8},{10,11... | collective-permute-start | bytes 294920 | tf_op jit(solution)/shard_map/ppermute | solution.py:657
  19.2 6.8 %collective-permute-start.10 = (bf16[192,128]{1,0:T(8,128)(2,1)S(1)}, bf16[192,128]{1,0:T(8,128)(2,1)S(1)}, u32[]{:S(2)}, u32[]{:S(2)}) collective-permute-start(bf16[192,128]{1,0:T(8,128)(2,1)S(1)} %shard_map.83.refs_0_.refs_2_), channel_id=1, source_target_pairs={{0,6},{1,7},{2,4},{3,5},{4,2},{5,3},{6,0},{7,1},{8,14},{9,15},{10,... | collective-permute-start | bytes 147464 | tf_op jit(solution)/shard_map/ppermute | solution.py:657
  22.0 4.1 %collective-permute-start.8 = (bf16[192,128]{1,0:T(8,128)(2,1)S(1)}, bf16[192,128]{1,0:T(8,128)(2,1)S(1)}, u32[]{:S(2)}, u32[]{:S(2)}) collective-permute-start(bf16[192,128]{1,0:T(8,128)(2,1)S(1)} %shard_map.83.refs_0_.refs_2_), channel_id=1, source_target_pairs={{0,2},{1,3},{2,0},{3,1},{4,6},{5,7},{6,4},{7,5},{8,10},{9,11},{10,... | collective-permute-start | bytes 147464 | tf_op jit(solution)/shard_map/ppermute | solution.py:657
  23.4 4.1 %collective-permute-start.9 = (bf16[192,128]{1,0:T(8,128)(2,1)S(1)}, bf16[192,128]{1,0:T(8,128)(2,1)S(1)}, u32[]{:S(2)}, u32[]{:S(2)}) collective-permute-start(bf16[192,128]{1,0:T(8,128)(2,1)S(1)} %shard_map.83.refs_0_.refs_2_), channel_id=1, source_target_pairs={{0,4},{1,5},{2,6},{3,7},{4,0},{5,1},{6,2},{7,3},{8,12},{9,13},{10,... | collective-permute-start | bytes 147464 | tf_op jit(solution)/shard_map/ppermute | solution.py:657
  25.9 4.3 %collective-permute-start.11 = (bf16[4,64,320]{2,1,0:T(8,128)(2,1)S(1)}, bf16[4,64,320]{2,1,0:T(8,128)(2,1)S(1)}, u32[]{:S(2)}, u32[]{:S(2)}) collective-permute-start(bf16[4,64,320]{2,1,0:T(8,128)(2,1)S(1)} %get-tuple-element.46), channel_id=1, source_target_pairs={{0,1},{1,0},{2,3},{3,2},{4,5},{5,4},{6,7},{7,6},{8,9},{9,8},{10,11... | collective-permute-start | bytes 491528 | tf_op jit(solution)/shard_map/ppermute | solution.py:657
  27.6 5.5 %collective-permute-start.12 = (bf16[192,128]{1,0:T(8,128)(2,1)S(1)}, bf16[192,128]{1,0:T(8,128)(2,1)S(1)}, u32[]{:S(2)}, u32[]{:S(2)}) collective-permute-start(bf16[192,128]{1,0:T(8,128)(2,1)S(1)} %shard_map.85.refs_0_.refs_1_), channel_id=1, source_target_pairs={{0,8},{1,9},{2,10},{3,11},{4,12},{5,13},{6,14},{7,15},{8,0},{9,1},... | collective-permute-start | bytes 147464 | tf_op jit(solution)/shard_map/ppermute | solution.py:657
  30.3 8.9 %collective-permute-start.15 = (bf16[4,64,320]{2,1,0:T(8,128)(2,1)S(1)}, bf16[4,64,320]{2,1,0:T(8,128)(2,1)S(1)}, u32[]{:S(2)}, u32[]{:S(2)}) collective-permute-start(bf16[4,64,320]{2,1,0:T(8,128)(2,1)S(1)} %shard_map.86.refs_0_), channel_id=1, source_target_pairs={{2,0},{3,1},{4,2},{5,3},{6,4},{7,5},{8,6},{9,7},{10,8},{11,9},{12,... | collective-permute-start | bytes 491528 | tf_op jit(solution)/shard_map/ppermute | solution.py:606
  33.1 4.7 %collective-permute-start.13 = (f32[192,128]{1,0:T(8,128)S(1)}, f32[192,128]{1,0:T(8,128)S(1)}, u32[]{:S(2)}, u32[]{:S(2)}) collective-permute-start(f32[192,128]{1,0:T(8,128)S(1)} %shard_map.87.refs_0_.refs_1_), channel_id=1, source_target_pairs={{0,16},{1,17},{2,18},{3,19},{4,20},{5,21},{6,22},{7,23},{8,24},{9,... | collective-permute-start | bytes 294920 | tf_op jit(solution)/shard_map/ppermute | solution.py:657
  37.8 1.4 %collective-permute-start.14 = (f32[192,128]{1,0:T(8,128)S(1)}, f32[192,128]{1,0:T(8,128)S(1)}, u32[]{:S(2)}, u32[]{:S(2)}) collective-permute-start(f32[192,128]{1,0:T(8,128)S(1)} %shard_map.89.refs_0_), channel_id=1, source_target_pairs={{0,1},{1,0},{2,3},{3,2},{4,5},{5,4},{6,7},{7,6},{8,9},{9,8},{10,11... | collective-permute-start | bytes 294920 | tf_op jit(solution)/shard_map/ppermute | solution.py:657

commit v6 on v5

--- a/solution.py
+++ b/solution.py
@@ -110,39 +110,41 @@
     fr4[h, at + STEP : at + STEP + block.shape[0]] = block
 
 
-def own_kernel(group_size, left, right, far, fl, fr, fr4, mixed, wide_buf):
+def own_kernel(group_size, left, right, fl, fr, fr4, mixed, wide_buf):
     rows, cols, channels = left.shape
-    base, half, wide = rows * cols, cols // 2, group_size * SLOT
+    base, wide = rows * cols, group_size * SLOT
     mixed[0:base] = right[...].reshape(base, channels)
     mixed[base : 2 * base] = left[...].reshape(base, channels)
-    mixed[2 * base :] = far[:, half:].reshape(base // 2, channels)
     wide_buf[...] = dot(mixed[...], channel_table(channels, group_size, False))
     tail = fr.shape[1]
     for h in range(rows):
         for ref in (fr, fr4):
             ref[h, 0:16] = jnp.zeros((16, wide), F32)
             ref[h, tail - 16 :] = jnp.zeros((16, wide), F32)
-        put_band((fr, fr4, cols), h, -cols - half, wide_buf[2 * base + h * half : 2 * base + (h + 1) * half])
         put_band((fr, fr4, cols), h, 0, wide_buf[h * cols : (h + 1) * cols])
         fl[h, 0:PAD] = jnp.zeros((PAD, wide), F32)
         fl[h, PAD + cols :] = jnp.zeros((PAD, wide), F32)
         fl[h, PAD : PAD + cols] = wide_buf[base + h * cols : base + (h + 1) * cols] * (1.0 / group_size)
 
 
-def volume_kernel(ends, group_size, near, by_even, by_odd, _fl, _fr, _fr4, fl, fr, fr4, vbuf, *rest):
+def volume_kernel(ends, group_size, near, far, by_even, by_odd, _fl, _fr, _fr4, fl, fr, fr4, vbuf, *rest):
     pays, (mixed, wide_buf) = rest[: len(ends)], rest[len(ends) :]
     rows, cols, channels = near.shape
     disp = vbuf.shape[1]
     reach = fr.shape[1] - cols - PAD
     wide = group_size * SLOT
-    base = rows * cols
-    mixed[0:base] = near[...].reshape(base, channels)
+    half, at_far = cols // 2, rows * cols
+    base = at_far + rows * half
+    mixed[0:at_far] = near[...].reshape(at_far, channels)
+    mixed[at_far:base] = far[:, half:].reshape(rows * half, channels)
     count = disp + 2 * rows
     for i, x in enumerate(end_columns(by_even, by_odd)):
         mixed[base + i * count : base + (i + 1) * count] = x.astype(BF16)
     wide_buf[...] = dot(mixed[...], channel_table(channels, group_size, False))
     for h in range(rows):
         put_band((fr, fr4, cols), h, -cols, wide_buf[h * cols : (h + 1) * cols])
+        at = at_far + h * half
+        put_band((fr, fr4, cols), h, -cols - half, wide_buf[at : at + half])
         at = base + disp + h
         fl[h, PAD - 1 : PAD] = wide_buf[at : at + 1] * (1.0 / group_size)
         at += count
@@ -403,7 +405,8 @@
                 accl[h, 8 * b : 8 * b + 8, 128 * j : 128 * (j + 1)] = accs[b][j] * (1.0 / group_size)
 
     for p, gv in enumerate(grads):
-        pl.loop(0, 2)(functools.partial(left_row, gv, p))
+        for hh in range(2):
+            left_row(gv, p, hh)
     whole = accl[...].reshape(rows * cols, wide).astype(BF16)
     out = dot(whole, channel_table(channels, group_size, True)).astype(BF16)
     lg[...] = out.reshape(rows, cols, channels)
@@ -464,7 +467,7 @@
         ]
         acc = dot(jnp.concatenate(slabs, axis=1), wc[...])
         for j in range(step):
-            both = acc[j * cols : (j + 1) * cols].T.astype(BF16)
+            both = acc[j * cols : (j + 1) * cols].astype(BF16).T
             for o in range(2):
                 block = both[rows * feat * o : rows * feat * (o + 1)]
                 held[2 * (q * step + j) + o] = block.reshape(rows, feat, cols)
@@ -676,34 +679,33 @@
     inner = range(1, n_col - 1, 2)
     by_even = swap(by_even, 1)
     by_odd = lax.ppermute(by_odd, "col", [(i, i + 1) for i in inner] + [(i + 1, i) for i in inner])
-    (passed,) = call(
-        pass_kernel, [((rows, cols, channels), BF16)], [], right_features, far, after=[ctl]
-    )
-    near = swap(passed, 1)
-    top, bot = halos(rims)
     band = 104 + cols + PAD
     banks = [((rows, total, wide), F32), ((rows, band, wide), F32), ((rows, band, wide), F32)]
-    spread_rows = 2 * rows * cols + rows * cols // 2
+    spread_rows = 2 * rows * cols
     fl, fr, fr4 = call(
         functools.partial(own_kernel, group_size),
         banks,
         [pltpu.VMEM((spread_rows, channels), BF16), pltpu.VMEM((spread_rows, wide), F32)],
         left_features,
         right_features,
-        far,
-        after=[passed],
-    )
+        after=[ctl],
+    )
+    (passed,) = call(
+        pass_kernel, [((rows, cols, channels), BF16)], [], right_features, far, after=[fl]
+    )
+    near = swap(passed, 1)
+    top, bot = halos(rims)
     corner_pays = call(
         functools.partial(corner_kernel, ends, rows, disp),
         [((16, 128), BF16)] * n,
         [pltpu.VMEM((2, disp, 128), F32), pltpu.VMEM((16, 128), F32)],
         by_even,
         by_odd,
-        after=[fl],
+        after=[passed],
         us=5.0,
     )
     tops, bots = halos(corner_pays)
-    spread_rows = rows * cols + 2 * count
+    spread_rows = rows * cols + rows * cols // 2 + 2 * count
     fl, fr, fr4, vbuf, *volume_rows = call(
         functools.partial(volume_kernel, ends, group_size),
         banks
@@ -711,13 +713,14 @@
         + [((disp // 2 * total, 128), BF16)] * n,
         [pltpu.VMEM((spread_rows, channels), BF16), pltpu.VMEM((spread_rows, wide), F32)],
         near,
+        far,
         by_even,
         by_odd,
         fl,
         fr,
         fr4,
         us=1.8,
-        alias=[(3, 0), (4, 1), (5, 2)],
+        alias=[(4, 0), (5, 1), (6, 2)],
     )
     vtop, vbot = halos(volume_rows)
     keep, give, ctsh = call(

time: 40.6 us -> 40.6 us (level)
  waiting for transfers between devices: 5.64 us -> 6.07 us
    ppermute x10, waiting for transfers between devices: 3.86 us -> 4.77 us  [swap(): return lax.ppermute(block, ('row', 'col'), route)]
    ppermute x2, waiting for transfers between devices: 1.77 us -> 1.29 us  [col_shift(): return lax.ppermute(block, 'col', route)]
    ppermute x3, starting transfers between devices: 3.66 us -> 3.25 us  [halos(): got = lax.ppermute(pays[0], 'row', [(0, 1), (1, 0)])]
  transfers between devices with their start and end apart: 16 -> 16, of which waited for: 6 -> 7; matrix products, arithmetic and copies ran while one was open for 0% -> 0% of each run, Pallas kernels for 31% -> 31%
where the time goes in v6:
time: 40.6 us; the launch traced here: 40.4 us
  starting transfers between devices  19.8 us (49%)
  Pallas kernels  13.6 us (33%)
  waiting for transfers between devices  6.07 us (15%)
  between operations  0.85 us (2%)
    pallas_call x17, Pallas kernels, call(): pl.pallas_call(lambda *refs: kernel(*refs[skip:]), out_shape=[jax.ShapeDt...  13.6 us
    ppermute x10, starting transfers between devices, swap(): return lax.ppermute(block, ('row', 'col'), route)  9.6 us
    ppermute x2, starting transfers between devices, col_shift(): return lax.ppermute(block, 'col', route)  6.31 us
    ppermute x10, waiting for transfers between devices, swap(): return lax.ppermute(block, ('row', 'col'), route)  4.77 us
    ppermute x3, starting transfers between devices, halos(): got = lax.ppermute(pays[0], 'row', [(0, 1), (1, 0)])  3.25 us
    ppermute x2, waiting for transfers between devices, col_shift(): return lax.ppermute(block, 'col', route)  1.29 us
  transfers between devices with their start and end apart: 16, of which 7 were waited for; matrix products, arithmetic and copies ran while one was open for 0% of the time, Pallas kernels for 31%

profile of v6, /device:TPU:0, one launch (start us, length us, event | category | flops | bytes accessed | tf_op | source)
XLA Modules:
  0.0 40.4 jit_solution(13531704108674399140)
XLA Ops:
  0.6 0.0 copy-start
  0.6 0.0 copy-start.3
  0.7 0.0 copy-start.2
  0.7 5.0 %collective-permute-start = (bf16[4,64,320]{2,1,0:T(8,128)(2,1)}, bf16[4,64,320]{2,1,0:T(8,128)(2,1)S(1)}, u32[]{:S(2)}, u32[]{:S(2)}) collective-permute-start(bf16[4,64,320]{2,1,0:T(8,128)(2,1)} %refs_1_.5), channel_id=1, source_target_pairs={{0,2},{1,3},{2,4},{3,5},{4,6},{5,7},{6,8},{7,9},{8,10},{9,11},{10,... | collective-permute-start | bytes 491528 | tf_op jit(solution)/shard_map/ppermute | solution.py:609
  5.7 0.0 copy-done
  5.7 0.0 copy-done.3
  5.7 0.0 copy-done.2
  5.7 0.3 shard_map.76
  6.1 0.1 collective-permute-start.2
  6.1 0.7 %collective-permute-start.3 = (bf16[32,320]{1,0:T(8,128)(2,1)S(1)}, bf16[32,320]{1,0:T(8,128)(2,1)S(1)}, u32[]{:S(2)}, u32[]{:S(2)}) collective-permute-start(bf16[32,320]{1,0:T(8,128)(2,1)S(1)} %get-tuple-element.34), channel_id=1, source_target_pairs={{1,2},{3,4},{5,6},{7,8},{9,10},{11,12},{13,14},{2,1},{4,3},{6,5},{... | collective-permute-start | bytes 61448 | tf_op jit(solution)/shard_map/ppermute | solution.py:681
  6.8 1.6 %collective-permute-start.4 = (bf16[6,64,128]{2,1,0:T(8,128)(2,1)S(1)}, bf16[6,64,128]{2,1,0:T(8,128)(2,1)S(1)}, u32[]{:S(2)}, u32[]{:S(2)}) collective-permute-start(bf16[6,64,128]{2,1,0:T(8,128)(2,1)S(1)} %get-tuple-element.38), channel_id=1, source_target_pairs={{0,16},{16,0},{1,17},{17,1},{2,18},{18,2},{3,19},{19,3},{4,20},{20... | collective-permute-start | bytes 294920 | tf_op jit(solution)/shard_map/ppermute | solution.py:620
  8.4 0.5 %shard_map.77 = (f32[4,80,512]{2,1,0:T(8,128)S(1)}, f32[4,176,512]{2,1,0:T(8,128)S(1)}, f32[4,176,512]{2,1,0:T(8,128)S(1)}) custom-call(bf16[24,64,128]{2,1,0:T(8,128)(2,1)S(1)} %get-tuple-element.31.refs_0_.refs_1_, bf16[4,64,320]{2,1,0:T(8,128)(2,1)S(1)} %copy-done.2, bf16[4,64,320]{2,1,0:T(8,128)(2,1)S(1)} %copy-done), custom_call_target="tpu_custom_call" | custom-call | tf_op jit(solution)/shard_map/pallas_call | solution.py:592
  8.8 1.3 %collective-permute-done.refs_2_.refs_1_ = bf16[4,64,320]{2,1,0:T(8,128)(2,1)S(1)} collective-permute-done((bf16[4,64,320]{2,1,0:T(8,128)(2,1)}, bf16[4,64,320]{2,1,0:T(8,128)(2,1)S(1)}, u32[]{:S(2)}, u32[]{:S(2)}) %collective-permute-start) | collective-permute-done | bytes 163872 | tf_op jit(solution)/shard_map/ppermute | solution.py:609
  10.1 0.1 shard_map.78.refs_0_
  10.2 1.4 %collective-permute-start.1 = (bf16[4,64,320]{2,1,0:T(8,128)(2,1)S(1)}, bf16[4,64,320]{2,1,0:T(8,128)(2,1)S(1)}, u32[]{:S(2)}, u32[]{:S(2)}) collective-permute-start(bf16[4,64,320]{2,1,0:T(8,128)(2,1)S(1)} %shard_map.78.refs_0_), channel_id=1, source_target_pairs={{0,1},{1,0},{2,3},{3,2},{4,5},{5,4},{6,7},{7,6},{8,9},{9,8},{10,11... | collective-permute-start | bytes 491528 | tf_op jit(solution)/shard_map/ppermute | solution.py:660
  11.6 0.0 collective-permute-done.2.refs_2_.refs_1_
  11.6 0.0 collective-permute-done.3.refs_3_.refs_2_
  11.6 0.1 shard_map.80
  11.7 0.6 %collective-permute-start.5 = (bf16[16,128]{1,0:T(8,128)(2,1)S(1)}, bf16[16,128]{1,0:T(8,128)(2,1)S(1)}, u32[]{:S(2)}, u32[]{:S(2)}) collective-permute-start(bf16[16,128]{1,0:T(8,128)(2,1)S(1)} %shard_map.80), channel_id=1, source_target_pairs={{0,16},{16,0},{1,17},{17,1},{2,18},{18,2},{3,19},{19,3},{4,20},{20... | collective-permute-start | bytes 12296 | tf_op jit(solution)/shard_map/ppermute | solution.py:620
  12.2 0.4 %collective-permute-done.1.refs_0_ = bf16[4,64,320]{2,1,0:T(8,128)(2,1)S(1)} collective-permute-done((bf16[4,64,320]{2,1,0:T(8,128)(2,1)S(1)}, bf16[4,64,320]{2,1,0:T(8,128)(2,1)S(1)}, u32[]{:S(2)}, u32[]{:S(2)}) %collective-permute-start.1) | collective-permute-done | bytes 163872 | tf_op jit(solution)/shard_map/ppermute | solution.py:660
  12.6 2.1 %shard_map.79 = (f32[4,80,512]{2,1,0:T(8,128)S(1)}, f32[4,176,512]{2,1,0:T(8,128)S(1)}, f32[4,176,512]{2,1,0:T(8,128)S(1)}, f32[2,24,80,128]{3,2,1,0:T(8,128)S(1)}, bf16[960,128]{1,0:T(8,128)(2,1)S(1)}) custom-call(bf16[4,64,320]{2,1,0:T(8,128)(2,1)S(1)} %collective-permute-done.1.refs_0_, ...), custom_call_target="tpu_custom_call", output_to_operand_aliasing={{0}: (4, {}), {1}: (5, {}), {2}: (6, {})} | custom-call | flops 2070000000 | bytes 6660000 | tf_op jit(solution)/shard_map/pallas_call | solution.py:592
  14.7 1.1 %collective-permute-start.7 = (bf16[960,128]{1,0:T(8,128)(2,1)S(1)}, bf16[960,128]{1,0:T(8,128)(2,1)S(1)}, u32[]{:S(2)}, u32[]{:S(2)}) collective-permute-start(bf16[960,128]{1,0:T(8,128)(2,1)S(1)} %get-tuple-element.45), channel_id=1, source_target_pairs={{0,16},{16,0},{1,17},{17,1},{2,18},{18,2},{3,19},{19,3},{4,20},{20... | collective-permute-start | bytes 737288 | tf_op jit(solution)/shard_map/ppermute | solution.py:620
  15.9 0.0 collective-permute-done.4.refs_4_.refs_5_
  15.9 0.0 collective-permute-done.5.refs_6_.refs_7_
  15.9 0.0 copy-start.1
  15.9 1.9 %shard_map.81 = (f32[192,128]{1,0:T(8,128)S(1)}, f32[192,128]{1,0:T(8,128)S(1)}, bf16[13,2,64,768]{3,2,1,0:T(8,128)(2,1)S(1)}) custom-call(f32[2,24,80,128]{3,2,1,0:T(8,128)S(1)} %get-tuple-element.37.refs_0_.refs_1_, bf16[24,64,128]{2,1,0:T(8,128)(2,1)S(1)} %get-tuple-element.31.refs_0_.refs_1_, bf16[32,320]{1,0:T(8,128)(2,1)S(1)} %collective-permute-done.2.refs_2_.refs_1_, ...), custom_call_target="tpu_custom_call" | custom-call | flops 2300000000 | bytes 7400000 | tf_op jit(solution)/shard_map/pallas_call | solution.py:592
  17.8 0.1 collective-permute-start.6
  17.9 0.0 copy-done.1
  17.9 0.8 %shard_map.82 = (bf16[1536,256]{1,0:T(8,128)(2,1)S(1)}, bf16[3072,256]{1,0:T(8,128)(2,1)S(1)}) custom-call(f32[192,128]{1,0:T(8,128)S(1)} %get-tuple-element.39.refs_0_.refs_1_, bf16[3,3,3,32,40]{4,3,2,1,0:T(8,128)(2,1)S(1)} %bitcast.4), custom_call_target="tpu_custom_call" | custom-call | tf_op jit(solution)/shard_map/pallas_call | solution.py:592
  18.7 0.4 %collective-permute-done.6.refs_2_ = f32[192,128]{1,0:T(8,128)S(1)} collective-permute-done((f32[192,128]{1,0:T(8,128)S(1)}, f32[192,128]{1,0:T(8,128)S(1)}, u32[]{:S(2)}, u32[]{:S(2)}) %collective-permute-start.6) | collective-permute-done | bytes 98336 | tf_op jit(solution)/shard_map/ppermute | solution.py:660
  19.2 2.9 %collective-permute-start.10 = (bf16[192,128]{1,0:T(8,128)(2,1)S(1)}, bf16[192,128]{1,0:T(8,128)(2,1)S(1)}, u32[]{:S(2)}, u32[]{:S(2)}) collective-permute-start(bf16[192,128]{1,0:T(8,128)(2,1)S(1)} %shard_map.83.refs_0_.refs_2_), channel_id=1, source_target_pairs={{0,6},{1,7},{2,4},{3,5},{4,2},{5,3},{6,0},{7,1},{8,14},{9,15},{10,... | collective-permute-start | bytes 147464 | tf_op jit(solution)/shard_map/ppermute | solution.py:660
  22.1 1.4 %collective-permute-start.8 = (bf16[192,128]{1,0:T(8,128)(2,1)S(1)}, bf16[192,128]{1,0:T(8,128)(2,1)S(1)}, u32[]{:S(2)}, u32[]{:S(2)}) collective-permute-start(bf16[192,128]{1,0:T(8,128)(2,1)S(1)} %shard_map.83.refs_0_.refs_2_), channel_id=1, source_target_pairs={{0,2},{1,3},{2,0},{3,1},{4,6},{5,7},{6,4},{7,5},{8,10},{9,11},{10,... | collective-permute-start | bytes 147464 | tf_op jit(solution)/shard_map/ppermute | solution.py:660
  23.5 0.0 collective-permute-start.9
  23.5 2.4 %shard_map.84 = (f32[2,24,64,128]{3,2,1,0:T(8,128)S(1)}, f32[2,24,64,128]{3,2,1,0:T(8,128)S(1)}, bf16[4,64,320]{2,1,0:T(8,128)(2,1)S(1)}, bf16[4,64,320]{2,1,0:T(8,128)(2,1)S(1)}, bf16[4,32,320]{2,1,0:T(8,128)(2,1)S(1)}) custom-call(bf16[192,128]{1,0:T(8,128)(2,1)S(1)} %shard_map.83.refs_0_.refs_2_, bf16[13,2,64,768]{3,2,1,0:T(8,128)(2,1)S(1)} %get-tuple-element.42.refs_1_, ...), custom_call_target="tpu_custom_call" | custom-call | flops 460000000 | bytes 1480000 | tf_op jit(solution)/shard_map/pallas_call | solution.py:592
  25.9 0.1 collective-permute-start.11
  26.0 0.0 collective-permute-done.10.refs_5_
  26.0 0.1 collective-permute-done.8.refs_3_
  26.2 1.4 %collective-permute-done.9.refs_4_ = bf16[192,128]{1,0:T(8,128)(2,1)S(1)} collective-permute-done((bf16[192,128]{1,0:T(8,128)(2,1)S(1)}, bf16[192,128]{1,0:T(8,128)(2,1)S(1)}, u32[]{:S(2)}, u32[]{:S(2)}) %collective-permute-start.9) | collective-permute-done | bytes 49184 | tf_op jit(solution)/shard_map/ppermute | solution.py:660
  27.6 0.0 collective-permute-done.7.refs_1_.refs_2_.refs_3_
  27.6 2.7 %collective-permute-start.12 = (bf16[192,128]{1,0:T(8,128)(2,1)S(1)}, bf16[192,128]{1,0:T(8,128)(2,1)S(1)}, u32[]{:S(2)}, u32[]{:S(2)}) collective-permute-start(bf16[192,128]{1,0:T(8,128)(2,1)S(1)} %shard_map.85.refs_0_.refs_1_), channel_id=1, source_target_pairs={{0,8},{1,9},{2,10},{3,11},{4,12},{5,13},{6,14},{7,15},{8,0},{9,1},... | collective-permute-start | bytes 147464 | tf_op jit(solution)/shard_map/ppermute | solution.py:660
  30.3 0.0 collective-permute-done.11.refs_1_.refs_3_
  30.3 0.1 shard_map.86.refs_0_
  30.4 1.3 %collective-permute-start.15 = (bf16[4,64,320]{2,1,0:T(8,128)(2,1)S(1)}, bf16[4,64,320]{2,1,0:T(8,128)(2,1)S(1)}, u32[]{:S(2)}, u32[]{:S(2)}) collective-permute-start(bf16[4,64,320]{2,1,0:T(8,128)(2,1)S(1)} %shard_map.86.refs_0_), channel_id=1, source_target_pairs={{2,0},{3,1},{4,2},{5,3},{6,4},{7,5},{8,6},{9,7},{10,8},{11,9},{12,... | collective-permute-start | bytes 491528 | tf_op jit(solution)/shard_map/ppermute | solution.py:609
  31.7 1.5 %collective-permute-done.12.refs_2_ = bf16[192,128]{1,0:T(8,128)(2,1)S(1)} collective-permute-done((bf16[192,128]{1,0:T(8,128)(2,1)S(1)}, bf16[192,128]{1,0:T(8,128)(2,1)S(1)}, u32[]{:S(2)}, u32[]{:S(2)}) %collective-permute-start.12) | collective-permute-done | bytes 49184 | tf_op jit(solution)/shard_map/ppermute | solution.py:660
  33.2 0.9 %collective-permute-start.13 = (f32[192,128]{1,0:T(8,128)S(1)}, f32[192,128]{1,0:T(8,128)S(1)}, u32[]{:S(2)}, u32[]{:S(2)}) collective-permute-start(f32[192,128]{1,0:T(8,128)S(1)} %shard_map.87.refs_0_.refs_1_), channel_id=1, source_target_pairs={{0,16},{1,17},{2,18},{3,19},{4,20},{5,21},{6,22},{7,23},{8,24},{9,... | collective-permute-start | bytes 294920 | tf_op jit(solution)/shard_map/ppermute | solution.py:660
  34.1 2.9 %shard_map.88 = (bf16[24,4,32,64]{3,2,1,0:T(8,128)(2,1)}, f32[8,128]{1,0:T(8,128)S(1)}) custom-call(f32[192,128]{1,0:T(8,128)S(1)} %shard_map.87.refs_0_.refs_1_, f32[2,24,80,128]{3,2,1,0:T(8,128)S(1)} %get-tuple-element.37.refs_0_.refs_1_, bf16[960,128]{1,0:T(8,128)(2,1)S(1)} %collective-permute-done.7.refs_1_.refs_2_.refs_3_, ...), custom_call_target="tpu_custom_call" | custom-call | flops 3449999872 | bytes 11100000 | tf_op jit(solution)/shard_map/pallas_call | solution.py:592
  37.1 0.8 %collective-permute-done.13.refs_2_ = f32[192,128]{1,0:T(8,128)S(1)} collective-permute-done((f32[192,128]{1,0:T(8,128)S(1)}, f32[192,128]{1,0:T(8,128)S(1)}, u32[]{:S(2)}, u32[]{:S(2)}) %collective-permute-start.13) | collective-permute-done | bytes 98336 | tf_op jit(solution)/shard_map/ppermute | solution.py:660
  37.9 0.1 collective-permute-start.14
  38.0 1.3 %shard_map.90.refs_5_ = bf16[4,64,320]{2,1,0:T(8,128)(2,1)S(1)} custom-call(f32[192,128]{1,0:T(8,128)S(1)} %shard_map.89.refs_0_, f32[4,176,512]{2,1,0:T(8,128)S(1)} %get-tuple-element.51.refs_1_, f32[4,176,512]{2,1,0:T(8,128)S(1)} %get-tuple-element.52.refs_2_, f32[2,24,64,128]{3,2,1,0:T(8,128)S(1)} %get-tuple-element.53.refs_3_, ...), custom_call_target="tpu_custom_call" | custom-call | flops 2184999936 | bytes 7030000 | tf_op jit(solution)/shard_map/pallas_call | solution.py:592
  39.3 0.0 collective-permute-done.15.refs_4_
  39.3 0.0 collective-permute-done.14.refs_1_
  39.3 1.1 %shard_map.91 = (f32[3,3,3,32,40]{4,3,2,1,0:T(8,128)}, bf16[4,64,320]{2,1,0:T(8,128)(2,1)}, bf16[4,64,320]{2,1,0:T(8,128)(2,1)}) custom-call(f32[192,128]{1,0:T(8,128)S(1)} %shard_map.89.refs_0_, f32[192,128]{1,0:T(8,128)S(1)} %collective-permute-done.14.refs_1_, bf16[4,64,320]{2,1,0:T(8,128)(2,1)S(1)} %get-tuple-element.44.refs_0_.refs_2_, ...), custom_call_target="tpu_custom_call" | custom-call | flops 1150000000 | bytes 3700000 | tf_op jit(solution)/shard_map/pallas_call | solution.py:592
  (5 shorter events, 0.1 us)
Async XLA Ops:
  0.6 5.1 %copy-start = (bf16[4,64,320]{2,1,0:T(8,128)(2,1)S(1)}, bf16[4,64,320]{2,1,0:T(8,128)(2,1)}, u32[]{:S(2)}) copy-start(bf16[4,64,320]{2,1,0:T(8,128)(2,1)} %refs_1_.5) | copy-start | bytes 491524
  0.6 5.1 %copy-start.3 = (bf16[24,4,64,32]{2,3,1,0:T(8,128)(2,1)S(1)}, bf16[24,4,64,32]{2,3,1,0:T(8,128)(2,1)}, u32[]{:S(2)}) copy-start(bf16[24,4,64,32]{2,3,1,0:T(8,128)(2,1)} %param.7) | copy-start | bytes 1179652
  0.7 5.1 %copy-start.2 = (bf16[4,64,320]{2,1,0:T(8,128)(2,1)S(1)}, bf16[4,64,320]{2,1,0:T(8,128)(2,1)}, u32[]{:S(2)}) copy-start(bf16[4,64,320]{2,1,0:T(8,128)(2,1)} %refs_1_.4) | copy-start | bytes 491524
  0.7 9.5 %collective-permute-start = (bf16[4,64,320]{2,1,0:T(8,128)(2,1)}, bf16[4,64,320]{2,1,0:T(8,128)(2,1)S(1)}, u32[]{:S(2)}, u32[]{:S(2)}) collective-permute-start(bf16[4,64,320]{2,1,0:T(8,128)(2,1)} %refs_1_.5), channel_id=1, source_target_pairs={{0,2},{1,3},{2,4},{3,5},{4,6},{5,7},{6,8},{7,9},{8,10},{9,11},{10,... | collective-permute-start | bytes 491528 | tf_op jit(solution)/shard_map/ppermute | solution.py:609
  6.1 5.5 %collective-permute-start.2 = (bf16[32,320]{1,0:T(8,128)(2,1)S(1)}, bf16[32,320]{1,0:T(8,128)(2,1)S(1)}, u32[]{:S(2)}, u32[]{:S(2)}) collective-permute-start(bf16[32,320]{1,0:T(8,128)(2,1)S(1)} %get-tuple-element.33), channel_id=1, source_target_pairs={{0,1},{1,0},{2,3},{3,2},{4,5},{5,4},{6,7},{7,6},{8,9},{9,8},{10,11... | collective-permute-start | bytes 61448 | tf_op jit(solution)/shard_map/ppermute | solution.py:660
  6.1 5.4 %collective-permute-start.3 = (bf16[32,320]{1,0:T(8,128)(2,1)S(1)}, bf16[32,320]{1,0:T(8,128)(2,1)S(1)}, u32[]{:S(2)}, u32[]{:S(2)}) collective-permute-start(bf16[32,320]{1,0:T(8,128)(2,1)S(1)} %get-tuple-element.34), channel_id=1, source_target_pairs={{1,2},{3,4},{5,6},{7,8},{9,10},{11,12},{13,14},{2,1},{4,3},{6,5},{... | collective-permute-start | bytes 61448 | tf_op jit(solution)/shard_map/ppermute | solution.py:681
  6.8 9.1 %collective-permute-start.4 = (bf16[6,64,128]{2,1,0:T(8,128)(2,1)S(1)}, bf16[6,64,128]{2,1,0:T(8,128)(2,1)S(1)}, u32[]{:S(2)}, u32[]{:S(2)}) collective-permute-start(bf16[6,64,128]{2,1,0:T(8,128)(2,1)S(1)} %get-tuple-element.38), channel_id=1, source_target_pairs={{0,16},{16,0},{1,17},{17,1},{2,18},{18,2},{3,19},{19,3},{4,20},{20... | collective-permute-start | bytes 294920 | tf_op jit(solution)/shard_map/ppermute | solution.py:620
  10.2 2.5 %collective-permute-start.1 = (bf16[4,64,320]{2,1,0:T(8,128)(2,1)S(1)}, bf16[4,64,320]{2,1,0:T(8,128)(2,1)S(1)}, u32[]{:S(2)}, u32[]{:S(2)}) collective-permute-start(bf16[4,64,320]{2,1,0:T(8,128)(2,1)S(1)} %shard_map.78.refs_0_), channel_id=1, source_target_pairs={{0,1},{1,0},{2,3},{3,2},{4,5},{5,4},{6,7},{7,6},{8,9},{9,8},{10,11... | collective-permute-start | bytes 491528 | tf_op jit(solution)/shard_map/ppermute | solution.py:660
  11.7 4.2 %collective-permute-start.5 = (bf16[16,128]{1,0:T(8,128)(2,1)S(1)}, bf16[16,128]{1,0:T(8,128)(2,1)S(1)}, u32[]{:S(2)}, u32[]{:S(2)}) collective-permute-start(bf16[16,128]{1,0:T(8,128)(2,1)S(1)} %shard_map.80), channel_id=1, source_target_pairs={{0,16},{16,0},{1,17},{17,1},{2,18},{18,2},{3,19},{19,3},{4,20},{20... | collective-permute-start | bytes 12296 | tf_op jit(solution)/shard_map/ppermute | solution.py:620
  14.7 12.9 %collective-permute-start.7 = (bf16[960,128]{1,0:T(8,128)(2,1)S(1)}, bf16[960,128]{1,0:T(8,128)(2,1)S(1)}, u32[]{:S(2)}, u32[]{:S(2)}) collective-permute-start(bf16[960,128]{1,0:T(8,128)(2,1)S(1)} %get-tuple-element.45), channel_id=1, source_target_pairs={{0,16},{16,0},{1,17},{17,1},{2,18},{18,2},{3,19},{19,3},{4,20},{20... | collective-permute-start | bytes 737288 | tf_op jit(solution)/shard_map/ppermute | solution.py:620
  15.9 2.0 %copy-start.1 = (bf16[3,3,3,40,32]{3,4,2,1,0:T(8,128)(2,1)S(1)}, bf16[3,3,3,40,32]{3,4,2,1,0:T(8,128)(2,1)}, u32[]{:S(2)}) copy-start(bf16[3,3,3,40,32]{3,4,2,1,0:T(8,128)(2,1)} %param.6) | copy-start | bytes 207364
  17.8 1.4 %collective-permute-start.6 = (f32[192,128]{1,0:T(8,128)S(1)}, f32[192,128]{1,0:T(8,128)S(1)}, u32[]{:S(2)}, u32[]{:S(2)}) collective-permute-start(f32[192,128]{1,0:T(8,128)S(1)} %get-tuple-element.41), channel_id=1, source_target_pairs={{0,1},{1,0},{2,3},{3,2},{4,5},{5,4},{6,7},{7,6},{8,9},{9,8},{10,11... | collective-permute-start | bytes 294920 | tf_op jit(solution)/shard_map/ppermute | solution.py:660
  19.2 6.9 %collective-permute-start.10 = (bf16[192,128]{1,0:T(8,128)(2,1)S(1)}, bf16[192,128]{1,0:T(8,128)(2,1)S(1)}, u32[]{:S(2)}, u32[]{:S(2)}) collective-permute-start(bf16[192,128]{1,0:T(8,128)(2,1)S(1)} %shard_map.83.refs_0_.refs_2_), channel_id=1, source_target_pairs={{0,6},{1,7},{2,4},{3,5},{4,2},{5,3},{6,0},{7,1},{8,14},{9,15},{10,... | collective-permute-start | bytes 147464 | tf_op jit(solution)/shard_map/ppermute | solution.py:660
  22.1 4.1 %collective-permute-start.8 = (bf16[192,128]{1,0:T(8,128)(2,1)S(1)}, bf16[192,128]{1,0:T(8,128)(2,1)S(1)}, u32[]{:S(2)}, u32[]{:S(2)}) collective-permute-start(bf16[192,128]{1,0:T(8,128)(2,1)S(1)} %shard_map.83.refs_0_.refs_2_), channel_id=1, source_target_pairs={{0,2},{1,3},{2,0},{3,1},{4,6},{5,7},{6,4},{7,5},{8,10},{9,11},{10,... | collective-permute-start | bytes 147464 | tf_op jit(solution)/shard_map/ppermute | solution.py:660
  23.5 4.1 %collective-permute-start.9 = (bf16[192,128]{1,0:T(8,128)(2,1)S(1)}, bf16[192,128]{1,0:T(8,128)(2,1)S(1)}, u32[]{:S(2)}, u32[]{:S(2)}) collective-permute-start(bf16[192,128]{1,0:T(8,128)(2,1)S(1)} %shard_map.83.refs_0_.refs_2_), channel_id=1, source_target_pairs={{0,4},{1,5},{2,6},{3,7},{4,0},{5,1},{6,2},{7,3},{8,12},{9,13},{10,... | collective-permute-start | bytes 147464 | tf_op jit(solution)/shard_map/ppermute | solution.py:660
  25.9 4.3 %collective-permute-start.11 = (bf16[4,64,320]{2,1,0:T(8,128)(2,1)S(1)}, bf16[4,64,320]{2,1,0:T(8,128)(2,1)S(1)}, u32[]{:S(2)}, u32[]{:S(2)}) collective-permute-start(bf16[4,64,320]{2,1,0:T(8,128)(2,1)S(1)} %get-tuple-element.46), channel_id=1, source_target_pairs={{0,1},{1,0},{2,3},{3,2},{4,5},{5,4},{6,7},{7,6},{8,9},{9,8},{10,11... | collective-permute-start | bytes 491528 | tf_op jit(solution)/shard_map/ppermute | solution.py:660
  27.6 5.5 %collective-permute-start.12 = (bf16[192,128]{1,0:T(8,128)(2,1)S(1)}, bf16[192,128]{1,0:T(8,128)(2,1)S(1)}, u32[]{:S(2)}, u32[]{:S(2)}) collective-permute-start(bf16[192,128]{1,0:T(8,128)(2,1)S(1)} %shard_map.85.refs_0_.refs_1_), channel_id=1, source_target_pairs={{0,8},{1,9},{2,10},{3,11},{4,12},{5,13},{6,14},{7,15},{8,0},{9,1},... | collective-permute-start | bytes 147464 | tf_op jit(solution)/shard_map/ppermute | solution.py:660
  30.4 8.9 %collective-permute-start.15 = (bf16[4,64,320]{2,1,0:T(8,128)(2,1)S(1)}, bf16[4,64,320]{2,1,0:T(8,128)(2,1)S(1)}, u32[]{:S(2)}, u32[]{:S(2)}) collective-permute-start(bf16[4,64,320]{2,1,0:T(8,128)(2,1)S(1)} %shard_map.86.refs_0_), channel_id=1, source_target_pairs={{2,0},{3,1},{4,2},{5,3},{6,4},{7,5},{8,6},{9,7},{10,8},{11,9},{12,... | collective-permute-start | bytes 491528 | tf_op jit(solution)/shard_map/ppermute | solution.py:609
  33.2 4.7 %collective-permute-start.13 = (f32[192,128]{1,0:T(8,128)S(1)}, f32[192,128]{1,0:T(8,128)S(1)}, u32[]{:S(2)}, u32[]{:S(2)}) collective-permute-start(f32[192,128]{1,0:T(8,128)S(1)} %shard_map.87.refs_0_.refs_1_), channel_id=1, source_target_pairs={{0,16},{1,17},{2,18},{3,19},{4,20},{5,21},{6,22},{7,23},{8,24},{9,... | collective-permute-start | bytes 294920 | tf_op jit(solution)/shard_map/ppermute | solution.py:660
  37.9 1.4 %collective-permute-start.14 = (f32[192,128]{1,0:T(8,128)S(1)}, f32[192,128]{1,0:T(8,128)S(1)}, u32[]{:S(2)}, u32[]{:S(2)}) collective-permute-start(f32[192,128]{1,0:T(8,128)S(1)} %shard_map.89.refs_0_), channel_id=1, source_target_pairs={{0,1},{1,0},{2,3},{3,2},{4,5},{5,4},{6,7},{7,6},{8,9},{9,8},{10,11... | collective-permute-start | bytes 294920 | tf_op jit(solution)/shard_map/ppermute | solution.py:660

commit v7 on v6

--- a/solution.py
+++ b/solution.py
@@ -318,21 +318,25 @@
     step = disp // 4
     low = lanes((step * cols, 128)) < SLOT
 
-    def conv(q, p, gv):
-        slabs = [
-            ctsh[pl.ds(q * step + s // 2, step), s % 2, :, 256 * e + 128 * p : 256 * e + 128 * (p + 1)]
-            for s in range(4)
-            for e in range(3)
-        ]
-        slabs = [x.reshape(step * cols, 128) for x in slabs]
-        acc = dot(jnp.concatenate(slabs, axis=1), w2[...]).astype(BF16).astype(F32)
-        for o in range(2):
-            x = acc[:, 128 * o : 128 * (o + 1)]
-            r = pltpu.roll(x, SLOT, 1)
-            for hh in range(2):
-                y = jnp.where(low, r, x) if hh else jnp.where(low, x, r)
-                for j in range(step):
-                    gv[hh, 2 * (q * step + j) + o] = y[j * cols : (j + 1) * cols]
+    def conv(q):
+        rows_of = []
+        for p in range(len(grads)):
+            slabs = [
+                ctsh[pl.ds(q * step + s // 2, step), s % 2, :, 256 * e + 128 * p : 256 * e + 128 * (p + 1)]
+                for s in range(4)
+                for e in range(3)
+            ]
+            slabs = [x.reshape(step * cols, 128) for x in slabs]
+            rows_of.append(jnp.concatenate(slabs, axis=1))
+        acc = dot(jnp.concatenate(rows_of, axis=0), w2[...]).astype(BF16).astype(F32)
+        for p, gv in enumerate(grads):
+            for o in range(2):
+                x = acc[p * step * cols : (p + 1) * step * cols, 128 * o : 128 * (o + 1)]
+                r = pltpu.roll(x, SLOT, 1)
+                for hh in range(2):
+                    y = jnp.where(low, r, x) if hh else jnp.where(low, x, r)
+                    for j in range(step):
+                        gv[hh, 2 * (q * step + j) + o] = y[j * cols : (j + 1) * cols]
 
     count = cols // 8
     back = acce.shape[1] - cols
@@ -362,9 +366,8 @@
                     buf[h, 8 * k : 8 * k + 8, 128 * j : 128 * (j + 1)] = x
         acco[h, 8 * (lead + count) :] = jnp.zeros((8, wide), F32)
 
-    for p, gv in enumerate(grads):
-        for q in range(2):
-            conv(q, p, gv)
+    for q in range(2):
+        conv(q)
     for p, gv in enumerate(grads):
         for hh in range(2):
             right_row(gv, p, hh)
@@ -774,7 +777,7 @@
     )
     order = [rg2]
     for mask in along_cols:
-        part = join(part, mask, F32, after=order, us=4.0)
+        part = join(part, mask, BF16, after=order, us=4.0)
         order = []
     output, conv_done = call(
         functools.partial(conv_kernel, masks, groups),
@@ -783,7 +786,7 @@
             pltpu.VMEM((disp // 2 + 1, 2, cols, 3 * rows * SLOT), BF16),
             pltpu.VMEM((rows // 2, disp, total, 128), F32),
             pltpu.VMEM((disp, rows, feat, cols), BF16),
-            pltpu.SemaphoreType.DMA((3,)),
+            pltpu.SemaphoreType.DMA((2,)),
         ],
         vbuf, vtop, vbot, wc,
         after=[part],

time: 40.6 us -> 40.6 us (level)
  waiting for transfers between devices: 6.07 us -> 5.25 us
  Pallas kernels: 13.6 us -> 14.4 us
    ppermute x10, waiting for transfers between devices: 4.77 us -> 3.95 us  [swap(): return lax.ppermute(block, ('row', 'col'), route)]
    pallas_call x17, Pallas kernels: 13.6 us -> 14.4 us  [call(): pl.pallas_call(lambda *refs: kernel(*refs[skip:]), out_shape=[jax.ShapeDt...]
  transfers between devices with their start and end apart: 16 -> 16, of which waited for: 7 -> 5; matrix products, arithmetic and copies ran while one was open for 0% -> 0% of each run, Pallas kernels for 31% -> 33%
where the time goes in v7:
time: 40.6 us; the launch traced here: 40.3 us
  starting transfers between devices  19.8 us (49%)
  Pallas kernels  14.4 us (35%)
  waiting for transfers between devices  5.25 us (13%)
  between operations  0.87 us (2%)
    pallas_call x17, Pallas kernels, call(): pl.pallas_call(lambda *refs: kernel(*refs[skip:]), out_shape=[jax.ShapeDt...  14.4 us
    ppermute x10, starting transfers between devices, swap(): return lax.ppermute(block, ('row', 'col'), route)  9.6 us
    ppermute x2, starting transfers between devices, col_shift(): return lax.ppermute(block, 'col', route)  6.31 us
    ppermute x10, waiting for transfers between devices, swap(): return lax.ppermute(block, ('row', 'col'), route)  3.95 us
    ppermute x3, starting transfers between devices, halos(): got = lax.ppermute(pays[0], 'row', [(0, 1), (1, 0)])  3.25 us
    ppermute x2, waiting for transfers between devices, col_shift(): return lax.ppermute(block, 'col', route)  1.29 us
  transfers between devices with their start and end apart: 16, of which 5 were waited for; matrix products, arithmetic and copies ran while one was open for 0% of the time, Pallas kernels for 33%

profile of v7, /device:TPU:0, one launch (start us, length us, event | category | flops | bytes accessed | tf_op | source)
XLA Modules:
  0.0 40.3 jit_solution(1343893564865500174)
XLA Ops:
  0.6 0.0 copy-start
  0.6 0.0 copy-start.3
  0.7 0.0 copy-start.2
  0.7 5.0 %collective-permute-start = (bf16[4,64,320]{2,1,0:T(8,128)(2,1)}, bf16[4,64,320]{2,1,0:T(8,128)(2,1)S(1)}, u32[]{:S(2)}, u32[]{:S(2)}) collective-permute-start(bf16[4,64,320]{2,1,0:T(8,128)(2,1)} %refs_1_.5), channel_id=1, source_target_pairs={{0,2},{1,3},{2,4},{3,5},{4,6},{5,7},{6,8},{7,9},{8,10},{9,11},{10,... | collective-permute-start | bytes 491528 | tf_op jit(solution)/shard_map/ppermute | solution.py:612
  5.7 0.0 copy-done
  5.7 0.0 copy-done.3
  5.7 0.0 copy-done.2
  5.7 0.3 shard_map.76
  6.1 0.1 collective-permute-start.2
  6.1 0.7 %collective-permute-start.3 = (bf16[32,320]{1,0:T(8,128)(2,1)S(1)}, bf16[32,320]{1,0:T(8,128)(2,1)S(1)}, u32[]{:S(2)}, u32[]{:S(2)}) collective-permute-start(bf16[32,320]{1,0:T(8,128)(2,1)S(1)} %get-tuple-element.34), channel_id=1, source_target_pairs={{1,2},{3,4},{5,6},{7,8},{9,10},{11,12},{13,14},{2,1},{4,3},{6,5},{... | collective-permute-start | bytes 61448 | tf_op jit(solution)/shard_map/ppermute | solution.py:684
  6.8 1.6 %collective-permute-start.4 = (bf16[6,64,128]{2,1,0:T(8,128)(2,1)S(1)}, bf16[6,64,128]{2,1,0:T(8,128)(2,1)S(1)}, u32[]{:S(2)}, u32[]{:S(2)}) collective-permute-start(bf16[6,64,128]{2,1,0:T(8,128)(2,1)S(1)} %get-tuple-element.38), channel_id=1, source_target_pairs={{0,16},{16,0},{1,17},{17,1},{2,18},{18,2},{3,19},{19,3},{4,20},{20... | collective-permute-start | bytes 294920 | tf_op jit(solution)/shard_map/ppermute | solution.py:623
  8.4 0.5 %shard_map.77 = (f32[4,80,512]{2,1,0:T(8,128)S(1)}, f32[4,176,512]{2,1,0:T(8,128)S(1)}, f32[4,176,512]{2,1,0:T(8,128)S(1)}) custom-call(bf16[24,64,128]{2,1,0:T(8,128)(2,1)S(1)} %get-tuple-element.31.refs_0_.refs_1_, bf16[4,64,320]{2,1,0:T(8,128)(2,1)S(1)} %copy-done.2, bf16[4,64,320]{2,1,0:T(8,128)(2,1)S(1)} %copy-done), custom_call_target="tpu_custom_call" | custom-call | tf_op jit(solution)/shard_map/pallas_call | solution.py:595
  8.8 1.3 %collective-permute-done.refs_2_.refs_1_ = bf16[4,64,320]{2,1,0:T(8,128)(2,1)S(1)} collective-permute-done((bf16[4,64,320]{2,1,0:T(8,128)(2,1)}, bf16[4,64,320]{2,1,0:T(8,128)(2,1)S(1)}, u32[]{:S(2)}, u32[]{:S(2)}) %collective-permute-start) | collective-permute-done | bytes 163872 | tf_op jit(solution)/shard_map/ppermute | solution.py:612
  10.1 0.1 shard_map.78.refs_0_
  10.2 1.4 %collective-permute-start.1 = (bf16[4,64,320]{2,1,0:T(8,128)(2,1)S(1)}, bf16[4,64,320]{2,1,0:T(8,128)(2,1)S(1)}, u32[]{:S(2)}, u32[]{:S(2)}) collective-permute-start(bf16[4,64,320]{2,1,0:T(8,128)(2,1)S(1)} %shard_map.78.refs_0_), channel_id=1, source_target_pairs={{0,1},{1,0},{2,3},{3,2},{4,5},{5,4},{6,7},{7,6},{8,9},{9,8},{10,11... | collective-permute-start | bytes 491528 | tf_op jit(solution)/shard_map/ppermute | solution.py:663
  11.6 0.0 collective-permute-done.2.refs_2_.refs_1_
  11.6 0.0 collective-permute-done.3.refs_3_.refs_2_
  11.6 0.1 shard_map.80
  11.7 0.6 %collective-permute-start.5 = (bf16[16,128]{1,0:T(8,128)(2,1)S(1)}, bf16[16,128]{1,0:T(8,128)(2,1)S(1)}, u32[]{:S(2)}, u32[]{:S(2)}) collective-permute-start(bf16[16,128]{1,0:T(8,128)(2,1)S(1)} %shard_map.80), channel_id=1, source_target_pairs={{0,16},{16,0},{1,17},{17,1},{2,18},{18,2},{3,19},{19,3},{4,20},{20... | collective-permute-start | bytes 12296 | tf_op jit(solution)/shard_map/ppermute | solution.py:623
  12.2 0.4 %collective-permute-done.1.refs_0_ = bf16[4,64,320]{2,1,0:T(8,128)(2,1)S(1)} collective-permute-done((bf16[4,64,320]{2,1,0:T(8,128)(2,1)S(1)}, bf16[4,64,320]{2,1,0:T(8,128)(2,1)S(1)}, u32[]{:S(2)}, u32[]{:S(2)}) %collective-permute-start.1) | collective-permute-done | bytes 163872 | tf_op jit(solution)/shard_map/ppermute | solution.py:663
  12.6 2.1 %shard_map.79 = (f32[4,80,512]{2,1,0:T(8,128)S(1)}, f32[4,176,512]{2,1,0:T(8,128)S(1)}, f32[4,176,512]{2,1,0:T(8,128)S(1)}, f32[2,24,80,128]{3,2,1,0:T(8,128)S(1)}, bf16[960,128]{1,0:T(8,128)(2,1)S(1)}) custom-call(bf16[4,64,320]{2,1,0:T(8,128)(2,1)S(1)} %collective-permute-done.1.refs_0_, ...), custom_call_target="tpu_custom_call", output_to_operand_aliasing={{0}: (4, {}), {1}: (5, {}), {2}: (6, {})} | custom-call | flops 2070000000 | bytes 6660000 | tf_op jit(solution)/shard_map/pallas_call | solution.py:595
  14.7 1.1 %collective-permute-start.7 = (bf16[960,128]{1,0:T(8,128)(2,1)S(1)}, bf16[960,128]{1,0:T(8,128)(2,1)S(1)}, u32[]{:S(2)}, u32[]{:S(2)}) collective-permute-start(bf16[960,128]{1,0:T(8,128)(2,1)S(1)} %get-tuple-element.45), channel_id=1, source_target_pairs={{0,16},{16,0},{1,17},{17,1},{2,18},{18,2},{3,19},{19,3},{4,20},{20... | collective-permute-start | bytes 737288 | tf_op jit(solution)/shard_map/ppermute | solution.py:623
  15.9 0.0 collective-permute-done.4.refs_4_.refs_5_
  15.9 0.0 collective-permute-done.5.refs_6_.refs_7_
  15.9 0.0 copy-start.1
  15.9 1.9 %shard_map.81 = (f32[192,128]{1,0:T(8,128)S(1)}, f32[192,128]{1,0:T(8,128)S(1)}, bf16[13,2,64,768]{3,2,1,0:T(8,128)(2,1)S(1)}) custom-call(f32[2,24,80,128]{3,2,1,0:T(8,128)S(1)} %get-tuple-element.37.refs_0_.refs_1_, bf16[24,64,128]{2,1,0:T(8,128)(2,1)S(1)} %get-tuple-element.31.refs_0_.refs_1_, bf16[32,320]{1,0:T(8,128)(2,1)S(1)} %collective-permute-done.2.refs_2_.refs_1_, ...), custom_call_target="tpu_custom_call" | custom-call | flops 2300000000 | bytes 7400000 | tf_op jit(solution)/shard_map/pallas_call | solution.py:595
  17.8 0.1 collective-permute-start.6
  17.9 0.0 copy-done.1
  17.9 0.8 %shard_map.82 = (bf16[1536,256]{1,0:T(8,128)(2,1)S(1)}, bf16[3072,256]{1,0:T(8,128)(2,1)S(1)}) custom-call(f32[192,128]{1,0:T(8,128)S(1)} %get-tuple-element.39.refs_0_.refs_1_, bf16[3,3,3,32,40]{4,3,2,1,0:T(8,128)(2,1)S(1)} %bitcast.4), custom_call_target="tpu_custom_call" | custom-call | tf_op jit(solution)/shard_map/pallas_call | solution.py:595
  18.7 0.4 %collective-permute-done.6.refs_2_ = f32[192,128]{1,0:T(8,128)S(1)} collective-permute-done((f32[192,128]{1,0:T(8,128)S(1)}, f32[192,128]{1,0:T(8,128)S(1)}, u32[]{:S(2)}, u32[]{:S(2)}) %collective-permute-start.6) | collective-permute-done | bytes 98336 | tf_op jit(solution)/shard_map/ppermute | solution.py:663
  19.2 2.9 %collective-permute-start.10 = (bf16[192,128]{1,0:T(8,128)(2,1)S(1)}, bf16[192,128]{1,0:T(8,128)(2,1)S(1)}, u32[]{:S(2)}, u32[]{:S(2)}) collective-permute-start(bf16[192,128]{1,0:T(8,128)(2,1)S(1)} %shard_map.83.refs_0_.refs_2_), channel_id=1, source_target_pairs={{0,6},{1,7},{2,4},{3,5},{4,2},{5,3},{6,0},{7,1},{8,14},{9,15},{10,... | collective-permute-start | bytes 147464 | tf_op jit(solution)/shard_map/ppermute | solution.py:663
  22.1 1.4 %collective-permute-start.8 = (bf16[192,128]{1,0:T(8,128)(2,1)S(1)}, bf16[192,128]{1,0:T(8,128)(2,1)S(1)}, u32[]{:S(2)}, u32[]{:S(2)}) collective-permute-start(bf16[192,128]{1,0:T(8,128)(2,1)S(1)} %shard_map.83.refs_0_.refs_2_), channel_id=1, source_target_pairs={{0,2},{1,3},{2,0},{3,1},{4,6},{5,7},{6,4},{7,5},{8,10},{9,11},{10,... | collective-permute-start | bytes 147464 | tf_op jit(solution)/shard_map/ppermute | solution.py:663
  23.5 0.0 collective-permute-start.9
  23.5 2.8 %shard_map.84 = (f32[2,24,64,128]{3,2,1,0:T(8,128)S(1)}, f32[2,24,64,128]{3,2,1,0:T(8,128)S(1)}, bf16[4,64,320]{2,1,0:T(8,128)(2,1)S(1)}, bf16[4,64,320]{2,1,0:T(8,128)(2,1)S(1)}, bf16[4,32,320]{2,1,0:T(8,128)(2,1)S(1)}) custom-call(bf16[192,128]{1,0:T(8,128)(2,1)S(1)} %shard_map.83.refs_0_.refs_2_, bf16[13,2,64,768]{3,2,1,0:T(8,128)(2,1)S(1)} %get-tuple-element.42.refs_1_, ...), custom_call_target="tpu_custom_call" | custom-call | flops 460000000 | bytes 1480000 | tf_op jit(solution)/shard_map/pallas_call | solution.py:595
  26.4 0.1 collective-permute-start.11
  26.4 0.0 collective-permute-done.10.refs_5_
  26.5 0.0 collective-permute-done.8.refs_3_
  26.5 1.1 %collective-permute-done.9.refs_4_ = bf16[192,128]{1,0:T(8,128)(2,1)S(1)} collective-permute-done((bf16[192,128]{1,0:T(8,128)(2,1)S(1)}, bf16[192,128]{1,0:T(8,128)(2,1)S(1)}, u32[]{:S(2)}, u32[]{:S(2)}) %collective-permute-start.9) | collective-permute-done | bytes 49184 | tf_op jit(solution)/shard_map/ppermute | solution.py:663
  27.6 0.0 collective-permute-done.7.refs_1_.refs_2_.refs_3_
  27.6 2.7 %collective-permute-start.12 = (bf16[192,128]{1,0:T(8,128)(2,1)S(1)}, bf16[192,128]{1,0:T(8,128)(2,1)S(1)}, u32[]{:S(2)}, u32[]{:S(2)}) collective-permute-start(bf16[192,128]{1,0:T(8,128)(2,1)S(1)} %shard_map.85.refs_0_.refs_1_), channel_id=1, source_target_pairs={{0,8},{1,9},{2,10},{3,11},{4,12},{5,13},{6,14},{7,15},{8,0},{9,1},... | collective-permute-start | bytes 147464 | tf_op jit(solution)/shard_map/ppermute | solution.py:663
  30.3 0.0 collective-permute-done.11.refs_1_.refs_3_
  30.3 0.1 shard_map.86.refs_0_
  30.4 1.3 %collective-permute-start.15 = (bf16[4,64,320]{2,1,0:T(8,128)(2,1)S(1)}, bf16[4,64,320]{2,1,0:T(8,128)(2,1)S(1)}, u32[]{:S(2)}, u32[]{:S(2)}) collective-permute-start(bf16[4,64,320]{2,1,0:T(8,128)(2,1)S(1)} %shard_map.86.refs_0_), channel_id=1, source_target_pairs={{2,0},{3,1},{4,2},{5,3},{6,4},{7,5},{8,6},{9,7},{10,8},{11,9},{12,... | collective-permute-start | bytes 491528 | tf_op jit(solution)/shard_map/ppermute | solution.py:612
  31.7 1.9 %collective-permute-done.12.refs_2_ = bf16[192,128]{1,0:T(8,128)(2,1)S(1)} collective-permute-done((bf16[192,128]{1,0:T(8,128)(2,1)S(1)}, bf16[192,128]{1,0:T(8,128)(2,1)S(1)}, u32[]{:S(2)}, u32[]{:S(2)}) %collective-permute-start.12) | collective-permute-done | bytes 49184 | tf_op jit(solution)/shard_map/ppermute | solution.py:663
  33.6 0.9 %collective-permute-start.13 = (bf16[192,128]{1,0:T(8,128)(2,1)S(1)}, bf16[192,128]{1,0:T(8,128)(2,1)S(1)}, u32[]{:S(2)}, u32[]{:S(2)}) collective-permute-start(bf16[192,128]{1,0:T(8,128)(2,1)S(1)} %shard_map.87.refs_0_.refs_1_), channel_id=1, source_target_pairs={{0,16},{1,17},{2,18},{3,19},{4,20},{5,21},{6,22},{7,23},{8,24},{9,... | collective-permute-start | bytes 147464 | tf_op jit(solution)/shard_map/ppermute | solution.py:663
  34.5 3.3 %shard_map.88 = (bf16[24,4,32,64]{3,2,1,0:T(8,128)(2,1)}, f32[8,128]{1,0:T(8,128)S(1)}) custom-call(bf16[192,128]{1,0:T(8,128)(2,1)S(1)} %shard_map.87.refs_0_.refs_1_, f32[2,24,80,128]{3,2,1,0:T(8,128)S(1)} %get-tuple-element.37.refs_0_.refs_1_, bf16[960,128]{1,0:T(8,128)(2,1)S(1)} %collective-permute-done.7.refs_1_.refs_2_.refs_3_, ...), custom_call_target="tpu_custom_call" | custom-call | flops 3449999872 | bytes 11100000 | tf_op jit(solution)/shard_map/pallas_call | solution.py:595
  37.8 0.0 collective-permute-done.13.refs_2_
  37.9 0.1 collective-permute-start.14
  37.9 1.3 %shard_map.90.refs_5_ = bf16[4,64,320]{2,1,0:T(8,128)(2,1)S(1)} custom-call(f32[192,128]{1,0:T(8,128)S(1)} %shard_map.89.refs_0_, f32[4,176,512]{2,1,0:T(8,128)S(1)} %get-tuple-element.51.refs_1_, f32[4,176,512]{2,1,0:T(8,128)S(1)} %get-tuple-element.52.refs_2_, f32[2,24,64,128]{3,2,1,0:T(8,128)S(1)} %get-tuple-element.53.refs_3_, ...), custom_call_target="tpu_custom_call" | custom-call | flops 2184999936 | bytes 7030000 | tf_op jit(solution)/shard_map/pallas_call | solution.py:595
  39.2 0.0 collective-permute-done.15.refs_4_
  39.2 0.0 collective-permute-done.14.refs_1_
  39.3 1.1 %shard_map.91 = (f32[3,3,3,32,40]{4,3,2,1,0:T(8,128)}, bf16[4,64,320]{2,1,0:T(8,128)(2,1)}, bf16[4,64,320]{2,1,0:T(8,128)(2,1)}) custom-call(f32[192,128]{1,0:T(8,128)S(1)} %shard_map.89.refs_0_, f32[192,128]{1,0:T(8,128)S(1)} %collective-permute-done.14.refs_1_, bf16[4,64,320]{2,1,0:T(8,128)(2,1)S(1)} %get-tuple-element.44.refs_0_.refs_2_, ...), custom_call_target="tpu_custom_call" | custom-call | flops 1150000000 | bytes 3700000 | tf_op jit(solution)/shard_map/pallas_call | solution.py:595
  (5 shorter events, 0.1 us)
Async XLA Ops:
  0.6 5.1 %copy-start = (bf16[4,64,320]{2,1,0:T(8,128)(2,1)S(1)}, bf16[4,64,320]{2,1,0:T(8,128)(2,1)}, u32[]{:S(2)}) copy-start(bf16[4,64,320]{2,1,0:T(8,128)(2,1)} %refs_1_.5) | copy-start | bytes 491524
  0.6 5.1 %copy-start.3 = (bf16[24,4,64,32]{2,3,1,0:T(8,128)(2,1)S(1)}, bf16[24,4,64,32]{2,3,1,0:T(8,128)(2,1)}, u32[]{:S(2)}) copy-start(bf16[24,4,64,32]{2,3,1,0:T(8,128)(2,1)} %param.7) | copy-start | bytes 1179652
  0.7 5.1 %copy-start.2 = (bf16[4,64,320]{2,1,0:T(8,128)(2,1)S(1)}, bf16[4,64,320]{2,1,0:T(8,128)(2,1)}, u32[]{:S(2)}) copy-start(bf16[4,64,320]{2,1,0:T(8,128)(2,1)} %refs_1_.4) | copy-start | bytes 491524
  0.7 9.5 %collective-permute-start = (bf16[4,64,320]{2,1,0:T(8,128)(2,1)}, bf16[4,64,320]{2,1,0:T(8,128)(2,1)S(1)}, u32[]{:S(2)}, u32[]{:S(2)}) collective-permute-start(bf16[4,64,320]{2,1,0:T(8,128)(2,1)} %refs_1_.5), channel_id=1, source_target_pairs={{0,2},{1,3},{2,4},{3,5},{4,6},{5,7},{6,8},{7,9},{8,10},{9,11},{10,... | collective-permute-start | bytes 491528 | tf_op jit(solution)/shard_map/ppermute | solution.py:612
  6.1 5.5 %collective-permute-start.2 = (bf16[32,320]{1,0:T(8,128)(2,1)S(1)}, bf16[32,320]{1,0:T(8,128)(2,1)S(1)}, u32[]{:S(2)}, u32[]{:S(2)}) collective-permute-start(bf16[32,320]{1,0:T(8,128)(2,1)S(1)} %get-tuple-element.33), channel_id=1, source_target_pairs={{0,1},{1,0},{2,3},{3,2},{4,5},{5,4},{6,7},{7,6},{8,9},{9,8},{10,11... | collective-permute-start | bytes 61448 | tf_op jit(solution)/shard_map/ppermute | solution.py:663
  6.1 5.4 %collective-permute-start.3 = (bf16[32,320]{1,0:T(8,128)(2,1)S(1)}, bf16[32,320]{1,0:T(8,128)(2,1)S(1)}, u32[]{:S(2)}, u32[]{:S(2)}) collective-permute-start(bf16[32,320]{1,0:T(8,128)(2,1)S(1)} %get-tuple-element.34), channel_id=1, source_target_pairs={{1,2},{3,4},{5,6},{7,8},{9,10},{11,12},{13,14},{2,1},{4,3},{6,5},{... | collective-permute-start | bytes 61448 | tf_op jit(solution)/shard_map/ppermute | solution.py:684
  6.8 9.1 %collective-permute-start.4 = (bf16[6,64,128]{2,1,0:T(8,128)(2,1)S(1)}, bf16[6,64,128]{2,1,0:T(8,128)(2,1)S(1)}, u32[]{:S(2)}, u32[]{:S(2)}) collective-permute-start(bf16[6,64,128]{2,1,0:T(8,128)(2,1)S(1)} %get-tuple-element.38), channel_id=1, source_target_pairs={{0,16},{16,0},{1,17},{17,1},{2,18},{18,2},{3,19},{19,3},{4,20},{20... | collective-permute-start | bytes 294920 | tf_op jit(solution)/shard_map/ppermute | solution.py:623
  10.2 2.5 %collective-permute-start.1 = (bf16[4,64,320]{2,1,0:T(8,128)(2,1)S(1)}, bf16[4,64,320]{2,1,0:T(8,128)(2,1)S(1)}, u32[]{:S(2)}, u32[]{:S(2)}) collective-permute-start(bf16[4,64,320]{2,1,0:T(8,128)(2,1)S(1)} %shard_map.78.refs_0_), channel_id=1, source_target_pairs={{0,1},{1,0},{2,3},{3,2},{4,5},{5,4},{6,7},{7,6},{8,9},{9,8},{10,11... | collective-permute-start | bytes 491528 | tf_op jit(solution)/shard_map/ppermute | solution.py:663
  11.7 4.2 %collective-permute-start.5 = (bf16[16,128]{1,0:T(8,128)(2,1)S(1)}, bf16[16,128]{1,0:T(8,128)(2,1)S(1)}, u32[]{:S(2)}, u32[]{:S(2)}) collective-permute-start(bf16[16,128]{1,0:T(8,128)(2,1)S(1)} %shard_map.80), channel_id=1, source_target_pairs={{0,16},{16,0},{1,17},{17,1},{2,18},{18,2},{3,19},{19,3},{4,20},{20... | collective-permute-start | bytes 12296 | tf_op jit(solution)/shard_map/ppermute | solution.py:623
  14.7 12.9 %collective-permute-start.7 = (bf16[960,128]{1,0:T(8,128)(2,1)S(1)}, bf16[960,128]{1,0:T(8,128)(2,1)S(1)}, u32[]{:S(2)}, u32[]{:S(2)}) collective-permute-start(bf16[960,128]{1,0:T(8,128)(2,1)S(1)} %get-tuple-element.45), channel_id=1, source_target_pairs={{0,16},{16,0},{1,17},{17,1},{2,18},{18,2},{3,19},{19,3},{4,20},{20... | collective-permute-start | bytes 737288 | tf_op jit(solution)/shard_map/ppermute | solution.py:623
  15.9 2.0 %copy-start.1 = (bf16[3,3,3,40,32]{3,4,2,1,0:T(8,128)(2,1)S(1)}, bf16[3,3,3,40,32]{3,4,2,1,0:T(8,128)(2,1)}, u32[]{:S(2)}) copy-start(bf16[3,3,3,40,32]{3,4,2,1,0:T(8,128)(2,1)} %param.6) | copy-start | bytes 207364
  17.8 1.4 %collective-permute-start.6 = (f32[192,128]{1,0:T(8,128)S(1)}, f32[192,128]{1,0:T(8,128)S(1)}, u32[]{:S(2)}, u32[]{:S(2)}) collective-permute-start(f32[192,128]{1,0:T(8,128)S(1)} %get-tuple-element.41), channel_id=1, source_target_pairs={{0,1},{1,0},{2,3},{3,2},{4,5},{5,4},{6,7},{7,6},{8,9},{9,8},{10,11... | collective-permute-start | bytes 294920 | tf_op jit(solution)/shard_map/ppermute | solution.py:663
  19.2 7.3 %collective-permute-start.10 = (bf16[192,128]{1,0:T(8,128)(2,1)S(1)}, bf16[192,128]{1,0:T(8,128)(2,1)S(1)}, u32[]{:S(2)}, u32[]{:S(2)}) collective-permute-start(bf16[192,128]{1,0:T(8,128)(2,1)S(1)} %shard_map.83.refs_0_.refs_2_), channel_id=1, source_target_pairs={{0,6},{1,7},{2,4},{3,5},{4,2},{5,3},{6,0},{7,1},{8,14},{9,15},{10,... | collective-permute-start | bytes 147464 | tf_op jit(solution)/shard_map/ppermute | solution.py:663
  22.1 4.4 %collective-permute-start.8 = (bf16[192,128]{1,0:T(8,128)(2,1)S(1)}, bf16[192,128]{1,0:T(8,128)(2,1)S(1)}, u32[]{:S(2)}, u32[]{:S(2)}) collective-permute-start(bf16[192,128]{1,0:T(8,128)(2,1)S(1)} %shard_map.83.refs_0_.refs_2_), channel_id=1, source_target_pairs={{0,2},{1,3},{2,0},{3,1},{4,6},{5,7},{6,4},{7,5},{8,10},{9,11},{10,... | collective-permute-start | bytes 147464 | tf_op jit(solution)/shard_map/ppermute | solution.py:663
  23.5 4.1 %collective-permute-start.9 = (bf16[192,128]{1,0:T(8,128)(2,1)S(1)}, bf16[192,128]{1,0:T(8,128)(2,1)S(1)}, u32[]{:S(2)}, u32[]{:S(2)}) collective-permute-start(bf16[192,128]{1,0:T(8,128)(2,1)S(1)} %shard_map.83.refs_0_.refs_2_), channel_id=1, source_target_pairs={{0,4},{1,5},{2,6},{3,7},{4,0},{5,1},{6,2},{7,3},{8,12},{9,13},{10,... | collective-permute-start | bytes 147464 | tf_op jit(solution)/shard_map/ppermute | solution.py:663
  26.4 3.9 %collective-permute-start.11 = (bf16[4,64,320]{2,1,0:T(8,128)(2,1)S(1)}, bf16[4,64,320]{2,1,0:T(8,128)(2,1)S(1)}, u32[]{:S(2)}, u32[]{:S(2)}) collective-permute-start(bf16[4,64,320]{2,1,0:T(8,128)(2,1)S(1)} %get-tuple-element.46), channel_id=1, source_target_pairs={{0,1},{1,0},{2,3},{3,2},{4,5},{5,4},{6,7},{7,6},{8,9},{9,8},{10,11... | collective-permute-start | bytes 491528 | tf_op jit(solution)/shard_map/ppermute | solution.py:663
  27.6 6.0 %collective-permute-start.12 = (bf16[192,128]{1,0:T(8,128)(2,1)S(1)}, bf16[192,128]{1,0:T(8,128)(2,1)S(1)}, u32[]{:S(2)}, u32[]{:S(2)}) collective-permute-start(bf16[192,128]{1,0:T(8,128)(2,1)S(1)} %shard_map.85.refs_0_.refs_1_), channel_id=1, source_target_pairs={{0,8},{1,9},{2,10},{3,11},{4,12},{5,13},{6,14},{7,15},{8,0},{9,1},... | collective-permute-start | bytes 147464 | tf_op jit(solution)/shard_map/ppermute | solution.py:663
  30.4 8.9 %collective-permute-start.15 = (bf16[4,64,320]{2,1,0:T(8,128)(2,1)S(1)}, bf16[4,64,320]{2,1,0:T(8,128)(2,1)S(1)}, u32[]{:S(2)}, u32[]{:S(2)}) collective-permute-start(bf16[4,64,320]{2,1,0:T(8,128)(2,1)S(1)} %shard_map.86.refs_0_), channel_id=1, source_target_pairs={{2,0},{3,1},{4,2},{5,3},{6,4},{7,5},{8,6},{9,7},{10,8},{11,9},{12,... | collective-permute-start | bytes 491528 | tf_op jit(solution)/shard_map/ppermute | solution.py:612
  33.6 4.2 %collective-permute-start.13 = (bf16[192,128]{1,0:T(8,128)(2,1)S(1)}, bf16[192,128]{1,0:T(8,128)(2,1)S(1)}, u32[]{:S(2)}, u32[]{:S(2)}) collective-permute-start(bf16[192,128]{1,0:T(8,128)(2,1)S(1)} %shard_map.87.refs_0_.refs_1_), channel_id=1, source_target_pairs={{0,16},{1,17},{2,18},{3,19},{4,20},{5,21},{6,22},{7,23},{8,24},{9,... | collective-permute-start | bytes 147464 | tf_op jit(solution)/shard_map/ppermute | solution.py:663
  37.9 1.4 %collective-permute-start.14 = (f32[192,128]{1,0:T(8,128)S(1)}, f32[192,128]{1,0:T(8,128)S(1)}, u32[]{:S(2)}, u32[]{:S(2)}) collective-permute-start(f32[192,128]{1,0:T(8,128)S(1)} %shard_map.89.refs_0_), channel_id=1, source_target_pairs={{0,1},{1,0},{2,3},{3,2},{4,5},{5,4},{6,7},{7,6},{8,9},{9,8},{10,11... | collective-permute-start | bytes 294920 | tf_op jit(solution)/shard_map/ppermute | solution.py:663

commit v8 on v6

--- a/solution.py
+++ b/solution.py
@@ -268,33 +268,26 @@
         fill(q)
         fill(q + half // per)
         first, size = q * per, per * 128
-        left = jnp.concatenate(
-            [
-                jnp.concatenate(
-                    [vt[p, :, 128 * (2 - a + first) : 128 * (2 - a + first) + size] for p in range(pairs)],
-                    axis=1,
-                )
-                for a in range(3)
-            ],
-            axis=0,
-        )
-        right = jnp.concatenate(
-            [
-                jnp.concatenate(
-                    [
-                        ctsh[(d + 1) // 2, (d + 1) % 2, :, 256 * e + 128 * p : 256 * e + 128 * (p + 1)]
-                        for e in range(3)
-                    ],
-                    axis=1,
-                )
-                for p in range(pairs)
-                for j in range(first, first + per)
-                for d in (j, j + half)
-            ],
-            axis=0,
-        )
-        part = dot(left, right)
-        full = part if full is None else full + part
+        for p in range(pairs):
+            left = jnp.concatenate(
+                [vt[p, :, 128 * (2 - a + first) : 128 * (2 - a + first) + size] for a in range(3)], axis=0
+            )
+            right = jnp.concatenate(
+                [
+                    jnp.concatenate(
+                        [
+                            ctsh[(d + 1) // 2, (d + 1) % 2, :, 256 * e + 128 * p : 256 * e + 128 * (p + 1)]
+                            for e in range(3)
+                        ],
+                        axis=1,
+                    )
+                    for j in range(first, first + per)
+                    for d in (j, j + half)
+                ],
+                axis=0,
+            )
+            part = dot(left, right)
+            full = part if full is None else full + part
     keep = lanes((groups, 128)) < 3 * feat
     sums[...] = jnp.zeros(sums.shape, F32)
     for a in range(3):
@@ -315,12 +308,12 @@
     rows, cols, channels = rg0.shape
     disp, wide = grads[0].shape[1], fl.shape[2]
     group_size = wide // SLOT
-    step = disp // 4
+    step = disp // 8
     low = lanes((step * cols, 128)) < SLOT
 
     def conv(q, p, gv):
         slabs = [
-            ctsh[pl.ds(q * step + s // 2, step), s % 2, :, 256 * e + 128 * p : 256 * e + 128 * (p + 1)]
+            ctsh[q * step + s // 2 : q * step + s // 2 + step, s % 2, :, 256 * e + 128 * p : 256 * e + 128 * (p + 1)]
             for s in range(4)
             for e in range(3)
         ]
@@ -362,12 +355,14 @@
                     buf[h, 8 * k : 8 * k + 8, 128 * j : 128 * (j + 1)] = x
         acco[h, 8 * (lead + count) :] = jnp.zeros((8, wide), F32)
 
+    parts = disp // 2 // step
     for p, gv in enumerate(grads):
-        for q in range(2):
+        for q in range(parts):
             conv(q, p, gv)
-    for p, gv in enumerate(grads):
-        for hh in range(2):
-            right_row(gv, p, hh)
+            if p and q % 2:
+                right_row(grads[p - 1], p - 1, q // 2)
+    for hh in range(2):
+        right_row(grads[-1], len(grads) - 1, hh)
     size = back + cols
     for h in range(rows):
         both[h * size : (h + 1) * size] = (acce[h] + acco[h, STEP : STEP + size]).astype(BF16)
@@ -774,7 +769,7 @@
     )
     order = [rg2]
     for mask in along_cols:
-        part = join(part, mask, F32, after=order, us=4.0)
+        part = join(part, mask, BF16, after=order, us=4.0)
         order = []
     output, conv_done = call(
         functools.partial(conv_kernel, masks, groups),
@@ -783,7 +778,7 @@
             pltpu.VMEM((disp // 2 + 1, 2, cols, 3 * rows * SLOT), BF16),
             pltpu.VMEM((rows // 2, disp, total, 128), F32),
             pltpu.VMEM((disp, rows, feat, cols), BF16),
-            pltpu.SemaphoreType.DMA((3,)),
+            pltpu.SemaphoreType.DMA((4,)),
         ],
         vbuf, vtop, vbot, wc,
         after=[part],

time: 40.6 us -> 40.2 us (level)
  waiting for transfers between devices: 6.07 us -> 5.65 us
    ppermute x10, waiting for transfers between devices: 4.77 us -> 4.34 us  [swap(): return lax.ppermute(block, ('row', 'col'), route)]
  transfers between devices with their start and end apart: 16 -> 16, of which waited for: 7 -> 6; matrix products, arithmetic and copies ran while one was open for 0% -> 0% of each run, Pallas kernels for 31% -> 31%
where the time goes in v8:
time: 40.2 us; the launch traced here: 39.9 us
  starting transfers between devices  19.8 us (49%)
  Pallas kernels  13.6 us (34%)
  waiting for transfers between devices  5.65 us (14%)
  between operations  0.85 us (2%)
    pallas_call x17, Pallas kernels, call(): pl.pallas_call(lambda *refs: kernel(*refs[skip:]), out_shape=[jax.ShapeDt...  13.6 us
    ppermute x10, starting transfers between devices, swap(): return lax.ppermute(block, ('row', 'col'), route)  9.6 us
    ppermute x2, starting transfers between devices, col_shift(): return lax.ppermute(block, 'col', route)  6.31 us
    ppermute x10, waiting for transfers between devices, swap(): return lax.ppermute(block, ('row', 'col'), route)  4.34 us
    ppermute x3, starting transfers between devices, halos(): got = lax.ppermute(pays[0], 'row', [(0, 1), (1, 0)])  3.25 us
    ppermute x2, waiting for transfers between devices, col_shift(): return lax.ppermute(block, 'col', route)  1.29 us
  transfers between devices with their start and end apart: 16, of which 6 were waited for; matrix products, arithmetic and copies ran while one was open for 0% of the time, Pallas kernels for 31%

profile of v8, /device:TPU:0, one launch (start us, length us, event | category | flops | bytes accessed | tf_op | source)
XLA Modules:
  0.0 39.9 jit_solution(11449455350048885705)
XLA Ops:
  0.6 0.0 copy-start
  0.6 0.0 copy-start.3
  0.7 0.0 copy-start.2
  0.7 5.0 %collective-permute-start = (bf16[4,64,320]{2,1,0:T(8,128)(2,1)}, bf16[4,64,320]{2,1,0:T(8,128)(2,1)S(1)}, u32[]{:S(2)}, u32[]{:S(2)}) collective-permute-start(bf16[4,64,320]{2,1,0:T(8,128)(2,1)} %refs_1_.5), channel_id=1, source_target_pairs={{0,2},{1,3},{2,4},{3,5},{4,6},{5,7},{6,8},{7,9},{8,10},{9,11},{10,... | collective-permute-start | bytes 491528 | tf_op jit(solution)/shard_map/ppermute | solution.py:604
  5.7 0.0 copy-done
  5.7 0.0 copy-done.3
  5.7 0.0 copy-done.2
  5.7 0.3 shard_map.76
  6.1 0.1 collective-permute-start.2
  6.1 0.7 %collective-permute-start.3 = (bf16[32,320]{1,0:T(8,128)(2,1)S(1)}, bf16[32,320]{1,0:T(8,128)(2,1)S(1)}, u32[]{:S(2)}, u32[]{:S(2)}) collective-permute-start(bf16[32,320]{1,0:T(8,128)(2,1)S(1)} %get-tuple-element.34), channel_id=1, source_target_pairs={{1,2},{3,4},{5,6},{7,8},{9,10},{11,12},{13,14},{2,1},{4,3},{6,5},{... | collective-permute-start | bytes 61448 | tf_op jit(solution)/shard_map/ppermute | solution.py:676
  6.8 1.6 %collective-permute-start.4 = (bf16[6,64,128]{2,1,0:T(8,128)(2,1)S(1)}, bf16[6,64,128]{2,1,0:T(8,128)(2,1)S(1)}, u32[]{:S(2)}, u32[]{:S(2)}) collective-permute-start(bf16[6,64,128]{2,1,0:T(8,128)(2,1)S(1)} %get-tuple-element.38), channel_id=1, source_target_pairs={{0,16},{16,0},{1,17},{17,1},{2,18},{18,2},{3,19},{19,3},{4,20},{20... | collective-permute-start | bytes 294920 | tf_op jit(solution)/shard_map/ppermute | solution.py:615
  8.4 0.5 %shard_map.77 = (f32[4,80,512]{2,1,0:T(8,128)S(1)}, f32[4,176,512]{2,1,0:T(8,128)S(1)}, f32[4,176,512]{2,1,0:T(8,128)S(1)}) custom-call(bf16[24,64,128]{2,1,0:T(8,128)(2,1)S(1)} %get-tuple-element.31.refs_0_.refs_1_, bf16[4,64,320]{2,1,0:T(8,128)(2,1)S(1)} %copy-done.2, bf16[4,64,320]{2,1,0:T(8,128)(2,1)S(1)} %copy-done), custom_call_target="tpu_custom_call" | custom-call | tf_op jit(solution)/shard_map/pallas_call | solution.py:587
  8.8 1.3 %collective-permute-done.refs_2_.refs_1_ = bf16[4,64,320]{2,1,0:T(8,128)(2,1)S(1)} collective-permute-done((bf16[4,64,320]{2,1,0:T(8,128)(2,1)}, bf16[4,64,320]{2,1,0:T(8,128)(2,1)S(1)}, u32[]{:S(2)}, u32[]{:S(2)}) %collective-permute-start) | collective-permute-done | bytes 163872 | tf_op jit(solution)/shard_map/ppermute | solution.py:604
  10.1 0.1 shard_map.78.refs_0_
  10.2 1.4 %collective-permute-start.1 = (bf16[4,64,320]{2,1,0:T(8,128)(2,1)S(1)}, bf16[4,64,320]{2,1,0:T(8,128)(2,1)S(1)}, u32[]{:S(2)}, u32[]{:S(2)}) collective-permute-start(bf16[4,64,320]{2,1,0:T(8,128)(2,1)S(1)} %shard_map.78.refs_0_), channel_id=1, source_target_pairs={{0,1},{1,0},{2,3},{3,2},{4,5},{5,4},{6,7},{7,6},{8,9},{9,8},{10,11... | collective-permute-start | bytes 491528 | tf_op jit(solution)/shard_map/ppermute | solution.py:655
  11.6 0.0 collective-permute-done.2.refs_2_.refs_1_
  11.6 0.0 collective-permute-done.3.refs_3_.refs_2_
  11.6 0.1 shard_map.80
  11.7 0.6 %collective-permute-start.5 = (bf16[16,128]{1,0:T(8,128)(2,1)S(1)}, bf16[16,128]{1,0:T(8,128)(2,1)S(1)}, u32[]{:S(2)}, u32[]{:S(2)}) collective-permute-start(bf16[16,128]{1,0:T(8,128)(2,1)S(1)} %shard_map.80), channel_id=1, source_target_pairs={{0,16},{16,0},{1,17},{17,1},{2,18},{18,2},{3,19},{19,3},{4,20},{20... | collective-permute-start | bytes 12296 | tf_op jit(solution)/shard_map/ppermute | solution.py:615
  12.2 0.4 %collective-permute-done.1.refs_0_ = bf16[4,64,320]{2,1,0:T(8,128)(2,1)S(1)} collective-permute-done((bf16[4,64,320]{2,1,0:T(8,128)(2,1)S(1)}, bf16[4,64,320]{2,1,0:T(8,128)(2,1)S(1)}, u32[]{:S(2)}, u32[]{:S(2)}) %collective-permute-start.1) | collective-permute-done | bytes 163872 | tf_op jit(solution)/shard_map/ppermute | solution.py:655
  12.6 2.1 %shard_map.79 = (f32[4,80,512]{2,1,0:T(8,128)S(1)}, f32[4,176,512]{2,1,0:T(8,128)S(1)}, f32[4,176,512]{2,1,0:T(8,128)S(1)}, f32[2,24,80,128]{3,2,1,0:T(8,128)S(1)}, bf16[960,128]{1,0:T(8,128)(2,1)S(1)}) custom-call(bf16[4,64,320]{2,1,0:T(8,128)(2,1)S(1)} %collective-permute-done.1.refs_0_, ...), custom_call_target="tpu_custom_call", output_to_operand_aliasing={{0}: (4, {}), {1}: (5, {}), {2}: (6, {})} | custom-call | flops 2070000000 | bytes 6660000 | tf_op jit(solution)/shard_map/pallas_call | solution.py:587
  14.7 1.1 %collective-permute-start.7 = (bf16[960,128]{1,0:T(8,128)(2,1)S(1)}, bf16[960,128]{1,0:T(8,128)(2,1)S(1)}, u32[]{:S(2)}, u32[]{:S(2)}) collective-permute-start(bf16[960,128]{1,0:T(8,128)(2,1)S(1)} %get-tuple-element.45), channel_id=1, source_target_pairs={{0,16},{16,0},{1,17},{17,1},{2,18},{18,2},{3,19},{19,3},{4,20},{20... | collective-permute-start | bytes 737288 | tf_op jit(solution)/shard_map/ppermute | solution.py:615
  15.9 0.0 collective-permute-done.4.refs_4_.refs_5_
  15.9 0.0 collective-permute-done.5.refs_6_.refs_7_
  15.9 0.0 copy-start.1
  15.9 1.9 %shard_map.81 = (f32[192,128]{1,0:T(8,128)S(1)}, f32[192,128]{1,0:T(8,128)S(1)}, bf16[13,2,64,768]{3,2,1,0:T(8,128)(2,1)S(1)}) custom-call(f32[2,24,80,128]{3,2,1,0:T(8,128)S(1)} %get-tuple-element.37.refs_0_.refs_1_, bf16[24,64,128]{2,1,0:T(8,128)(2,1)S(1)} %get-tuple-element.31.refs_0_.refs_1_, bf16[32,320]{1,0:T(8,128)(2,1)S(1)} %collective-permute-done.2.refs_2_.refs_1_, ...), custom_call_target="tpu_custom_call" | custom-call | flops 2300000000 | bytes 7400000 | tf_op jit(solution)/shard_map/pallas_call | solution.py:587
  17.8 0.1 collective-permute-start.6
  17.9 0.0 copy-done.1
  17.9 0.8 %shard_map.82 = (bf16[1536,256]{1,0:T(8,128)(2,1)S(1)}, bf16[3072,256]{1,0:T(8,128)(2,1)S(1)}) custom-call(f32[192,128]{1,0:T(8,128)S(1)} %get-tuple-element.39.refs_0_.refs_1_, bf16[3,3,3,32,40]{4,3,2,1,0:T(8,128)(2,1)S(1)} %bitcast.4), custom_call_target="tpu_custom_call" | custom-call | tf_op jit(solution)/shard_map/pallas_call | solution.py:587
  18.7 0.4 %collective-permute-done.6.refs_2_ = f32[192,128]{1,0:T(8,128)S(1)} collective-permute-done((f32[192,128]{1,0:T(8,128)S(1)}, f32[192,128]{1,0:T(8,128)S(1)}, u32[]{:S(2)}, u32[]{:S(2)}) %collective-permute-start.6) | collective-permute-done | bytes 98336 | tf_op jit(solution)/shard_map/ppermute | solution.py:655
  19.2 2.9 %collective-permute-start.10 = (bf16[192,128]{1,0:T(8,128)(2,1)S(1)}, bf16[192,128]{1,0:T(8,128)(2,1)S(1)}, u32[]{:S(2)}, u32[]{:S(2)}) collective-permute-start(bf16[192,128]{1,0:T(8,128)(2,1)S(1)} %shard_map.83.refs_0_.refs_2_), channel_id=1, source_target_pairs={{0,6},{1,7},{2,4},{3,5},{4,2},{5,3},{6,0},{7,1},{8,14},{9,15},{10,... | collective-permute-start | bytes 147464 | tf_op jit(solution)/shard_map/ppermute | solution.py:655
  22.1 1.4 %collective-permute-start.8 = (bf16[192,128]{1,0:T(8,128)(2,1)S(1)}, bf16[192,128]{1,0:T(8,128)(2,1)S(1)}, u32[]{:S(2)}, u32[]{:S(2)}) collective-permute-start(bf16[192,128]{1,0:T(8,128)(2,1)S(1)} %shard_map.83.refs_0_.refs_2_), channel_id=1, source_target_pairs={{0,2},{1,3},{2,0},{3,1},{4,6},{5,7},{6,4},{7,5},{8,10},{9,11},{10,... | collective-permute-start | bytes 147464 | tf_op jit(solution)/shard_map/ppermute | solution.py:655
  23.5 0.0 collective-permute-start.9
  23.5 2.5 %shard_map.84 = (f32[2,24,64,128]{3,2,1,0:T(8,128)S(1)}, f32[2,24,64,128]{3,2,1,0:T(8,128)S(1)}, bf16[4,64,320]{2,1,0:T(8,128)(2,1)S(1)}, bf16[4,64,320]{2,1,0:T(8,128)(2,1)S(1)}, bf16[4,32,320]{2,1,0:T(8,128)(2,1)S(1)}) custom-call(bf16[192,128]{1,0:T(8,128)(2,1)S(1)} %shard_map.83.refs_0_.refs_2_, bf16[13,2,64,768]{3,2,1,0:T(8,128)(2,1)S(1)} %get-tuple-element.42.refs_1_, ...), custom_call_target="tpu_custom_call" | custom-call | flops 460000000 | bytes 1480000 | tf_op jit(solution)/shard_map/pallas_call | solution.py:587
  26.0 0.1 collective-permute-start.11
  26.1 0.0 collective-permute-done.10.refs_5_
  26.1 0.0 collective-permute-done.8.refs_3_
  26.2 1.4 %collective-permute-done.9.refs_4_ = bf16[192,128]{1,0:T(8,128)(2,1)S(1)} collective-permute-done((bf16[192,128]{1,0:T(8,128)(2,1)S(1)}, bf16[192,128]{1,0:T(8,128)(2,1)S(1)}, u32[]{:S(2)}, u32[]{:S(2)}) %collective-permute-start.9) | collective-permute-done | bytes 49184 | tf_op jit(solution)/shard_map/ppermute | solution.py:655
  27.6 0.0 collective-permute-done.7.refs_1_.refs_2_.refs_3_
  27.6 2.7 %collective-permute-start.12 = (bf16[192,128]{1,0:T(8,128)(2,1)S(1)}, bf16[192,128]{1,0:T(8,128)(2,1)S(1)}, u32[]{:S(2)}, u32[]{:S(2)}) collective-permute-start(bf16[192,128]{1,0:T(8,128)(2,1)S(1)} %shard_map.85.refs_0_.refs_1_), channel_id=1, source_target_pairs={{0,8},{1,9},{2,10},{3,11},{4,12},{5,13},{6,14},{7,15},{8,0},{9,1},... | collective-permute-start | bytes 147464 | tf_op jit(solution)/shard_map/ppermute | solution.py:655
  30.3 0.0 collective-permute-done.11.refs_1_.refs_3_
  30.3 0.1 shard_map.86.refs_0_
  30.4 1.3 %collective-permute-start.15 = (bf16[4,64,320]{2,1,0:T(8,128)(2,1)S(1)}, bf16[4,64,320]{2,1,0:T(8,128)(2,1)S(1)}, u32[]{:S(2)}, u32[]{:S(2)}) collective-permute-start(bf16[4,64,320]{2,1,0:T(8,128)(2,1)S(1)} %shard_map.86.refs_0_), channel_id=1, source_target_pairs={{2,0},{3,1},{4,2},{5,3},{6,4},{7,5},{8,6},{9,7},{10,8},{11,9},{12,... | collective-permute-start | bytes 491528 | tf_op jit(solution)/shard_map/ppermute | solution.py:604
  31.7 1.6 %collective-permute-done.12.refs_2_ = bf16[192,128]{1,0:T(8,128)(2,1)S(1)} collective-permute-done((bf16[192,128]{1,0:T(8,128)(2,1)S(1)}, bf16[192,128]{1,0:T(8,128)(2,1)S(1)}, u32[]{:S(2)}, u32[]{:S(2)}) %collective-permute-start.12) | collective-permute-done | bytes 49184 | tf_op jit(solution)/shard_map/ppermute | solution.py:655
  33.3 0.9 %collective-permute-start.13 = (bf16[192,128]{1,0:T(8,128)(2,1)S(1)}, bf16[192,128]{1,0:T(8,128)(2,1)S(1)}, u32[]{:S(2)}, u32[]{:S(2)}) collective-permute-start(bf16[192,128]{1,0:T(8,128)(2,1)S(1)} %shard_map.87.refs_0_.refs_1_), channel_id=1, source_target_pairs={{0,16},{1,17},{2,18},{3,19},{4,20},{5,21},{6,22},{7,23},{8,24},{9,... | collective-permute-start | bytes 147464 | tf_op jit(solution)/shard_map/ppermute | solution.py:655
  34.2 2.8 %shard_map.88 = (bf16[24,4,32,64]{3,2,1,0:T(8,128)(2,1)}, f32[8,128]{1,0:T(8,128)S(1)}) custom-call(bf16[192,128]{1,0:T(8,128)(2,1)S(1)} %shard_map.87.refs_0_.refs_1_, f32[2,24,80,128]{3,2,1,0:T(8,128)S(1)} %get-tuple-element.37.refs_0_.refs_1_, bf16[960,128]{1,0:T(8,128)(2,1)S(1)} %collective-permute-done.7.refs_1_.refs_2_.refs_3_, ...), custom_call_target="tpu_custom_call" | custom-call | flops 3449999872 | bytes 11100000 | tf_op jit(solution)/shard_map/pallas_call | solution.py:587
  37.1 0.4 collective-permute-done.13.refs_2_
  37.5 0.1 collective-permute-start.14
  37.5 1.3 %shard_map.90.refs_5_ = bf16[4,64,320]{2,1,0:T(8,128)(2,1)S(1)} custom-call(f32[192,128]{1,0:T(8,128)S(1)} %shard_map.89.refs_0_, f32[4,176,512]{2,1,0:T(8,128)S(1)} %get-tuple-element.51.refs_1_, f32[4,176,512]{2,1,0:T(8,128)S(1)} %get-tuple-element.52.refs_2_, f32[2,24,64,128]{3,2,1,0:T(8,128)S(1)} %get-tuple-element.53.refs_3_, ...), custom_call_target="tpu_custom_call" | custom-call | flops 2184999936 | bytes 7030000 | tf_op jit(solution)/shard_map/pallas_call | solution.py:587
  38.8 0.0 collective-permute-done.15.refs_4_
  38.8 0.0 collective-permute-done.14.refs_1_
  38.9 1.1 %shard_map.91 = (f32[3,3,3,32,40]{4,3,2,1,0:T(8,128)}, bf16[4,64,320]{2,1,0:T(8,128)(2,1)}, bf16[4,64,320]{2,1,0:T(8,128)(2,1)}) custom-call(f32[192,128]{1,0:T(8,128)S(1)} %shard_map.89.refs_0_, f32[192,128]{1,0:T(8,128)S(1)} %collective-permute-done.14.refs_1_, bf16[4,64,320]{2,1,0:T(8,128)(2,1)S(1)} %get-tuple-element.44.refs_0_.refs_2_, ...), custom_call_target="tpu_custom_call" | custom-call | flops 1150000000 | bytes 3700000 | tf_op jit(solution)/shard_map/pallas_call | solution.py:587
  (5 shorter events, 0.1 us)
Async XLA Ops:
  0.6 5.1 %copy-start = (bf16[4,64,320]{2,1,0:T(8,128)(2,1)S(1)}, bf16[4,64,320]{2,1,0:T(8,128)(2,1)}, u32[]{:S(2)}) copy-start(bf16[4,64,320]{2,1,0:T(8,128)(2,1)} %refs_1_.5) | copy-start | bytes 491524
  0.6 5.1 %copy-start.3 = (bf16[24,4,64,32]{2,3,1,0:T(8,128)(2,1)S(1)}, bf16[24,4,64,32]{2,3,1,0:T(8,128)(2,1)}, u32[]{:S(2)}) copy-start(bf16[24,4,64,32]{2,3,1,0:T(8,128)(2,1)} %param.7) | copy-start | bytes 1179652
  0.7 5.1 %copy-start.2 = (bf16[4,64,320]{2,1,0:T(8,128)(2,1)S(1)}, bf16[4,64,320]{2,1,0:T(8,128)(2,1)}, u32[]{:S(2)}) copy-start(bf16[4,64,320]{2,1,0:T(8,128)(2,1)} %refs_1_.4) | copy-start | bytes 491524
  0.7 9.5 %collective-permute-start = (bf16[4,64,320]{2,1,0:T(8,128)(2,1)}, bf16[4,64,320]{2,1,0:T(8,128)(2,1)S(1)}, u32[]{:S(2)}, u32[]{:S(2)}) collective-permute-start(bf16[4,64,320]{2,1,0:T(8,128)(2,1)} %refs_1_.5), channel_id=1, source_target_pairs={{0,2},{1,3},{2,4},{3,5},{4,6},{5,7},{6,8},{7,9},{8,10},{9,11},{10,... | collective-permute-start | bytes 491528 | tf_op jit(solution)/shard_map/ppermute | solution.py:604
  6.1 5.5 %collective-permute-start.2 = (bf16[32,320]{1,0:T(8,128)(2,1)S(1)}, bf16[32,320]{1,0:T(8,128)(2,1)S(1)}, u32[]{:S(2)}, u32[]{:S(2)}) collective-permute-start(bf16[32,320]{1,0:T(8,128)(2,1)S(1)} %get-tuple-element.33), channel_id=1, source_target_pairs={{0,1},{1,0},{2,3},{3,2},{4,5},{5,4},{6,7},{7,6},{8,9},{9,8},{10,11... | collective-permute-start | bytes 61448 | tf_op jit(solution)/shard_map/ppermute | solution.py:655
  6.1 5.4 %collective-permute-start.3 = (bf16[32,320]{1,0:T(8,128)(2,1)S(1)}, bf16[32,320]{1,0:T(8,128)(2,1)S(1)}, u32[]{:S(2)}, u32[]{:S(2)}) collective-permute-start(bf16[32,320]{1,0:T(8,128)(2,1)S(1)} %get-tuple-element.34), channel_id=1, source_target_pairs={{1,2},{3,4},{5,6},{7,8},{9,10},{11,12},{13,14},{2,1},{4,3},{6,5},{... | collective-permute-start | bytes 61448 | tf_op jit(solution)/shard_map/ppermute | solution.py:676
  6.8 9.1 %collective-permute-start.4 = (bf16[6,64,128]{2,1,0:T(8,128)(2,1)S(1)}, bf16[6,64,128]{2,1,0:T(8,128)(2,1)S(1)}, u32[]{:S(2)}, u32[]{:S(2)}) collective-permute-start(bf16[6,64,128]{2,1,0:T(8,128)(2,1)S(1)} %get-tuple-element.38), channel_id=1, source_target_pairs={{0,16},{16,0},{1,17},{17,1},{2,18},{18,2},{3,19},{19,3},{4,20},{20... | collective-permute-start | bytes 294920 | tf_op jit(solution)/shard_map/ppermute | solution.py:615
  10.2 2.5 %collective-permute-start.1 = (bf16[4,64,320]{2,1,0:T(8,128)(2,1)S(1)}, bf16[4,64,320]{2,1,0:T(8,128)(2,1)S(1)}, u32[]{:S(2)}, u32[]{:S(2)}) collective-permute-start(bf16[4,64,320]{2,1,0:T(8,128)(2,1)S(1)} %shard_map.78.refs_0_), channel_id=1, source_target_pairs={{0,1},{1,0},{2,3},{3,2},{4,5},{5,4},{6,7},{7,6},{8,9},{9,8},{10,11... | collective-permute-start | bytes 491528 | tf_op jit(solution)/shard_map/ppermute | solution.py:655
  11.7 4.2 %collective-permute-start.5 = (bf16[16,128]{1,0:T(8,128)(2,1)S(1)}, bf16[16,128]{1,0:T(8,128)(2,1)S(1)}, u32[]{:S(2)}, u32[]{:S(2)}) collective-permute-start(bf16[16,128]{1,0:T(8,128)(2,1)S(1)} %shard_map.80), channel_id=1, source_target_pairs={{0,16},{16,0},{1,17},{17,1},{2,18},{18,2},{3,19},{19,3},{4,20},{20... | collective-permute-start | bytes 12296 | tf_op jit(solution)/shard_map/ppermute | solution.py:615
  14.7 12.9 %collective-permute-start.7 = (bf16[960,128]{1,0:T(8,128)(2,1)S(1)}, bf16[960,128]{1,0:T(8,128)(2,1)S(1)}, u32[]{:S(2)}, u32[]{:S(2)}) collective-permute-start(bf16[960,128]{1,0:T(8,128)(2,1)S(1)} %get-tuple-element.45), channel_id=1, source_target_pairs={{0,16},{16,0},{1,17},{17,1},{2,18},{18,2},{3,19},{19,3},{4,20},{20... | collective-permute-start | bytes 737288 | tf_op jit(solution)/shard_map/ppermute | solution.py:615
  15.9 2.0 %copy-start.1 = (bf16[3,3,3,40,32]{3,4,2,1,0:T(8,128)(2,1)S(1)}, bf16[3,3,3,40,32]{3,4,2,1,0:T(8,128)(2,1)}, u32[]{:S(2)}) copy-start(bf16[3,3,3,40,32]{3,4,2,1,0:T(8,128)(2,1)} %param.6) | copy-start | bytes 207364
  17.8 1.4 %collective-permute-start.6 = (f32[192,128]{1,0:T(8,128)S(1)}, f32[192,128]{1,0:T(8,128)S(1)}, u32[]{:S(2)}, u32[]{:S(2)}) collective-permute-start(f32[192,128]{1,0:T(8,128)S(1)} %get-tuple-element.41), channel_id=1, source_target_pairs={{0,1},{1,0},{2,3},{3,2},{4,5},{5,4},{6,7},{7,6},{8,9},{9,8},{10,11... | collective-permute-start | bytes 294920 | tf_op jit(solution)/shard_map/ppermute | solution.py:655
  19.2 7.0 %collective-permute-start.10 = (bf16[192,128]{1,0:T(8,128)(2,1)S(1)}, bf16[192,128]{1,0:T(8,128)(2,1)S(1)}, u32[]{:S(2)}, u32[]{:S(2)}) collective-permute-start(bf16[192,128]{1,0:T(8,128)(2,1)S(1)} %shard_map.83.refs_0_.refs_2_), channel_id=1, source_target_pairs={{0,6},{1,7},{2,4},{3,5},{4,2},{5,3},{6,0},{7,1},{8,14},{9,15},{10,... | collective-permute-start | bytes 147464 | tf_op jit(solution)/shard_map/ppermute | solution.py:655
  22.1 4.1 %collective-permute-start.8 = (bf16[192,128]{1,0:T(8,128)(2,1)S(1)}, bf16[192,128]{1,0:T(8,128)(2,1)S(1)}, u32[]{:S(2)}, u32[]{:S(2)}) collective-permute-start(bf16[192,128]{1,0:T(8,128)(2,1)S(1)} %shard_map.83.refs_0_.refs_2_), channel_id=1, source_target_pairs={{0,2},{1,3},{2,0},{3,1},{4,6},{5,7},{6,4},{7,5},{8,10},{9,11},{10,... | collective-permute-start | bytes 147464 | tf_op jit(solution)/shard_map/ppermute | solution.py:655
  23.5 4.1 %collective-permute-start.9 = (bf16[192,128]{1,0:T(8,128)(2,1)S(1)}, bf16[192,128]{1,0:T(8,128)(2,1)S(1)}, u32[]{:S(2)}, u32[]{:S(2)}) collective-permute-start(bf16[192,128]{1,0:T(8,128)(2,1)S(1)} %shard_map.83.refs_0_.refs_2_), channel_id=1, source_target_pairs={{0,4},{1,5},{2,6},{3,7},{4,0},{5,1},{6,2},{7,3},{8,12},{9,13},{10,... | collective-permute-start | bytes 147464 | tf_op jit(solution)/shard_map/ppermute | solution.py:655
  26.0 4.2 %collective-permute-start.11 = (bf16[4,64,320]{2,1,0:T(8,128)(2,1)S(1)}, bf16[4,64,320]{2,1,0:T(8,128)(2,1)S(1)}, u32[]{:S(2)}, u32[]{:S(2)}) collective-permute-start(bf16[4,64,320]{2,1,0:T(8,128)(2,1)S(1)} %get-tuple-element.46), channel_id=1, source_target_pairs={{0,1},{1,0},{2,3},{3,2},{4,5},{5,4},{6,7},{7,6},{8,9},{9,8},{10,11... | collective-permute-start | bytes 491528 | tf_op jit(solution)/shard_map/ppermute | solution.py:655
  27.6 5.6 %collective-permute-start.12 = (bf16[192,128]{1,0:T(8,128)(2,1)S(1)}, bf16[192,128]{1,0:T(8,128)(2,1)S(1)}, u32[]{:S(2)}, u32[]{:S(2)}) collective-permute-start(bf16[192,128]{1,0:T(8,128)(2,1)S(1)} %shard_map.85.refs_0_.refs_1_), channel_id=1, source_target_pairs={{0,8},{1,9},{2,10},{3,11},{4,12},{5,13},{6,14},{7,15},{8,0},{9,1},... | collective-permute-start | bytes 147464 | tf_op jit(solution)/shard_map/ppermute | solution.py:655
  30.4 8.5 %collective-permute-start.15 = (bf16[4,64,320]{2,1,0:T(8,128)(2,1)S(1)}, bf16[4,64,320]{2,1,0:T(8,128)(2,1)S(1)}, u32[]{:S(2)}, u32[]{:S(2)}) collective-permute-start(bf16[4,64,320]{2,1,0:T(8,128)(2,1)S(1)} %shard_map.86.refs_0_), channel_id=1, source_target_pairs={{2,0},{3,1},{4,2},{5,3},{6,4},{7,5},{8,6},{9,7},{10,8},{11,9},{12,... | collective-permute-start | bytes 491528 | tf_op jit(solution)/shard_map/ppermute | solution.py:604
  33.3 4.2 %collective-permute-start.13 = (bf16[192,128]{1,0:T(8,128)(2,1)S(1)}, bf16[192,128]{1,0:T(8,128)(2,1)S(1)}, u32[]{:S(2)}, u32[]{:S(2)}) collective-permute-start(bf16[192,128]{1,0:T(8,128)(2,1)S(1)} %shard_map.87.refs_0_.refs_1_), channel_id=1, source_target_pairs={{0,16},{1,17},{2,18},{3,19},{4,20},{5,21},{6,22},{7,23},{8,24},{9,... | collective-permute-start | bytes 147464 | tf_op jit(solution)/shard_map/ppermute | solution.py:655
  37.5 1.4 %collective-permute-start.14 = (f32[192,128]{1,0:T(8,128)S(1)}, f32[192,128]{1,0:T(8,128)S(1)}, u32[]{:S(2)}, u32[]{:S(2)}) collective-permute-start(f32[192,128]{1,0:T(8,128)S(1)} %shard_map.89.refs_0_), channel_id=1, source_target_pairs={{0,1},{1,0},{2,3},{3,2},{4,5},{5,4},{6,7},{7,6},{8,9},{9,8},{10,11... | collective-permute-start | bytes 294920 | tf_op jit(solution)/shard_map/ppermute | solution.py:655

commit v9 on v8

--- a/solution.py
+++ b/solution.py
@@ -155,20 +155,19 @@
     pairs, times, lots = rows // 2, disp // 2, wide // 128
     count = total // 16
 
-    def products(i, _):
-        p, at = lax.rem(i, pairs), pl.multiple_of(lax.div(i, pairs) * (8 * count), 8)
+    def products(p, at):
         lefts = [
             [
-                [fl[2 * p + o, pl.ds(at + 8 * b, 8), 128 * j : 128 * (j + 1)] for j in range(lots)]
+                [fl[2 * p + o, at + 8 * b : at + 8 * b + 8, 128 * j : 128 * (j + 1)] for j in range(lots)]
                 for b in range(count)
             ]
             for o in range(2)
         ]
         for odd, band in enumerate((fr, fr4)):
             for r in range(1 - times, count):
-                start = pl.multiple_of(at + reach - PAD + 8 * r, 8)
+                start = at + reach - PAD + 8 * r
                 here = [
-                    [band[2 * p + o, pl.ds(start, 8), 128 * j : 128 * (j + 1)] for j in range(lots)]
+                    [band[2 * p + o, start : start + 8, 128 * j : 128 * (j + 1)] for j in range(lots)]
                     for o in range(2)
                 ]
                 for t in range(max(0, -r), min(times, count - r)):
@@ -178,10 +177,12 @@
                         for j in range(1, lots):
                             acc = acc + lefts[o][r + t][j] * here[o][j]
                         sums.append(acc + pltpu.roll(acc, SLOT, 1))
-                    vbuf[p, 2 * t + odd, pl.ds(at + 8 * (r + t), 8)] = jnp.where(low, *sums)
-        return 0
-
-    lax.fori_loop(0, 2 * pairs, products, 0)
+                    row = at + 8 * (r + t)
+                    vbuf[p, 2 * t + odd, row : row + 8] = jnp.where(low, *sums)
+
+    for at in (8 * count, 0):
+        for p in range(pairs):
+            products(p, at)
     big = lanes((total, 128)) < SLOT
 
     for dd in range(disp // 2):
@@ -308,7 +309,7 @@
     rows, cols, channels = rg0.shape
     disp, wide = grads[0].shape[1], fl.shape[2]
     group_size = wide // SLOT
-    step = disp // 8
+    step = disp // 4
     low = lanes((step * cols, 128)) < SLOT
 
     def conv(q, p, gv):
@@ -359,8 +360,8 @@
     for p, gv in enumerate(grads):
         for q in range(parts):
             conv(q, p, gv)
-            if p and q % 2:
-                right_row(grads[p - 1], p - 1, q // 2)
+            if p:
+                right_row(grads[p - 1], p - 1, q)
     for hh in range(2):
         right_row(grads[-1], len(grads) - 1, hh)
     size = back + cols

time: 40.2 us -> 39.6 us (0.985)
  Pallas kernels: 13.6 us -> 13 us
    pallas_call x17, Pallas kernels: 13.6 us -> 13 us  [call(): pl.pallas_call(lambda *refs: kernel(*refs[skip:]), out_shape=[jax.ShapeDt...]
  transfers between devices with their start and end apart: 16 -> 16, of which waited for: 6 -> 7; matrix products, arithmetic and copies ran while one was open for 0% -> 0% of each run, Pallas kernels for 31% -> 30%
where the time goes in v9:
time: 39.6 us; the launch traced here: 39.4 us
  starting transfers between devices  19.8 us (50%)
  Pallas kernels  13 us (33%)
  waiting for transfers between devices  5.63 us (14%)
  between operations  0.85 us (2%)
    pallas_call x17, Pallas kernels, call(): pl.pallas_call(lambda *refs: kernel(*refs[skip:]), out_shape=[jax.ShapeDt...  13 us
    ppermute x10, starting transfers between devices, swap(): return lax.ppermute(block, ('row', 'col'), route)  9.61 us
    ppermute x2, starting transfers between devices, col_shift(): return lax.ppermute(block, 'col', route)  6.31 us
    ppermute x10, waiting for transfers between devices, swap(): return lax.ppermute(block, ('row', 'col'), route)  4.33 us
    ppermute x3, starting transfers between devices, halos(): got = lax.ppermute(pays[0], 'row', [(0, 1), (1, 0)])  3.25 us
    ppermute x2, waiting for transfers between devices, col_shift(): return lax.ppermute(block, 'col', route)  1.29 us
  transfers between devices with their start and end apart: 16, of which 7 were waited for; matrix products, arithmetic and copies ran while one was open for 0% of the time, Pallas kernels for 30%

profile of v9, /device:TPU:0, one launch (start us, length us, event | category | flops | bytes accessed | tf_op | source)
XLA Modules:
  0.0 39.4 jit_solution(10934657736873564071)
XLA Ops:
  0.6 0.0 copy-start
  0.6 0.0 copy-start.3
  0.7 0.0 copy-start.2
  0.7 5.0 %collective-permute-start = (bf16[4,64,320]{2,1,0:T(8,128)(2,1)}, bf16[4,64,320]{2,1,0:T(8,128)(2,1)S(1)}, u32[]{:S(2)}, u32[]{:S(2)}) collective-permute-start(bf16[4,64,320]{2,1,0:T(8,128)(2,1)} %refs_1_.5), channel_id=1, source_target_pairs={{0,2},{1,3},{2,4},{3,5},{4,6},{5,7},{6,8},{7,9},{8,10},{9,11},{10,... | collective-permute-start | bytes 491528 | tf_op jit(solution)/shard_map/ppermute | solution.py:605
  5.7 0.0 copy-done
  5.7 0.0 copy-done.3
  5.7 0.0 copy-done.2
  5.7 0.3 shard_map.76
  6.1 0.1 collective-permute-start.2
  6.1 0.7 %collective-permute-start.3 = (bf16[32,320]{1,0:T(8,128)(2,1)S(1)}, bf16[32,320]{1,0:T(8,128)(2,1)S(1)}, u32[]{:S(2)}, u32[]{:S(2)}) collective-permute-start(bf16[32,320]{1,0:T(8,128)(2,1)S(1)} %get-tuple-element.34), channel_id=1, source_target_pairs={{1,2},{3,4},{5,6},{7,8},{9,10},{11,12},{13,14},{2,1},{4,3},{6,5},{... | collective-permute-start | bytes 61448 | tf_op jit(solution)/shard_map/ppermute | solution.py:677
  6.8 1.6 %collective-permute-start.4 = (bf16[6,64,128]{2,1,0:T(8,128)(2,1)S(1)}, bf16[6,64,128]{2,1,0:T(8,128)(2,1)S(1)}, u32[]{:S(2)}, u32[]{:S(2)}) collective-permute-start(bf16[6,64,128]{2,1,0:T(8,128)(2,1)S(1)} %get-tuple-element.38), channel_id=1, source_target_pairs={{0,16},{16,0},{1,17},{17,1},{2,18},{18,2},{3,19},{19,3},{4,20},{20... | collective-permute-start | bytes 294920 | tf_op jit(solution)/shard_map/ppermute | solution.py:616
  8.4 0.5 %shard_map.77 = (f32[4,80,512]{2,1,0:T(8,128)S(1)}, f32[4,176,512]{2,1,0:T(8,128)S(1)}, f32[4,176,512]{2,1,0:T(8,128)S(1)}) custom-call(bf16[24,64,128]{2,1,0:T(8,128)(2,1)S(1)} %get-tuple-element.31.refs_0_.refs_1_, bf16[4,64,320]{2,1,0:T(8,128)(2,1)S(1)} %copy-done.2, bf16[4,64,320]{2,1,0:T(8,128)(2,1)S(1)} %copy-done), custom_call_target="tpu_custom_call" | custom-call | tf_op jit(solution)/shard_map/pallas_call | solution.py:588
  8.8 1.3 %collective-permute-done.refs_2_.refs_1_ = bf16[4,64,320]{2,1,0:T(8,128)(2,1)S(1)} collective-permute-done((bf16[4,64,320]{2,1,0:T(8,128)(2,1)}, bf16[4,64,320]{2,1,0:T(8,128)(2,1)S(1)}, u32[]{:S(2)}, u32[]{:S(2)}) %collective-permute-start) | collective-permute-done | bytes 163872 | tf_op jit(solution)/shard_map/ppermute | solution.py:605
  10.1 0.1 shard_map.78.refs_0_
  10.2 1.4 %collective-permute-start.1 = (bf16[4,64,320]{2,1,0:T(8,128)(2,1)S(1)}, bf16[4,64,320]{2,1,0:T(8,128)(2,1)S(1)}, u32[]{:S(2)}, u32[]{:S(2)}) collective-permute-start(bf16[4,64,320]{2,1,0:T(8,128)(2,1)S(1)} %shard_map.78.refs_0_), channel_id=1, source_target_pairs={{0,1},{1,0},{2,3},{3,2},{4,5},{5,4},{6,7},{7,6},{8,9},{9,8},{10,11... | collective-permute-start | bytes 491528 | tf_op jit(solution)/shard_map/ppermute | solution.py:656
  11.6 0.0 collective-permute-done.2.refs_2_.refs_1_
  11.6 0.0 collective-permute-done.3.refs_3_.refs_2_
  11.6 0.1 shard_map.80
  11.7 0.6 %collective-permute-start.5 = (bf16[16,128]{1,0:T(8,128)(2,1)S(1)}, bf16[16,128]{1,0:T(8,128)(2,1)S(1)}, u32[]{:S(2)}, u32[]{:S(2)}) collective-permute-start(bf16[16,128]{1,0:T(8,128)(2,1)S(1)} %shard_map.80), channel_id=1, source_target_pairs={{0,16},{16,0},{1,17},{17,1},{2,18},{18,2},{3,19},{19,3},{4,20},{20... | collective-permute-start | bytes 12296 | tf_op jit(solution)/shard_map/ppermute | solution.py:616
  12.2 0.4 %collective-permute-done.1.refs_0_ = bf16[4,64,320]{2,1,0:T(8,128)(2,1)S(1)} collective-permute-done((bf16[4,64,320]{2,1,0:T(8,128)(2,1)S(1)}, bf16[4,64,320]{2,1,0:T(8,128)(2,1)S(1)}, u32[]{:S(2)}, u32[]{:S(2)}) %collective-permute-start.1) | collective-permute-done | bytes 163872 | tf_op jit(solution)/shard_map/ppermute | solution.py:656
  12.6 1.6 %shard_map.79 = (f32[4,80,512]{2,1,0:T(8,128)S(1)}, f32[4,176,512]{2,1,0:T(8,128)S(1)}, f32[4,176,512]{2,1,0:T(8,128)S(1)}, f32[2,24,80,128]{3,2,1,0:T(8,128)S(1)}, bf16[960,128]{1,0:T(8,128)(2,1)S(1)}) custom-call(bf16[4,64,320]{2,1,0:T(8,128)(2,1)S(1)} %collective-permute-done.1.refs_0_, ...), custom_call_target="tpu_custom_call", output_to_operand_aliasing={{0}: (4, {}), {1}: (5, {}), {2}: (6, {})} | custom-call | flops 2070000000 | bytes 6660000 | tf_op jit(solution)/shard_map/pallas_call | solution.py:588
  14.2 1.1 %collective-permute-start.7 = (bf16[960,128]{1,0:T(8,128)(2,1)S(1)}, bf16[960,128]{1,0:T(8,128)(2,1)S(1)}, u32[]{:S(2)}, u32[]{:S(2)}) collective-permute-start(bf16[960,128]{1,0:T(8,128)(2,1)S(1)} %get-tuple-element.45), channel_id=1, source_target_pairs={{0,16},{16,0},{1,17},{17,1},{2,18},{18,2},{3,19},{19,3},{4,20},{20... | collective-permute-start | bytes 737288 | tf_op jit(solution)/shard_map/ppermute | solution.py:616
  15.4 0.0 collective-permute-done.4.refs_4_.refs_5_
  15.4 0.0 collective-permute-done.5.refs_6_.refs_7_
  15.4 0.0 copy-start.1
  15.4 1.9 %shard_map.81 = (f32[192,128]{1,0:T(8,128)S(1)}, f32[192,128]{1,0:T(8,128)S(1)}, bf16[13,2,64,768]{3,2,1,0:T(8,128)(2,1)S(1)}) custom-call(f32[2,24,80,128]{3,2,1,0:T(8,128)S(1)} %get-tuple-element.37.refs_0_.refs_1_, bf16[24,64,128]{2,1,0:T(8,128)(2,1)S(1)} %get-tuple-element.31.refs_0_.refs_1_, bf16[32,320]{1,0:T(8,128)(2,1)S(1)} %collective-permute-done.2.refs_2_.refs_1_, ...), custom_call_target="tpu_custom_call" | custom-call | flops 2300000000 | bytes 7400000 | tf_op jit(solution)/shard_map/pallas_call | solution.py:588
  17.3 0.1 collective-permute-start.6
  17.4 0.0 copy-done.1
  17.4 0.8 %shard_map.82 = (bf16[1536,256]{1,0:T(8,128)(2,1)S(1)}, bf16[3072,256]{1,0:T(8,128)(2,1)S(1)}) custom-call(f32[192,128]{1,0:T(8,128)S(1)} %get-tuple-element.39.refs_0_.refs_1_, bf16[3,3,3,32,40]{4,3,2,1,0:T(8,128)(2,1)S(1)} %bitcast.4), custom_call_target="tpu_custom_call" | custom-call | tf_op jit(solution)/shard_map/pallas_call | solution.py:588
  18.2 0.4 %collective-permute-done.6.refs_2_ = f32[192,128]{1,0:T(8,128)S(1)} collective-permute-done((f32[192,128]{1,0:T(8,128)S(1)}, f32[192,128]{1,0:T(8,128)S(1)}, u32[]{:S(2)}, u32[]{:S(2)}) %collective-permute-start.6) | collective-permute-done | bytes 98336 | tf_op jit(solution)/shard_map/ppermute | solution.py:656
  18.7 2.9 %collective-permute-start.10 = (bf16[192,128]{1,0:T(8,128)(2,1)S(1)}, bf16[192,128]{1,0:T(8,128)(2,1)S(1)}, u32[]{:S(2)}, u32[]{:S(2)}) collective-permute-start(bf16[192,128]{1,0:T(8,128)(2,1)S(1)} %shard_map.83.refs_0_.refs_2_), channel_id=1, source_target_pairs={{0,6},{1,7},{2,4},{3,5},{4,2},{5,3},{6,0},{7,1},{8,14},{9,15},{10,... | collective-permute-start | bytes 147464 | tf_op jit(solution)/shard_map/ppermute | solution.py:656
  21.6 1.4 %collective-permute-start.8 = (bf16[192,128]{1,0:T(8,128)(2,1)S(1)}, bf16[192,128]{1,0:T(8,128)(2,1)S(1)}, u32[]{:S(2)}, u32[]{:S(2)}) collective-permute-start(bf16[192,128]{1,0:T(8,128)(2,1)S(1)} %shard_map.83.refs_0_.refs_2_), channel_id=1, source_target_pairs={{0,2},{1,3},{2,0},{3,1},{4,6},{5,7},{6,4},{7,5},{8,10},{9,11},{10,... | collective-permute-start | bytes 147464 | tf_op jit(solution)/shard_map/ppermute | solution.py:656
  23.0 0.0 collective-permute-start.9
  23.0 2.4 %shard_map.84 = (f32[2,24,64,128]{3,2,1,0:T(8,128)S(1)}, f32[2,24,64,128]{3,2,1,0:T(8,128)S(1)}, bf16[4,64,320]{2,1,0:T(8,128)(2,1)S(1)}, bf16[4,64,320]{2,1,0:T(8,128)(2,1)S(1)}, bf16[4,32,320]{2,1,0:T(8,128)(2,1)S(1)}) custom-call(bf16[192,128]{1,0:T(8,128)(2,1)S(1)} %shard_map.83.refs_0_.refs_2_, bf16[13,2,64,768]{3,2,1,0:T(8,128)(2,1)S(1)} %get-tuple-element.42.refs_1_, ...), custom_call_target="tpu_custom_call" | custom-call | flops 460000000 | bytes 1480000 | tf_op jit(solution)/shard_map/pallas_call | solution.py:588
  25.5 0.1 collective-permute-start.11
  25.6 0.0 collective-permute-done.10.refs_5_
  25.6 0.1 collective-permute-done.8.refs_3_
  25.7 1.4 %collective-permute-done.9.refs_4_ = bf16[192,128]{1,0:T(8,128)(2,1)S(1)} collective-permute-done((bf16[192,128]{1,0:T(8,128)(2,1)S(1)}, bf16[192,128]{1,0:T(8,128)(2,1)S(1)}, u32[]{:S(2)}, u32[]{:S(2)}) %collective-permute-start.9) | collective-permute-done | bytes 49184 | tf_op jit(solution)/shard_map/ppermute | solution.py:656
  27.1 0.0 collective-permute-done.7.refs_1_.refs_2_.refs_3_
  27.2 2.7 %collective-permute-start.12 = (bf16[192,128]{1,0:T(8,128)(2,1)S(1)}, bf16[192,128]{1,0:T(8,128)(2,1)S(1)}, u32[]{:S(2)}, u32[]{:S(2)}) collective-permute-start(bf16[192,128]{1,0:T(8,128)(2,1)S(1)} %shard_map.85.refs_0_.refs_1_), channel_id=1, source_target_pairs={{0,8},{1,9},{2,10},{3,11},{4,12},{5,13},{6,14},{7,15},{8,0},{9,1},... | collective-permute-start | bytes 147464 | tf_op jit(solution)/shard_map/ppermute | solution.py:656
  29.8 0.0 collective-permute-done.11.refs_1_.refs_3_
  29.8 0.1 shard_map.86.refs_0_
  29.9 1.3 %collective-permute-start.15 = (bf16[4,64,320]{2,1,0:T(8,128)(2,1)S(1)}, bf16[4,64,320]{2,1,0:T(8,128)(2,1)S(1)}, u32[]{:S(2)}, u32[]{:S(2)}) collective-permute-start(bf16[4,64,320]{2,1,0:T(8,128)(2,1)S(1)} %shard_map.86.refs_0_), channel_id=1, source_target_pairs={{2,0},{3,1},{4,2},{5,3},{6,4},{7,5},{8,6},{9,7},{10,8},{11,9},{12,... | collective-permute-start | bytes 491528 | tf_op jit(solution)/shard_map/ppermute | solution.py:605
  31.2 1.5 %collective-permute-done.12.refs_2_ = bf16[192,128]{1,0:T(8,128)(2,1)S(1)} collective-permute-done((bf16[192,128]{1,0:T(8,128)(2,1)S(1)}, bf16[192,128]{1,0:T(8,128)(2,1)S(1)}, u32[]{:S(2)}, u32[]{:S(2)}) %collective-permute-start.12) | collective-permute-done | bytes 49184 | tf_op jit(solution)/shard_map/ppermute | solution.py:656
  32.7 0.9 %collective-permute-start.13 = (bf16[192,128]{1,0:T(8,128)(2,1)S(1)}, bf16[192,128]{1,0:T(8,128)(2,1)S(1)}, u32[]{:S(2)}, u32[]{:S(2)}) collective-permute-start(bf16[192,128]{1,0:T(8,128)(2,1)S(1)} %shard_map.87.refs_0_.refs_1_), channel_id=1, source_target_pairs={{0,16},{1,17},{2,18},{3,19},{4,20},{5,21},{6,22},{7,23},{8,24},{9,... | collective-permute-start | bytes 147464 | tf_op jit(solution)/shard_map/ppermute | solution.py:656
  33.7 2.8 %shard_map.88 = (bf16[24,4,32,64]{3,2,1,0:T(8,128)(2,1)}, f32[8,128]{1,0:T(8,128)S(1)}) custom-call(bf16[192,128]{1,0:T(8,128)(2,1)S(1)} %shard_map.87.refs_0_.refs_1_, f32[2,24,80,128]{3,2,1,0:T(8,128)S(1)} %get-tuple-element.37.refs_0_.refs_1_, bf16[960,128]{1,0:T(8,128)(2,1)S(1)} %collective-permute-done.7.refs_1_.refs_2_.refs_3_, ...), custom_call_target="tpu_custom_call" | custom-call | flops 3449999872 | bytes 11100000 | tf_op jit(solution)/shard_map/pallas_call | solution.py:588
  36.5 0.4 collective-permute-done.13.refs_2_
  36.9 0.1 collective-permute-start.14
  37.0 1.3 %shard_map.90.refs_5_ = bf16[4,64,320]{2,1,0:T(8,128)(2,1)S(1)} custom-call(f32[192,128]{1,0:T(8,128)S(1)} %shard_map.89.refs_0_, f32[4,176,512]{2,1,0:T(8,128)S(1)} %get-tuple-element.51.refs_1_, f32[4,176,512]{2,1,0:T(8,128)S(1)} %get-tuple-element.52.refs_2_, f32[2,24,64,128]{3,2,1,0:T(8,128)S(1)} %get-tuple-element.53.refs_3_, ...), custom_call_target="tpu_custom_call" | custom-call | flops 2184999936 | bytes 7030000 | tf_op jit(solution)/shard_map/pallas_call | solution.py:588
  38.3 0.0 collective-permute-done.15.refs_4_
  38.3 0.0 collective-permute-done.14.refs_1_
  38.3 1.1 %shard_map.91 = (f32[3,3,3,32,40]{4,3,2,1,0:T(8,128)}, bf16[4,64,320]{2,1,0:T(8,128)(2,1)}, bf16[4,64,320]{2,1,0:T(8,128)(2,1)}) custom-call(f32[192,128]{1,0:T(8,128)S(1)} %shard_map.89.refs_0_, f32[192,128]{1,0:T(8,128)S(1)} %collective-permute-done.14.refs_1_, bf16[4,64,320]{2,1,0:T(8,128)(2,1)S(1)} %get-tuple-element.44.refs_0_.refs_2_, ...), custom_call_target="tpu_custom_call" | custom-call | flops 1150000000 | bytes 3700000 | tf_op jit(solution)/shard_map/pallas_call | solution.py:588
  (5 shorter events, 0.1 us)
Async XLA Ops:
  0.6 5.1 %copy-start = (bf16[4,64,320]{2,1,0:T(8,128)(2,1)S(1)}, bf16[4,64,320]{2,1,0:T(8,128)(2,1)}, u32[]{:S(2)}) copy-start(bf16[4,64,320]{2,1,0:T(8,128)(2,1)} %refs_1_.5) | copy-start | bytes 491524
  0.6 5.1 %copy-start.3 = (bf16[24,4,64,32]{2,3,1,0:T(8,128)(2,1)S(1)}, bf16[24,4,64,32]{2,3,1,0:T(8,128)(2,1)}, u32[]{:S(2)}) copy-start(bf16[24,4,64,32]{2,3,1,0:T(8,128)(2,1)} %param.7) | copy-start | bytes 1179652
  0.7 5.1 %copy-start.2 = (bf16[4,64,320]{2,1,0:T(8,128)(2,1)S(1)}, bf16[4,64,320]{2,1,0:T(8,128)(2,1)}, u32[]{:S(2)}) copy-start(bf16[4,64,320]{2,1,0:T(8,128)(2,1)} %refs_1_.4) | copy-start | bytes 491524
  0.7 9.5 %collective-permute-start = (bf16[4,64,320]{2,1,0:T(8,128)(2,1)}, bf16[4,64,320]{2,1,0:T(8,128)(2,1)S(1)}, u32[]{:S(2)}, u32[]{:S(2)}) collective-permute-start(bf16[4,64,320]{2,1,0:T(8,128)(2,1)} %refs_1_.5), channel_id=1, source_target_pairs={{0,2},{1,3},{2,4},{3,5},{4,6},{5,7},{6,8},{7,9},{8,10},{9,11},{10,... | collective-permute-start | bytes 491528 | tf_op jit(solution)/shard_map/ppermute | solution.py:605
  6.1 5.5 %collective-permute-start.2 = (bf16[32,320]{1,0:T(8,128)(2,1)S(1)}, bf16[32,320]{1,0:T(8,128)(2,1)S(1)}, u32[]{:S(2)}, u32[]{:S(2)}) collective-permute-start(bf16[32,320]{1,0:T(8,128)(2,1)S(1)} %get-tuple-element.33), channel_id=1, source_target_pairs={{0,1},{1,0},{2,3},{3,2},{4,5},{5,4},{6,7},{7,6},{8,9},{9,8},{10,11... | collective-permute-start | bytes 61448 | tf_op jit(solution)/shard_map/ppermute | solution.py:656
  6.1 5.4 %collective-permute-start.3 = (bf16[32,320]{1,0:T(8,128)(2,1)S(1)}, bf16[32,320]{1,0:T(8,128)(2,1)S(1)}, u32[]{:S(2)}, u32[]{:S(2)}) collective-permute-start(bf16[32,320]{1,0:T(8,128)(2,1)S(1)} %get-tuple-element.34), channel_id=1, source_target_pairs={{1,2},{3,4},{5,6},{7,8},{9,10},{11,12},{13,14},{2,1},{4,3},{6,5},{... | collective-permute-start | bytes 61448 | tf_op jit(solution)/shard_map/ppermute | solution.py:677
  6.8 8.6 %collective-permute-start.4 = (bf16[6,64,128]{2,1,0:T(8,128)(2,1)S(1)}, bf16[6,64,128]{2,1,0:T(8,128)(2,1)S(1)}, u32[]{:S(2)}, u32[]{:S(2)}) collective-permute-start(bf16[6,64,128]{2,1,0:T(8,128)(2,1)S(1)} %get-tuple-element.38), channel_id=1, source_target_pairs={{0,16},{16,0},{1,17},{17,1},{2,18},{18,2},{3,19},{19,3},{4,20},{20... | collective-permute-start | bytes 294920 | tf_op jit(solution)/shard_map/ppermute | solution.py:616
  10.2 2.5 %collective-permute-start.1 = (bf16[4,64,320]{2,1,0:T(8,128)(2,1)S(1)}, bf16[4,64,320]{2,1,0:T(8,128)(2,1)S(1)}, u32[]{:S(2)}, u32[]{:S(2)}) collective-permute-start(bf16[4,64,320]{2,1,0:T(8,128)(2,1)S(1)} %shard_map.78.refs_0_), channel_id=1, source_target_pairs={{0,1},{1,0},{2,3},{3,2},{4,5},{5,4},{6,7},{7,6},{8,9},{9,8},{10,11... | collective-permute-start | bytes 491528 | tf_op jit(solution)/shard_map/ppermute | solution.py:656
  11.7 3.7 %collective-permute-start.5 = (bf16[16,128]{1,0:T(8,128)(2,1)S(1)}, bf16[16,128]{1,0:T(8,128)(2,1)S(1)}, u32[]{:S(2)}, u32[]{:S(2)}) collective-permute-start(bf16[16,128]{1,0:T(8,128)(2,1)S(1)} %shard_map.80), channel_id=1, source_target_pairs={{0,16},{16,0},{1,17},{17,1},{2,18},{18,2},{3,19},{19,3},{4,20},{20... | collective-permute-start | bytes 12296 | tf_op jit(solution)/shard_map/ppermute | solution.py:616
  14.2 12.9 %collective-permute-start.7 = (bf16[960,128]{1,0:T(8,128)(2,1)S(1)}, bf16[960,128]{1,0:T(8,128)(2,1)S(1)}, u32[]{:S(2)}, u32[]{:S(2)}) collective-permute-start(bf16[960,128]{1,0:T(8,128)(2,1)S(1)} %get-tuple-element.45), channel_id=1, source_target_pairs={{0,16},{16,0},{1,17},{17,1},{2,18},{18,2},{3,19},{19,3},{4,20},{20... | collective-permute-start | bytes 737288 | tf_op jit(solution)/shard_map/ppermute | solution.py:616
  15.4 2.0 %copy-start.1 = (bf16[3,3,3,40,32]{3,4,2,1,0:T(8,128)(2,1)S(1)}, bf16[3,3,3,40,32]{3,4,2,1,0:T(8,128)(2,1)}, u32[]{:S(2)}) copy-start(bf16[3,3,3,40,32]{3,4,2,1,0:T(8,128)(2,1)} %param.6) | copy-start | bytes 207364
  17.3 1.4 %collective-permute-start.6 = (f32[192,128]{1,0:T(8,128)S(1)}, f32[192,128]{1,0:T(8,128)S(1)}, u32[]{:S(2)}, u32[]{:S(2)}) collective-permute-start(f32[192,128]{1,0:T(8,128)S(1)} %get-tuple-element.41), channel_id=1, source_target_pairs={{0,1},{1,0},{2,3},{3,2},{4,5},{5,4},{6,7},{7,6},{8,9},{9,8},{10,11... | collective-permute-start | bytes 294920 | tf_op jit(solution)/shard_map/ppermute | solution.py:656
  18.7 6.9 %collective-permute-start.10 = (bf16[192,128]{1,0:T(8,128)(2,1)S(1)}, bf16[192,128]{1,0:T(8,128)(2,1)S(1)}, u32[]{:S(2)}, u32[]{:S(2)}) collective-permute-start(bf16[192,128]{1,0:T(8,128)(2,1)S(1)} %shard_map.83.refs_0_.refs_2_), channel_id=1, source_target_pairs={{0,6},{1,7},{2,4},{3,5},{4,2},{5,3},{6,0},{7,1},{8,14},{9,15},{10,... | collective-permute-start | bytes 147464 | tf_op jit(solution)/shard_map/ppermute | solution.py:656
  21.6 4.1 %collective-permute-start.8 = (bf16[192,128]{1,0:T(8,128)(2,1)S(1)}, bf16[192,128]{1,0:T(8,128)(2,1)S(1)}, u32[]{:S(2)}, u32[]{:S(2)}) collective-permute-start(bf16[192,128]{1,0:T(8,128)(2,1)S(1)} %shard_map.83.refs_0_.refs_2_), channel_id=1, source_target_pairs={{0,2},{1,3},{2,0},{3,1},{4,6},{5,7},{6,4},{7,5},{8,10},{9,11},{10,... | collective-permute-start | bytes 147464 | tf_op jit(solution)/shard_map/ppermute | solution.py:656
  23.0 4.1 %collective-permute-start.9 = (bf16[192,128]{1,0:T(8,128)(2,1)S(1)}, bf16[192,128]{1,0:T(8,128)(2,1)S(1)}, u32[]{:S(2)}, u32[]{:S(2)}) collective-permute-start(bf16[192,128]{1,0:T(8,128)(2,1)S(1)} %shard_map.83.refs_0_.refs_2_), channel_id=1, source_target_pairs={{0,4},{1,5},{2,6},{3,7},{4,0},{5,1},{6,2},{7,3},{8,12},{9,13},{10,... | collective-permute-start | bytes 147464 | tf_op jit(solution)/shard_map/ppermute | solution.py:656
  25.5 4.3 %collective-permute-start.11 = (bf16[4,64,320]{2,1,0:T(8,128)(2,1)S(1)}, bf16[4,64,320]{2,1,0:T(8,128)(2,1)S(1)}, u32[]{:S(2)}, u32[]{:S(2)}) collective-permute-start(bf16[4,64,320]{2,1,0:T(8,128)(2,1)S(1)} %get-tuple-element.46), channel_id=1, source_target_pairs={{0,1},{1,0},{2,3},{3,2},{4,5},{5,4},{6,7},{7,6},{8,9},{9,8},{10,11... | collective-permute-start | bytes 491528 | tf_op jit(solution)/shard_map/ppermute | solution.py:656
  27.2 5.5 %collective-permute-start.12 = (bf16[192,128]{1,0:T(8,128)(2,1)S(1)}, bf16[192,128]{1,0:T(8,128)(2,1)S(1)}, u32[]{:S(2)}, u32[]{:S(2)}) collective-permute-start(bf16[192,128]{1,0:T(8,128)(2,1)S(1)} %shard_map.85.refs_0_.refs_1_), channel_id=1, source_target_pairs={{0,8},{1,9},{2,10},{3,11},{4,12},{5,13},{6,14},{7,15},{8,0},{9,1},... | collective-permute-start | bytes 147464 | tf_op jit(solution)/shard_map/ppermute | solution.py:656
  29.9 8.4 %collective-permute-start.15 = (bf16[4,64,320]{2,1,0:T(8,128)(2,1)S(1)}, bf16[4,64,320]{2,1,0:T(8,128)(2,1)S(1)}, u32[]{:S(2)}, u32[]{:S(2)}) collective-permute-start(bf16[4,64,320]{2,1,0:T(8,128)(2,1)S(1)} %shard_map.86.refs_0_), channel_id=1, source_target_pairs={{2,0},{3,1},{4,2},{5,3},{6,4},{7,5},{8,6},{9,7},{10,8},{11,9},{12,... | collective-permute-start | bytes 491528 | tf_op jit(solution)/shard_map/ppermute | solution.py:605
  32.7 4.2 %collective-permute-start.13 = (bf16[192,128]{1,0:T(8,128)(2,1)S(1)}, bf16[192,128]{1,0:T(8,128)(2,1)S(1)}, u32[]{:S(2)}, u32[]{:S(2)}) collective-permute-start(bf16[192,128]{1,0:T(8,128)(2,1)S(1)} %shard_map.87.refs_0_.refs_1_), channel_id=1, source_target_pairs={{0,16},{1,17},{2,18},{3,19},{4,20},{5,21},{6,22},{7,23},{8,24},{9,... | collective-permute-start | bytes 147464 | tf_op jit(solution)/shard_map/ppermute | solution.py:656
  36.9 1.4 %collective-permute-start.14 = (f32[192,128]{1,0:T(8,128)S(1)}, f32[192,128]{1,0:T(8,128)S(1)}, u32[]{:S(2)}, u32[]{:S(2)}) collective-permute-start(f32[192,128]{1,0:T(8,128)S(1)} %shard_map.89.refs_0_), channel_id=1, source_target_pairs={{0,1},{1,0},{2,3},{3,2},{4,5},{5,4},{6,7},{7,6},{8,9},{9,8},{10,11... | collective-permute-start | bytes 294920 | tf_op jit(solution)/shard_map/ppermute | solution.py:656

commit v10 on v9

--- a/solution.py
+++ b/solution.py
@@ -265,10 +265,12 @@
             x = jnp.concatenate(block, axis=0).astype(BF16)
             vt[p, :, 128 * (j + 1) : 128 * (j + 2)] = x.T
     full = None
-    for q in range(half // per):
-        fill(q)
-        fill(q + half // per)
+    count = half // per
+    fill(0)
+    fill(count)
+    for q in range(count):
         first, size = q * per, per * 128
+        sums_of = []
         for p in range(pairs):
             left = jnp.concatenate(
                 [vt[p, :, 128 * (2 - a + first) : 128 * (2 - a + first) + size] for a in range(3)], axis=0
@@ -287,7 +289,11 @@
                 ],
                 axis=0,
             )
-            part = dot(left, right)
+            sums_of.append(dot(left, right))
+        if q + 1 < count:
+            fill(q + 1)
+            fill(q + 1 + count)
+        for part in sums_of:
             full = part if full is None else full + part
     keep = lanes((groups, 128)) < 3 * feat
     sums[...] = jnp.zeros(sums.shape, F32)
@@ -453,15 +459,21 @@
     parts = sems.shape[0]
     step = disp // 2 // parts
     copies = []
-    build(0)
-    for q in range(parts):
+
+    def build_part(q):
         for dd in range(q * step + 1, min((q + 1) * step + 1, disp // 2)):
             build(dd)
+
+    build(0)
+    build_part(0)
+    for q in range(parts):
         slabs = [
             taps[q * step + s // 2 : q * step + s // 2 + step, s % 2].reshape(step * cols, taps.shape[3])
             for s in range(4)
         ]
         acc = dot(jnp.concatenate(slabs, axis=1), wc[...])
+        if q + 1 < parts:
+            build_part(q + 1)
         for j in range(step):
             both = acc[j * cols : (j + 1) * cols].astype(BF16).T
             for o in range(2):

time: 39.6 us -> 39.6 us (level)
  no operation moved by 1% of the time
where the time goes in v10:
time: 39.6 us; the launch traced here: 39.4 us
  starting transfers between devices  19.8 us (50%)
  Pallas kernels  13 us (33%)
  waiting for transfers between devices  5.63 us (14%)
  between operations  0.85 us (2%)
    pallas_call x17, Pallas kernels, call(): pl.pallas_call(lambda *refs: kernel(*refs[skip:]), out_shape=[jax.ShapeDt...  13 us
    ppermute x10, starting transfers between devices, swap(): return lax.ppermute(block, ('row', 'col'), route)  9.61 us
    ppermute x2, starting transfers between devices, col_shift(): return lax.ppermute(block, 'col', route)  6.31 us
    ppermute x10, waiting for transfers between devices, swap(): return lax.ppermute(block, ('row', 'col'), route)  4.33 us
    ppermute x3, starting transfers between devices, halos(): got = lax.ppermute(pays[0], 'row', [(0, 1), (1, 0)])  3.25 us
    ppermute x2, waiting for transfers between devices, col_shift(): return lax.ppermute(block, 'col', route)  1.29 us
  transfers between devices with their start and end apart: 16, of which 7 were waited for; matrix products, arithmetic and copies ran while one was open for 0% of the time, Pallas kernels for 30%

profile of v10, /device:TPU:0, one launch (start us, length us, event | category | flops | bytes accessed | tf_op | source)
XLA Modules:
  0.0 39.4 jit_solution(14147867370025847654)
XLA Ops:
  0.6 0.0 copy-start
  0.6 0.0 copy-start.3
  0.7 0.0 copy-start.2
  0.7 5.0 %collective-permute-start = (bf16[4,64,320]{2,1,0:T(8,128)(2,1)}, bf16[4,64,320]{2,1,0:T(8,128)(2,1)S(1)}, u32[]{:S(2)}, u32[]{:S(2)}) collective-permute-start(bf16[4,64,320]{2,1,0:T(8,128)(2,1)} %refs_1_.5), channel_id=1, source_target_pairs={{0,2},{1,3},{2,4},{3,5},{4,6},{5,7},{6,8},{7,9},{8,10},{9,11},{10,... | collective-permute-start | bytes 491528 | tf_op jit(solution)/shard_map/ppermute | solution.py:617
  5.7 0.0 copy-done
  5.7 0.0 copy-done.3
  5.7 0.0 copy-done.2
  5.7 0.3 shard_map.76
  6.1 0.1 collective-permute-start.2
  6.1 0.7 %collective-permute-start.3 = (bf16[32,320]{1,0:T(8,128)(2,1)S(1)}, bf16[32,320]{1,0:T(8,128)(2,1)S(1)}, u32[]{:S(2)}, u32[]{:S(2)}) collective-permute-start(bf16[32,320]{1,0:T(8,128)(2,1)S(1)} %get-tuple-element.34), channel_id=1, source_target_pairs={{1,2},{3,4},{5,6},{7,8},{9,10},{11,12},{13,14},{2,1},{4,3},{6,5},{... | collective-permute-start | bytes 61448 | tf_op jit(solution)/shard_map/ppermute | solution.py:689
  6.8 1.6 %collective-permute-start.4 = (bf16[6,64,128]{2,1,0:T(8,128)(2,1)S(1)}, bf16[6,64,128]{2,1,0:T(8,128)(2,1)S(1)}, u32[]{:S(2)}, u32[]{:S(2)}) collective-permute-start(bf16[6,64,128]{2,1,0:T(8,128)(2,1)S(1)} %get-tuple-element.38), channel_id=1, source_target_pairs={{0,16},{16,0},{1,17},{17,1},{2,18},{18,2},{3,19},{19,3},{4,20},{20... | collective-permute-start | bytes 294920 | tf_op jit(solution)/shard_map/ppermute | solution.py:628
  8.4 0.5 %shard_map.77 = (f32[4,80,512]{2,1,0:T(8,128)S(1)}, f32[4,176,512]{2,1,0:T(8,128)S(1)}, f32[4,176,512]{2,1,0:T(8,128)S(1)}) custom-call(bf16[24,64,128]{2,1,0:T(8,128)(2,1)S(1)} %get-tuple-element.31.refs_0_.refs_1_, bf16[4,64,320]{2,1,0:T(8,128)(2,1)S(1)} %copy-done.2, bf16[4,64,320]{2,1,0:T(8,128)(2,1)S(1)} %copy-done), custom_call_target="tpu_custom_call" | custom-call | tf_op jit(solution)/shard_map/pallas_call | solution.py:600
  8.8 1.3 %collective-permute-done.refs_2_.refs_1_ = bf16[4,64,320]{2,1,0:T(8,128)(2,1)S(1)} collective-permute-done((bf16[4,64,320]{2,1,0:T(8,128)(2,1)}, bf16[4,64,320]{2,1,0:T(8,128)(2,1)S(1)}, u32[]{:S(2)}, u32[]{:S(2)}) %collective-permute-start) | collective-permute-done | bytes 163872 | tf_op jit(solution)/shard_map/ppermute | solution.py:617
  10.1 0.1 shard_map.78.refs_0_
  10.2 1.4 %collective-permute-start.1 = (bf16[4,64,320]{2,1,0:T(8,128)(2,1)S(1)}, bf16[4,64,320]{2,1,0:T(8,128)(2,1)S(1)}, u32[]{:S(2)}, u32[]{:S(2)}) collective-permute-start(bf16[4,64,320]{2,1,0:T(8,128)(2,1)S(1)} %shard_map.78.refs_0_), channel_id=1, source_target_pairs={{0,1},{1,0},{2,3},{3,2},{4,5},{5,4},{6,7},{7,6},{8,9},{9,8},{10,11... | collective-permute-start | bytes 491528 | tf_op jit(solution)/shard_map/ppermute | solution.py:668
  11.6 0.0 collective-permute-done.2.refs_2_.refs_1_
  11.6 0.0 collective-permute-done.3.refs_3_.refs_2_
  11.6 0.1 shard_map.80
  11.7 0.6 %collective-permute-start.5 = (bf16[16,128]{1,0:T(8,128)(2,1)S(1)}, bf16[16,128]{1,0:T(8,128)(2,1)S(1)}, u32[]{:S(2)}, u32[]{:S(2)}) collective-permute-start(bf16[16,128]{1,0:T(8,128)(2,1)S(1)} %shard_map.80), channel_id=1, source_target_pairs={{0,16},{16,0},{1,17},{17,1},{2,18},{18,2},{3,19},{19,3},{4,20},{20... | collective-permute-start | bytes 12296 | tf_op jit(solution)/shard_map/ppermute | solution.py:628
  12.2 0.4 %collective-permute-done.1.refs_0_ = bf16[4,64,320]{2,1,0:T(8,128)(2,1)S(1)} collective-permute-done((bf16[4,64,320]{2,1,0:T(8,128)(2,1)S(1)}, bf16[4,64,320]{2,1,0:T(8,128)(2,1)S(1)}, u32[]{:S(2)}, u32[]{:S(2)}) %collective-permute-start.1) | collective-permute-done | bytes 163872 | tf_op jit(solution)/shard_map/ppermute | solution.py:668
  12.6 1.6 %shard_map.79 = (f32[4,80,512]{2,1,0:T(8,128)S(1)}, f32[4,176,512]{2,1,0:T(8,128)S(1)}, f32[4,176,512]{2,1,0:T(8,128)S(1)}, f32[2,24,80,128]{3,2,1,0:T(8,128)S(1)}, bf16[960,128]{1,0:T(8,128)(2,1)S(1)}) custom-call(bf16[4,64,320]{2,1,0:T(8,128)(2,1)S(1)} %collective-permute-done.1.refs_0_, ...), custom_call_target="tpu_custom_call", output_to_operand_aliasing={{0}: (4, {}), {1}: (5, {}), {2}: (6, {})} | custom-call | flops 2070000000 | bytes 6660000 | tf_op jit(solution)/shard_map/pallas_call | solution.py:600
  14.2 1.1 %collective-permute-start.7 = (bf16[960,128]{1,0:T(8,128)(2,1)S(1)}, bf16[960,128]{1,0:T(8,128)(2,1)S(1)}, u32[]{:S(2)}, u32[]{:S(2)}) collective-permute-start(bf16[960,128]{1,0:T(8,128)(2,1)S(1)} %get-tuple-element.45), channel_id=1, source_target_pairs={{0,16},{16,0},{1,17},{17,1},{2,18},{18,2},{3,19},{19,3},{4,20},{20... | collective-permute-start | bytes 737288 | tf_op jit(solution)/shard_map/ppermute | solution.py:628
  15.4 0.0 collective-permute-done.4.refs_4_.refs_5_
  15.4 0.0 collective-permute-done.5.refs_6_.refs_7_
  15.4 0.0 copy-start.1
  15.4 1.9 %shard_map.81 = (f32[192,128]{1,0:T(8,128)S(1)}, f32[192,128]{1,0:T(8,128)S(1)}, bf16[13,2,64,768]{3,2,1,0:T(8,128)(2,1)S(1)}) custom-call(f32[2,24,80,128]{3,2,1,0:T(8,128)S(1)} %get-tuple-element.37.refs_0_.refs_1_, bf16[24,64,128]{2,1,0:T(8,128)(2,1)S(1)} %get-tuple-element.31.refs_0_.refs_1_, bf16[32,320]{1,0:T(8,128)(2,1)S(1)} %collective-permute-done.2.refs_2_.refs_1_, ...), custom_call_target="tpu_custom_call" | custom-call | flops 2300000000 | bytes 7400000 | tf_op jit(solution)/shard_map/pallas_call | solution.py:600
  17.3 0.1 collective-permute-start.6
  17.4 0.0 copy-done.1
  17.4 0.8 %shard_map.82 = (bf16[1536,256]{1,0:T(8,128)(2,1)S(1)}, bf16[3072,256]{1,0:T(8,128)(2,1)S(1)}) custom-call(f32[192,128]{1,0:T(8,128)S(1)} %get-tuple-element.39.refs_0_.refs_1_, bf16[3,3,3,32,40]{4,3,2,1,0:T(8,128)(2,1)S(1)} %bitcast.4), custom_call_target="tpu_custom_call" | custom-call | tf_op jit(solution)/shard_map/pallas_call | solution.py:600
  18.2 0.4 %collective-permute-done.6.refs_2_ = f32[192,128]{1,0:T(8,128)S(1)} collective-permute-done((f32[192,128]{1,0:T(8,128)S(1)}, f32[192,128]{1,0:T(8,128)S(1)}, u32[]{:S(2)}, u32[]{:S(2)}) %collective-permute-start.6) | collective-permute-done | bytes 98336 | tf_op jit(solution)/shard_map/ppermute | solution.py:668
  18.7 2.9 %collective-permute-start.10 = (bf16[192,128]{1,0:T(8,128)(2,1)S(1)}, bf16[192,128]{1,0:T(8,128)(2,1)S(1)}, u32[]{:S(2)}, u32[]{:S(2)}) collective-permute-start(bf16[192,128]{1,0:T(8,128)(2,1)S(1)} %shard_map.83.refs_0_.refs_2_), channel_id=1, source_target_pairs={{0,6},{1,7},{2,4},{3,5},{4,2},{5,3},{6,0},{7,1},{8,14},{9,15},{10,... | collective-permute-start | bytes 147464 | tf_op jit(solution)/shard_map/ppermute | solution.py:668
  21.6 1.4 %collective-permute-start.8 = (bf16[192,128]{1,0:T(8,128)(2,1)S(1)}, bf16[192,128]{1,0:T(8,128)(2,1)S(1)}, u32[]{:S(2)}, u32[]{:S(2)}) collective-permute-start(bf16[192,128]{1,0:T(8,128)(2,1)S(1)} %shard_map.83.refs_0_.refs_2_), channel_id=1, source_target_pairs={{0,2},{1,3},{2,0},{3,1},{4,6},{5,7},{6,4},{7,5},{8,10},{9,11},{10,... | collective-permute-start | bytes 147464 | tf_op jit(solution)/shard_map/ppermute | solution.py:668
  23.0 0.0 collective-permute-start.9
  23.0 2.4 %shard_map.84 = (f32[2,24,64,128]{3,2,1,0:T(8,128)S(1)}, f32[2,24,64,128]{3,2,1,0:T(8,128)S(1)}, bf16[4,64,320]{2,1,0:T(8,128)(2,1)S(1)}, bf16[4,64,320]{2,1,0:T(8,128)(2,1)S(1)}, bf16[4,32,320]{2,1,0:T(8,128)(2,1)S(1)}) custom-call(bf16[192,128]{1,0:T(8,128)(2,1)S(1)} %shard_map.83.refs_0_.refs_2_, bf16[13,2,64,768]{3,2,1,0:T(8,128)(2,1)S(1)} %get-tuple-element.42.refs_1_, ...), custom_call_target="tpu_custom_call" | custom-call | flops 460000000 | bytes 1480000 | tf_op jit(solution)/shard_map/pallas_call | solution.py:600
  25.5 0.1 collective-permute-start.11
  25.6 0.0 collective-permute-done.10.refs_5_
  25.6 0.1 collective-permute-done.8.refs_3_
  25.7 1.4 %collective-permute-done.9.refs_4_ = bf16[192,128]{1,0:T(8,128)(2,1)S(1)} collective-permute-done((bf16[192,128]{1,0:T(8,128)(2,1)S(1)}, bf16[192,128]{1,0:T(8,128)(2,1)S(1)}, u32[]{:S(2)}, u32[]{:S(2)}) %collective-permute-start.9) | collective-permute-done | bytes 49184 | tf_op jit(solution)/shard_map/ppermute | solution.py:668
  27.1 0.0 collective-permute-done.7.refs_1_.refs_2_.refs_3_
  27.2 2.7 %collective-permute-start.12 = (bf16[192,128]{1,0:T(8,128)(2,1)S(1)}, bf16[192,128]{1,0:T(8,128)(2,1)S(1)}, u32[]{:S(2)}, u32[]{:S(2)}) collective-permute-start(bf16[192,128]{1,0:T(8,128)(2,1)S(1)} %shard_map.85.refs_0_.refs_1_), channel_id=1, source_target_pairs={{0,8},{1,9},{2,10},{3,11},{4,12},{5,13},{6,14},{7,15},{8,0},{9,1},... | collective-permute-start | bytes 147464 | tf_op jit(solution)/shard_map/ppermute | solution.py:668
  29.8 0.0 collective-permute-done.11.refs_1_.refs_3_
  29.8 0.1 shard_map.86.refs_0_
  29.9 1.3 %collective-permute-start.15 = (bf16[4,64,320]{2,1,0:T(8,128)(2,1)S(1)}, bf16[4,64,320]{2,1,0:T(8,128)(2,1)S(1)}, u32[]{:S(2)}, u32[]{:S(2)}) collective-permute-start(bf16[4,64,320]{2,1,0:T(8,128)(2,1)S(1)} %shard_map.86.refs_0_), channel_id=1, source_target_pairs={{2,0},{3,1},{4,2},{5,3},{6,4},{7,5},{8,6},{9,7},{10,8},{11,9},{12,... | collective-permute-start | bytes 491528 | tf_op jit(solution)/shard_map/ppermute | solution.py:617
  31.2 1.5 %collective-permute-done.12.refs_2_ = bf16[192,128]{1,0:T(8,128)(2,1)S(1)} collective-permute-done((bf16[192,128]{1,0:T(8,128)(2,1)S(1)}, bf16[192,128]{1,0:T(8,128)(2,1)S(1)}, u32[]{:S(2)}, u32[]{:S(2)}) %collective-permute-start.12) | collective-permute-done | bytes 49184 | tf_op jit(solution)/shard_map/ppermute | solution.py:668
  32.7 0.9 %collective-permute-start.13 = (bf16[192,128]{1,0:T(8,128)(2,1)S(1)}, bf16[192,128]{1,0:T(8,128)(2,1)S(1)}, u32[]{:S(2)}, u32[]{:S(2)}) collective-permute-start(bf16[192,128]{1,0:T(8,128)(2,1)S(1)} %shard_map.87.refs_0_.refs_1_), channel_id=1, source_target_pairs={{0,16},{1,17},{2,18},{3,19},{4,20},{5,21},{6,22},{7,23},{8,24},{9,... | collective-permute-start | bytes 147464 | tf_op jit(solution)/shard_map/ppermute | solution.py:668
  33.7 2.8 %shard_map.88 = (bf16[24,4,32,64]{3,2,1,0:T(8,128)(2,1)}, f32[8,128]{1,0:T(8,128)S(1)}) custom-call(bf16[192,128]{1,0:T(8,128)(2,1)S(1)} %shard_map.87.refs_0_.refs_1_, f32[2,24,80,128]{3,2,1,0:T(8,128)S(1)} %get-tuple-element.37.refs_0_.refs_1_, bf16[960,128]{1,0:T(8,128)(2,1)S(1)} %collective-permute-done.7.refs_1_.refs_2_.refs_3_, ...), custom_call_target="tpu_custom_call" | custom-call | flops 3449999872 | bytes 11100000 | tf_op jit(solution)/shard_map/pallas_call | solution.py:600
  36.5 0.4 collective-permute-done.13.refs_2_
  36.9 0.1 collective-permute-start.14
  37.0 1.3 %shard_map.90.refs_5_ = bf16[4,64,320]{2,1,0:T(8,128)(2,1)S(1)} custom-call(f32[192,128]{1,0:T(8,128)S(1)} %shard_map.89.refs_0_, f32[4,176,512]{2,1,0:T(8,128)S(1)} %get-tuple-element.51.refs_1_, f32[4,176,512]{2,1,0:T(8,128)S(1)} %get-tuple-element.52.refs_2_, f32[2,24,64,128]{3,2,1,0:T(8,128)S(1)} %get-tuple-element.53.refs_3_, ...), custom_call_target="tpu_custom_call" | custom-call | flops 2184999936 | bytes 7030000 | tf_op jit(solution)/shard_map/pallas_call | solution.py:600
  38.3 0.0 collective-permute-done.15.refs_4_
  38.3 0.0 collective-permute-done.14.refs_1_
  38.3 1.1 %shard_map.91 = (f32[3,3,3,32,40]{4,3,2,1,0:T(8,128)}, bf16[4,64,320]{2,1,0:T(8,128)(2,1)}, bf16[4,64,320]{2,1,0:T(8,128)(2,1)}) custom-call(f32[192,128]{1,0:T(8,128)S(1)} %shard_map.89.refs_0_, f32[192,128]{1,0:T(8,128)S(1)} %collective-permute-done.14.refs_1_, bf16[4,64,320]{2,1,0:T(8,128)(2,1)S(1)} %get-tuple-element.44.refs_0_.refs_2_, ...), custom_call_target="tpu_custom_call" | custom-call | flops 1150000000 | bytes 3700000 | tf_op jit(solution)/shard_map/pallas_call | solution.py:600
  (5 shorter events, 0.1 us)
Async XLA Ops:
  0.6 5.1 %copy-start = (bf16[4,64,320]{2,1,0:T(8,128)(2,1)S(1)}, bf16[4,64,320]{2,1,0:T(8,128)(2,1)}, u32[]{:S(2)}) copy-start(bf16[4,64,320]{2,1,0:T(8,128)(2,1)} %refs_1_.5) | copy-start | bytes 491524
  0.6 5.1 %copy-start.3 = (bf16[24,4,64,32]{2,3,1,0:T(8,128)(2,1)S(1)}, bf16[24,4,64,32]{2,3,1,0:T(8,128)(2,1)}, u32[]{:S(2)}) copy-start(bf16[24,4,64,32]{2,3,1,0:T(8,128)(2,1)} %param.7) | copy-start | bytes 1179652
  0.7 5.1 %copy-start.2 = (bf16[4,64,320]{2,1,0:T(8,128)(2,1)S(1)}, bf16[4,64,320]{2,1,0:T(8,128)(2,1)}, u32[]{:S(2)}) copy-start(bf16[4,64,320]{2,1,0:T(8,128)(2,1)} %refs_1_.4) | copy-start | bytes 491524
  0.7 9.5 %collective-permute-start = (bf16[4,64,320]{2,1,0:T(8,128)(2,1)}, bf16[4,64,320]{2,1,0:T(8,128)(2,1)S(1)}, u32[]{:S(2)}, u32[]{:S(2)}) collective-permute-start(bf16[4,64,320]{2,1,0:T(8,128)(2,1)} %refs_1_.5), channel_id=1, source_target_pairs={{0,2},{1,3},{2,4},{3,5},{4,6},{5,7},{6,8},{7,9},{8,10},{9,11},{10,... | collective-permute-start | bytes 491528 | tf_op jit(solution)/shard_map/ppermute | solution.py:617
  6.1 5.5 %collective-permute-start.2 = (bf16[32,320]{1,0:T(8,128)(2,1)S(1)}, bf16[32,320]{1,0:T(8,128)(2,1)S(1)}, u32[]{:S(2)}, u32[]{:S(2)}) collective-permute-start(bf16[32,320]{1,0:T(8,128)(2,1)S(1)} %get-tuple-element.33), channel_id=1, source_target_pairs={{0,1},{1,0},{2,3},{3,2},{4,5},{5,4},{6,7},{7,6},{8,9},{9,8},{10,11... | collective-permute-start | bytes 61448 | tf_op jit(solution)/shard_map/ppermute | solution.py:668
  6.1 5.4 %collective-permute-start.3 = (bf16[32,320]{1,0:T(8,128)(2,1)S(1)}, bf16[32,320]{1,0:T(8,128)(2,1)S(1)}, u32[]{:S(2)}, u32[]{:S(2)}) collective-permute-start(bf16[32,320]{1,0:T(8,128)(2,1)S(1)} %get-tuple-element.34), channel_id=1, source_target_pairs={{1,2},{3,4},{5,6},{7,8},{9,10},{11,12},{13,14},{2,1},{4,3},{6,5},{... | collective-permute-start | bytes 61448 | tf_op jit(solution)/shard_map/ppermute | solution.py:689
  6.8 8.6 %collective-permute-start.4 = (bf16[6,64,128]{2,1,0:T(8,128)(2,1)S(1)}, bf16[6,64,128]{2,1,0:T(8,128)(2,1)S(1)}, u32[]{:S(2)}, u32[]{:S(2)}) collective-permute-start(bf16[6,64,128]{2,1,0:T(8,128)(2,1)S(1)} %get-tuple-element.38), channel_id=1, source_target_pairs={{0,16},{16,0},{1,17},{17,1},{2,18},{18,2},{3,19},{19,3},{4,20},{20... | collective-permute-start | bytes 294920 | tf_op jit(solution)/shard_map/ppermute | solution.py:628
  10.2 2.5 %collective-permute-start.1 = (bf16[4,64,320]{2,1,0:T(8,128)(2,1)S(1)}, bf16[4,64,320]{2,1,0:T(8,128)(2,1)S(1)}, u32[]{:S(2)}, u32[]{:S(2)}) collective-permute-start(bf16[4,64,320]{2,1,0:T(8,128)(2,1)S(1)} %shard_map.78.refs_0_), channel_id=1, source_target_pairs={{0,1},{1,0},{2,3},{3,2},{4,5},{5,4},{6,7},{7,6},{8,9},{9,8},{10,11... | collective-permute-start | bytes 491528 | tf_op jit(solution)/shard_map/ppermute | solution.py:668
  11.7 3.7 %collective-permute-start.5 = (bf16[16,128]{1,0:T(8,128)(2,1)S(1)}, bf16[16,128]{1,0:T(8,128)(2,1)S(1)}, u32[]{:S(2)}, u32[]{:S(2)}) collective-permute-start(bf16[16,128]{1,0:T(8,128)(2,1)S(1)} %shard_map.80), channel_id=1, source_target_pairs={{0,16},{16,0},{1,17},{17,1},{2,18},{18,2},{3,19},{19,3},{4,20},{20... | collective-permute-start | bytes 12296 | tf_op jit(solution)/shard_map/ppermute | solution.py:628
  14.2 12.9 %collective-permute-start.7 = (bf16[960,128]{1,0:T(8,128)(2,1)S(1)}, bf16[960,128]{1,0:T(8,128)(2,1)S(1)}, u32[]{:S(2)}, u32[]{:S(2)}) collective-permute-start(bf16[960,128]{1,0:T(8,128)(2,1)S(1)} %get-tuple-element.45), channel_id=1, source_target_pairs={{0,16},{16,0},{1,17},{17,1},{2,18},{18,2},{3,19},{19,3},{4,20},{20... | collective-permute-start | bytes 737288 | tf_op jit(solution)/shard_map/ppermute | solution.py:628
  15.4 2.0 %copy-start.1 = (bf16[3,3,3,40,32]{3,4,2,1,0:T(8,128)(2,1)S(1)}, bf16[3,3,3,40,32]{3,4,2,1,0:T(8,128)(2,1)}, u32[]{:S(2)}) copy-start(bf16[3,3,3,40,32]{3,4,2,1,0:T(8,128)(2,1)} %param.6) | copy-start | bytes 207364
  17.3 1.4 %collective-permute-start.6 = (f32[192,128]{1,0:T(8,128)S(1)}, f32[192,128]{1,0:T(8,128)S(1)}, u32[]{:S(2)}, u32[]{:S(2)}) collective-permute-start(f32[192,128]{1,0:T(8,128)S(1)} %get-tuple-element.41), channel_id=1, source_target_pairs={{0,1},{1,0},{2,3},{3,2},{4,5},{5,4},{6,7},{7,6},{8,9},{9,8},{10,11... | collective-permute-start | bytes 294920 | tf_op jit(solution)/shard_map/ppermute | solution.py:668
  18.7 6.9 %collective-permute-start.10 = (bf16[192,128]{1,0:T(8,128)(2,1)S(1)}, bf16[192,128]{1,0:T(8,128)(2,1)S(1)}, u32[]{:S(2)}, u32[]{:S(2)}) collective-permute-start(bf16[192,128]{1,0:T(8,128)(2,1)S(1)} %shard_map.83.refs_0_.refs_2_), channel_id=1, source_target_pairs={{0,6},{1,7},{2,4},{3,5},{4,2},{5,3},{6,0},{7,1},{8,14},{9,15},{10,... | collective-permute-start | bytes 147464 | tf_op jit(solution)/shard_map/ppermute | solution.py:668
  21.6 4.1 %collective-permute-start.8 = (bf16[192,128]{1,0:T(8,128)(2,1)S(1)}, bf16[192,128]{1,0:T(8,128)(2,1)S(1)}, u32[]{:S(2)}, u32[]{:S(2)}) collective-permute-start(bf16[192,128]{1,0:T(8,128)(2,1)S(1)} %shard_map.83.refs_0_.refs_2_), channel_id=1, source_target_pairs={{0,2},{1,3},{2,0},{3,1},{4,6},{5,7},{6,4},{7,5},{8,10},{9,11},{10,... | collective-permute-start | bytes 147464 | tf_op jit(solution)/shard_map/ppermute | solution.py:668
  23.0 4.1 %collective-permute-start.9 = (bf16[192,128]{1,0:T(8,128)(2,1)S(1)}, bf16[192,128]{1,0:T(8,128)(2,1)S(1)}, u32[]{:S(2)}, u32[]{:S(2)}) collective-permute-start(bf16[192,128]{1,0:T(8,128)(2,1)S(1)} %shard_map.83.refs_0_.refs_2_), channel_id=1, source_target_pairs={{0,4},{1,5},{2,6},{3,7},{4,0},{5,1},{6,2},{7,3},{8,12},{9,13},{10,... | collective-permute-start | bytes 147464 | tf_op jit(solution)/shard_map/ppermute | solution.py:668
  25.5 4.3 %collective-permute-start.11 = (bf16[4,64,320]{2,1,0:T(8,128)(2,1)S(1)}, bf16[4,64,320]{2,1,0:T(8,128)(2,1)S(1)}, u32[]{:S(2)}, u32[]{:S(2)}) collective-permute-start(bf16[4,64,320]{2,1,0:T(8,128)(2,1)S(1)} %get-tuple-element.46), channel_id=1, source_target_pairs={{0,1},{1,0},{2,3},{3,2},{4,5},{5,4},{6,7},{7,6},{8,9},{9,8},{10,11... | collective-permute-start | bytes 491528 | tf_op jit(solution)/shard_map/ppermute | solution.py:668
  27.2 5.5 %collective-permute-start.12 = (bf16[192,128]{1,0:T(8,128)(2,1)S(1)}, bf16[192,128]{1,0:T(8,128)(2,1)S(1)}, u32[]{:S(2)}, u32[]{:S(2)}) collective-permute-start(bf16[192,128]{1,0:T(8,128)(2,1)S(1)} %shard_map.85.refs_0_.refs_1_), channel_id=1, source_target_pairs={{0,8},{1,9},{2,10},{3,11},{4,12},{5,13},{6,14},{7,15},{8,0},{9,1},... | collective-permute-start | bytes 147464 | tf_op jit(solution)/shard_map/ppermute | solution.py:668
  29.9 8.4 %collective-permute-start.15 = (bf16[4,64,320]{2,1,0:T(8,128)(2,1)S(1)}, bf16[4,64,320]{2,1,0:T(8,128)(2,1)S(1)}, u32[]{:S(2)}, u32[]{:S(2)}) collective-permute-start(bf16[4,64,320]{2,1,0:T(8,128)(2,1)S(1)} %shard_map.86.refs_0_), channel_id=1, source_target_pairs={{2,0},{3,1},{4,2},{5,3},{6,4},{7,5},{8,6},{9,7},{10,8},{11,9},{12,... | collective-permute-start | bytes 491528 | tf_op jit(solution)/shard_map/ppermute | solution.py:617
  32.7 4.2 %collective-permute-start.13 = (bf16[192,128]{1,0:T(8,128)(2,1)S(1)}, bf16[192,128]{1,0:T(8,128)(2,1)S(1)}, u32[]{:S(2)}, u32[]{:S(2)}) collective-permute-start(bf16[192,128]{1,0:T(8,128)(2,1)S(1)} %shard_map.87.refs_0_.refs_1_), channel_id=1, source_target_pairs={{0,16},{1,17},{2,18},{3,19},{4,20},{5,21},{6,22},{7,23},{8,24},{9,... | collective-permute-start | bytes 147464 | tf_op jit(solution)/shard_map/ppermute | solution.py:668
  36.9 1.4 %collective-permute-start.14 = (f32[192,128]{1,0:T(8,128)S(1)}, f32[192,128]{1,0:T(8,128)S(1)}, u32[]{:S(2)}, u32[]{:S(2)}) collective-permute-start(f32[192,128]{1,0:T(8,128)S(1)} %shard_map.89.refs_0_), channel_id=1, source_target_pairs={{0,1},{1,0},{2,3},{3,2},{4,5},{5,4},{6,7},{7,6},{8,9},{9,8},{10,11... | collective-permute-start | bytes 294920 | tf_op jit(solution)/shard_map/ppermute | solution.py:668
